TPU v7x, 32 devices: a whole 2x2x4 slice. The times are simulated.
32 devices in a mesh: seq: 16 (over z, x, core), batch: 2 (over y).
Axes of the slice: x: 2, y: 2, z: 4, core: 2. Of those that a mesh axis runs over, the one named last changes fastest.
Arguments:
- tokens: bfloat16 [2, 2048, 1536], P('batch', 'seq'), may hold values from -6 to 6
- doc_ids: int32 [2, 2048], P('batch', 'seq'), may hold values from 0 to 3, never falling along the last dimension, each value on 1 to 1024 neighbouring positions
- norm_gain: float32 [1536], P(('seq', 'batch')), may hold values from 0.5 to 1.5
- query_weight: float32 [1536, 1536], P(('seq', 'batch')), may hold values from -0.15625 to 0.15625
- key_weight: float32 [1536, 1536], P(('seq', 'batch')), may hold values from -0.15625 to 0.15625
- value_weight: float32 [1536, 1536], P(('seq', 'batch')), may hold values from -0.15625 to 0.15625
- house_weight: float32 [1536, 1536], P(('seq', 'batch')), may hold values from -0.15625 to 0.15625
- beta_weight: float32 [1536, 12], P(('seq', 'batch')), may hold values from -0.3125 to 0.3125
- out_weight: float32 [1536, 1536], P(('seq', 'batch')), may hold values from -1.75 to 1.75
- ffn_gain: float32 [1536], P(('seq', 'batch')), may hold values from 0.5 to 1.5
- gate_weight: float32 [1536, 4096], P(('seq', 'batch')), may hold values from -0.15625 to 0.15625
- up_weight: float32 [1536, 4096], P(('seq', 'batch')), may hold values from -0.15625 to 0.15625
- down_weight: float32 [4096, 1536], P(('seq', 'batch')), may hold values from -0.09375 to 0.09375
- cotangent: bfloat16 [2, 2048, 1536], P('batch', 'seq'), may hold values from -6 to 6
Outputs:
- output: bfloat16 [2, 2048, 1536], P('batch', 'seq')
- grad_tokens: bfloat16 [2, 2048, 1536], P('batch', 'seq')
- grad_norm_gain: float32 [1536], P(('seq', 'batch'))
- grad_query_weight: float32 [1536, 1536], P(('seq', 'batch'))
- grad_key_weight: float32 [1536, 1536], P(('seq', 'batch'))
- grad_value_weight: float32 [1536, 1536], P(('seq', 'batch'))
- grad_house_weight: float32 [1536, 1536], P(('seq', 'batch'))
- grad_beta_weight: float32 [1536, 12], P(('seq', 'batch'))
- grad_out_weight: float32 [1536, 1536], P(('seq', 'batch'))
- grad_ffn_gain: float32 [1536], P(('seq', 'batch'))
- grad_gate_weight: float32 [1536, 4096], P(('seq', 'batch'))
- grad_up_weight: float32 [1536, 4096], P(('seq', 'batch'))
- grad_down_weight: float32 [4096, 1536], P(('seq', 'batch'))
Inputs may be any that keep to these rules, and one draw needn't show every extreme that they name: `doc_ids`: documents cover consecutive positions of one sequence, numbered upward from 0; none holds more than 1024 positions and some holds exactly that many.
All inputs are finite; a program needn't handle non-finite values.
Results may differ from a plain program's by a relative error of at most 0.017.
The roundings to bfloat16 on the way count: a program that leaves them out, or rounds other values in their place, can miss the bound.
Values may be sent and summed in bfloat16 or wider, within the bound.
A program may use at most 448 MiB of HBM per device.

v0:
```python
import jax
import jax.numpy as jnp
from jax import lax
from jax.sharding import PartitionSpec as P

HEADS = 12
HEAD_DIM = 128


PRECISE = lax.Precision.HIGHEST
EPSILON = 1e-06
NEGATIVE = -1e30


def from_behind(value, axis, steps):
    count = lax.axis_size(axis)
    initial, last = (max(0, -steps), min(count, count - steps))
    return lax.ppermute(value, axis, [(source, source + steps) for source in range(initial, last)])


def low_dot(left, right):
    return jnp.dot(left, right, preferred_element_type=jnp.float32)


def rms_scale(values, gain):
    return values * lax.rsqrt(jnp.mean(values * values, axis=-1, keepdims=True) + EPSILON) * gain


def split_heads(values):
    return jnp.transpose(values.reshape(values.shape[0], HEADS, HEAD_DIM), (1, 0, 2))


def merge_heads(values):
    return jnp.transpose(values, (1, 0, 2)).reshape(values.shape[1], HEADS * HEAD_DIM)


def prepare(query_rows, key_rows, house_rows, rate_rows):
    block_rows = query_rows.shape[0]
    query_heads = split_heads(query_rows)
    key_heads = split_heads(key_rows)
    house_heads = split_heads(house_rows)
    unit_dirs = house_heads * lax.rsqrt(
        jnp.sum(house_heads * house_heads, axis=-1, keepdims=True) + EPSILON
    )
    strength = 2.0 * jax.nn.sigmoid(jnp.transpose(rate_rows))
    row_index = lax.broadcasted_iota(jnp.int32, (block_rows, block_rows), 0)
    col_index = lax.broadcasted_iota(jnp.int32, (block_rows, block_rows), 1)
    lower_mask = row_index > col_index
    causal_mask = row_index >= col_index
    zero_block = jnp.zeros((HEADS, block_rows, block_rows), jnp.float32)
    inner_dots = jnp.einsum("hsd,htd->hst", unit_dirs, unit_dirs, precision=PRECISE)
    system = jnp.eye(block_rows, dtype=jnp.float32)[None] + jnp.where(
        lower_mask[None], strength[:, :, None] * inner_dots, zero_block
    )
    project = jnp.where(
        causal_mask[None],
        jnp.einsum("hid,htd->hit", query_heads, unit_dirs, precision=PRECISE),
        zero_block,
    )
    coeffs = lax.linalg.triangular_solve(
        system, project, left_side=False, lower=True, transpose_a=False, unit_diagonal=True
    )
    carry_basis = lax.linalg.triangular_solve(
        system, unit_dirs, left_side=True, lower=True, transpose_a=True, unit_diagonal=True
    )
    reach_terms = jnp.where(
        lower_mask[None],
        strength[:, :, None] * jnp.einsum("htd,hjd->htj", unit_dirs, key_heads, precision=PRECISE),
        zero_block,
    )
    within = jnp.einsum("hid,hjd->hij", query_heads, key_heads, precision=PRECISE) - jnp.einsum(
        "hit,htj->hij", coeffs, reach_terms, precision=PRECISE
    )
    query_hat = query_heads - jnp.einsum(
        "hit,htd->hid", coeffs, strength[:, :, None] * unit_dirs, precision=PRECISE
    )
    key_hat = key_heads - jnp.einsum("htj,htd->hjd", reach_terms, carry_basis, precision=PRECISE)
    return (query_hat, key_hat, within, carry_basis, unit_dirs, strength)


def carry_keys(travel, carry_basis, unit_dirs, strength):
    weights_on = (
        jnp.einsum("hnd,htd->hnt", travel, unit_dirs, precision=PRECISE) * strength[:, None, :]
    )
    return travel - jnp.einsum("hnt,htd->hnd", weights_on, carry_basis, precision=PRECISE)


def on_device(
    tokens,
    doc_ids,
    norm_gain,
    query_weight,
    key_weight,
    value_weight,
    house_weight,
    beta_weight,
    out_weight,
    ffn_gain,
    gate_weight,
    up_weight,
    down_weight,
    cotangent,
):
    gathered = (
        lax.all_gather(norm_gain.astype(jnp.bfloat16), ("seq", "batch"), axis=0, tiled=True),
        lax.all_gather(query_weight.astype(jnp.bfloat16), ("seq", "batch"), axis=0, tiled=True),
        lax.all_gather(key_weight.astype(jnp.bfloat16), ("seq", "batch"), axis=0, tiled=True),
        lax.all_gather(value_weight.astype(jnp.bfloat16), ("seq", "batch"), axis=0, tiled=True),
        lax.all_gather(house_weight.astype(jnp.bfloat16), ("seq", "batch"), axis=0, tiled=True),
        lax.all_gather(beta_weight.astype(jnp.bfloat16), ("seq", "batch"), axis=0, tiled=True),
        lax.all_gather(out_weight.astype(jnp.bfloat16), ("seq", "batch"), axis=0, tiled=True),
        lax.all_gather(ffn_gain.astype(jnp.bfloat16), ("seq", "batch"), axis=0, tiled=True),
        lax.all_gather(gate_weight.astype(jnp.bfloat16), ("seq", "batch"), axis=0, tiled=True),
        lax.all_gather(up_weight.astype(jnp.bfloat16), ("seq", "batch"), axis=0, tiled=True),
        lax.all_gather(down_weight.astype(jnp.bfloat16), ("seq", "batch"), axis=0, tiled=True),
    )
    inputs = tokens[0].astype(jnp.float32)
    block_rows = inputs.shape[0]
    score_scale = HEAD_DIM ** (-0.5)
    cycle_size = lax.axis_size("seq")
    position = lax.axis_index("seq")
    gain_first = gathered[0].astype(jnp.float32)
    normed, pull_first = jax.vjp(rms_scale, inputs, gain_first)
    normed_low = normed.astype(jnp.bfloat16)
    query_rows = low_dot(normed_low, gathered[1])
    key_rows = low_dot(normed_low, gathered[2])
    value_rows = low_dot(normed_low, gathered[3])
    house_rows = low_dot(normed_low, gathered[4])
    rate_rows = low_dot(normed_low, gathered[5])
    prepared, pull_prep = jax.vjp(prepare, query_rows, key_rows, house_rows, rate_rows)
    query_hat, key_hat, within, carry_basis, unit_dirs, strength = prepared
    query_low = query_hat.astype(jnp.bfloat16)
    key_low = key_hat.astype(jnp.bfloat16)
    value_low = split_heads(value_rows.astype(jnp.bfloat16))
    doc_all = lax.all_gather(doc_ids, "seq", axis=1, tiled=True)[0]
    doc_own = doc_ids[0]
    row_index = lax.broadcasted_iota(jnp.int32, (block_rows, block_rows), 0)
    col_index = lax.broadcasted_iota(jnp.int32, (block_rows, block_rows), 1)
    local_mask = (row_index >= col_index) & (doc_own[:, None] == doc_own[None, :])
    local_scores = jnp.where(local_mask[None], within * score_scale, NEGATIVE)
    row_top = jnp.max(local_scores, axis=-1)
    local_weights = jnp.exp(local_scores - row_top[..., None])
    row_total = jnp.sum(local_weights, axis=-1)
    row_accum = jnp.einsum(
        "hij,hjd->hid",
        local_weights.astype(jnp.bfloat16),
        value_low,
        preferred_element_type=jnp.float32,
    )

    def cross_mask(step_index):
        source = position - step_index
        doc_start = jnp.maximum(source, 0) * block_rows
        doc_keys = lax.dynamic_slice_in_dim(doc_all, doc_start, block_rows)
        return (source >= 0) & (doc_own[:, None] == doc_keys[None, :])

    zero_store = jnp.zeros((cycle_size - 1,) + key_low.shape, jnp.bfloat16)
    stores = ()

    def forward_hop(step_index, loop_state):
        travel_keys, travel_values, row_top, row_total, row_accum, stores = loop_state
        travel_keys, travel_values = from_behind((travel_keys, travel_values), "seq", 1)
        key_mask = cross_mask(step_index)
        scores = jnp.where(
            key_mask[None],
            jnp.einsum("hid,hnd->hin", query_low, travel_keys, preferred_element_type=jnp.float32)
            * score_scale,
            NEGATIVE,
        )
        new_top = jnp.maximum(row_top, jnp.max(scores, axis=-1))
        factor = jnp.exp(row_top - new_top)
        cross_weights = jnp.exp(scores - new_top[..., None])
        row_total = row_total * factor + jnp.sum(cross_weights, axis=-1)
        row_accum = row_accum * factor[..., None] + jnp.einsum(
            "hin,hnd->hid",
            cross_weights.astype(jnp.bfloat16),
            travel_values,
            preferred_element_type=jnp.float32,
        )
        moved_keys = carry_keys(
            travel_keys.astype(jnp.float32), carry_basis, unit_dirs, strength
        ).astype(jnp.bfloat16)
        return (moved_keys, travel_values, new_top, row_total, row_accum, stores)

    loop_state = lax.fori_loop(
        1, cycle_size, forward_hop, (key_low, value_low, row_top, row_total, row_accum, stores)
    )
    unused_keys, unused_values, row_top, row_total, row_accum, stores = loop_state
    attended_heads = row_accum / row_total[..., None]
    attended_low = merge_heads(attended_heads).astype(jnp.bfloat16)
    hidden = inputs + low_dot(attended_low, gathered[6])
    gain_second = gathered[7].astype(jnp.float32)
    normed_two, pull_second = jax.vjp(rms_scale, hidden, gain_second)
    normed_two_low = normed_two.astype(jnp.bfloat16)
    gate_rows = low_dot(normed_two_low, gathered[8])
    upward = low_dot(normed_two_low, gathered[9])
    sigmoid_gate = jax.nn.sigmoid(gate_rows)
    silu_gate = gate_rows * sigmoid_gate
    active_low = (silu_gate * upward).astype(jnp.bfloat16)
    result = hidden + low_dot(active_low, gathered[10])
    output = result.astype(jnp.bfloat16)[None]
    regathered = (
        lax.all_gather(norm_gain.astype(jnp.bfloat16), ("seq", "batch"), axis=0, tiled=True),
        lax.all_gather(query_weight.astype(jnp.bfloat16), ("seq", "batch"), axis=0, tiled=True),
        lax.all_gather(key_weight.astype(jnp.bfloat16), ("seq", "batch"), axis=0, tiled=True),
        lax.all_gather(value_weight.astype(jnp.bfloat16), ("seq", "batch"), axis=0, tiled=True),
        lax.all_gather(house_weight.astype(jnp.bfloat16), ("seq", "batch"), axis=0, tiled=True),
        lax.all_gather(beta_weight.astype(jnp.bfloat16), ("seq", "batch"), axis=0, tiled=True),
        lax.all_gather(out_weight.astype(jnp.bfloat16), ("seq", "batch"), axis=0, tiled=True),
        lax.all_gather(ffn_gain.astype(jnp.bfloat16), ("seq", "batch"), axis=0, tiled=True),
        lax.all_gather(gate_weight.astype(jnp.bfloat16), ("seq", "batch"), axis=0, tiled=True),
        lax.all_gather(up_weight.astype(jnp.bfloat16), ("seq", "batch"), axis=0, tiled=True),
        lax.all_gather(down_weight.astype(jnp.bfloat16), ("seq", "batch"), axis=0, tiled=True),
    )
    grad_out = cotangent[0]
    grad_active = low_dot(grad_out, regathered[10].T)
    grad_gate = (
        grad_active * upward * (sigmoid_gate * (1.0 + gate_rows * (1.0 - sigmoid_gate)))
    ).astype(jnp.bfloat16)
    grad_up = (grad_active * silu_gate).astype(jnp.bfloat16)
    grad_normed_two = low_dot(grad_gate, regathered[8].T) + low_dot(grad_up, regathered[9].T)
    grad_hidden_norm, grad_gain_two = pull_second(grad_normed_two)
    grad_hidden = grad_out.astype(jnp.float32) + grad_hidden_norm
    grad_branch = grad_hidden.astype(jnp.bfloat16)
    grad_att = split_heads(low_dot(grad_branch, regathered[6].T).astype(jnp.bfloat16)).astype(
        jnp.float32
    )
    grad_scaled = (grad_att / row_total[..., None]).astype(jnp.bfloat16)
    grad_total = -jnp.sum(grad_att * attended_heads, axis=-1) / row_total
    final_local = jnp.exp(local_scores - row_top[..., None])
    grad_weights_local = jnp.einsum(
        "hid,hjd->hij", grad_scaled, value_low, preferred_element_type=jnp.float32
    )
    grad_within = final_local * (grad_weights_local + grad_total[..., None]) * score_scale
    grad_value_own = jnp.einsum(
        "hij,hid->hjd",
        final_local.astype(jnp.bfloat16),
        grad_scaled,
        preferred_element_type=jnp.float32,
    )

    def again_hop(step_index, again_state):
        travel_keys, travel_values, key_store, value_store = again_state
        travel_keys, travel_values = from_behind((travel_keys, travel_values), "seq", 1)
        key_store = lax.dynamic_update_index_in_dim(key_store, travel_keys, step_index - 1, 0)
        value_store = lax.dynamic_update_index_in_dim(value_store, travel_values, step_index - 1, 0)
        moved_keys = carry_keys(
            travel_keys.astype(jnp.float32), carry_basis, unit_dirs, strength
        ).astype(jnp.bfloat16)
        return (moved_keys, travel_values, key_store, value_store)

    again_state = lax.fori_loop(
        1, cycle_size, again_hop, (key_low, value_low, zero_store, zero_store)
    )
    key_store, value_store = (again_state[2], again_state[3])

    def backward_hop(counter, back_state):
        grad_keys, grad_values, grad_query, grad_basis, grad_units, grad_strength = back_state
        step_index = cycle_size - 1 - counter
        travel_keys = lax.dynamic_index_in_dim(key_store, step_index - 1, 0, keepdims=False)
        travel_values = lax.dynamic_index_in_dim(value_store, step_index - 1, 0, keepdims=False)
        key_mask = cross_mask(step_index)
        scores = jnp.where(
            key_mask[None],
            jnp.einsum("hid,hnd->hin", query_low, travel_keys, preferred_element_type=jnp.float32)
            * score_scale,
            NEGATIVE,
        )
        cross_weights = jnp.exp(scores - row_top[..., None])
        grad_weights = jnp.einsum(
            "hid,hnd->hin", grad_scaled, travel_values, preferred_element_type=jnp.float32
        )
        grad_raw = (cross_weights * (grad_weights + grad_total[..., None]) * score_scale).astype(
            jnp.bfloat16
        )
        grad_query = grad_query + jnp.einsum(
            "hin,hnd->hid", grad_raw, travel_keys, preferred_element_type=jnp.float32
        )
        local_keys = jnp.einsum(
            "hin,hid->hnd", grad_raw, query_low, preferred_element_type=jnp.float32
        )
        local_values = jnp.einsum(
            "hin,hid->hnd",
            cross_weights.astype(jnp.bfloat16),
            grad_scaled,
            preferred_element_type=jnp.float32,
        )
        unused_moved, pull_carry = jax.vjp(
            carry_keys, travel_keys.astype(jnp.float32), carry_basis, unit_dirs, strength
        )
        back_keys, back_basis, back_units, back_strength = pull_carry(grad_keys)
        grad_keys, grad_values = (
            from_behind((local_keys + back_keys).astype(jnp.bfloat16), "seq", -1).astype(
                jnp.float32
            ),
            from_behind((grad_values + local_values).astype(jnp.bfloat16), "seq", -1).astype(
                jnp.float32
            ),
        )
        return (
            grad_keys,
            grad_values,
            grad_query,
            grad_basis + back_basis,
            grad_units + back_units,
            grad_strength + back_strength,
        )

    zero_heads = jnp.zeros(key_low.shape, jnp.float32)
    back_state = lax.fori_loop(
        0,
        cycle_size - 1,
        backward_hop,
        (
            zero_heads,
            zero_heads,
            zero_heads,
            zero_heads,
            zero_heads,
            jnp.zeros(strength.shape, jnp.float32),
        ),
    )
    grad_key_hat, grad_values, grad_query_hat, grad_basis, grad_units, grad_strength = back_state
    grad_query_rows, grad_key_rows, grad_house_rows, grad_rate_rows = pull_prep(
        (grad_query_hat, grad_key_hat, grad_within, grad_basis, grad_units, grad_strength)
    )
    grad_query_low = grad_query_rows.astype(jnp.bfloat16)
    grad_key_low = grad_key_rows.astype(jnp.bfloat16)
    grad_value_low = merge_heads(grad_values + grad_value_own).astype(jnp.bfloat16)
    grad_house_low = grad_house_rows.astype(jnp.bfloat16)
    grad_rate_low = grad_rate_rows.astype(jnp.bfloat16)
    grad_normed = (
        low_dot(grad_query_low, regathered[1].T)
        + low_dot(grad_key_low, regathered[2].T)
        + low_dot(grad_value_low, regathered[3].T)
        + low_dot(grad_house_low, regathered[4].T)
        + low_dot(grad_rate_low, regathered[5].T)
    )
    grad_inputs_norm, grad_gain_one = pull_first(grad_normed)
    grad_inputs = (grad_hidden + grad_inputs_norm).astype(jnp.bfloat16)[None]
    grad_project = jnp.concatenate(
        (grad_query_low, grad_key_low, grad_value_low, grad_house_low, grad_rate_low), axis=1
    )
    grad_feed = jnp.concatenate((grad_gate, grad_up), axis=1)
    width = query_weight.shape[1]
    heads_count = beta_weight.shape[1]
    hidden_units = gate_weight.shape[1]
    first = low_dot(normed_low.T, grad_project)
    second = low_dot(attended_low.T, grad_branch)
    third = low_dot(normed_two_low.T, grad_feed)
    gain_one_rows = grad_gain_one[:, None]
    gain_two_rows = grad_gain_two[:, None]
    summed = lax.psum_scatter(
        jnp.concatenate((gain_one_rows, first, second, gain_two_rows, third), axis=1),
        ("seq", "batch"),
        scatter_dimension=0,
        tiled=True,
    )
    grad_down_w = lax.psum_scatter(
        low_dot(active_low.T, grad_out), ("seq", "batch"), scatter_dimension=0, tiled=True
    )
    offset = 1
    grad_query_w = summed[:, offset : offset + width]
    offset = offset + width
    grad_key_w = summed[:, offset : offset + width]
    offset = offset + width
    grad_value_w = summed[:, offset : offset + width]
    offset = offset + width
    grad_house_w = summed[:, offset : offset + width]
    offset = offset + width
    grad_beta_w = summed[:, offset : offset + heads_count]
    offset = offset + heads_count
    grad_out_w = summed[:, offset : offset + width]
    offset = offset + width
    grad_gain_two_rows = summed[:, offset]
    offset = offset + 1
    grad_gate_w = summed[:, offset : offset + hidden_units]
    offset = offset + hidden_units
    grad_up_w = summed[:, offset : offset + hidden_units]
    return (
        output,
        grad_inputs,
        summed[:, 0],
        grad_query_w,
        grad_key_w,
        grad_value_w,
        grad_house_w,
        grad_beta_w,
        grad_out_w,
        grad_gain_two_rows,
        grad_gate_w,
        grad_up_w,
        grad_down_w,
    )


def solution(mesh):
    in_specs = (
        P("batch", "seq", None),
        P("batch", "seq"),
        P(("seq", "batch")),
        P(("seq", "batch"), None),
        P(("seq", "batch"), None),
        P(("seq", "batch"), None),
        P(("seq", "batch"), None),
        P(("seq", "batch"), None),
        P(("seq", "batch"), None),
        P(("seq", "batch")),
        P(("seq", "batch"), None),
        P(("seq", "batch"), None),
        P(("seq", "batch"), None),
        P("batch", "seq", None),
    )
    out_specs = (
        P("batch", "seq", None),
        P("batch", "seq", None),
        P(("seq", "batch")),
        P(("seq", "batch"), None),
        P(("seq", "batch"), None),
        P(("seq", "batch"), None),
        P(("seq", "batch"), None),
        P(("seq", "batch"), None),
        P(("seq", "batch"), None),
        P(("seq", "batch")),
        P(("seq", "batch"), None),
        P(("seq", "batch"), None),
        P(("seq", "batch"), None),
    )
    return jax.shard_map(
        on_device, mesh=mesh, in_specs=in_specs, out_specs=out_specs, check_vma=False
    )
```

profile of v0, /device:TPU:0, one launch (start us, length us, event | category | flops | bytes accessed | tf_op | source)
XLA Modules:
  0.0 2832.5 jit_solution(4034168207043390916)
XLA Ops:
  22.9 42.4 %all-reduce.2 = (bf16[1536]{0:T(1024)(128)(2,1)S(1)}, bf16[1536]{0:T(1024)(128)(2,1)S(1)}) all-reduce(bf16[1536]{0:T(1024)(128)(2,1)S(1)} %dynamic-update-slice, bf16[1536]{0:T(1024)(128)(2,1)S(1)} %dynamic-update-slice.1), channel_id=1, replica_groups=mesh['seq'=16,'batch'=2] {'seq','batch'}, use_global_device_ids=true, to_apply=%add | all-reduce | flops 3072 | bytes 12288
  66.0 22.0 all_gather.51
  89.4 65.2 %all-gather = bf16[32,48,12]{1,2,0:T(8,128)(2,1)S(1)} all-gather(bf16[1,48,12]{1,2,0:T(8,128)(2,1)S(1)} %convert_bitcast_fusion.1), channel_id=1, replica_groups=mesh['seq'=16,'batch'=2] {'seq','batch'}, dimensions={0}, use_global_device_ids=true | all-gather | bytes 38016 | tf_op jit(solution)/shard_map/all_gather | solution.py:110
  175.1 119.3 %custom-call.11 = f32[12,1,128,128]{2,3,1,0:T(8,128)} custom-call(f32[12,1,128,128]{3,2,1,0:T(8,128)} %add_bitcast_fusion), custom_call_target="InvertDiagBlocksLowerTriangular" | custom-call | tf_op jit(solution)/shard_map/jvp()/triangular_solve | solution.py:63
  335.0 420.7 %while.72 = (s32[]{:T(128)}, bf16[12,128,128]{2,1,0:T(8,128)(2,1)}, bf16[12,128,128]{2,1,0:T(8,128)(2,1)}, f32[12,128]{1,0:T(8,128)S(1)}, f32[12,128]{1,0:T(8,12...) while((s32[]{:T(128)}, bf16[12,128,128]{2,1,0:T(8,128)(2,1)}, ...), condition=%wide.region_7.8_spmd, body=%wide.region_4.7_spmd.sunk | while | flops 707234816 | bytes 13508929 | solution.py:185
  369.0 7.6 collective-permute-start
  393.1 15.3 collective-permute-start
  425.0 16.3 collective-permute-start
  457.8 12.9 collective-permute-start
  509.5 11.1 collective-permute-start
  537.2 20.8 collective-permute-start
  574.4 21.5 collective-permute-start
  612.4 17.5 collective-permute-start
  646.5 19.2 collective-permute-start
  682.3 13.4 collective-permute-start
  763.8 7.8 fusion.177
  771.6 7.7 fusion.176
  779.3 11.1 multiply_convert_fusion
  790.5 9.6 fusion.178
  800.2 10.0 multiply_reduce_fusion.1
  822.5 265.7 %while.73 = (s32[]{:T(128)}, bf16[12,128,128]{2,1,0:T(8,128)(2,1)}, bf16[12,128,128]{2,1,0:T(8,128)(2,1)}, bf16[15,12,128,128]{3,2,1,0:T(8,128)(2,1)}, bf16[15,1...) while((s32[]{:T(128)}, bf16[12,128,128]{2,1,0:T(8,128)(2,1)}, ...), condition=%wide.region_11.12_spmd, body=%wide.region_10.11_spmd.sunk | while | flops 604766208 | bytes 9836733 | solution.py:252
  856.4 7.4 collective-permute-start.3
  910.0 7.3 collective-permute-start.3
  945.6 7.3 collective-permute-start.3
  999.1 7.3 collective-permute-start.3
  1088.2 426.1 %while.74 = (s32[]{:T(128)}, f32[12,128,128]{2,1,0:T(8,128)S(1)}, f32[12,128,128]{2,1,0:T(8,128)}, f32[12,128,128]{2,1,0:T(8,128)}, f32[12,128,128]{2,1,0:T(8,12...) while((s32[]{:T(128)}, f32[12,128,128]{2,1,0:T(8,128)S(1)}, ...), condition=%wide.region_15.16_spmd.clone, body=%wide.region_13.15_spmd.clone.sunk | while | flops 1767933440 | bytes 44132976 | solution.py:310
  1540.7 21.3 fusion.48
  1612.1 15.1 fusion.164
  1627.2 111.9 %concatenate.11 = f32[1536,15886]{1,0:T(8,128)} concatenate(f32[1536,1]{1,0:T(8,128)S(1)} %broadcast_in_dim.219, f32[1536,6156]{1,0:T(8,128)} %fusion.164, f32[1536,1536]{1,0:T(8,128)} %fusion.147, f32[1536,1]{1,0:T(8,128)S(1)} %copy-done.51, f32[1536,8192]{1,0:T(8,128)} %fusion.48), dimensions={1} | concatenate | bytes 195207168 | tf_op jit(solution)/shard_map/concatenate | solution.py:354
  1740.4 10.0 fusion.122
  1760.8 812.2 %reduce-scatter.3.cloned.1.call-done = f32[48,15886]{1,0:T(8,128)} async-done(((f32[1536,15886]{1,0:T(8,128)}), f32[48,15886]{1,0:T(8,128)}) %reduce-scatter.3.cloned.1.call-update) | async-done | bytes 3050128 | tf_op jit(solution)/shard_map/reduce_scatter | solution.py:353
  2581.8 243.6 %reduce-scatter.5.cloned.1.call-done = f32[128,1536]{1,0:T(8,128)} async-done(((f32[4096,1536]{1,0:T(8,128)}), f32[128,1536]{1,0:T(8,128)}) %reduce-scatter.5.cloned.1.call-update) | async-done | bytes 786448 | tf_op jit(solution)/shard_map/reduce_scatter | solution.py:359
  (1147 shorter events, 1118.2 us)
Async XLA Ops:
  7.3 148.4 %all-gather.14.cloned.1.call-start = ((), (), s32[]{:S(2)}) async-start(), calls=%async_computation.4 | async-start | bytes 4866048 | tf_op jit(solution)/shard_map/all_gather | solution.py:108
  9.1 151.1 %all-gather.12.cloned.1.call-start = ((), (), s32[]{:S(2)}) async-start(), calls=%async_computation.3 | async-start | bytes 4866048 | tf_op jit(solution)/shard_map/all_gather | solution.py:109
  10.8 285.7 %all-gather.10.cloned.1.call-start = ((), (), s32[]{:S(2)}) async-start(), calls=%async_computation.2 | async-start | bytes 4866048 | tf_op jit(solution)/shard_map/all_gather | solution.py:107
  12.5 299.8 %all-gather.16.cloned.1.call-start = ((), (), s32[]{:S(2)}) async-start(), calls=%async_computation.5 | async-start | bytes 4866048 | tf_op jit(solution)/shard_map/all_gather | solution.py:106
  14.2 745.0 %all-gather.18.cloned.1.call-start = ((), (), s32[]{:S(2)}) async-start(), calls=%async_computation.6 | async-start | bytes 4866048 | tf_op jit(solution)/shard_map/all_gather | solution.py:111
  15.9 747.8 %all-gather.22.cloned.1.call-start = ((), (), s32[]{:S(2)}) async-start(), calls=%async_computation.8 | async-start | bytes 12976128 | tf_op jit(solution)/shard_map/all_gather | solution.py:114
  17.9 753.6 %all-gather.20.cloned.1.call-start = ((), (), s32[]{:S(2)}) async-start(), calls=%async_computation.7 | async-start | bytes 12976128 | tf_op jit(solution)/shard_map/all_gather | solution.py:113
  18.9 760.5 %all-gather.24.cloned.1.call-start = ((), (), s32[]{:S(2)}) async-start(), calls=%async_computation.9 | async-start | bytes 12976128 | tf_op jit(solution)/shard_map/all_gather | solution.py:115
  19.7 2553.3 %reduce-scatter.3.cloned.1.call-start = ((), (), s32[]{:S(2)}) async-start(), calls=%async_computation.10 | async-start | bytes 101376000 | tf_op jit(solution)/shard_map/reduce_scatter | solution.py:353
  393.1 22.0 collective-permute-start
  425.0 23.0 collective-permute-start
  457.8 19.9 collective-permute-start
  537.2 27.3 collective-permute-start
  574.4 28.1 collective-permute-start
  612.4 24.1 collective-permute-start
  646.5 25.9 collective-permute-start
  682.3 20.3 collective-permute-start
  1120.2 20.3 collective-permute-start.5
  1147.9 20.3 collective-permute-start.5
  1175.7 20.3 collective-permute-start.5
  1203.5 20.3 collective-permute-start.5
  1231.3 20.3 collective-permute-start.5
  1259.0 20.3 collective-permute-start.5
  1287.2 20.3 collective-permute-start.5
  1316.3 20.3 collective-permute-start.5
  1345.3 20.3 collective-permute-start.5
  1374.3 20.3 collective-permute-start.5
  1403.4 20.3 collective-permute-start.5
  1432.4 20.3 collective-permute-start.5
  1461.5 20.3 collective-permute-start.5
  1490.5 20.3 collective-permute-start.5
  1739.1 1086.3 %reduce-scatter.5.cloned.1.call-start = ((), (), s32[]{:S(2)}) async-start(), calls=%async_computation.11 | async-start | bytes 25952256 | tf_op jit(solution)/shard_map/reduce_scatter | solution.py:359
  (249 other events, 2308.8 us)
Sparse Core Ops, SparseCore 0:
  11.6 66.8 all-gather.13
  81.9 63.0 all-gather.11
  148.5 63.8 all-gather.9
  215.8 64.5 all-gather.15
  283.7 64.8 all-gather.17
  351.4 111.3 all-gather.21
  465.6 104.4 all-gather.19
  573.0 112.3 all-gather.23
  1739.2 833.7 reduce-scatter.2
  2581.0 244.3 reduce-scatter.4
where the time goes:
time: 2850 us; the launch traced here: 2830 us
  waiting for transfers between devices  1070 us (38%)
  matrix products  639 us (22%)
  starting transfers between devices  449 us (16%)
  local copies, waits for them, and re-layouts  290 us (10%)
  other arithmetic  238 us (8%)
  blocking collectives  130 us (5%)
    reduce_scatter x1, waiting for transfers between devices, on_device(): lax.psum_scatter(jnp.concatenate((gain_one_rows, first, second, gain_two_...  812 us
    ppermute x90, starting transfers between devices, from_behind(): lax.ppermute(value, axis, [(source, source + steps) for source in range(i...  449 us
    reduce_scatter x1, waiting for transfers between devices, on_device(): lax.psum_scatter(low_dot(active_low.T, grad_out), ('seq', 'batch'), scatt...  244 us
    dot_general x22, matrix products, low_dot(): return jnp.dot(left, right, preferred_element_type=jnp.float32)  141 us
    dot_general x60, matrix products, carry_keys(): jnp.einsum('hnt,htd->hnd', weights_on, carry_basis, precision=PRECISE)  132 us
    another operation x5, other arithmetic, prepare(): lax.linalg.triangular_solve(system, unit_dirs, left_side=True, lower=True...  122 us
    dot_general x75, matrix products, carry_keys(): jnp.einsum('hnd,htd->hnt', travel, unit_dirs, precision=PRECISE)  114 us
    concatenate x1, local copies, waits for them, and re-layouts, on_device(): jnp.concatenate((gain_one_rows, first, second, gain_two_rows, third), axi...  112 us
  transfers between devices with their start and end apart: 100, of which 11 were waited for; matrix products, arithmetic and copies ran while one was open for 26% of the time, Pallas kernels for 0%

commit v1 on v0

v1 whole, which is shorter than its diff:
```python
import functools

import jax
import jax.numpy as jnp
from jax import lax
from jax.experimental import pallas as pl
from jax.experimental.pallas import tpu as pltpu
from jax.sharding import Mesh
from jax.sharding import PartitionSpec as P

HEADS = 12
HEAD_DIM = 128
GROUP = 4
OWN = HEADS // GROUP
WIDE = OWN * HEAD_DIM
BLOCK = 128
EXTRA = 128
EPSILON = 1e-06
NEGATIVE = -1e30
SCALE = HEAD_DIM ** (-0.5)
MESH = pl.DeviceIdType.MESH
F32 = jnp.float32
BF16 = jnp.bfloat16
NN = (((1,), (0,)), ((), ()))
NT = (((1,), (1,)), ((), ()))
TN = (((0,), (0,)), ((), ()))


def dot(left, right, dims=NN):
    return lax.dot_general(left, right, dims, preferred_element_type=F32)


def split(value):
    high = value.astype(BF16)
    return high, (value - high.astype(F32)).astype(BF16)


def dot3(left, right, dims=NN):
    left_high, left_low = split(left)
    right_high, right_low = split(right)
    return dot(left_high, right_high, dims) + (
        dot(left_high, right_low, dims) + dot(left_low, right_high, dims)
    )


def dot2(left, right, dims=NN):
    high, low = split(right)
    return dot(left, high, dims) + dot(left, low, dims)


def tile(index, count=1):
    return pl.ds(index * BLOCK, count * BLOCK)


def iota(axis, shape=(BLOCK, BLOCK)):
    return lax.broadcasted_iota(jnp.int32, shape, axis)


def invert(strict):
    row, col = iota(0), iota(1)
    eye = jnp.where(row == col, 1.0, 0.0)

    def part(size):
        return (row // (2 * size) == col // (2 * size)) & (row // size > col // size)

    totals = [eye - jnp.where(part(1), value, 0.0) for value in strict]
    size = 2
    while size < BLOCK:
        mask = part(size)
        pieces = [jnp.where(mask, value, 0.0) for value in strict]
        inner = [dot3(piece, total) for piece, total in zip(pieces, totals)]
        outer = [dot3(total, value) for total, value in zip(totals, inner)]
        totals = [total - value for total, value in zip(totals, outer)]
        size *= 2
    return totals


def unit_of(house):
    scale = lax.rsqrt(jnp.sum(house * house, axis=-1, keepdims=True) + EPSILON)
    return house * scale, scale


def products(query, key, unit):
    both = dot3(jnp.concatenate([unit, query], 0), jnp.concatenate([unit, key], 0), NT)
    return both[:BLOCK, :BLOCK], both[:BLOCK, BLOCK:], both[BLOCK:, :BLOCK], both[BLOCK:, BLOCK:]


def prepare_kernel(rows_ref, query_ref, key_ref, value_ref, within_ref, map_ref, inverse_ref):
    row, col = iota(0), iota(1)

    def one_block(block, carry):
        at = tile(block)
        kept, strict = [], []
        for head in range(OWN):
            query, key, value, house = [
                rows_ref[at, pl.ds(part * WIDE + head * BLOCK, BLOCK)] for part in range(4)
            ]
            rate = rows_ref[at, pl.ds(4 * WIDE, EXTRA)][:, head : head + 1]
            value_ref[at, tile(head)] = value.astype(BF16)
            unit, _ = unit_of(house)
            strength = 2.0 * jax.nn.sigmoid(rate)
            unit_unit, unit_key, query_unit, query_key = products(query, key, unit)
            strict.append(jnp.where(row > col, strength * unit_unit, 0.0))
            reach = jnp.where(row > col, strength * unit_key, 0.0)
            project = jnp.where(row >= col, query_unit, 0.0)
            kept.append((query, key, unit, strength, reach, project, query_key))
        inverses = invert(strict)
        for head in range(OWN):
            query, key, unit, strength, reach, project, query_key = kept[head]
            inverse = inverses[head]
            solved = dot3(inverse, jnp.concatenate([strength * unit, reach], 1))
            from_query = dot3(project, solved)
            from_unit = dot3(solved, unit, TN)
            query_ref[at, tile(head)] = (query - from_query[:, :BLOCK]).astype(BF16)
            within_ref[at, tile(head)] = query_key - from_query[:, BLOCK:]
            map_ref[at, tile(head)] = jnp.where(row == col, 1.0, 0.0) - from_unit[:BLOCK]
            key_ref[at, tile(head)] = (key - from_unit[BLOCK:]).astype(BF16)
            inverse_ref[at, tile(head)] = inverse
        return carry

    lax.fori_loop(0, GROUP, one_block, 0)


def prepare(rows):
    length = rows.shape[0]
    return pl.pallas_call(
        prepare_kernel,
        out_shape=[jax.ShapeDtypeStruct((length, WIDE), kind) for kind in (BF16, BF16, BF16, F32, F32, F32)],
        compiler_params=pltpu.CompilerParams(vmem_limit_bytes=48 << 20),
        name="prepare",
    )(rows)


def prepare_back_kernel(rows_ref, inverse_ref, query_grad_ref, key_grad_ref, within_grad_ref, map_grad_ref, value_grad_ref, out_ref):
    row, col = iota(0), iota(1)

    def one_block(block, carry):
        at = tile(block)
        rates = jnp.zeros((BLOCK, EXTRA), F32)
        for head in range(OWN):
            query, key, value, house = [
                rows_ref[at, pl.ds(part * WIDE + head * BLOCK, BLOCK)] for part in range(4)
            ]
            rate = rows_ref[at, pl.ds(4 * WIDE, EXTRA)][:, head : head + 1]
            query_grad = query_grad_ref[at, tile(head)]
            key_grad = key_grad_ref[at, tile(head)]
            within_grad = within_grad_ref[at, tile(head)]
            map_grad = map_grad_ref[at, tile(head)]
            inverse = inverse_ref[at, tile(head)]
            unit, scale = unit_of(house)
            strength = 2.0 * jax.nn.sigmoid(rate)
            unit_unit, unit_key, query_unit, query_key = products(query, key, unit)
            reach = jnp.where(row > col, strength * unit_key, 0.0)
            project = jnp.where(row >= col, query_unit, 0.0)
            solved = dot3(inverse, jnp.concatenate([strength * unit, reach], 1))
            both_grad = jnp.concatenate([query_grad, within_grad], 1)
            project_grad = jnp.where(row >= col, -dot3(both_grad, solved, NT), 0.0)
            solved_grad = -(
                dot3(project, both_grad, TN)
                + dot3(unit, jnp.concatenate([map_grad, key_grad], 0), NT)
            )
            given_grad = dot3(inverse, solved_grad, TN)
            strict_grad = jnp.where(row > col, -dot3(given_grad, solved, NT), 0.0)
            scaled_grad = given_grad[:, :BLOCK]
            reach_grad = jnp.where(row > col, given_grad[:, BLOCK:], 0.0)
            strength_grad = jnp.sum(
                scaled_grad * unit + reach_grad * unit_key + strict_grad * unit_unit, axis=1, keepdims=True
            )
            reach_part = strength * reach_grad
            inner_part = strength * strict_grad
            unit_grad = (
                strength * scaled_grad
                + dot3(reach_part, key)
                + dot3(inner_part + inner_part.T, unit)
                + dot3(project_grad, query, TN)
                - dot3(solved[:, :BLOCK], map_grad)
                - dot3(solved[:, BLOCK:], key_grad)
            )
            query_out = query_grad + dot3(within_grad, key) + dot3(project_grad, unit)
            key_out = key_grad + dot3(within_grad, query, TN) + dot3(reach_part, unit, TN)
            house_out = scale * (unit_grad - unit * jnp.sum(unit * unit_grad, axis=1, keepdims=True))
            rate_out = strength_grad * strength * (1.0 - 0.5 * strength)
            rates = jnp.where(iota(1, (BLOCK, EXTRA)) == head, rate_out, rates)
            out_ref[at, pl.ds(head * BLOCK, BLOCK)] = query_out.astype(BF16)
            out_ref[at, pl.ds(WIDE + head * BLOCK, BLOCK)] = key_out.astype(BF16)
            out_ref[at, pl.ds(2 * WIDE + head * BLOCK, BLOCK)] = value_grad_ref[at, tile(head)].astype(BF16)
            out_ref[at, pl.ds(3 * WIDE + head * BLOCK, BLOCK)] = house_out.astype(BF16)
        out_ref[at, pl.ds(4 * WIDE, EXTRA)] = rates.astype(BF16)
        return carry

    lax.fori_loop(0, GROUP, one_block, 0)


def prepare_back(*args):
    return pl.pallas_call(
        prepare_back_kernel,
        out_shape=jax.ShapeDtypeStruct(args[0].shape, BF16),
        compiler_params=pltpu.CompilerParams(vmem_limit_bytes=48 << 20),
        name="prepare_back",
    )(*args)


def meet_neighbours(groups):
    place = lax.axis_index("g")
    others = {"m": lax.axis_index("m"), "b": lax.axis_index("b")}
    barrier = pltpu.get_barrier_semaphore()

    @pl.when(place > 0)
    def _():
        pl.semaphore_signal(barrier, 1, device_id={"g": place - 1, **others}, device_id_type=MESH)

    @pl.when(place < groups - 1)
    def _():
        pl.semaphore_signal(barrier, 1, device_id={"g": place + 1, **others}, device_id_type=MESH)

    pl.semaphore_wait(barrier, (place > 0).astype(jnp.int32) + (place < groups - 1).astype(jnp.int32))
    return place, others


def masked(scores, counts):
    return jnp.where(counts, scores * SCALE, NEGATIVE)


def attend_kernel(
    groups,
    hops,
    query_ref,
    key_ref,
    value_ref,
    within_ref,
    map_ref,
    doc_query_ref,
    doc_key_ref,
    attended_ref,
    low_ref,
    stats_ref,
    moved_ref,
    values_ref,
    leave_ref,
    top_ref,
    total_ref,
    accum_ref,
    key_send,
    key_recv,
    value_send,
    value_recv,
):
    place, others = meet_neighbours(groups)
    following = {"g": place + 1, **others}
    has_next = place < groups - 1

    def value_copy(source, slot):
        return pltpu.make_async_remote_copy(
            src_ref=source,
            dst_ref=values_ref.at[slot],
            send_sem=value_send.at[slot],
            recv_sem=value_recv.at[slot],
            device_id=following,
            device_id_type=MESH,
        )

    def key_copy(slot):
        return pltpu.make_async_remote_copy(
            src_ref=leave_ref.at[slot],
            dst_ref=moved_ref.at[slot + 1, 0],
            send_sem=key_send.at[slot],
            recv_sem=key_recv.at[slot],
            device_id=following,
            device_id_type=MESH,
        )

    def move(keys, block, head):
        return dot2(keys, map_ref[tile(block), tile(head)]).astype(BF16)

    for head in range(OWN):
        keys = key_ref[tile(0), tile(head)]
        for block in range(1, GROUP):
            moved_ref[0, block, tile(0, block), tile(head)] = keys
            keys = jnp.concatenate([move(keys, block, head), key_ref[tile(block), tile(head)]], 0)
        leave_ref[0, :, tile(head)] = keys

    @pl.when(has_next)
    def _():
        key_copy(0).start()
        value_copy(value_ref, 0).start()

    def row_counts(block, hop, first, count):
        return doc_query_ref[tile(block), :] == doc_key_ref[hop, :, tile(first, count)]

    for block in range(GROUP):
        counts = row_counts(block, 0, 0, block + 1)
        wide = (BLOCK, (block + 1) * BLOCK)
        counts = counts & (iota(0, wide) + block * BLOCK >= iota(1, wide))
        for head in range(OWN):
            scores = within_ref[tile(block), tile(head)]
            if block:
                before = dot(query_ref[tile(block), tile(head)], moved_ref[0, block, tile(0, block), tile(head)], NT)
                scores = jnp.concatenate([before, scores], 1)
            scores = masked(scores, counts)
            top = jnp.max(scores, axis=1, keepdims=True)
            weights = jnp.exp(scores - top)
            top_ref[head, tile(block), :] = jnp.broadcast_to(top, (BLOCK, BLOCK))
            total_ref[head, tile(block), :] = jnp.broadcast_to(jnp.sum(weights, axis=1, keepdims=True), (BLOCK, BLOCK))
            accum_ref[tile(block), tile(head)] = dot(weights.astype(BF16), value_ref[tile(0, block + 1), tile(head)])

    def hop_step(hop, last):
        @pl.when(place >= hop)
        def _():
            key_copy(hop - 1).wait_recv()
            for head in range(OWN):
                keys = moved_ref[hop, 0, :, tile(head)]
                for block in range(GROUP):
                    if last:
                        if block == GROUP - 1:
                            break
                        keys = move(keys[BLOCK:], block, head)
                        moved_ref[hop, block + 1, tile(block + 1, GROUP - 1 - block), tile(head)] = keys
                    else:
                        keys = move(keys, block, head)
                        if block < GROUP - 1:
                            moved_ref[hop, block + 1, :, tile(head)] = keys
                        else:
                            leave_ref[hop, :, tile(head)] = keys
            value_copy(value_ref, hop - 1).wait_recv()
            if not last:

                @pl.when(has_next)
                def _():
                    key_copy(hop).start()
                    value_copy(values_ref.at[hop - 1], hop).start()

            for block in range(GROUP):
                first = block if last else 0
                count = GROUP - first
                counts = row_counts(block, hop, first, count)
                for head in range(OWN):
                    scores = masked(
                        dot(query_ref[tile(block), tile(head)], moved_ref[hop, block, tile(first, count), tile(head)], NT),
                        counts,
                    )
                    old = top_ref[head, tile(block), :]
                    top = jnp.maximum(old, jnp.broadcast_to(jnp.max(scores, axis=1, keepdims=True), (BLOCK, BLOCK)))
                    factor = jnp.exp(old - top)
                    weights = jnp.exp(scores - jnp.concatenate([top] * count, 1))
                    top_ref[head, tile(block), :] = top
                    total_ref[head, tile(block), :] = total_ref[head, tile(block), :] * factor + jnp.sum(
                        weights, axis=1, keepdims=True
                    )
                    accum_ref[tile(block), tile(head)] = accum_ref[tile(block), tile(head)] * factor + dot(
                        weights.astype(BF16), values_ref[hop - 1, tile(first, count), tile(head)]
                    )

    if hops > 2:

        def between(hop, carry):
            hop_step(hop, False)
            return carry

        lax.fori_loop(1, hops, between, 0)
    else:
        for hop in range(1, hops):
            hop_step(hop, False)
    hop_step(hops, True)

    for block in range(GROUP):
        stats = jnp.zeros((BLOCK, BLOCK), F32)
        for head in range(OWN):
            total = total_ref[head, tile(block), :]
            result = accum_ref[tile(block), tile(head)] / total
            attended_ref[tile(block), tile(head)] = result
            low_ref[tile(block), tile(head)] = result.astype(BF16)
            stats = jnp.where(iota(1) == head, top_ref[head, tile(block), :], stats)
            stats = jnp.where(iota(1) == OWN + head, total, stats)
        stats_ref[tile(block), :] = stats

    def settle(slot, carry):
        @pl.when(has_next & (place >= slot))
        def _():
            key_copy(slot).wait_send()
            value_copy(value_ref, slot).wait_send()

        return carry

    lax.fori_loop(0, hops, settle, 0)


def attend(groups, hops, *args):
    length = args[0].shape[0]
    out = [
        jax.ShapeDtypeStruct((length, WIDE), F32),
        jax.ShapeDtypeStruct((length, WIDE), BF16),
        jax.ShapeDtypeStruct((length, BLOCK), F32),
        jax.ShapeDtypeStruct((hops + 1, GROUP, length, WIDE), BF16),
        jax.ShapeDtypeStruct((hops, length, WIDE), BF16),
    ]
    return pl.pallas_call(
        functools.partial(attend_kernel, groups, hops),
        out_shape=out,
        in_specs=[pl.BlockSpec(memory_space=pltpu.VMEM)] * len(args),
        out_specs=[pl.BlockSpec(memory_space=pltpu.VMEM)] * len(out),
        scratch_shapes=[
            pltpu.VMEM((hops, length, WIDE), BF16),
            pltpu.VMEM((OWN, length, BLOCK), F32),
            pltpu.VMEM((OWN, length, BLOCK), F32),
            pltpu.VMEM((length, WIDE), F32),
            pltpu.SemaphoreType.DMA((hops,)),
            pltpu.SemaphoreType.DMA((hops,)),
            pltpu.SemaphoreType.DMA((hops,)),
            pltpu.SemaphoreType.DMA((hops,)),
        ],
        compiler_params=pltpu.CompilerParams(collective_id=1, has_side_effects=True, vmem_limit_bytes=58 << 20),
        name="attend",
    )(*args)


def attend_back_kernel(
    groups,
    hops,
    query_ref,
    value_ref,
    within_ref,
    map_ref,
    doc_query_ref,
    doc_key_ref,
    attended_ref,
    stats_ref,
    moved_ref,
    values_ref,
    att_grad_ref,
    query_grad_ref,
    key_grad_ref,
    within_grad_ref,
    map_grad_ref,
    value_grad_ref,
    scaled_ref,
    dots_ref,
    direct_ref,
    direct_value_ref,
    running_ref,
    key_leave_ref,
    value_leave_ref,
    key_land_ref,
    value_land_ref,
    key_send,
    key_recv,
    value_send,
    value_recv,
):
    place, others = meet_neighbours(groups)
    previous = {"g": place - 1, **others}
    has_next = place < groups - 1

    def key_copy(hop):
        slot = hop - 1
        return pltpu.make_async_remote_copy(
            src_ref=key_leave_ref.at[slot],
            dst_ref=key_land_ref.at[slot],
            send_sem=key_send.at[slot],
            recv_sem=key_recv.at[slot],
            device_id=previous,
            device_id_type=MESH,
        )

    def value_copy(hop):
        slot = hop - 1
        return pltpu.make_async_remote_copy(
            src_ref=value_leave_ref.at[slot],
            dst_ref=value_land_ref.at[slot],
            send_sem=value_send.at[slot],
            recv_sem=value_recv.at[slot],
            device_id=previous,
            device_id_type=MESH,
        )

    map_grad_ref[...] = jnp.zeros_like(map_grad_ref)
    query_grad_ref[...] = jnp.zeros_like(query_grad_ref)
    for block in range(GROUP):
        for head in range(OWN):
            at = (tile(block), tile(head))
            grad = att_grad_ref[at].astype(F32)
            total = stats_ref[tile(block), OWN + head : OWN + head + 1]
            scaled_ref[at] = (grad / total).astype(BF16)
            dots = -jnp.sum(grad * attended_ref[at], axis=1, keepdims=True) / total
            dots_ref[head, tile(block), :] = jnp.broadcast_to(dots, (BLOCK, BLOCK))

    def pair(block, head, scores, counts, values):
        count = scores.shape[1] // BLOCK
        top = stats_ref[tile(block), head : head + 1]
        weights = jnp.exp(masked(scores, counts) - top)
        weight_grad = dot(scaled_ref[tile(block), tile(head)], values, NT)
        dots = jnp.concatenate([dots_ref[head, tile(block), :]] * count, 1)
        return weights, weights * (weight_grad + dots) * SCALE

    def row_counts(block, hop, first, count):
        return doc_query_ref[tile(block), :] == doc_key_ref[hop, :, tile(first, count)]

    def hop_direct(hop, slot, last):
        for head in range(OWN):
            direct_value_ref[slot, :, tile(head)] = jnp.zeros((GROUP * BLOCK, BLOCK), F32)
        for block in range(GROUP):
            first = block if last else 0
            count = GROUP - first
            counts = row_counts(block, hop, first, count)
            for head in range(OWN):
                query = query_ref[tile(block), tile(head)]
                keys = moved_ref[hop, block, tile(first, count), tile(head)]
                weights, grad = pair(
                    block, head, dot(query, keys, NT), counts, values_ref[hop - 1, tile(first, count), tile(head)]
                )
                raw = grad.astype(BF16)
                query_grad_ref[tile(block), tile(head)] += dot(raw, keys)
                direct_ref[slot, block, tile(first, count), tile(head)] = dot(raw, query, TN)
                direct_value_ref[slot, tile(first, count), tile(head)] += dot(
                    weights.astype(BF16), scaled_ref[tile(block), tile(head)], TN
                )

    def collect_map(block, head, keys, grads):
        map_grad_ref[tile(block), tile(head)] += dot2(keys, grads, TN)

    def hop_chain(hop, slot, last):
        for head in range(OWN):
            if last:
                grads = direct_ref[slot, GROUP - 1, tile(GROUP - 1), tile(head)]
                for block in range(GROUP - 2, -1, -1):
                    rows = tile(block + 1, GROUP - 1 - block)
                    collect_map(block, head, moved_ref[hop, block, rows, tile(head)], grads)
                    back = dot3(grads, map_ref[tile(block), tile(head)], NT)
                    direct = direct_ref[slot, block, tile(block, GROUP - block), tile(head)]
                    grads = jnp.concatenate([direct[:BLOCK], direct[BLOCK:] + back], 0)
                key_leave_ref[hop - 1, :, tile(head)] = grads.astype(BF16)
                value_leave_ref[hop - 1, :, tile(head)] = direct_value_ref[slot, :, tile(head)].astype(BF16)
            else:
                grads = running_ref[:, tile(head)]
                for block in range(GROUP - 1, -1, -1):
                    collect_map(block, head, moved_ref[hop, block, :, tile(head)], grads)
                    grads = direct_ref[slot, block, :, tile(head)] + dot3(grads, map_ref[tile(block), tile(head)], NT)
                key_leave_ref[hop - 1, :, tile(head)] = grads.astype(BF16)

    def take(hop):
        @pl.when(has_next)
        def _():
            key_copy(hop).wait_recv()
            running_ref[...] = key_land_ref[hop - 1].astype(F32)

        @pl.when(jnp.logical_not(has_next))
        def _():
            running_ref[...] = jnp.zeros_like(running_ref)

    @pl.when(place >= hops)
    def _():
        hop_direct(hops, hops % 2, True)
        hop_chain(hops, hops % 2, True)
        key_copy(hops).start()
        value_copy(hops).start()

    def between(hop):
        @pl.when(place >= hop)
        def _():
            slot = lax.rem(hop, 2) if hops > 2 else hop % 2
            hop_direct(hop, slot, False)
            take(hop + 1)
            hop_chain(hop, slot, False)
            key_copy(hop).start()

            @pl.when(has_next)
            def _():
                value_copy(hop + 1).wait_recv()
                for head in range(OWN):
                    value_leave_ref[hop - 1, :, tile(head)] = (
                        direct_value_ref[slot, :, tile(head)] + value_land_ref[hop, :, tile(head)].astype(F32)
                    ).astype(BF16)

            @pl.when(jnp.logical_not(has_next))
            def _():
                for head in range(OWN):
                    value_leave_ref[hop - 1, :, tile(head)] = direct_value_ref[slot, :, tile(head)].astype(BF16)

            value_copy(hop).start()

    if hops > 2:

        def step(counter, carry):
            between(hops - 1 - counter)
            return carry

        lax.fori_loop(0, hops - 1, step, 0)
    else:
        for hop in range(hops - 1, 0, -1):
            between(hop)

    for head in range(OWN):
        direct_value_ref[0, :, tile(head)] = jnp.zeros((GROUP * BLOCK, BLOCK), F32)
    for block in range(GROUP):
        wide = (BLOCK, (block + 1) * BLOCK)
        counts = row_counts(block, 0, 0, block + 1) & (iota(0, wide) + block * BLOCK >= iota(1, wide))
        for head in range(OWN):
            query = query_ref[tile(block), tile(head)]
            scores = within_ref[tile(block), tile(head)]
            if block:
                keys = moved_ref[0, block, tile(0, block), tile(head)]
                scores = jnp.concatenate([dot(query, keys, NT), scores], 1)
            weights, grad = pair(block, head, scores, counts, value_ref[tile(0, block + 1), tile(head)])
            within_grad_ref[tile(block), tile(head)] = grad[:, block * BLOCK :]
            direct_value_ref[0, tile(0, block + 1), tile(head)] += dot(
                weights.astype(BF16), scaled_ref[tile(block), tile(head)], TN
            )
            if block:
                raw = grad[:, : block * BLOCK].astype(BF16)
                query_grad_ref[tile(block), tile(head)] += dot(raw, keys)
                direct_ref[0, block, tile(0, block), tile(head)] = dot(raw, query, TN)
    take(1)
    for head in range(OWN):
        grads = running_ref[:, tile(head)]
        for block in range(GROUP - 1, 0, -1):
            key_grad_ref[tile(block), tile(head)] = grads[block * BLOCK :]
            grads = grads[: block * BLOCK]
            collect_map(block, head, moved_ref[0, block, tile(0, block), tile(head)], grads)
            grads = direct_ref[0, block, tile(0, block), tile(head)] + dot3(grads, map_ref[tile(block), tile(head)], NT)
        key_grad_ref[tile(0), tile(head)] = grads

    @pl.when(has_next)
    def _():
        value_copy(1).wait_recv()
        value_grad_ref[...] = direct_value_ref[0] + value_land_ref[0].astype(F32)

    @pl.when(jnp.logical_not(has_next))
    def _():
        value_grad_ref[...] = direct_value_ref[0]

    def settle(hop, carry):
        @pl.when(place >= hop)
        def _():
            key_copy(hop).wait_send()
            value_copy(hop).wait_send()

        return carry

    lax.fori_loop(1, hops + 1, settle, 0)


def attend_back(groups, hops, *args):
    length = args[0].shape[0]
    out = [jax.ShapeDtypeStruct((length, WIDE), F32)] * 5
    return pl.pallas_call(
        functools.partial(attend_back_kernel, groups, hops),
        out_shape=out,
        in_specs=[pl.BlockSpec(memory_space=pltpu.VMEM)] * len(args),
        out_specs=[pl.BlockSpec(memory_space=pltpu.VMEM)] * len(out),
        scratch_shapes=[
            pltpu.VMEM((length, WIDE), BF16),
            pltpu.VMEM((OWN, length, BLOCK), F32),
            pltpu.VMEM((2, GROUP, length, WIDE), F32),
            pltpu.VMEM((2, length, WIDE), F32),
            pltpu.VMEM((length, WIDE), F32),
            pltpu.VMEM((hops, length, WIDE), BF16),
            pltpu.VMEM((hops, length, WIDE), BF16),
            pltpu.VMEM((hops, length, WIDE), BF16),
            pltpu.VMEM((hops, length, WIDE), BF16),
            pltpu.SemaphoreType.DMA((hops,)),
            pltpu.SemaphoreType.DMA((hops,)),
            pltpu.SemaphoreType.DMA((hops,)),
            pltpu.SemaphoreType.DMA((hops,)),
        ],
        compiler_params=pltpu.CompilerParams(collective_id=2, has_side_effects=True, vmem_limit_bytes=58 << 20),
        name="attend_back",
    )(*args)


def rms_scale(values, gain):
    return values * lax.rsqrt(jnp.mean(values * values, axis=-1, keepdims=True) + EPSILON) * gain


def rms_back(values, gain, grad):
    scale = lax.rsqrt(jnp.mean(values * values, axis=-1, keepdims=True) + EPSILON)
    straight = values * scale
    lifted = grad * gain
    back = scale * (lifted - straight * jnp.mean(lifted * straight, axis=-1, keepdims=True))
    return back, jnp.sum(grad * straight, axis=0)


def on_device(
    tokens,
    doc_ids,
    norm_gain,
    query_weight,
    key_weight,
    value_weight,
    house_weight,
    beta_weight,
    out_weight,
    ffn_gain,
    gate_weight,
    up_weight,
    down_weight,
    cotangent,
):
    groups, batch = lax.axis_size("g"), lax.axis_size("b")
    devices = groups * GROUP * batch
    rows, width = query_weight.shape
    hidden_rows = down_weight.shape[0]
    hidden_own = gate_weight.shape[1] // GROUP
    block_rows = tokens.shape[1]
    hops = groups // 2
    doc_columns = -(-block_rows // rows)
    place, member, line = lax.axis_index("g"), lax.axis_index("m"), lax.axis_index("b")

    def columns(weight):
        return jnp.transpose(weight.astype(BF16).reshape(rows, GROUP, -1), (1, 0, 2))

    docs = jnp.pad(doc_ids[0].astype(BF16), (0, rows * doc_columns - block_rows)).reshape(rows, doc_columns)
    same = jnp.concatenate([norm_gain.astype(BF16)[:, None], ffn_gain.astype(BF16)[:, None], docs], 1)
    same = jnp.broadcast_to(same[None], (GROUP,) + same.shape)
    same = jnp.pad(same, ((0, 0), (0, 0), (0, EXTRA - OWN - same.shape[2])))
    first_parts = jnp.concatenate(
        [columns(w) for w in (query_weight, key_weight, value_weight, house_weight, beta_weight)] + [same], 2
    )

    def gather(parts):
        parts = lax.all_to_all(parts, "m", 0, 0, tiled=True)
        whole = lax.all_gather(parts, ("g", "b"), axis=0, tiled=False)
        whole = whole.reshape((groups, batch) + parts.shape)
        return jnp.transpose(whole, (0, 2, 1, 3, 4)).reshape(devices * parts.shape[1], parts.shape[2])

    def unit_columns(weight):
        parts = weight.astype(BF16).reshape(rows, groups, GROUP, batch, hidden_rows)
        return jnp.transpose(parts, (2, 0, 1, 3, 4)).reshape(GROUP, rows, hidden_own)

    first = gather(first_parts)
    feed = gather(jnp.concatenate([unit_columns(gate_weight), unit_columns(up_weight)], 2))
    gate_full, up_full = feed[:, :hidden_own], feed[:, hidden_own:]
    down_full = lax.all_gather(down_weight.astype(BF16), ("g", "b"), axis=0, tiled=True)
    out_all = lax.all_gather(out_weight.astype(BF16), ("g", "m", "b"), axis=0, tiled=True)
    out_full = lax.dynamic_slice_in_dim(out_all, member * WIDE, WIDE)

    def group_gather(value):
        return lax.all_gather(value, "m", axis=0, tiled=True)

    def group_sum(value):
        return lax.psum_scatter(value.astype(BF16), "m", scatter_dimension=0, tiled=True).astype(F32)

    extra = first[:, 4 * WIDE :]
    gain_one = extra[:, OWN].astype(F32)
    gain_two = extra[:, OWN + 1].astype(F32)
    docs = extra[:, OWN + 2 : OWN + 2 + doc_columns].astype(jnp.int32)
    docs = docs.reshape(devices, -1)[:, :block_rows].reshape(groups, GROUP, batch, block_rows)
    docs = lax.dynamic_index_in_dim(docs, line, 2, keepdims=False).reshape(groups, GROUP * block_rows)
    doc_key = jnp.stack(
        [
            jnp.where(place >= hop, lax.dynamic_index_in_dim(docs, jnp.maximum(place - hop, 0), 0, keepdims=False), -1)
            for hop in range(hops + 1)
        ]
    )[:, None, :]
    doc_query = lax.dynamic_index_in_dim(docs, place, 0, keepdims=False)[:, None]

    tokens_all = group_gather(tokens[0])
    cotangent_all = group_gather(cotangent[0])
    inputs = tokens[0].astype(F32)
    normed = rms_scale(tokens_all.astype(F32), gain_one).astype(BF16)
    projected = dot(normed, first)
    query, key, value, within, maps, inverse = prepare(projected)
    attended, attended_low, stats, moved, values = attend(
        groups, hops, query, key, value, within, maps, doc_query, doc_key
    )
    hidden = inputs + group_sum(dot(attended_low, out_full))
    normed_two = group_gather(rms_scale(hidden, gain_two).astype(BF16))
    gate = dot(normed_two, gate_full)
    up = dot(normed_two, up_full)
    sigmoid = jax.nn.sigmoid(gate)
    silu = gate * sigmoid
    active = (silu * up).astype(BF16)
    output = (hidden + group_sum(dot(active, down_full))).astype(BF16)[None]

    active_grad = dot(cotangent_all, down_full, NT)
    gate_grad = (active_grad * up * (sigmoid * (1.0 + gate * (1.0 - sigmoid)))).astype(BF16)
    up_grad = (active_grad * silu).astype(BF16)
    normed_two_grad = group_sum(dot(gate_grad, gate_full, NT) + dot(up_grad, up_full, NT))
    hidden_back, gain_two_grad = rms_back(hidden, gain_two, normed_two_grad)
    hidden_grad = cotangent[0].astype(F32) + hidden_back
    branch_grad = group_gather(hidden_grad.astype(BF16))
    att_grad = dot(branch_grad, out_full, NT).astype(BF16)
    query_grad, key_grad, within_grad, map_grad, value_grad = attend_back(
        groups, hops, query, value, within, maps, doc_query, doc_key, attended, stats, moved, values, att_grad
    )
    rows_grad = prepare_back(projected, inverse, query_grad, key_grad, within_grad, map_grad, value_grad)
    normed_grad = group_sum(dot(rows_grad, first, NT))
    inputs_back, gain_one_grad = rms_back(inputs, gain_one, normed_grad)
    tokens_grad = (hidden_grad + inputs_back).astype(BF16)[None]

    def scatter(full):
        parts = full.astype(BF16).reshape(groups, GROUP, batch, rows, full.shape[1])
        parts = jnp.transpose(parts, (0, 2, 1, 3, 4)).reshape(groups * batch, GROUP, rows, full.shape[1])
        parts = lax.psum_scatter(parts, ("g", "b"), scatter_dimension=0, tiled=False)
        return lax.all_to_all(parts, "m", 0, 0, tiled=True).astype(F32)

    first_grad = dot(normed, rows_grad, TN)
    lane = iota(1, (1, first_grad.shape[1]))
    first_grad = jnp.where(lane == 4 * WIDE + OWN, gain_one_grad[:, None], first_grad)
    first_grad = jnp.where(lane == 4 * WIDE + OWN + 1, gain_two_grad[:, None], first_grad)
    first_grad = scatter(first_grad)

    def whole_columns(parts):
        return jnp.transpose(parts, (1, 0, 2)).reshape(rows, -1)

    query_weight_grad, key_weight_grad, value_weight_grad, house_weight_grad = [
        whole_columns(first_grad[:, :, part * WIDE : (part + 1) * WIDE]) for part in range(4)
    ]
    beta_weight_grad = whole_columns(first_grad[:, :, 4 * WIDE : 4 * WIDE + OWN])
    gains_grad = jnp.sum(first_grad[:, :, 4 * WIDE + OWN : 4 * WIDE + OWN + 2], axis=0)
    feed_grad = scatter(
        jnp.concatenate([dot(normed_two, gate_grad, TN), dot(normed_two, up_grad, TN)], 1)
    )

    def unit_whole(parts):
        parts = parts.reshape(GROUP, rows, groups, batch, hidden_rows)
        return jnp.transpose(parts, (1, 2, 0, 3, 4)).reshape(rows, -1)

    gate_weight_grad = unit_whole(feed_grad[:, :, :hidden_own])
    up_weight_grad = unit_whole(feed_grad[:, :, hidden_own:])
    down_weight_grad = lax.psum_scatter(
        dot(active, cotangent_all, TN).astype(BF16), ("g", "b"), scatter_dimension=0, tiled=True
    ).astype(F32)
    out_grad = lax.psum(dot(attended_low, branch_grad, TN).astype(BF16), ("g", "b"))
    out_grad = group_gather(out_grad)
    own = (place * GROUP + member) * batch + line
    out_weight_grad = lax.dynamic_slice_in_dim(out_grad, own * rows, rows).astype(F32)
    return (
        output,
        tokens_grad,
        gains_grad[:, 0],
        query_weight_grad,
        key_weight_grad,
        value_weight_grad,
        house_weight_grad,
        beta_weight_grad,
        out_weight_grad,
        gains_grad[:, 1],
        gate_weight_grad,
        up_weight_grad,
        down_weight_grad,
    )


def solution(mesh):
    groups = mesh.shape["seq"] // GROUP
    inner = Mesh(mesh.devices.reshape(groups, GROUP, mesh.shape["batch"]), ("g", "m", "b"))
    line = P("b", ("g", "m"), None)
    vector = P(("g", "m", "b"))
    matrix = P(("g", "m", "b"), None)
    in_specs = (line, P("b", ("g", "m")), vector) + (matrix,) * 6 + (vector,) + (matrix,) * 3 + (line,)
    out_specs = (line, line, vector) + (matrix,) * 6 + (vector,) + (matrix,) * 3
    return jax.shard_map(on_device, mesh=inner, in_specs=in_specs, out_specs=out_specs, check_vma=False)
```

time: 2850 us -> 1110 us (0.39)
  matrix products: 639 us -> 67.7 us
  starting transfers between devices: 449 us -> 9.01 us
  waiting for transfers between devices: 1070 us -> 789 us
  local copies, waits for them, and re-layouts: 290 us -> 44 us
  other arithmetic: 238 us -> 26.2 us
  Pallas kernels: 0 us -> 117 us
  blocking collectives: 130 us -> 35.3 us
    reduce_scatter x2 -> x7, waiting for transfers between devices: 1060 us -> 385 us  [the longest x2 221 us: scatter(): lax.psum_scatter(parts, ('g', 'b'), scatter_dimension=0, tiled=False)]
    dot_general x288 -> x15, matrix products: 626 us -> 67.7 us  [dot(): return lax.dot_general(left, right, dims, preferred_element_type=F32)]
    ppermute x90 -> x0, starting transfers between devices: 449 us -> none  [from_behind(): lax.ppermute(value, axis, [(source, source + steps) for source in range(i...]
    all_gather x8 -> x9, waiting for transfers between devices: 0.07 us -> 328 us  [the longest x2 182 us: gather(): whole = lax.all_gather(parts, ('g', 'b'), axis=0, tiled=False)]
    another operation x5 -> x1, other arithmetic: 122 us -> 0.01 us  [on_device(): jnp.stack([jnp.where(place >= hop, lax.dynamic_index_in_dim(docs, jnp.max...]
    pallas_call x0 -> x4, Pallas kernels: none -> 117 us  [the longest x1 46.1 us: attend_back(): pl.pallas_call(functools.partial(attend_back_kernel, groups, hops), out_s...]
    concatenate x1 -> x3, local copies, waits for them, and re-layouts: 112 us -> 4.58 us  [the longest x1 3.81 us: on_device(): jnp.concatenate([dot(normed_two, gate_grad, TN), dot(normed_two, up_grad,...]
    all_gather x2 -> x0, blocking collectives: 87.1 us -> none  [the longest x1 65.2 us: on_device(): lax.all_gather(beta_weight.astype(jnp.bfloat16), ('seq', 'batch'), axis=0...]
  transfers between devices with their start and end apart: 100 -> 19, of which waited for: 11 -> 17; matrix products, arithmetic and copies ran while one was open for 26% -> 8% of each run, Pallas kernels for 0% -> 4%
where the time goes in v1:
time: 1110 us; the launch traced here: 1100 us
  waiting for transfers between devices  789 us (71%)
  Pallas kernels  117 us (11%)
  matrix products  67.7 us (6%)
  local copies, waits for them, and re-layouts  44 us (4%)
  blocking collectives  35.3 us (3%)
  other arithmetic  26.2 us (2%)
  between operations  15.1 us (1%)
    reduce_scatter x2, waiting for transfers between devices, scatter(): lax.psum_scatter(parts, ('g', 'b'), scatter_dimension=0, tiled=False)  221 us
    all_gather x2, waiting for transfers between devices, gather(): whole = lax.all_gather(parts, ('g', 'b'), axis=0, tiled=False)  182 us
    reduce_scatter x4, waiting for transfers between devices, group_sum(): lax.psum_scatter(value.astype(BF16), 'm', scatter_dimension=0, tiled=True)  86.5 us
    all_gather x5, waiting for transfers between devices, group_gather(): return lax.all_gather(value, 'm', axis=0, tiled=True)  79.9 us
    reduce_scatter x1, waiting for transfers between devices, on_device(): lax.psum_scatter(dot(active, cotangent_all, TN).astype(BF16), ('g', 'b'),...  77.2 us
    psum x1, waiting for transfers between devices, on_device(): lax.psum(dot(attended_low, branch_grad, TN).astype(BF16), ('g', 'b'))  75.1 us
    dot_general x15, matrix products, dot(): return lax.dot_general(left, right, dims, preferred_element_type=F32)  67.7 us
    all_gather x1, waiting for transfers between devices, on_device(): lax.all_gather(down_weight.astype(BF16), ('g', 'b'), axis=0, tiled=True)  62.9 us
  transfers between devices with their start and end apart: 19, of which 17 were waited for; matrix products, arithmetic and copies ran while one was open for 8% of the time, Pallas kernels for 4%

profile of v1, /device:TPU:0, one launch (start us, length us, event | category | flops | bytes accessed | tf_op | source)
XLA Modules:
  0.0 1102.9 jit_solution(15559879670250892464)
XLA Ops:
  13.7 20.4 %all_to_all.20 = bf16[4,48,1664]{2,1,0:T(8,128)(2,1)} all-to-all(bf16[4,48,1664]{2,1,0:T(8,128)(2,1)S(1)} %copy.127), channel_id=1, replica_groups=mesh['g'=4,'m'=4,'b'=2] {'m'}, dimensions={0} | all-to-all | bytes 1277952 | tf_op jit(solution)/shard_map/all_to_all | solution.py:719
  39.5 85.8 %all-gather.26.cloned.1.call-done = bf16[32,48,1664]{2,1,0:T(8,128)(2,1)} async-done(((bf16[4,48,1664]{2,1,0:T(8,128)(2,1)}), bf16[32,48,1664]{2,1,0:T(8,128)(2,1)}) %all-gather.26.cloned.1.call-update) | async-done | bytes 5111824 | tf_op jit(solution)/shard_map/all_gather | solution.py:720
  130.6 4.9 fusion.35.rows_ref
  135.5 17.4 %prepare.1 = (bf16[512,384]{1,0:T(8,128)(2,1)S(1)}, bf16[512,384]{1,0:T(8,128)(2,1)S(1)}, bf16[512,384]{1,0:T(8,128)(2,1)S(1)}, f32[512,384]{1,0:T(8,128)S(1)}, ...) custom-call(f32[512,1664]{1,0:T(8,128)} %fusion.35.rows_ref), custom_call_target="tpu_custom_call" | custom-call | tf_op jit(solution)/shard_map/prepare/pallas_call | solution.py:126
  158.7 32.2 %attend.1 = (f32[512,384]{1,0:T(8,128)}, bf16[512,384]{1,0:T(8,128)(2,1)}, f32[512,128]{1,0:T(8,128)}, bf16[3,4,512,384]{3,2,1,0:T(8,128)(2,1)}, bf16[2,512,384]{2,1,0:T(8,128)(2,1)}) custom-call(bf16[512,384]{1,0:T(8,128)(2,1)} %copy-done.2, bf16[512,384]{1,0:T(8,128)(2,1)} %copy-done.9, bf16[512,384]{1,0:T(8,128)(2,1)} %copy-done.3, f32[512,384]{1,0:T(8,128)} %copy-done, ...), custom_call_target="tpu_custom_call" | custom-call | tf_op jit(solution)/shard_map/attend/pallas_call | solution.py:396
  199.6 14.9 %all_to_all.21 = bf16[4,48,2048]{2,1,0:T(8,128)(2,1)} all-to-all(bf16[4,48,2048]{2,1,0:T(8,128)(2,1)S(1)} %pad_maximum_fusion.1), channel_id=1, replica_groups=mesh['g'=4,'m'=4,'b'=2] {'m'}, dimensions={0} | all-to-all | bytes 1572864 | tf_op jit(solution)/shard_map/all_to_all | solution.py:719
  214.6 32.7 %reduce-scatter.8.cloned.1.call-done = bf16[128,1536]{1,0:T(8,128)(2,1)} async-done(((bf16[512,1536]{1,0:T(8,128)(2,1)}), bf16[128,1536]{1,0:T(8,128)(2,1)}) %reduce-scatter.8.cloned.1.call-update) | async-done | bytes 393232 | tf_op jit(solution)/shard_map/reduce_scatter | solution.py:739
  252.5 96.1 %all-gather.28.cloned.1.call-done = bf16[32,48,2048]{2,1,0:T(8,128)(2,1)} async-done(((bf16[4,48,2048]{2,1,0:T(8,128)(2,1)}), bf16[32,48,2048]{2,1,0:T(8,128)(2,1)}) %all-gather.28.cloned.1.call-update) | async-done | bytes 6291472 | tf_op jit(solution)/shard_map/all_gather | solution.py:720
  348.6 6.6 copy.132
  355.2 13.4 %all-gather.16.cloned.1.call-done = bf16[512,1536]{1,0:T(8,128)(2,1)} async-done(((bf16[128,1536]{1,0:T(8,128)(2,1)}), bf16[512,1536]{1,0:T(8,128)(2,1)}) %all-gather.16.cloned.1.call-update) | async-done | bytes 1572880 | tf_op jit(solution)/shard_map/all_gather | solution.py:736
  368.6 5.7 fusion.9
  377.4 12.5 %all-gather.30.cloned.1.call-done = bf16[1,512,1536]{2,1,0:T(8,128)(2,1)} async-done(((bf16[1,128,1536]{2,1,0:T(8,128)(2,1)}), bf16[1,512,1536]{2,1,0:T(8,128)(2,1)}) %all-gather.30.cloned.1.call-update) | async-done | bytes 1572880 | tf_op jit(solution)/shard_map/all_gather | solution.py:736
  389.9 62.9 %all-gather.18.cloned.1.call-done = bf16[1024,1536]{1,0:T(8,128)(2,1)} async-done(((bf16[128,1536]{1,0:T(8,128)(2,1)}), bf16[1024,1536]{1,0:T(8,128)(2,1)}) %all-gather.18.cloned.1.call-update) | async-done | bytes 3145744 | tf_op jit(solution)/shard_map/all_gather | solution.py:731
  452.8 7.1 multiply_convert_fusion
  459.9 4.5 fusion.7
  464.4 5.0 fusion.3
  469.4 26.9 %reduce-scatter.12.cloned.1.call-done = bf16[128,1536]{1,0:T(8,128)(2,1)} async-done(((bf16[512,1536]{1,0:T(8,128)(2,1)}), bf16[128,1536]{1,0:T(8,128)(2,1)}) %reduce-scatter.12.cloned.1.call-update) | async-done | bytes 393232 | tf_op jit(solution)/shard_map/reduce_scatter | solution.py:739
  499.9 19.8 %all-gather.20.cloned.1.call-done = bf16[512,1536]{1,0:T(8,128)(2,1)} async-done(((bf16[128,1536]{1,0:T(8,128)(2,1)}), bf16[512,1536]{1,0:T(8,128)(2,1)}) %all-gather.20.cloned.1.call-update) | async-done | bytes 1572880 | tf_op jit(solution)/shard_map/all_gather | solution.py:736
  523.2 46.1 %attend_back.1 = (f32[512,384]{1,0:T(8,128)}, f32[512,384]{1,0:T(8,128)}, f32[512,384]{1,0:T(8,128)}, f32[512,384]{1,0:T(8,128)}, f32[512,384]{1,0:T(8,128)}) custom-call(bf16[512,384]{1,0:T(8,128)(2,1)} %copy-done.2, bf16[512,384]{1,0:T(8,128)(2,1)} %copy-done.3, f32[512,384]{1,0:T(8,128)} %copy-done, f32[512,384]{1,0:T(8,128)} %copy-done.1, ...), custom_call_target="tpu_custom_call" | custom-call | tf_op jit(solution)/shard_map/attend_back/pallas_call | solution.py:644
  575.0 20.8 %prepare_back.1 = bf16[512,1664]{1,0:T(8,128)(2,1)} custom-call(f32[512,1664]{1,0:T(8,128)} %fusion.35.rows_ref, f32[512,384]{1,0:T(8,128)S(1)} %get-tuple-element.35.inverse_ref, f32[512,384]{1,0:T(8,128)S(1)} %copy-done.4, f32[512,384]{1,0:T(8,128)S(1)} %copy-done.5, f32[512,384]{1,0:T(8,128)S(1)} %copy-done.6, f32[512,384]{1,0:T(8,128)S(1)} %copy-done.7, ...), custom_call_target="tpu_custom_call" | custom-call | tf_op jit(solution)/shard_map/prepare_back/pallas_call | solution.py:195
  595.8 5.7 convolution_convert_fusion.5
  605.1 4.7 convolution_convert_fusion
  620.9 3.8 copy.144
  625.1 5.3 convolution_convert_fusion.3
  632.6 4.6 select_convert_fusion
  640.1 75.1 %all-reduce.4.cloned.1.call-done = bf16[384,1536]{1,0:T(8,128)(2,1)} async-done(((bf16[384,1536]{1,0:T(8,128)(2,1)}), bf16[384,1536]{1,0:T(8,128)(2,1)}) %all-reduce.4.cloned.1.call-update) | async-done | bytes 1179664 | tf_op jit(solution)/shard_map/psum | solution.py:822
  715.2 77.2 %reduce-scatter.20.cloned.1.call-done = bf16[128,1536]{1,0:T(8,128)(2,1)} async-done(((bf16[1024,1536]{1,0:T(8,128)(2,1)}), bf16[128,1536]{1,0:T(8,128)(2,1)}) %reduce-scatter.20.cloned.1.call-update) | async-done | bytes 393232 | tf_op jit(solution)/shard_map/reduce_scatter | solution.py:819
  794.3 118.5 %reduce-scatter.18.cloned.1.call-done = bf16[1,4,48,2048]{3,2,1,0:T(8,128)(2,1)} async-done(((bf16[8,4,48,2048]{3,2,1,0:T(8,128)(2,1)}), bf16[1,4,48,2048]{3,2,1,0:T(8,128)(2,1)}) %reduce-scatter.18.cloned.1.call-update) | async-done | bytes 786448 | tf_op jit(solution)/shard_map/reduce_scatter | solution.py:792
  916.4 26.2 %reduce-scatter.10.cloned.1.call-done = bf16[128,1536]{1,0:T(8,128)(2,1)} async-done(((bf16[512,1536]{1,0:T(8,128)(2,1)}), bf16[128,1536]{1,0:T(8,128)(2,1)}) %reduce-scatter.10.cloned.1.call-update) | async-done | bytes 393232 | tf_op jit(solution)/shard_map/reduce_scatter | solution.py:739
  945.1 102.3 %reduce-scatter.16.cloned.1.call-done = bf16[1,4,48,1664]{3,2,1,0:T(8,128)(2,1)} async-done(((bf16[8,4,48,1664]{3,2,1,0:T(8,128)(2,1)}), bf16[1,4,48,1664]{3,2,1,0:T(8,128)(2,1)}) %reduce-scatter.16.cloned.1.call-update) | async-done | bytes 638992 | tf_op jit(solution)/shard_map/reduce_scatter | solution.py:792
  1047.4 4.2 all-to-all-start.2
  1057.0 31.5 %all-gather.22.cloned.1.call-done = bf16[1536,1536]{1,0:T(8,128)(2,1)} async-done(((bf16[384,1536]{1,0:T(8,128)(2,1)}), bf16[1536,1536]{1,0:T(8,128)(2,1)}) %all-gather.22.cloned.1.call-update) | async-done | bytes 4718608 | tf_op jit(solution)/shard_map/all_gather | solution.py:736
  (201 shorter events, 93.1 us)
Async XLA Ops:
  7.2 30.5 %all-gather.24.cloned.1.call-start = ((), (), s32[]{:S(2)}) async-start(), calls=%async_computation.24 | async-start | bytes 1966080 | tf_op jit(solution)/shard_map/all_gather | solution.py:736
  8.0 117.4 %all-gather.26.cloned.1.call-start = ((), (), s32[]{:S(2)}) async-start(), calls=%async_computation.25 | async-start | bytes 5750784 | tf_op jit(solution)/shard_map/all_gather | solution.py:720
  10.1 24.1 %copy-start.22 = (f32[48,1536]{1,0:T(8,128)S(1)}, f32[48,1536]{1,0:T(8,128)}, u32[]{:S(2)}) copy-start(f32[48,1536]{1,0:T(8,128)} %param.22) | copy-start | bytes 884740
  34.1 160.0 %all-gather.14.cloned.1.call-start = ((), (), s32[]{:S(2)}) async-start(), calls=%async_computation.11 | async-start | bytes 4866048 | tf_op jit(solution)/shard_map/all_gather | solution.py:732
  34.8 212.5 %reduce-scatter.8.cloned.1.call-start = ((), (), s32[]{:S(2)}) async-start(), calls=%async_computation.12 | async-start | bytes 1966080 | tf_op jit(solution)/shard_map/reduce_scatter | solution.py:739
  39.5 89.6 %copy-start.24 = (f32[512]{0:T(512)}, f32[512]{0:T(512)S(1)}, u32[]{:S(2)}) copy-start(f32[512]{0:T(512)S(1)} %add_rsqrt_fusion) | copy-start | bytes 6148
  191.0 6.6 copy-start.19
  197.6 151.1 %all-gather.28.cloned.1.call-start = ((), (), s32[]{:S(2)}) async-start(), calls=%async_computation.26 | async-start | bytes 7077888 | tf_op jit(solution)/shard_map/all_gather | solution.py:720
  198.7 48.6 %copy-start.10 = (bf16[1,128,1536]{2,1,0:T(8,128)(2,1)S(1)}, bf16[1,128,1536]{2,1,0:T(8,128)(2,1)}, u32[]{:S(2)}) copy-start(bf16[1,128,1536]{2,1,0:T(8,128)(2,1)} %param.14) | copy-start | bytes 1179652
  199.6 51.7 %copy-start.21 = (f32[128,1536]{1,0:T(8,128)S(1)}, f32[128,1536]{1,0:T(8,128)}, u32[]{:S(2)}) copy-start(f32[128,1536]{1,0:T(8,128)} %param.26) | copy-start | bytes 2359300
  214.6 154.0 %all-gather.16.cloned.1.call-start = ((), (), s32[]{:S(2)}) async-start(), calls=%async_computation.13 | async-start | bytes 1966080 | tf_op jit(solution)/shard_map/all_gather | solution.py:736
  250.5 139.4 %all-gather.30.cloned.1.call-start = ((), (), s32[]{:S(2)}) async-start(), calls=%async_computation.27 | async-start | bytes 1966080 | tf_op jit(solution)/shard_map/all_gather | solution.py:736
  251.2 201.6 %all-gather.18.cloned.1.call-start = ((), (), s32[]{:S(2)}) async-start(), calls=%async_computation.14 | async-start | bytes 3538944 | tf_op jit(solution)/shard_map/all_gather | solution.py:731
  252.1 244.3 %reduce-scatter.12.cloned.1.call-start = ((), (), s32[]{:S(2)}) async-start(), calls=%async_computation.16 | async-start | bytes 1966080 | tf_op jit(solution)/shard_map/reduce_scatter | solution.py:739
  464.4 32.0 %copy-start.11 = (bf16[128,1536]{1,0:T(8,128)(2,1)S(1)}, bf16[128,1536]{1,0:T(8,128)(2,1)}, u32[]{:S(2)}) copy-start(bf16[128,1536]{1,0:T(8,128)(2,1)} %reduce-scatter.8.cloned.1.call-done) | copy-start | bytes 1179652
  464.4 33.4 %copy-start.15 = (bf16[1,128,1536]{2,1,0:T(8,128)(2,1)S(1)}, bf16[1,128,1536]{2,1,0:T(8,128)(2,1)}, u32[]{:S(2)}) copy-start(bf16[1,128,1536]{2,1,0:T(8,128)(2,1)} %param.27) | copy-start | bytes 1179652
  469.4 50.3 %all-gather.20.cloned.1.call-start = ((), (), s32[]{:S(2)}) async-start(), calls=%async_computation.17 | async-start | bytes 1966080 | tf_op jit(solution)/shard_map/all_gather | solution.py:736
  499.9 131.4 %reduce-scatter.14.cloned.1.call-start = ((), (), s32[]{:S(2)}) async-start(), calls=%async_computation.18 | async-start | bytes 1966080 | tf_op jit(solution)/shard_map/reduce_scatter | solution.py:739
  523.2 72.6 %slice-start = ((s8[5111808]{0:T(1024)(128)(4,1)}), s8[917504]{0:T(1024)(128)(4,1)S(1)}, s32[]{:S(2)}) async-start(s8[5111808]{0:T(1024)(128)(4,1)} %bitcast.133), calls=%async_computation.28 | async-start | bytes 1835008
  575.0 20.8 %slice-start.1 = ((s8[5111808]{0:T(1024)(128)(4,1)}), s8[4194304]{0:T(1024)(128)(4,1)S(1)}, s32[]{:S(2)}) async-start(s8[5111808]{0:T(1024)(128)(4,1)} %bitcast.133), calls=%async_computation.29 | async-start | bytes 8388608
  601.5 113.6 %all-reduce.4.cloned.1.call-start = ((), (), s32[]{:S(2)}) async-start(), calls=%async_computation.20 | async-start | bytes 2359296 | tf_op jit(solution)/shard_map/psum | solution.py:822
  605.0 187.3 %reduce-scatter.20.cloned.1.call-start = ((), (), s32[]{:S(2)}) async-start(), calls=%async_computation.23 | async-start | bytes 3538944 | tf_op jit(solution)/shard_map/reduce_scatter | solution.py:819
  609.8 303.1 %reduce-scatter.18.cloned.1.call-start = ((), (), s32[]{:S(2)}) async-start(), calls=%async_computation.22 | async-start | bytes 7077888 | tf_op jit(solution)/shard_map/reduce_scatter | solution.py:792
  624.8 7.8 copy-start.16
  624.8 7.8 copy-start.25
  624.8 317.8 %reduce-scatter.10.cloned.1.call-start = ((), (), s32[]{:S(2)}) async-start(), calls=%async_computation.15 | async-start | bytes 1966080 | tf_op jit(solution)/shard_map/reduce_scatter | solution.py:739
  630.4 416.9 %reduce-scatter.16.cloned.1.call-start = ((), (), s32[]{:S(2)}) async-start(), calls=%async_computation.19 | async-start | bytes 5750784 | tf_op jit(solution)/shard_map/reduce_scatter | solution.py:792
  640.0 302.6 %copy-start.14 = (bf16[128,1536]{1,0:T(8,128)(2,1)S(1)}, bf16[128,1536]{1,0:T(8,128)(2,1)}, u32[]{:S(2)}) copy-start(bf16[128,1536]{1,0:T(8,128)(2,1)} %reduce-scatter.12.cloned.1.call-done) | copy-start | bytes 1179652
  640.0 302.6 %copy-start.18 = (bf16[128,1536]{1,0:T(8,128)(2,1)S(1)}, bf16[128,1536]{1,0:T(8,128)(2,1)}, u32[]{:S(2)}) copy-start(bf16[128,1536]{1,0:T(8,128)(2,1)} %reduce-scatter.14.cloned.1.call-done) | copy-start | bytes 1179652
  640.0 448.5 %all-gather.22.cloned.1.call-start = ((), (), s32[]{:S(2)}) async-start(), calls=%async_computation.21 | async-start | bytes 5898240 | tf_op jit(solution)/shard_map/all_gather | solution.py:736
  912.9 32.2 %all-to-all-start.3 = ((bf16[4,48,2048]{2,1,0:T(8,128)(2,1)}), bf16[4,48,2048]{2,1,0:T(8,128)(2,1)S(1)}, u32[]{:S(2)}, u32[]{:S(2)}) async-start(bf16[4,48,2048]{2,1,0:T(8,128)(2,1)} %bitcast.149), calls=%async_computation.9 | async-start | bytes 1572864 | tf_op jit(solution)/shard_map/all_to_all | solution.py:793
  1047.4 42.8 %all-to-all-start.2 = ((bf16[4,48,1664]{2,1,0:T(8,128)(2,1)}), bf16[4,48,1664]{2,1,0:T(8,128)(2,1)}, u32[]{:S(2)}, u32[]{:S(2)}) async-start(bf16[4,48,1664]{2,1,0:T(8,128)(2,1)} %bitcast.150), calls=%async_computation.7 | async-start | bytes 1277952 | tf_op jit(solution)/shard_map/all_to_all | solution.py:793
  (24 other events, 67.9 us)
Sparse Core Ops, SparseCore 0:
  9.6 28.0 all-gather.23
  39.9 85.4 all-gather.25
  128.8 65.1 all-gather.13
  197.7 49.5 reduce-scatter.7
  249.6 99.0 all-gather.27
  350.7 17.8 all-gather.15
  370.2 19.6 all-gather.29
  392.3 60.4 all-gather.17
  469.5 26.7 reduce-scatter.11
  500.0 19.6 all-gather.19
  601.6 29.5 reduce-scatter.13
  635.0 80.0 all-reduce.3
  718.7 73.6 reduce-scatter.19
  795.8 117.0 reduce-scatter.17
  915.2 27.3 reduce-scatter.9
  946.6 100.7 reduce-scatter.15
  1048.9 39.5 all-gather.21

commit v2 on v1

--- a/solution.py
+++ b/solution.py
@@ -85,7 +85,7 @@
     return both[:BLOCK, :BLOCK], both[:BLOCK, BLOCK:], both[BLOCK:, :BLOCK], both[BLOCK:, BLOCK:]
 
 
-def prepare_kernel(rows_ref, query_ref, key_ref, value_ref, within_ref, map_ref, inverse_ref):
+def prepare_blocks(first, last, rows_ref, query_ref, key_ref, value_ref, within_ref, map_ref, inverse_ref):
     row, col = iota(0), iota(1)
 
     def one_block(block, carry):
@@ -118,20 +118,10 @@
             inverse_ref[at, tile(head)] = inverse
         return carry
 
-    lax.fori_loop(0, GROUP, one_block, 0)
-
-
-def prepare(rows):
-    length = rows.shape[0]
-    return pl.pallas_call(
-        prepare_kernel,
-        out_shape=[jax.ShapeDtypeStruct((length, WIDE), kind) for kind in (BF16, BF16, BF16, F32, F32, F32)],
-        compiler_params=pltpu.CompilerParams(vmem_limit_bytes=48 << 20),
-        name="prepare",
-    )(rows)
-
-
-def prepare_back_kernel(rows_ref, inverse_ref, query_grad_ref, key_grad_ref, within_grad_ref, map_grad_ref, value_grad_ref, out_ref):
+    lax.fori_loop(first, last, one_block, 0)
+
+
+def prepare_back_blocks(rows_ref, inverse_ref, query_grad_ref, key_grad_ref, within_grad_ref, map_grad_ref, value_grad_ref, out_ref):
     row, col = iota(0), iota(1)
 
     def one_block(block, carry):
@@ -191,51 +181,642 @@
     lax.fori_loop(0, GROUP, one_block, 0)
 
 
-def prepare_back(*args):
-    return pl.pallas_call(
-        prepare_back_kernel,
-        out_shape=jax.ShapeDtypeStruct(args[0].shape, BF16),
-        compiler_params=pltpu.CompilerParams(vmem_limit_bytes=48 << 20),
-        name="prepare_back",
-    )(*args)
-
-
-def meet_neighbours(groups):
-    place = lax.axis_index("g")
-    others = {"m": lax.axis_index("m"), "b": lax.axis_index("b")}
-    barrier = pltpu.get_barrier_semaphore()
-
-    @pl.when(place > 0)
-    def _():
-        pl.semaphore_signal(barrier, 1, device_id={"g": place - 1, **others}, device_id_type=MESH)
-
-    @pl.when(place < groups - 1)
-    def _():
-        pl.semaphore_signal(barrier, 1, device_id={"g": place + 1, **others}, device_id_type=MESH)
-
-    pl.semaphore_wait(barrier, (place > 0).astype(jnp.int32) + (place < groups - 1).astype(jnp.int32))
-    return place, others
+def remote(source, target, send, recv, device):
+    return pltpu.make_async_remote_copy(
+        src_ref=source, dst_ref=target, send_sem=send, recv_sem=recv, device_id=device, device_id_type=MESH
+    )
+
+
+class Place:
+    def __init__(self, groups, lines):
+        self.groups, self.lines = groups, lines
+        self.g, self.m, self.b = lax.axis_index("g"), lax.axis_index("m"), lax.axis_index("b")
+        self.below, self.above = self.g > 0, self.g < groups - 1
+
+    def other(self, offset):
+        return {1: self.m + 1 - 2 * (self.m % 2), 2: (self.m + 2) % GROUP, 3: GROUP - 1 - self.m}[offset]
+
+    def member(self, offset):
+        return {"g": self.g, "m": self.other(offset), "b": self.b}
+
+    def up(self):
+        return {"g": self.g + 1, "m": self.m, "b": self.b}
+
+    def down(self):
+        return {"g": self.g - 1, "m": self.m, "b": self.b}
+
+    def across(self):
+        return {"g": self.g, "m": self.m, "b": 1 - self.b}
+
+    def meet(self, members=True, chain=True, lines=True):
+        barrier = pltpu.get_barrier_semaphore()
+
+        def greet(device):
+            pl.semaphore_signal(barrier, 1, device_id=device, device_id_type=MESH)
+
+        count = 0
+        if members:
+            for offset in range(1, GROUP):
+                greet(self.member(offset))
+            count = count + GROUP - 1
+        if lines:
+            greet(self.across())
+            count = count + 1
+        if chain:
+            pl.when(self.above)(lambda: greet(self.up()))
+            pl.when(self.below)(lambda: greet(self.down()))
+            count = count + self.above.astype(jnp.int32) + self.below.astype(jnp.int32)
+        pl.semaphore_wait(barrier, count)
+
+
+class Gather:
+    SEMS = 8
+
+    def __init__(self, place, parts, full, sems, mixed=True):
+        self.place, self.parts, self.full, self.mixed = place, parts, full, mixed
+        (self.part_send, self.part_recv, self.up_send, self.down_send, self.chain_recv, self.line_send, self.line_recv,
+         self.own_sem) = sems
+
+    @staticmethod
+    def scratch(groups):
+        dma = pltpu.SemaphoreType.DMA
+        return [dma((GROUP,)), dma((GROUP,)), dma((groups,)), dma((groups,)), dma((groups,)), dma((groups,)), dma((groups,)), dma((1,))]
+
+    def unit(self, group, line):
+        return self.full.at[group, :, line] if self.mixed else self.full.at[group, line]
+
+    def own(self):
+        p = self.place
+        if self.mixed:
+            return pltpu.make_async_copy(self.parts.at[p.m], self.full.at[p.g, p.m, p.b], self.own_sem.at[0])
+        return pltpu.make_async_copy(self.parts, self.full.at[p.g, p.b], self.own_sem.at[0])
+
+    def part(self, offset):
+        p = self.place
+        other = p.other(offset)
+        return remote(
+            self.parts.at[other], self.full.at[p.g, p.m, p.b], self.part_send.at[offset], self.part_recv.at[offset], p.member(offset)
+        )
+
+    def start(self):
+        if self.mixed:
+            for offset in (2, 3, 1):
+                self.part(offset).start()
+        self.own().start()
+
+    def chain(self, source, up):
+        p = self.place
+        unit = self.unit(source, p.b)
+        sems = self.up_send if up else self.down_send
+        return remote(unit, unit, sems.at[source], self.chain_recv.at[source], p.up() if up else p.down())
+
+    def across(self, source):
+        p = self.place
+        unit = self.unit(source, p.b)
+        return remote(unit, unit, self.line_send.at[source], self.line_recv.at[source], p.across())
+
+    def begin(self):
+        p = self.place
+        self.own().wait()
+        if self.mixed:
+            for offset in (2, 3, 1):
+                self.part(offset).wait()
+        pl.when(p.above)(lambda: self.chain(p.g, True).start())
+        pl.when(p.below)(lambda: self.chain(p.g, False).start())
+        self.across(p.g).start()
+
+    def step(self, distance):
+        p = self.place
+
+        @pl.when(p.g >= distance)
+        def _():
+            source = p.g - distance
+            self.chain(source, True).wait_recv()
+            pl.when(p.above)(lambda: self.chain(source, True).start())
+            self.across(source).start()
+
+        @pl.when(p.g + distance < p.groups)
+        def _():
+            source = p.g + distance
+            self.chain(source, False).wait_recv()
+            pl.when(p.below)(lambda: self.chain(source, False).start())
+            self.across(source).start()
+
+    def finish(self):
+        p = self.place
+
+        def settle(source, carry):
+            self.across(source).wait()
+            pl.when(p.above & (source <= p.g))(lambda: self.chain(source, True).wait_send())
+            pl.when(p.below & (source >= p.g))(lambda: self.chain(source, False).wait_send())
+            return carry
+
+        lax.fori_loop(0, p.groups, settle, 0)
+
+
+class HomeGather:
+    def __init__(self, place, part, full, sems):
+        self.place, self.part_ref, self.full = place, part, full
+        self.home = place.groups // GROUP
+        self.part_send, self.part_recv, self.up_send, self.down_send, self.chain_recv, self.line_send, self.line_recv = sems
+
+    @staticmethod
+    def scratch(groups):
+        home = groups // GROUP
+        dma = pltpu.SemaphoreType.DMA
+        return [dma((1,)), dma((GROUP,)), dma((home,)), dma((home,)), dma((home,)), dma((home,)), dma((home,))]
+
+    def at_home(self):
+        return self.place.m == self.place.g // self.home
+
+    def slot(self):
+        p = self.place
+        return self.full.at[p.g % self.home, p.m, p.b]
+
+    def hand(self):
+        p = self.place
+        keeper = p.g // self.home
+        device = {"g": p.g, "m": keeper, "b": p.b}
+        return remote(self.part_ref, self.slot(), self.part_send.at[0], self.part_recv.at[p.m], device)
+
+    def taken(self, source):
+        p = self.place
+        target = self.full.at[p.g % self.home, source, p.b]
+        return remote(self.part_ref, target, self.part_send.at[0], self.part_recv.at[source], p.member(1))
+
+    def own(self):
+        return pltpu.make_async_copy(self.part_ref, self.slot(), self.part_send.at[0])
+
+    def start(self):
+        pl.when(self.at_home())(lambda: self.own().start())
+        pl.when(jnp.logical_not(self.at_home()))(lambda: self.hand().start())
+
+    def chain(self, slot, up):
+        p = self.place
+        unit = self.full.at[slot, :, p.b]
+        sems = self.up_send if up else self.down_send
+        return remote(unit, unit, sems.at[slot], self.chain_recv.at[slot], p.up() if up else p.down())
+
+    def across(self, slot):
+        p = self.place
+        unit = self.full.at[slot, :, p.b]
+        return remote(unit, unit, self.line_send.at[slot], self.line_recv.at[slot], p.across())
+
+    def begin(self):
+        p = self.place
+
+        @pl.when(self.at_home())
+        def _():
+            self.own().wait()
+            for offset in range(1, GROUP):
+                self.taken(p.other(offset)).wait_recv()
+            slot = p.g % self.home
+            pl.when(p.above)(lambda: self.chain(slot, True).start())
+            pl.when(p.below)(lambda: self.chain(slot, False).start())
+            self.across(slot).start()
+
+        pl.when(jnp.logical_not(self.at_home()))(lambda: self.hand().wait_send())
+
+    def step(self, distance):
+        p = self.place
+        for slot in range(self.home):
+            source = p.m * self.home + slot
+
+            @pl.when(p.g - source == distance)
+            def _():
+                self.chain(slot, True).wait_recv()
+                pl.when(p.above)(lambda: self.chain(slot, True).start())
+                self.across(slot).start()
+
+            @pl.when(source - p.g == distance)
+            def _():
+                self.chain(slot, False).wait_recv()
+                pl.when(p.below)(lambda: self.chain(slot, False).start())
+                self.across(slot).start()
+
+    def finish(self):
+        p = self.place
+        for slot in range(self.home):
+            source = p.m * self.home + slot
+            self.across(slot).wait()
+            pl.when(p.above & (p.g >= source))(lambda: self.chain(slot, True).wait_send())
+            pl.when(p.below & (p.g <= source))(lambda: self.chain(slot, False).wait_send())
+
+
+class Scatter:
+    def __init__(self, place, partial, result, refs):
+        self.place, self.partial, self.result = place, partial, result
+        (self.land, self.chain_land, self.leave, self.mine_sem, self.line_send, self.line_recv, self.chain_send,
+         self.chain_recv, self.part_send, self.part_recv) = refs
+        self.parts = partial.shape[1]
+
+    @staticmethod
+    def scratch(groups, shape):
+        dma = pltpu.SemaphoreType.DMA
+        unit = (shape[1],) + tuple(shape[3:])
+        return [
+            pltpu.VMEM((groups,) + unit, BF16),
+            pltpu.VMEM((groups + 1,) + unit, BF16),
+            pltpu.VMEM((groups,) + unit, BF16),
+            dma((groups,)),
+            dma((groups,)),
+            dma((groups,)),
+            dma((groups,)),
+            dma((groups + 1,)),
+            dma((GROUP,)),
+            dma((GROUP,)),
+        ]
+
+    def load(self, target):
+        return pltpu.make_async_copy(self.partial.at[target, :, self.place.b], self.leave.at[target], self.mine_sem.at[target])
+
+    def line(self, target):
+        p = self.place
+        return remote(
+            self.partial.at[target, :, 1 - p.b], self.land.at[target], self.line_send.at[target], self.line_recv.at[target], p.across()
+        )
+
+    def up(self, target):
+        p = self.place
+        return remote(
+            self.leave.at[target], self.chain_land.at[target], self.chain_send.at[target], self.chain_recv.at[target], p.up()
+        )
+
+    def down(self, target, slot):
+        p = self.place
+        return remote(
+            self.leave.at[target], self.chain_land.at[slot], self.chain_send.at[target], self.chain_recv.at[slot], p.down()
+        )
+
+    def send_up(self, target):
+        self.up(target).start()
+
+    def send_down(self, target):
+        p = self.place
+        pl.when(p.g - 1 == target)(lambda: self.down(target, p.groups).start())
+        pl.when(p.g - 1 != target)(lambda: self.down(target, target).start())
+
+    def arrived(self, slot):
+        p = self.place
+        return remote(self.leave.at[0], self.chain_land.at[slot], self.chain_send.at[0], self.chain_recv.at[slot], p.across())
+
+    def order(self, act):
+        p = self.place
+        for step in range(p.groups - 1):
+            pl.when(p.groups - 1 - step > p.g)(lambda: act(p.groups - 1 - step))
+            pl.when(step < p.g)(lambda: act(step))
+        act(p.g)
+
+    def start(self):
+        p = self.place
+
+        def act(target):
+            self.line(target).start()
+            self.load(target).start()
+
+        self.order(act)
+
+        @pl.when(jnp.logical_not(p.below))
+        def _():
+            self.chain_land[p.g] = jnp.zeros(self.chain_land.shape[1:], BF16)
+
+        @pl.when(jnp.logical_not(p.above))
+        def _():
+            self.chain_land[p.groups] = jnp.zeros(self.chain_land.shape[1:], BF16)
+
+    def both(self, target, part):
+        return self.leave[target, part].astype(F32) + self.land[target, part].astype(F32)
+
+    def step(self, step):
+        p = self.place
+        above, below = p.groups - 1 - step, step
+
+        def ready(target):
+            self.load(target).wait()
+            self.line(target).wait_recv()
+
+        def send(target, inner, copy):
+            @pl.when(inner)
+            def _():
+                self.arrived(target).wait_recv()
+                for part in range(self.parts):
+                    self.leave[target, part] = (self.both(target, part) + self.chain_land[target, part].astype(F32)).astype(BF16)
+
+            @pl.when(jnp.logical_not(inner))
+            def _():
+                for part in range(self.parts):
+                    self.leave[target, part] = self.both(target, part).astype(BF16)
+
+            copy(target)
+
+        @pl.when(above > p.g)
+        def _():
+            ready(above)
+            send(above, p.below, self.send_up)
+
+        @pl.when(below < p.g)
+        def _():
+            ready(below)
+            send(below, p.above, self.send_down)
+
+    def hand(self, offset):
+        p = self.place
+        return remote(
+            self.leave.at[p.g, p.other(offset)], self.result.at[p.m], self.part_send.at[offset], self.part_recv.at[offset], p.member(offset)
+        )
+
+    def last(self):
+        p = self.place
+        self.load(p.g).wait()
+        self.line(p.g).wait_recv()
+        pl.when(p.below)(lambda: self.arrived(p.g).wait_recv())
+        pl.when(p.above)(lambda: self.arrived(p.groups).wait_recv())
+        for part in range(self.parts):
+            total = self.both(p.g, part) + self.chain_land[p.g, part].astype(F32) + self.chain_land[p.groups, part].astype(F32)
+            if self.parts == 1:
+                self.result[part] = total.astype(self.result.dtype)
+            else:
+                self.leave[p.g, part] = total.astype(BF16)
+        if self.parts > 1:
+            for offset in (2, 3, 1):
+                self.hand(offset).start()
+            self.result[p.m] = self.leave[p.g, p.m]
+
+    def finish(self):
+        p = self.place
+        for target in range(p.groups):
+            self.line(target).wait_send()
+            pl.when(p.g != target)(lambda: self.up(target).wait_send())
+        if self.parts > 1:
+            for offset in (2, 3, 1):
+                self.hand(offset).wait()
+
+
+class HomeScatter:
+    def __init__(self, place, partial, result, refs):
+        self.place, self.partial, self.result = place, partial, result
+        (self.land, self.chain_land, self.leave, self.mine_sem, self.line_send, self.line_recv, self.chain_send,
+         self.chain_recv, self.part_send, self.part_recv) = refs
+        self.home = place.groups // GROUP
+
+    @staticmethod
+    def scratch(groups, shape):
+        dma = pltpu.SemaphoreType.DMA
+        home = groups // GROUP
+        unit = (GROUP,) + tuple(shape[3:])
+        return [
+            pltpu.VMEM((home,) + unit, BF16),
+            pltpu.VMEM((home, 2) + unit, BF16),
+            pltpu.VMEM((home,) + unit, BF16),
+            dma((home,)),
+            dma((home,)),
+            dma((home,)),
+            dma((home,)),
+            dma((home, 2)),
+            dma((GROUP,)),
+            dma((1,)),
+        ]
+
+    def load(self, slot):
+        return pltpu.make_async_copy(self.partial.at[slot, :, self.place.b], self.leave.at[slot], self.mine_sem.at[slot])
+
+    def line(self, slot):
+        p = self.place
+        return remote(self.partial.at[slot, :, 1 - p.b], self.land.at[slot], self.line_send.at[slot], self.line_recv.at[slot], p.across())
+
+    def chain(self, slot, up):
+        p = self.place
+        side = 0 if up else 1
+        return remote(
+            self.leave.at[slot], self.chain_land.at[slot, side], self.chain_send.at[slot], self.chain_recv.at[slot, side],
+            p.up() if up else p.down(),
+        )
+
+    def start(self):
+        p = self.place
+        for slot in range(self.home):
+            self.line(slot).start()
+            self.load(slot).start()
+        for side, present in ((0, p.below), (1, p.above)):
+
+            @pl.when(jnp.logical_not(present))
+            def _():
+                for slot in range(self.home):
+                    self.chain_land[slot, side] = jnp.zeros(self.chain_land.shape[2:], BF16)
+
+    def add(self, slot, sides):
+        for part in range(GROUP):
+            total = self.leave[slot, part].astype(F32) + self.land[slot, part].astype(F32)
+            for side in sides:
+                total = total + self.chain_land[slot, side, part].astype(F32)
+            self.leave[slot, part] = total.astype(BF16)
+
+    def step(self, step):
+        p = self.place
+        for slot in range(self.home):
+            target = p.m * self.home + slot
+
+            @pl.when((p.g < target) & (p.g == step))
+            def _():
+                self.load(slot).wait()
+                self.line(slot).wait_recv()
+                pl.when(p.below)(lambda: self.chain(slot, True).wait_recv())
+                self.add(slot, [0])
+                self.chain(slot, True).start()
+
+            @pl.when((p.g > target) & (p.groups - 1 - p.g == step))
+            def _():
+                self.load(slot).wait()
+                self.line(slot).wait_recv()
+                pl.when(p.above)(lambda: self.chain(slot, False).wait_recv())
+                self.add(slot, [1])
+                self.chain(slot, False).start()
+
+    def hand(self, slot, other):
+        p = self.place
+        return remote(
+            self.leave.at[slot, other], self.result, self.part_send.at[other], self.part_recv.at[0], {"g": p.g, "m": other, "b": p.b}
+        )
+
+    def last(self):
+        p = self.place
+
+        @pl.when(p.m == p.g // self.home)
+        def _():
+            slot = p.g % self.home
+            self.load(slot).wait()
+            self.line(slot).wait_recv()
+            pl.when(p.below)(lambda: self.chain(slot, True).wait_recv())
+            pl.when(p.above)(lambda: self.chain(slot, False).wait_recv())
+            self.add(slot, [0, 1])
+            for offset in range(1, GROUP):
+                self.hand(slot, p.other(offset)).start()
+            self.result[...] = self.leave[slot, p.m]
+
+    def finish(self):
+        p = self.place
+        keeper = p.m == p.g // self.home
+
+        @pl.when(keeper)
+        def _():
+            for offset in range(1, GROUP):
+                self.hand(p.g % self.home, p.other(offset)).wait_send()
+
+        pl.when(jnp.logical_not(keeper))(lambda: self.hand(0, p.other(1)).wait_recv())
+        for slot in range(self.home):
+            self.line(slot).wait_send()
+            pl.when(p.g != p.m * self.home + slot)(lambda: self.chain(slot, True).wait_send())
+
+
+CHUNKS = 4
+
+
+class GroupSum:
+    def __init__(self, place, partial, refs):
+        self.place, self.partial = place, partial
+        self.pair_land, self.leave, self.land, self.pair_send, self.pair_recv, self.send, self.recv = refs
+        self.size = partial.shape[0] // GROUP
+        self.rows = self.size // CHUNKS
+
+    @staticmethod
+    def scratch(size, width):
+        dma = pltpu.SemaphoreType.DMA
+        return [
+            pltpu.VMEM((2, size, width), BF16),
+            pltpu.VMEM((size, width), BF16),
+            pltpu.VMEM((size, width), BF16),
+            dma((2, CHUNKS)),
+            dma((2, CHUNKS)),
+            dma((CHUNKS,)),
+            dma((CHUNKS,)),
+        ]
+
+    def at(self, chunk, member=0):
+        return pl.ds(pl.multiple_of(member * self.size + chunk * self.rows, self.rows), self.rows)
+
+    def pair(self, chunk, far):
+        p = self.place
+        member = p.other(3 if far else 1)
+        slot = 1 if far else 0
+        return remote(
+            self.partial.at[self.at(chunk, member)], self.pair_land.at[slot, self.at(chunk)], self.pair_send.at[slot, chunk],
+            self.pair_recv.at[slot, chunk], p.member(1),
+        )
+
+    def cross(self, chunk):
+        return remote(
+            self.leave.at[self.at(chunk)], self.land.at[self.at(chunk)], self.send.at[chunk], self.recv.at[chunk], self.place.member(2)
+        )
+
+    def start(self):
+        for chunk in range(CHUNKS):
+            self.pair(chunk, True).start()
+        for chunk in range(CHUNKS):
+            self.pair(chunk, False).start()
+
+    def pass_on(self, chunk):
+        self.pair(chunk, True).wait_recv()
+        own = self.partial[self.at(chunk, self.place.other(2)), :].astype(F32)
+        self.leave[self.at(chunk), :] = (own + self.pair_land[1, self.at(chunk), :].astype(F32)).astype(BF16)
+        self.cross(chunk).start()
+
+    def take(self, chunk):
+        self.pair(chunk, False).wait_recv()
+        self.cross(chunk).wait_recv()
+        own = self.partial[self.at(chunk, self.place.m), :].astype(F32)
+        return own + self.pair_land[0, self.at(chunk), :].astype(F32) + self.land[self.at(chunk), :].astype(F32)
+
+    def finish(self):
+        for chunk in range(CHUNKS):
+            self.pair(chunk, True).wait_send()
+            self.pair(chunk, False).wait_send()
+            self.cross(chunk).wait_send()
+
+
+class GroupGather:
+    def __init__(self, place, whole, refs):
+        self.place, self.whole = place, whole
+        self.send, self.recv = refs
+        self.size = whole.shape[0] // GROUP
+        self.rows = self.size // CHUNKS
+
+    @staticmethod
+    def scratch():
+        dma = pltpu.SemaphoreType.DMA
+        return [dma((3, CHUNKS)), dma((3, CHUNKS))]
+
+    def at(self, chunk, member):
+        return pl.ds(pl.multiple_of(member * self.size + chunk * self.rows, self.rows), self.rows)
+
+    def copy(self, chunk, way):
+        p = self.place
+        rows = self.whole.at[self.at(chunk, p.other(2) if way == 2 else p.m)]
+        return remote(rows, rows, self.send.at[way, chunk], self.recv.at[way, chunk], p.member(2 if way == 0 else 1))
+
+    def give(self, chunk):
+        self.copy(chunk, 0).start()
+        self.copy(chunk, 1).start()
+
+    def pass_on(self, chunk):
+        self.copy(chunk, 0).wait_recv()
+        self.copy(chunk, 2).start()
+
+    def finish(self):
+        for chunk in range(CHUNKS):
+            self.copy(chunk, 1).wait_recv()
+            self.copy(chunk, 2).wait_recv()
+            for way in range(3):
+                self.copy(chunk, way).wait_send()
 
 
 def masked(scores, counts):
     return jnp.where(counts, scores * SCALE, NEGATIVE)
+
+
+class Pauses:
+    def __init__(self, *steps):
+        self.steps = list(steps)
+
+    def __call__(self):
+        if self.steps:
+            for act in self.steps.pop(0):
+                act()
+
+    def rest(self):
+        while self.steps:
+            self()
+
+
+def several(refs, *counts):
+    refs = list(refs)
+    taken = []
+    for count in counts:
+        taken.append(refs[:count])
+        refs = refs[count:]
+    return taken
 
 
 def attend_kernel(
     groups,
     hops,
+    rows_ref,
+    doc_query_ref,
+    doc_key_ref,
+    out_part_ref,
+    feed_parts_ref,
     query_ref,
-    key_ref,
     value_ref,
     within_ref,
     map_ref,
-    doc_query_ref,
-    doc_key_ref,
+    inverse_ref,
     attended_ref,
     low_ref,
     stats_ref,
     moved_ref,
     values_ref,
+    out_full_ref,
+    feed_full_ref,
+    key_ref,
     leave_ref,
     top_ref,
     total_ref,
@@ -244,10 +825,27 @@
     key_recv,
     value_send,
     value_recv,
+    *sems,
 ):
-    place, others = meet_neighbours(groups)
-    following = {"g": place + 1, **others}
-    has_next = place < groups - 1
+    here = Place(groups, feed_full_ref.shape[2])
+    here.meet()
+    place, has_next, following = here.g, here.above, here.up()
+    home_sems, feed_sems = several(sems, len(HomeGather.scratch(groups)), len(Gather.scratch(groups)))
+    out_gather = HomeGather(here, out_part_ref, out_full_ref, home_sems)
+    feed_gather = Gather(here, feed_parts_ref, feed_full_ref, feed_sems)
+    out_gather.start()
+    feed_gather.start()
+    pauses = Pauses(
+        *[
+            (functools.partial(out_gather.step, distance), functools.partial(feed_gather.step, distance))
+            for distance in range(1, groups)
+        ]
+    )
+    prepared = (rows_ref, query_ref, key_ref, value_ref, within_ref, map_ref, inverse_ref)
+    prepare_blocks(0, GROUP // 2, *prepared)
+    out_gather.begin()
+    feed_gather.begin()
+    prepare_blocks(GROUP // 2, GROUP, *prepared)
 
     def value_copy(source, slot):
         return pltpu.make_async_remote_copy(
@@ -283,6 +881,8 @@
     def _():
         key_copy(0).start()
         value_copy(value_ref, 0).start()
+
+    pauses()
 
     def row_counts(block, hop, first, count):
         return doc_query_ref[tile(block), :] == doc_key_ref[hop, :, tile(first, count)]
@@ -359,7 +959,9 @@
         lax.fori_loop(1, hops, between, 0)
     else:
         for hop in range(1, hops):
+            pauses()
             hop_step(hop, False)
+    pauses()
     hop_step(hops, True)
 
     for block in range(GROUP):
@@ -382,35 +984,67 @@
         return carry
 
     lax.fori_loop(0, hops, settle, 0)
-
-
-def attend(groups, hops, *args):
-    length = args[0].shape[0]
-    out = [
-        jax.ShapeDtypeStruct((length, WIDE), F32),
-        jax.ShapeDtypeStruct((length, WIDE), BF16),
-        jax.ShapeDtypeStruct((length, BLOCK), F32),
-        jax.ShapeDtypeStruct((hops + 1, GROUP, length, WIDE), BF16),
-        jax.ShapeDtypeStruct((hops, length, WIDE), BF16),
-    ]
+    pauses.rest()
+    out_gather.finish()
+    feed_gather.finish()
+
+
+def in_vmem(count):
+    return [pl.BlockSpec(memory_space=pltpu.VMEM)] * count
+
+
+def anywhere(count):
+    return [pl.BlockSpec(memory_space=pl.ANY)] * count
+
+
+def shape(kind, *dims):
+    return jax.ShapeDtypeStruct(dims, kind)
+
+
+def communicating(number, name, vmem=58):
+    return {
+        "compiler_params": pltpu.CompilerParams(collective_id=number, has_side_effects=True, vmem_limit_bytes=vmem << 20),
+        "name": name,
+    }
+
+
+def attend(groups, lines, hops, projected, doc_query, doc_key, out_part, feed_parts):
+    length = projected.shape[0]
+    rows, width = out_part.shape
+    dma = pltpu.SemaphoreType.DMA
     return pl.pallas_call(
         functools.partial(attend_kernel, groups, hops),
-        out_shape=out,
-        in_specs=[pl.BlockSpec(memory_space=pltpu.VMEM)] * len(args),
-        out_specs=[pl.BlockSpec(memory_space=pltpu.VMEM)] * len(out),
+        out_shape=[
+            shape(BF16, length, WIDE),
+            shape(BF16, length, WIDE),
+            shape(F32, length, WIDE),
+            shape(F32, length, WIDE),
+            shape(F32, length, WIDE),
+            shape(F32, length, WIDE),
+            shape(BF16, length, WIDE),
+            shape(F32, length, BLOCK),
+            shape(BF16, hops + 1, GROUP, length, WIDE),
+            shape(BF16, hops, length, WIDE),
+            shape(BF16, groups // GROUP, GROUP, lines, rows, width),
+            shape(BF16, groups, GROUP, lines, rows, feed_parts.shape[2]),
+        ],
+        in_specs=in_vmem(3) + anywhere(2),
+        out_specs=in_vmem(10) + anywhere(2),
         scratch_shapes=[
+            pltpu.VMEM((length, WIDE), BF16),
             pltpu.VMEM((hops, length, WIDE), BF16),
             pltpu.VMEM((OWN, length, BLOCK), F32),
             pltpu.VMEM((OWN, length, BLOCK), F32),
             pltpu.VMEM((length, WIDE), F32),
-            pltpu.SemaphoreType.DMA((hops,)),
-            pltpu.SemaphoreType.DMA((hops,)),
-            pltpu.SemaphoreType.DMA((hops,)),
-            pltpu.SemaphoreType.DMA((hops,)),
-        ],
-        compiler_params=pltpu.CompilerParams(collective_id=1, has_side_effects=True, vmem_limit_bytes=58 << 20),
-        name="attend",
-    )(*args)
+            dma((hops,)),
+            dma((hops,)),
+            dma((hops,)),
+            dma((hops,)),
+        ]
+        + HomeGather.scratch(groups)
+        + Gather.scratch(groups),
+        **communicating(1, "attend"),
+    )(projected, doc_query, doc_key, out_part, feed_parts)
 
 
 def attend_back_kernel(
@@ -427,6 +1061,11 @@
     moved_ref,
     values_ref,
     att_grad_ref,
+    rows_ref,
+    inverse_ref,
+    feed_partial_ref,
+    rows_grad_ref,
+    feed_result_ref,
     query_grad_ref,
     key_grad_ref,
     within_grad_ref,
@@ -437,24 +1076,26 @@
     direct_ref,
     direct_value_ref,
     running_ref,
-    key_leave_ref,
-    value_leave_ref,
-    key_land_ref,
-    value_land_ref,
+    key_slots_ref,
+    value_slots_ref,
     key_send,
     key_recv,
     value_send,
     value_recv,
+    *refs,
 ):
-    place, others = meet_neighbours(groups)
-    previous = {"g": place - 1, **others}
-    has_next = place < groups - 1
+    here = Place(groups, feed_partial_ref.shape[2])
+    here.meet()
+    place, has_next, previous = here.g, here.above, here.down()
+    feed_scatter = Scatter(here, feed_partial_ref, feed_result_ref, refs)
+    feed_scatter.start()
+    pauses = Pauses(*[(functools.partial(feed_scatter.step, step),) for step in range(groups - 1)])
 
     def key_copy(hop):
         slot = hop - 1
         return pltpu.make_async_remote_copy(
-            src_ref=key_leave_ref.at[slot],
-            dst_ref=key_land_ref.at[slot],
+            src_ref=key_slots_ref.at[hop],
+            dst_ref=key_slots_ref.at[slot],
             send_sem=key_send.at[slot],
             recv_sem=key_recv.at[slot],
             device_id=previous,
@@ -464,8 +1105,8 @@
     def value_copy(hop):
         slot = hop - 1
         return pltpu.make_async_remote_copy(
-            src_ref=value_leave_ref.at[slot],
-            dst_ref=value_land_ref.at[slot],
+            src_ref=value_slots_ref.at[hop],
+            dst_ref=value_slots_ref.at[slot],
             send_sem=value_send.at[slot],
             recv_sem=value_recv.at[slot],
             device_id=previous,
@@ -494,9 +1135,9 @@
     def row_counts(block, hop, first, count):
         return doc_query_ref[tile(block), :] == doc_key_ref[hop, :, tile(first, count)]
 
-    def hop_direct(hop, slot, last):
+    def hop_direct(hop, last):
         for head in range(OWN):
-            direct_value_ref[slot, :, tile(head)] = jnp.zeros((GROUP * BLOCK, BLOCK), F32)
+            direct_value_ref[:, tile(head)] = jnp.zeros((GROUP * BLOCK, BLOCK), F32)
         for block in range(GROUP):
             first = block if last else 0
             count = GROUP - first
@@ -509,38 +1150,38 @@
                 )
                 raw = grad.astype(BF16)
                 query_grad_ref[tile(block), tile(head)] += dot(raw, keys)
-                direct_ref[slot, block, tile(first, count), tile(head)] = dot(raw, query, TN)
-                direct_value_ref[slot, tile(first, count), tile(head)] += dot(
+                direct_ref[block, tile(first, count), tile(head)] = dot(raw, query, TN)
+                direct_value_ref[tile(first, count), tile(head)] += dot(
                     weights.astype(BF16), scaled_ref[tile(block), tile(head)], TN
                 )
 
     def collect_map(block, head, keys, grads):
         map_grad_ref[tile(block), tile(head)] += dot2(keys, grads, TN)
 
-    def hop_chain(hop, slot, last):
+    def hop_chain(hop, last):
         for head in range(OWN):
             if last:
-                grads = direct_ref[slot, GROUP - 1, tile(GROUP - 1), tile(head)]
+                grads = direct_ref[GROUP - 1, tile(GROUP - 1), tile(head)]
                 for block in range(GROUP - 2, -1, -1):
                     rows = tile(block + 1, GROUP - 1 - block)
                     collect_map(block, head, moved_ref[hop, block, rows, tile(head)], grads)
                     back = dot3(grads, map_ref[tile(block), tile(head)], NT)
-                    direct = direct_ref[slot, block, tile(block, GROUP - block), tile(head)]
+                    direct = direct_ref[block, tile(block, GROUP - block), tile(head)]
                     grads = jnp.concatenate([direct[:BLOCK], direct[BLOCK:] + back], 0)
-                key_leave_ref[hop - 1, :, tile(head)] = grads.astype(BF16)
-                value_leave_ref[hop - 1, :, tile(head)] = direct_value_ref[slot, :, tile(head)].astype(BF16)
+                key_slots_ref[hop, :, tile(head)] = grads.astype(BF16)
+                value_slots_ref[hop, :, tile(head)] = direct_value_ref[:, tile(head)].astype(BF16)
             else:
                 grads = running_ref[:, tile(head)]
                 for block in range(GROUP - 1, -1, -1):
                     collect_map(block, head, moved_ref[hop, block, :, tile(head)], grads)
-                    grads = direct_ref[slot, block, :, tile(head)] + dot3(grads, map_ref[tile(block), tile(head)], NT)
-                key_leave_ref[hop - 1, :, tile(head)] = grads.astype(BF16)
+                    grads = direct_ref[block, :, tile(head)] + dot3(grads, map_ref[tile(block), tile(head)], NT)
+                key_slots_ref[hop, :, tile(head)] = grads.astype(BF16)
 
     def take(hop):
         @pl.when(has_next)
         def _():
             key_copy(hop).wait_recv()
-            running_ref[...] = key_land_ref[hop - 1].astype(F32)
+            running_ref[...] = key_slots_ref[hop - 1].astype(F32)
 
         @pl.when(jnp.logical_not(has_next))
         def _():
@@ -548,32 +1189,33 @@
 
     @pl.when(place >= hops)
     def _():
-        hop_direct(hops, hops % 2, True)
-        hop_chain(hops, hops % 2, True)
+        hop_direct(hops, True)
+        hop_chain(hops, True)
         key_copy(hops).start()
         value_copy(hops).start()
+
+    pauses()
 
     def between(hop):
         @pl.when(place >= hop)
         def _():
-            slot = lax.rem(hop, 2) if hops > 2 else hop % 2
-            hop_direct(hop, slot, False)
+            hop_direct(hop, False)
             take(hop + 1)
-            hop_chain(hop, slot, False)
+            hop_chain(hop, False)
             key_copy(hop).start()
 
             @pl.when(has_next)
             def _():
                 value_copy(hop + 1).wait_recv()
                 for head in range(OWN):
-                    value_leave_ref[hop - 1, :, tile(head)] = (
-                        direct_value_ref[slot, :, tile(head)] + value_land_ref[hop, :, tile(head)].astype(F32)
+                    value_slots_ref[hop, :, tile(head)] = (
+                        direct_value_ref[:, tile(head)] + value_slots_ref[hop, :, tile(head)].astype(F32)
                     ).astype(BF16)
 
             @pl.when(jnp.logical_not(has_next))
             def _():
                 for head in range(OWN):
-                    value_leave_ref[hop - 1, :, tile(head)] = direct_value_ref[slot, :, tile(head)].astype(BF16)
+                    value_slots_ref[hop, :, tile(head)] = direct_value_ref[:, tile(head)].astype(BF16)
 
             value_copy(hop).start()
 
@@ -587,9 +1229,10 @@
     else:
         for hop in range(hops - 1, 0, -1):
             between(hop)
+            pauses()
 
     for head in range(OWN):
-        direct_value_ref[0, :, tile(head)] = jnp.zeros((GROUP * BLOCK, BLOCK), F32)
+        direct_value_ref[:, tile(head)] = jnp.zeros((GROUP * BLOCK, BLOCK), F32)
     for block in range(GROUP):
         wide = (BLOCK, (block + 1) * BLOCK)
         counts = row_counts(block, 0, 0, block + 1) & (iota(0, wide) + block * BLOCK >= iota(1, wide))
@@ -601,13 +1244,13 @@
                 scores = jnp.concatenate([dot(query, keys, NT), scores], 1)
             weights, grad = pair(block, head, scores, counts, value_ref[tile(0, block + 1), tile(head)])
             within_grad_ref[tile(block), tile(head)] = grad[:, block * BLOCK :]
-            direct_value_ref[0, tile(0, block + 1), tile(head)] += dot(
+            direct_value_ref[tile(0, block + 1), tile(head)] += dot(
                 weights.astype(BF16), scaled_ref[tile(block), tile(head)], TN
             )
             if block:
                 raw = grad[:, : block * BLOCK].astype(BF16)
                 query_grad_ref[tile(block), tile(head)] += dot(raw, keys)
-                direct_ref[0, block, tile(0, block), tile(head)] = dot(raw, query, TN)
+                direct_ref[block, tile(0, block), tile(head)] = dot(raw, query, TN)
     take(1)
     for head in range(OWN):
         grads = running_ref[:, tile(head)]
@@ -615,17 +1258,17 @@
             key_grad_ref[tile(block), tile(head)] = grads[block * BLOCK :]
             grads = grads[: block * BLOCK]
             collect_map(block, head, moved_ref[0, block, tile(0, block), tile(head)], grads)
-            grads = direct_ref[0, block, tile(0, block), tile(head)] + dot3(grads, map_ref[tile(block), tile(head)], NT)
+            grads = direct_ref[block, tile(0, block), tile(head)] + dot3(grads, map_ref[tile(block), tile(head)], NT)
         key_grad_ref[tile(0), tile(head)] = grads
 
     @pl.when(has_next)
     def _():
         value_copy(1).wait_recv()
-        value_grad_ref[...] = direct_value_ref[0] + value_land_ref[0].astype(F32)
+        value_grad_ref[...] = direct_value_ref[...] + value_slots_ref[0].astype(F32)
 
     @pl.when(jnp.logical_not(has_next))
     def _():
-        value_grad_ref[...] = direct_value_ref[0]
+        value_grad_ref[...] = direct_value_ref[...]
 
     def settle(hop, carry):
         @pl.when(place >= hop)
@@ -636,37 +1279,84 @@
         return carry
 
     lax.fori_loop(1, hops + 1, settle, 0)
+    pauses.rest()
+    prepare_back_blocks(
+        rows_ref, inverse_ref, query_grad_ref, key_grad_ref, within_grad_ref, map_grad_ref, value_grad_ref, rows_grad_ref
+    )
+    feed_scatter.last()
+    feed_scatter.finish()
 
 
 def attend_back(groups, hops, *args):
     length = args[0].shape[0]
-    out = [jax.ShapeDtypeStruct((length, WIDE), F32)] * 5
+    feed = args[-1]
+    dma = pltpu.SemaphoreType.DMA
     return pl.pallas_call(
         functools.partial(attend_back_kernel, groups, hops),
-        out_shape=out,
-        in_specs=[pl.BlockSpec(memory_space=pltpu.VMEM)] * len(args),
-        out_specs=[pl.BlockSpec(memory_space=pltpu.VMEM)] * len(out),
-        scratch_shapes=[
+        out_shape=[shape(BF16, *args[-3].shape), shape(BF16, GROUP, *feed.shape[3:])],
+        in_specs=in_vmem(len(args) - 1) + anywhere(1),
+        out_specs=in_vmem(2),
+        scratch_shapes=[pltpu.VMEM((length, WIDE), F32)] * 5
+        + [
             pltpu.VMEM((length, WIDE), BF16),
             pltpu.VMEM((OWN, length, BLOCK), F32),
-            pltpu.VMEM((2, GROUP, length, WIDE), F32),
-            pltpu.VMEM((2, length, WIDE), F32),
+            pltpu.VMEM((GROUP, length, WIDE), F32),
             pltpu.VMEM((length, WIDE), F32),
-            pltpu.VMEM((hops, length, WIDE), BF16),
-            pltpu.VMEM((hops, length, WIDE), BF16),
-            pltpu.VMEM((hops, length, WIDE), BF16),
-            pltpu.VMEM((hops, length, WIDE), BF16),
-            pltpu.SemaphoreType.DMA((hops,)),
-            pltpu.SemaphoreType.DMA((hops,)),
-            pltpu.SemaphoreType.DMA((hops,)),
-            pltpu.SemaphoreType.DMA((hops,)),
+            pltpu.VMEM((length, WIDE), F32),
+            pltpu.VMEM((hops + 1, length, WIDE), BF16),
+            pltpu.VMEM((hops + 1, length, WIDE), BF16),
+            dma((hops,)),
+            dma((hops,)),
+            dma((hops,)),
+            dma((hops,)),
+        ]
+        + Scatter.scratch(groups, feed.shape),
+        **communicating(2, "attend_back", 60),
+    )(*args)
+
+
+def gather_kernel(groups, parts_ref, tokens_ref, cotangent_ref, full_ref, tokens_all_ref, cotangent_all_ref, send, recv, local, *sems):
+    here = Place(groups, full_ref.shape[2])
+    here.meet()
+    gather = Gather(here, parts_ref, full_ref, sems)
+    gather.start()
+    size = tokens_ref.shape[0]
+    own = pl.ds(pl.multiple_of(here.m * size, size), size)
+    copies = []
+    for index, (source, target) in enumerate(((tokens_ref, tokens_all_ref), (cotangent_ref, cotangent_all_ref))):
+        copies.append(pltpu.make_async_copy(source, target.at[own], local.at[index]))
+        for offset in (2, 3, 1):
+            copies.append(
+                remote(source, target.at[own], send.at[index, offset], recv.at[index, offset], here.member(offset))
+            )
+    for copy in copies:
+        copy.start()
+    gather.begin()
+    for distance in range(1, groups):
+        gather.step(distance)
+    for copy in copies:
+        copy.wait()
+    gather.finish()
+
+
+def gather_first(groups, lines, parts, tokens, cotangent):
+    dma = pltpu.SemaphoreType.DMA
+    size, width = tokens.shape
+    return pl.pallas_call(
+        functools.partial(gather_kernel, groups),
+        out_shape=[
+            shape(BF16, groups, GROUP, lines, *parts.shape[1:]),
+            shape(BF16, GROUP * size, width),
+            shape(BF16, GROUP * size, width),
         ],
-        compiler_params=pltpu.CompilerParams(collective_id=2, has_side_effects=True, vmem_limit_bytes=58 << 20),
-        name="attend_back",
-    )(*args)
-
-
-def rms_scale(values, gain):
+        in_specs=anywhere(3),
+        out_specs=anywhere(3),
+        scratch_shapes=[dma((2, GROUP)), dma((2, GROUP)), dma((2,))] + Gather.scratch(groups),
+        **communicating(0, "gather_first", 16),
+    )(parts, tokens, cotangent)
+
+
+def rms_norm(values, gain):
     return values * lax.rsqrt(jnp.mean(values * values, axis=-1, keepdims=True) + EPSILON) * gain
 
 
@@ -675,7 +1365,157 @@
     straight = values * scale
     lifted = grad * gain
     back = scale * (lifted - straight * jnp.mean(lifted * straight, axis=-1, keepdims=True))
-    return back, jnp.sum(grad * straight, axis=0)
+    return back, grad * straight
+
+
+def branch_kernel(groups, partial_ref, tokens_ref, gain_ref, down_ref, hidden_ref, normed_ref, down_full_ref, *refs):
+    here = Place(groups, down_full_ref.shape[1])
+    here.meet()
+    sum_refs, gather_refs, down_refs = several(refs, 7, 2, len(Gather.scratch(groups)))
+    total = GroupSum(here, partial_ref, sum_refs)
+    whole = GroupGather(here, normed_ref, gather_refs)
+    down = Gather(here, down_ref, down_full_ref, down_refs, mixed=False)
+    pauses = Pauses(*[(functools.partial(down.step, distance),) for distance in range(1, groups)])
+    total.start()
+    down.start()
+    down.begin()
+    for chunk in range(CHUNKS):
+        total.pass_on(chunk)
+    pauses()
+    for chunk in range(CHUNKS):
+        hidden = tokens_ref[total.at(chunk), :].astype(F32) + total.take(chunk)
+        hidden_ref[total.at(chunk), :] = hidden
+        normed_ref[whole.at(chunk, here.m), :] = rms_norm(hidden, gain_ref[...]).astype(BF16)
+        whole.give(chunk)
+    pauses()
+    for chunk in range(CHUNKS):
+        whole.pass_on(chunk)
+    pauses.rest()
+    whole.finish()
+    total.finish()
+    down.finish()
+
+
+def branch(groups, lines, partial, tokens, gain, down):
+    size, width = tokens.shape
+    return pl.pallas_call(
+        functools.partial(branch_kernel, groups),
+        out_shape=[shape(F32, size, width), shape(BF16, GROUP * size, width), shape(BF16, groups, lines, *down.shape)],
+        in_specs=in_vmem(3) + anywhere(1),
+        out_specs=in_vmem(2) + anywhere(1),
+        scratch_shapes=GroupSum.scratch(size, width) + GroupGather.scratch() + Gather.scratch(groups),
+        **communicating(3, "branch", 32),
+    )(partial, tokens, gain, down)
+
+
+def branch_back_kernel(
+    groups, partial_ref, hidden_ref, cotangent_ref, gain_ref, down_ref, grad_ref, grad_low_ref, gain_grad_ref, down_result_ref, *refs
+):
+    here = Place(groups, down_ref.shape[2])
+    here.meet()
+    sum_refs, gather_refs, down_refs = several(refs, 7, 2, len(Scatter.scratch(groups, down_ref.shape)))
+    total = GroupSum(here, partial_ref, sum_refs)
+    whole = GroupGather(here, grad_low_ref, gather_refs)
+    down = Scatter(here, down_ref, down_result_ref, down_refs)
+    pauses = Pauses(*[(functools.partial(down.step, step),) for step in range(groups - 1)])
+    total.start()
+    down.start()
+    for chunk in range(CHUNKS):
+        total.pass_on(chunk)
+    pauses()
+    gain_grad = jnp.zeros((1, gain_ref.shape[1]), F32)
+    for chunk in range(CHUNKS):
+        back, gain_rows = rms_back(hidden_ref[total.at(chunk), :], gain_ref[...], total.take(chunk))
+        grad = cotangent_ref[total.at(chunk), :].astype(F32) + back
+        gain_grad = gain_grad + jnp.sum(gain_rows, axis=0, keepdims=True)
+        grad_ref[total.at(chunk), :] = grad
+        grad_low_ref[whole.at(chunk, here.m), :] = grad.astype(BF16)
+        whole.give(chunk)
+    gain_grad_ref[...] = gain_grad
+    pauses()
+    for chunk in range(CHUNKS):
+        whole.pass_on(chunk)
+    pauses.rest()
+    whole.finish()
+    total.finish()
+    down.last()
+    down.finish()
+
+
+def branch_back(groups, partial, hidden, cotangent, gain, down):
+    size, width = hidden.shape
+    return pl.pallas_call(
+        functools.partial(branch_back_kernel, groups),
+        out_shape=[shape(F32, size, width), shape(BF16, GROUP * size, width), shape(F32, 1, width), shape(F32, 1, *down.shape[3:])],
+        in_specs=in_vmem(4) + anywhere(1),
+        out_specs=in_vmem(4),
+        scratch_shapes=GroupSum.scratch(size, width) + GroupGather.scratch() + Scatter.scratch(groups, down.shape),
+        **communicating(4, "branch_back", 48),
+    )(partial, hidden, cotangent, gain, down)
+
+
+def finish_kernel(
+    groups,
+    first_ref,
+    out_ref,
+    normed_partial_ref,
+    output_partial_ref,
+    tokens_ref,
+    hidden_ref,
+    grad_ref,
+    gain_ref,
+    first_result_ref,
+    out_result_ref,
+    tokens_grad_ref,
+    output_ref,
+    *refs,
+):
+    here = Place(groups, first_ref.shape[2])
+    here.meet()
+    first_refs, out_refs, normed_refs, output_refs = several(
+        refs, len(Scatter.scratch(groups, first_ref.shape)), len(HomeScatter.scratch(groups, out_ref.shape)), 7, 7
+    )
+    first = Scatter(here, first_ref, first_result_ref, first_refs)
+    out = HomeScatter(here, out_ref, out_result_ref, out_refs)
+    normed = GroupSum(here, normed_partial_ref, normed_refs)
+    output = GroupSum(here, output_partial_ref, output_refs)
+    out.start()
+    first.start()
+    normed.start()
+    output.start()
+    for chunk in range(CHUNKS):
+        normed.pass_on(chunk)
+    for chunk in range(CHUNKS):
+        output.pass_on(chunk)
+    for step in range(groups - 1):
+        out.step(step)
+        first.step(step)
+    for chunk in range(CHUNKS):
+        back, _ = rms_back(tokens_ref[normed.at(chunk), :].astype(F32), gain_ref[...], normed.take(chunk))
+        tokens_grad_ref[normed.at(chunk), :] = (grad_ref[normed.at(chunk), :] + back).astype(BF16)
+    for chunk in range(CHUNKS):
+        output_ref[output.at(chunk), :] = (hidden_ref[output.at(chunk), :] + output.take(chunk)).astype(BF16)
+    out.last()
+    first.last()
+    normed.finish()
+    output.finish()
+    out.finish()
+    first.finish()
+
+
+def finish(groups, first, out, normed_partial, output_partial, tokens, hidden, grad, gain):
+    size, width = tokens.shape
+    return pl.pallas_call(
+        functools.partial(finish_kernel, groups),
+        out_shape=[shape(BF16, GROUP, *first.shape[3:]), shape(BF16, *out.shape[3:]), shape(BF16, size, width), shape(BF16, size, width)],
+        in_specs=anywhere(2) + in_vmem(6),
+        out_specs=in_vmem(4),
+        scratch_shapes=Scatter.scratch(groups, first.shape)
+        + HomeScatter.scratch(groups, out.shape)
+        + GroupSum.scratch(size, width)
+        + GroupSum.scratch(size, width),
+        **communicating(5, "finish"),
+    )(first, out, normed_partial, output_partial, tokens, hidden, grad, gain)
 
 
 def on_device(
@@ -702,7 +1542,7 @@
     block_rows = tokens.shape[1]
     hops = groups // 2
     doc_columns = -(-block_rows // rows)
-    place, member, line = lax.axis_index("g"), lax.axis_index("m"), lax.axis_index("b")
+    place, line = lax.axis_index("g"), lax.axis_index("b")
 
     def columns(weight):
         return jnp.transpose(weight.astype(BF16).reshape(rows, GROUP, -1), (1, 0, 2))
@@ -715,32 +1555,17 @@
         [columns(w) for w in (query_weight, key_weight, value_weight, house_weight, beta_weight)] + [same], 2
     )
 
-    def gather(parts):
-        parts = lax.all_to_all(parts, "m", 0, 0, tiled=True)
-        whole = lax.all_gather(parts, ("g", "b"), axis=0, tiled=False)
-        whole = whole.reshape((groups, batch) + parts.shape)
-        return jnp.transpose(whole, (0, 2, 1, 3, 4)).reshape(devices * parts.shape[1], parts.shape[2])
-
     def unit_columns(weight):
         parts = weight.astype(BF16).reshape(rows, groups, GROUP, batch, hidden_rows)
         return jnp.transpose(parts, (2, 0, 1, 3, 4)).reshape(GROUP, rows, hidden_own)
 
-    first = gather(first_parts)
-    feed = gather(jnp.concatenate([unit_columns(gate_weight), unit_columns(up_weight)], 2))
-    gate_full, up_full = feed[:, :hidden_own], feed[:, hidden_own:]
-    down_full = lax.all_gather(down_weight.astype(BF16), ("g", "b"), axis=0, tiled=True)
-    out_all = lax.all_gather(out_weight.astype(BF16), ("g", "m", "b"), axis=0, tiled=True)
-    out_full = lax.dynamic_slice_in_dim(out_all, member * WIDE, WIDE)
-
-    def group_gather(value):
-        return lax.all_gather(value, "m", axis=0, tiled=True)
-
-    def group_sum(value):
-        return lax.psum_scatter(value.astype(BF16), "m", scatter_dimension=0, tiled=True).astype(F32)
+    feed_parts = jnp.concatenate([unit_columns(gate_weight), unit_columns(up_weight)], 2)
+    first, tokens_all, cotangent_all = gather_first(groups, batch, first_parts, tokens[0], cotangent[0])
+    first = first.reshape(width, -1)
 
     extra = first[:, 4 * WIDE :]
-    gain_one = extra[:, OWN].astype(F32)
-    gain_two = extra[:, OWN + 1].astype(F32)
+    gain_one = extra[:, OWN].astype(F32)[None]
+    gain_two = extra[:, OWN + 1].astype(F32)[None]
     docs = extra[:, OWN + 2 : OWN + 2 + doc_columns].astype(jnp.int32)
     docs = docs.reshape(devices, -1)[:, :block_rows].reshape(groups, GROUP, batch, block_rows)
     docs = lax.dynamic_index_in_dim(docs, line, 2, keepdims=False).reshape(groups, GROUP * block_rows)
@@ -752,51 +1577,55 @@
     )[:, None, :]
     doc_query = lax.dynamic_index_in_dim(docs, place, 0, keepdims=False)[:, None]
 
-    tokens_all = group_gather(tokens[0])
-    cotangent_all = group_gather(cotangent[0])
-    inputs = tokens[0].astype(F32)
-    normed = rms_scale(tokens_all.astype(F32), gain_one).astype(BF16)
+    tokens_wide = tokens_all.astype(F32)
+    straight = tokens_wide * lax.rsqrt(jnp.mean(tokens_wide * tokens_wide, axis=-1, keepdims=True) + EPSILON)
+    normed = (straight * gain_one).astype(BF16)
     projected = dot(normed, first)
-    query, key, value, within, maps, inverse = prepare(projected)
-    attended, attended_low, stats, moved, values = attend(
-        groups, hops, query, key, value, within, maps, doc_query, doc_key
+    (query, value, within, maps, inverse, attended, attended_low, stats, moved, values, out_full, feed) = attend(
+        groups, batch, hops, projected, doc_query, doc_key, out_weight.astype(BF16), feed_parts
     )
-    hidden = inputs + group_sum(dot(attended_low, out_full))
-    normed_two = group_gather(rms_scale(hidden, gain_two).astype(BF16))
-    gate = dot(normed_two, gate_full)
-    up = dot(normed_two, up_full)
+    out_full = out_full.reshape(WIDE, width)
+    feed = feed.reshape(width, -1)
+    hidden, normed_two, down_full = branch(
+        groups, batch, dot(attended_low, out_full).astype(BF16), tokens[0], gain_two, down_weight.astype(BF16)
+    )
+    down_full = down_full.reshape(hidden_own, width)
+    both = dot(normed_two, feed)
+    gate, up = both[:, :hidden_own], both[:, hidden_own:]
     sigmoid = jax.nn.sigmoid(gate)
     silu = gate * sigmoid
     active = (silu * up).astype(BF16)
-    output = (hidden + group_sum(dot(active, down_full))).astype(BF16)[None]
+    output_partial = dot(active, down_full).astype(BF16)
 
     active_grad = dot(cotangent_all, down_full, NT)
     gate_grad = (active_grad * up * (sigmoid * (1.0 + gate * (1.0 - sigmoid)))).astype(BF16)
     up_grad = (active_grad * silu).astype(BF16)
-    normed_two_grad = group_sum(dot(gate_grad, gate_full, NT) + dot(up_grad, up_full, NT))
-    hidden_back, gain_two_grad = rms_back(hidden, gain_two, normed_two_grad)
-    hidden_grad = cotangent[0].astype(F32) + hidden_back
-    branch_grad = group_gather(hidden_grad.astype(BF16))
+    feed_grads = jnp.concatenate([gate_grad, up_grad], 1)
+    down_partial = dot(active, cotangent_all, TN).astype(BF16).reshape(groups, 1, batch, hidden_rows, width)
+    hidden_grad, branch_grad, gain_two_grad, down_weight_grad = branch_back(
+        groups, dot(feed_grads, feed, NT).astype(BF16), hidden, cotangent[0], gain_two, down_partial
+    )
     att_grad = dot(branch_grad, out_full, NT).astype(BF16)
-    query_grad, key_grad, within_grad, map_grad, value_grad = attend_back(
-        groups, hops, query, value, within, maps, doc_query, doc_key, attended, stats, moved, values, att_grad
+    feed_partial = dot(normed_two, feed_grads, TN).astype(BF16).reshape(groups, GROUP, batch, rows, -1)
+    rows_grad, feed_grad = attend_back(
+        groups, hops, query, value, within, maps, doc_query, doc_key, attended, stats, moved, values, att_grad, projected, inverse,
+        feed_partial,
     )
-    rows_grad = prepare_back(projected, inverse, query_grad, key_grad, within_grad, map_grad, value_grad)
-    normed_grad = group_sum(dot(rows_grad, first, NT))
-    inputs_back, gain_one_grad = rms_back(inputs, gain_one, normed_grad)
-    tokens_grad = (hidden_grad + inputs_back).astype(BF16)[None]
-
-    def scatter(full):
-        parts = full.astype(BF16).reshape(groups, GROUP, batch, rows, full.shape[1])
-        parts = jnp.transpose(parts, (0, 2, 1, 3, 4)).reshape(groups * batch, GROUP, rows, full.shape[1])
-        parts = lax.psum_scatter(parts, ("g", "b"), scatter_dimension=0, tiled=False)
-        return lax.all_to_all(parts, "m", 0, 0, tiled=True).astype(F32)
-
-    first_grad = dot(normed, rows_grad, TN)
-    lane = iota(1, (1, first_grad.shape[1]))
-    first_grad = jnp.where(lane == 4 * WIDE + OWN, gain_one_grad[:, None], first_grad)
-    first_grad = jnp.where(lane == 4 * WIDE + OWN + 1, gain_two_grad[:, None], first_grad)
-    first_grad = scatter(first_grad)
+    normed_grad = dot(rows_grad, first, NT)
+    gain_one_grad = jnp.sum(normed_grad * straight, axis=0)
+    first_partial = dot(normed, rows_grad, TN)
+    lane = iota(1, (1, first_partial.shape[1]))
+    first_partial = jnp.where(lane == 4 * WIDE + OWN, gain_one_grad[:, None], first_partial)
+    first_partial = jnp.where(lane == 4 * WIDE + OWN + 1, gain_two_grad[0][:, None], first_partial)
+    first_partial = first_partial.astype(BF16).reshape(groups, GROUP, batch, rows, -1)
+    out_partial = dot(attended_low, branch_grad, TN).astype(BF16).reshape(groups // GROUP, GROUP, batch, rows, width)
+    first_grad, out_weight_grad, tokens_grad, output = finish(
+        groups, first_partial, out_partial, normed_grad.astype(BF16), output_partial, tokens[0], hidden, hidden_grad, gain_one
+    )
+    first_grad = first_grad.astype(F32)
+    output, tokens_grad = output[None], tokens_grad[None]
+    out_weight_grad = out_weight_grad.astype(F32)
+    down_weight_grad = down_weight_grad[0]
 
     def whole_columns(parts):
         return jnp.transpose(parts, (1, 0, 2)).reshape(rows, -1)
@@ -806,23 +1635,13 @@
     ]
     beta_weight_grad = whole_columns(first_grad[:, :, 4 * WIDE : 4 * WIDE + OWN])
     gains_grad = jnp.sum(first_grad[:, :, 4 * WIDE + OWN : 4 * WIDE + OWN + 2], axis=0)
-    feed_grad = scatter(
-        jnp.concatenate([dot(normed_two, gate_grad, TN), dot(normed_two, up_grad, TN)], 1)
-    )
 
     def unit_whole(parts):
-        parts = parts.reshape(GROUP, rows, groups, batch, hidden_rows)
+        parts = parts.astype(F32).reshape(GROUP, rows, groups, batch, hidden_rows)
         return jnp.transpose(parts, (1, 2, 0, 3, 4)).reshape(rows, -1)
 
     gate_weight_grad = unit_whole(feed_grad[:, :, :hidden_own])
     up_weight_grad = unit_whole(feed_grad[:, :, hidden_own:])
-    down_weight_grad = lax.psum_scatter(
-        dot(active, cotangent_all, TN).astype(BF16), ("g", "b"), scatter_dimension=0, tiled=True
-    ).astype(F32)
-    out_grad = lax.psum(dot(attended_low, branch_grad, TN).astype(BF16), ("g", "b"))
-    out_grad = group_gather(out_grad)
-    own = (place * GROUP + member) * batch + line
-    out_weight_grad = lax.dynamic_slice_in_dim(out_grad, own * rows, rows).astype(F32)
     return (
         output,
         tokens_grad,

time: 1110 us -> 627 us (0.56)
  waiting for transfers between devices: 789 us -> 0 us
  Pallas kernels: 117 us -> 532 us
  blocking collectives: 35.3 us -> 0 us
  local copies, waits for them, and re-layouts: 44 us -> 22.2 us
  other arithmetic: 26.2 us -> 9.31 us
  matrix products: 67.7 us -> 51.2 us
  between operations: 15.1 us -> 1.76 us
    reduce_scatter x7 -> x0, waiting for transfers between devices: 385 us -> none  [the longest x2 221 us: scatter(): lax.psum_scatter(parts, ('g', 'b'), scatter_dimension=0, tiled=False)]
    all_gather x9 -> x0, waiting for transfers between devices: 328 us -> none  [the longest x2 182 us: gather(): whole = lax.all_gather(parts, ('g', 'b'), axis=0, tiled=False)]
    pallas_call x2 -> x4, Pallas kernels: 38.2 us -> 298 us  [the longest x1 112 us: finish(): pl.pallas_call(functools.partial(finish_kernel, groups), out_shape=[shape...]
    pallas_call x1, Pallas kernels: 46.1 us -> 136 us  [attend_back(): pl.pallas_call(functools.partial(attend_back_kernel, groups, hops), out_s...]
    psum x1 -> x0, waiting for transfers between devices: 75.1 us -> none  [on_device(): lax.psum(dot(attended_low, branch_grad, TN).astype(BF16), ('g', 'b'))]
    pallas_call x1, Pallas kernels: 32.2 us -> 97.7 us  [attend(): pl.pallas_call(functools.partial(attend_kernel, groups, hops), out_shape=...]
    all_to_all x2 -> x0, blocking collectives: 35.3 us -> none  [gather(): parts = lax.all_to_all(parts, 'm', 0, 0, tiled=True)]
    dot_general x15 -> x12, matrix products: 67.7 us -> 51.2 us  [dot(): return lax.dot_general(left, right, dims, preferred_element_type=F32)]
  transfers between devices with their start and end apart: 19 -> 0, of which waited for: 17 -> 0; matrix products, arithmetic and copies ran while one was open for 8% -> 0% of each run, Pallas kernels for 4% -> 0%
where the time goes in v2:
time: 627 us; the launch traced here: 617 us
  Pallas kernels  532 us (85%)
  matrix products  51.2 us (8%)
  local copies, waits for them, and re-layouts  22.2 us (4%)
  other arithmetic  9.31 us (1%)
    pallas_call x1, Pallas kernels, attend_back(): pl.pallas_call(functools.partial(attend_back_kernel, groups, hops), out_s...  136 us
    pallas_call x1, Pallas kernels, finish(): pl.pallas_call(functools.partial(finish_kernel, groups), out_shape=[shape...  112 us
    pallas_call x1, Pallas kernels, attend(): pl.pallas_call(functools.partial(attend_kernel, groups, hops), out_shape=...  97.7 us
    pallas_call x1, Pallas kernels, gather_first(): pl.pallas_call(functools.partial(gather_kernel, groups), out_shape=[shape...  75.3 us
    pallas_call x1, Pallas kernels, branch(): pl.pallas_call(functools.partial(branch_kernel, groups), out_shape=[shape...  58.5 us
    pallas_call x1, Pallas kernels, branch_back(): pl.pallas_call(functools.partial(branch_back_kernel, groups), out_shape=[...  52.6 us
    dot_general x12, matrix products, dot(): return lax.dot_general(left, right, dims, preferred_element_type=F32)  51.2 us

profile of v2, /device:TPU:0, one launch (start us, length us, event | category | flops | bytes accessed | tf_op | source)
XLA Modules:
  0.0 616.6 jit_solution(1073259236081555221)
XLA Ops:
  0.7 1.0 convert_element_type.128
  1.7 1.1 convert_element_type.129
  2.8 1.0 convert_element_type.126
  4.9 75.3 %gather_first.1 = (bf16[4,4,2,48,1664]{4,3,2,1,0:T(8,128)(2,1)S(1)}, bf16[512,1536]{1,0:T(8,128)(2,1)S(1)}, bf16[512,1536]{1,0:T(8,128)(2,1)S(1)}) custom-call(bf16[4,48,1664]{2,1,0:T(8,128)(2,1)S(1)} %concatenate.13.parts_ref, bf16[128,1536]{1,0:T(8,128)(2,1)S(1)} %bitcast.104, bf16[128,1536]{1,0:T(8,128)(2,1)S(1)} %bitcast.106), custom_call_target="tpu_custom_call" | custom-call | tf_op jit(solution)/shard_map/gather_first/pallas_call | solution.py:1345
  80.3 1.1 copy-done.8
  81.4 2.3 copy-done.7
  85.0 0.9 copy.103.doc_query_ref
  85.9 1.4 fusion.12
  87.9 7.3 %fusion.7.rows_ref = f32[512,1664]{1,0:T(8,128)} fusion(bf16[1536,1664]{1,0:T(8,128)(2,1)} %bitcast.111, bf16[512,1536]{1,0:T(8,128)(2,1)S(1)} %get-tuple-element.42, f32[1536]{0:T(1024)S(1)} %convert_reduce_fusion, f32[512]{0:T(512)S(1)} %add_rsqrt_fusion), kind=kOutput, calls=%fused_computation.22 | convolution fusion | flops 2620391424 | bytes 10100736 | tf_op jit(solution)/shard_map/dot_general | solution.py:30
  97.3 0.9 pad_maximum_fusion.3.feed_parts_ref
  98.9 97.7 %attend.1 = (bf16[512,384]{1,0:T(8,128)(2,1)}, bf16[512,384]{1,0:T(8,128)(2,1)}, f32[512,384]{1,0:T(8,128)}, f32[512,384]{1,0:T(8,128)}, f32[512,384]{1,0:T(8,12...) custom-call(f32[512,1664]{1,0:T(8,128)} %fusion.7.rows_ref, ...), custom_call_target="tpu_custom_call" | custom-call | tf_op jit(solution)/shard_map/attend/pallas_call | solution.py:1015
  196.6 2.4 convolution_convert_fusion.4.partial_ref
  199.3 58.5 %branch.1 = (f32[128,1536]{1,0:T(8,128)S(1)}, bf16[512,1536]{1,0:T(8,128)(2,1)S(1)}, bf16[4,2,128,1536]{3,2,1,0:T(8,128)(2,1)S(1)}) custom-call(bf16[512,1536]{1,0:T(8,128)(2,1)S(1)} %convolution_convert_fusion.4.partial_ref, bf16[128,1536]{1,0:T(8,128)(2,1)S(1)} %bitcast.105, f32[1,1536]{1,0:T(1,128)S(1)} %bitcast_convert_fusion.gain_ref, ...), custom_call_target="tpu_custom_call" | custom-call | tf_op jit(solution)/shard_map/branch/pallas_call | solution.py:1401
  257.8 5.8 fusion.14
  263.7 2.5 multiply_convert_fusion.2
  266.2 3.0 convolution_convert_fusion.2.output_partial_ref
  269.2 3.6 convolution_convert_fusion.1
  272.8 3.5 convolution_convert_fusion.3.partial_ref
  276.3 52.6 %branch_back.1 = (f32[128,1536]{1,0:T(8,128)S(1)}, bf16[512,1536]{1,0:T(8,128)(2,1)S(1)}, f32[1,1536]{1,0:T(1,128)S(1)}, f32[1,128,1536]{2,1,0:T(8,128)S(1)}) custom-call(bf16[512,1536]{1,0:T(8,128)(2,1)S(1)} %convolution_convert_fusion.3.partial_ref, f32[128,1536]{1,0:T(8,128)S(1)} %get-tuple-element.49.hidden_ref, bf16[128,1536]{1,0:T(8,128)(2,1)S(1)} %bitcast.107, ...), custom_call_target="tpu_custom_call" | custom-call | tf_op jit(solution)/shard_map/branch_back/pallas_call | solution.py:1447
  329.0 1.8 convolution_convert_fusion.5
  330.8 5.5 convolution_convert_fusion
  336.3 1.7 convolution_convert_fusion.6.att_grad_ref
  338.1 136.3 %attend_back.1 = (bf16[512,1664]{1,0:T(8,128)(2,1)}, bf16[4,48,2048]{2,1,0:T(8,128)(2,1)}) custom-call(bf16[512,384]{1,0:T(8,128)(2,1)} %get-tuple-element.51.query_ref, bf16[512,384]{1,0:T(8,128)(2,1)} %get-tuple-element.52.value_ref, f32[512,384]{1,0:T(8,128)} %get-tuple-element.53.within_ref, f32[512,384]{1,0:T(8,128)} %get-tuple-element.54.map_ref, ...), custom_call_target="tpu_custom_call" | custom-call | tf_op jit(solution)/shard_map/attend_back/pallas_call | solution.py:1294
  474.4 7.2 %fusion.13 = (bf16[512,1536]{1,0:T(8,128)(2,1)}, bf16[1536]{0:T(1024)(128)(2,1)S(1)}) fusion(f32[512]{0:T(512)S(1)} %add_rsqrt_fusion, bf16[512,1536]{1,0:T(8,128)(2,1)S(1)} %copy-done.3, bf16[512,1664]{1,0:T(8,128)(2,1)} %get-tuple-element.61, bf16[1536,1664]{1,0:T(8,128)(2,1)} %bitcast.112), kind=kOutput, calls=%fused_computation.60 | convolution fusion | flops 2621176320 | bytes 9966592 | tf_op jit(solution)/shard_map/dot_general | solution.py:30
  481.7 6.7 %select_convert_fusion = bf16[1536,1664]{1,0:T(8,128)(2,1)} fusion(bf16[512,1664]{1,0:T(8,128)(2,1)} %get-tuple-element.61, bf16[1536]{0:T(1024)(128)(2,1)S(1)} %get-tuple-element.77, bf16[1536]{0:T(1024)(128)(2,1)S(1)} %reduce.2, pred[1664]{0:T(1024)(128)(4,1)S(1)} %get-tuple-element.92, pred[1664]{0:T(1024)(128)(4,1)S(1)} %get-tuple-element.93, ...), kind=kOutput, calls=%fused_computation | convolution fusion | flops 2625503232 | bytes 8406272 | tf_op jit(solution)/shard_map/dot_general | solution.py:30
  489.0 111.6 %finish.1 = (bf16[4,48,1664]{2,1,0:T(8,128)(2,1)}, bf16[48,1536]{1,0:T(8,128)(2,1)}, bf16[128,1536]{1,0:T(8,128)(2,1)}, bf16[128,1536]{1,0:T(8,128)(2,1)}) custom-call(bf16[4,4,2,48,1664]{4,3,2,1,0:T(8,128)(2,1)} %bitcast.116, bf16[1,4,2,48,1536]{4,3,2,1,0:T(8,128)(2,1)} %bitcast.122, bf16[512,1536]{1,0:T(8,128)(2,1)} %get-tuple-element.76.normed_partial_ref, ...), custom_call_target="tpu_custom_call" | custom-call | tf_op jit(solution)/shard_map/finish/pallas_call | solution.py:1508
  600.6 1.2 convert_element_type.159
  607.1 1.3 slice_convert_fusion
  609.5 1.5 reshape.218
  612.2 1.5 reshape.220
  614.4 0.7 copy.138
  615.2 0.9 copy.139
  (111 shorter events, 14.6 us)
Async XLA Ops:
  0.6 3.2 copy-start.17
  0.7 3.2 copy-start.21
  0.7 3.4 copy-start.22
  0.7 3.5 copy-start.23
  0.7 3.7 copy-start.20
  1.7 3.2 copy-start
  1.7 3.2 copy-start.4
  80.3 1.2 copy-start.8
  81.4 2.3 copy-start.7
  81.4 6.5 %copy-start.2 = (bf16[512,1536]{1,0:T(8,128)(2,1)}, bf16[512,1536]{1,0:T(8,128)(2,1)S(1)}, u32[]{:S(2)}) copy-start(bf16[512,1536]{1,0:T(8,128)(2,1)S(1)} %get-tuple-element.42) | copy-start | bytes 4718596
  87.9 7.3 %copy-start.11 = (f32[48,4096]{1,0:T(8,128)S(1)}, f32[48,4096]{1,0:T(8,128)}, u32[]{:S(2)}) copy-start(f32[48,4096]{1,0:T(8,128)} %param.24) | copy-start | bytes 2359300
  95.3 1.1 copy-start.12
  96.4 1.8 copy-start.18
  196.6 2.7 copy-start.13
  257.8 18.5 %copy-start.1 = (f32[128,1536]{1,0:T(8,128)}, f32[128,1536]{1,0:T(8,128)S(1)}, u32[]{:S(2)}) copy-start(f32[128,1536]{1,0:T(8,128)S(1)} %get-tuple-element.49.hidden_ref) | copy-start | bytes 2359300
  257.8 5.8 copy-start.9
  266.2 6.6 %slice-start = ((s8[6291456]{0:T(1024)(128)(4,1)}), s8[4194304]{0:T(1024)(128)(4,1)S(1)}, s32[]{:S(2)}) async-start(s8[6291456]{0:T(1024)(128)(4,1)} %bitcast.140), calls=%async_computation | async-start | bytes 8388608
  269.2 3.6 slice-start.1
  272.8 3.5 copy-start.5
  276.3 52.6 %copy-start.14 = (bf16[512,384]{1,0:T(8,128)(2,1)S(1)}, bf16[512,384]{1,0:T(8,128)(2,1)}, u32[]{:S(2)}) copy-start(bf16[512,384]{1,0:T(8,128)(2,1)} %get-tuple-element.44) | copy-start | bytes 1179652
  328.9 1.8 copy-start.6
  330.8 5.6 copy-start.10
  338.1 136.3 %copy-start.3 = (bf16[512,1536]{1,0:T(8,128)(2,1)S(1)}, bf16[512,1536]{1,0:T(8,128)(2,1)}, u32[]{:S(2)}) copy-start(bf16[512,1536]{1,0:T(8,128)(2,1)} %copy-done.2) | copy-start | bytes 4718596
  601.8 4.6 copy-start.19
  611.0 2.6 copy-start.16
  611.7 2.7 copy-start.15

commit v3 on v2

--- a/solution.py
+++ b/solution.py
@@ -121,7 +121,7 @@
     lax.fori_loop(first, last, one_block, 0)
 
 
-def prepare_back_blocks(rows_ref, inverse_ref, query_grad_ref, key_grad_ref, within_grad_ref, map_grad_ref, value_grad_ref, out_ref):
+def prepare_back_blocks(first, last, rows_ref, inverse_ref, query_grad_ref, key_grad_ref, within_grad_ref, map_grad_ref, value_grad_ref, out_ref):
     row, col = iota(0), iota(1)
 
     def one_block(block, carry):
@@ -178,7 +178,7 @@
         out_ref[at, pl.ds(4 * WIDE, EXTRA)] = rates.astype(BF16)
         return carry
 
-    lax.fori_loop(0, GROUP, one_block, 0)
+    lax.fori_loop(first, last, one_block, 0)
 
 
 def remote(source, target, send, recv, device):
@@ -208,24 +208,26 @@
     def across(self):
         return {"g": self.g, "m": self.m, "b": 1 - self.b}
 
-    def meet(self, members=True, chain=True, lines=True):
+    def column(self, group):
+        return {"g": group, "m": self.m, "b": self.b}
+
+    def meet(self, column=False):
         barrier = pltpu.get_barrier_semaphore()
 
         def greet(device):
             pl.semaphore_signal(barrier, 1, device_id=device, device_id_type=MESH)
 
-        count = 0
-        if members:
-            for offset in range(1, GROUP):
-                greet(self.member(offset))
-            count = count + GROUP - 1
-        if lines:
-            greet(self.across())
-            count = count + 1
-        if chain:
+        for offset in range(1, GROUP):
+            greet(self.member(offset))
+        greet(self.across())
+        if column:
+            for step in range(1, self.groups):
+                greet(self.column((self.g + step) % self.groups))
+            count = GROUP + self.groups - 1
+        else:
             pl.when(self.above)(lambda: greet(self.up()))
             pl.when(self.below)(lambda: greet(self.down()))
-            count = count + self.above.astype(jnp.int32) + self.below.astype(jnp.int32)
+            count = GROUP + self.above.astype(jnp.int32) + self.below.astype(jnp.int32)
         pl.semaphore_wait(barrier, count)
 
 
@@ -460,21 +462,23 @@
         p = self.place
         return remote(self.leave.at[0], self.chain_land.at[slot], self.chain_send.at[0], self.chain_recv.at[slot], p.across())
 
-    def order(self, act):
-        p = self.place
-        for step in range(p.groups - 1):
-            pl.when(p.groups - 1 - step > p.g)(lambda: act(p.groups - 1 - step))
-            pl.when(step < p.g)(lambda: act(step))
-        act(p.g)
-
-    def start(self):
+    def wave(self, wave, act_up, act_down):
+        p = self.place
+        pl.when(wave > p.g)(lambda: act_up(p.groups - wave + p.g))
+        pl.when(wave >= p.groups - p.g)(lambda: act_down(wave - p.groups + p.g))
+
+    def start(self, before_own=None):
         p = self.place
 
         def act(target):
             self.line(target).start()
             self.load(target).start()
 
-        self.order(act)
+        for wave in range(1, p.groups):
+            self.wave(wave, act, act)
+        if before_own is not None:
+            before_own()
+        act(p.g)
 
         @pl.when(jnp.logical_not(p.below))
         def _():
@@ -487,15 +491,13 @@
     def both(self, target, part):
         return self.leave[target, part].astype(F32) + self.land[target, part].astype(F32)
 
-    def step(self, step):
-        p = self.place
-        above, below = p.groups - 1 - step, step
-
-        def ready(target):
+    def step(self, wave):
+        p = self.place
+
+        def send(target, inner, copy):
             self.load(target).wait()
             self.line(target).wait_recv()
 
-        def send(target, inner, copy):
             @pl.when(inner)
             def _():
                 self.arrived(target).wait_recv()
@@ -509,15 +511,11 @@
 
             copy(target)
 
-        @pl.when(above > p.g)
-        def _():
-            ready(above)
-            send(above, p.below, self.send_up)
-
-        @pl.when(below < p.g)
-        def _():
-            ready(below)
-            send(below, p.above, self.send_down)
+        self.wave(
+            wave,
+            lambda target: send(target, p.below, self.send_up),
+            lambda target: send(target, p.above, self.send_down),
+        )
 
     def hand(self, offset):
         p = self.place
@@ -555,8 +553,8 @@
 class HomeScatter:
     def __init__(self, place, partial, result, refs):
         self.place, self.partial, self.result = place, partial, result
-        (self.land, self.chain_land, self.leave, self.mine_sem, self.line_send, self.line_recv, self.chain_send,
-         self.chain_recv, self.part_send, self.part_recv) = refs
+        (self.land, self.home_land, self.leave, self.mine_sem, self.line_send, self.line_recv, self.home_send, self.home_recv,
+         self.part_send, self.part_recv) = refs
         self.home = place.groups // GROUP
 
     @staticmethod
@@ -566,13 +564,13 @@
         unit = (GROUP,) + tuple(shape[3:])
         return [
             pltpu.VMEM((home,) + unit, BF16),
-            pltpu.VMEM((home, 2) + unit, BF16),
+            pltpu.VMEM((groups - 1,) + unit, BF16),
             pltpu.VMEM((home,) + unit, BF16),
             dma((home,)),
             dma((home,)),
             dma((home,)),
             dma((home,)),
-            dma((home, 2)),
+            dma((groups - 1,)),
             dma((GROUP,)),
             dma((1,)),
         ]
@@ -584,53 +582,35 @@
         p = self.place
         return remote(self.partial.at[slot, :, 1 - p.b], self.land.at[slot], self.line_send.at[slot], self.line_recv.at[slot], p.across())
 
-    def chain(self, slot, up):
-        p = self.place
-        side = 0 if up else 1
-        return remote(
-            self.leave.at[slot], self.chain_land.at[slot, side], self.chain_send.at[slot], self.chain_recv.at[slot, side],
-            p.up() if up else p.down(),
-        )
-
     def start(self):
-        p = self.place
         for slot in range(self.home):
             self.line(slot).start()
             self.load(slot).start()
-        for side, present in ((0, p.below), (1, p.above)):
-
-            @pl.when(jnp.logical_not(present))
-            def _():
-                for slot in range(self.home):
-                    self.chain_land[slot, side] = jnp.zeros(self.chain_land.shape[2:], BF16)
-
-    def add(self, slot, sides):
-        for part in range(GROUP):
-            total = self.leave[slot, part].astype(F32) + self.land[slot, part].astype(F32)
-            for side in sides:
-                total = total + self.chain_land[slot, side, part].astype(F32)
-            self.leave[slot, part] = total.astype(BF16)
-
-    def step(self, step):
+
+    def home_copy(self, slot):
+        p = self.place
+        target = p.m * self.home + slot
+        index = (p.g - target + p.groups - 1) % p.groups
+        return remote(
+            self.leave.at[slot], self.home_land.at[index], self.home_send.at[slot], self.home_recv.at[index], p.column(target)
+        )
+
+    def landed(self, index):
+        p = self.place
+        return remote(self.leave.at[0], self.home_land.at[index], self.home_send.at[0], self.home_recv.at[index], p.across())
+
+    def push(self):
         p = self.place
         for slot in range(self.home):
-            target = p.m * self.home + slot
-
-            @pl.when((p.g < target) & (p.g == step))
+
+            @pl.when(p.g != p.m * self.home + slot)
             def _():
                 self.load(slot).wait()
                 self.line(slot).wait_recv()
-                pl.when(p.below)(lambda: self.chain(slot, True).wait_recv())
-                self.add(slot, [0])
-                self.chain(slot, True).start()
-
-            @pl.when((p.g > target) & (p.groups - 1 - p.g == step))
-            def _():
-                self.load(slot).wait()
-                self.line(slot).wait_recv()
-                pl.when(p.above)(lambda: self.chain(slot, False).wait_recv())
-                self.add(slot, [1])
-                self.chain(slot, False).start()
+                for part in range(GROUP):
+                    total = self.leave[slot, part].astype(F32) + self.land[slot, part].astype(F32)
+                    self.leave[slot, part] = total.astype(BF16)
+                self.home_copy(slot).start()
 
     def hand(self, slot, other):
         p = self.place
@@ -646,9 +626,13 @@
             slot = p.g % self.home
             self.load(slot).wait()
             self.line(slot).wait_recv()
-            pl.when(p.below)(lambda: self.chain(slot, True).wait_recv())
-            pl.when(p.above)(lambda: self.chain(slot, False).wait_recv())
-            self.add(slot, [0, 1])
+            for index in range(p.groups - 1):
+                self.landed(index).wait_recv()
+            for part in range(GROUP):
+                total = self.leave[slot, part].astype(F32) + self.land[slot, part].astype(F32)
+                for index in range(p.groups - 1):
+                    total = total + self.home_land[index, part].astype(F32)
+                self.leave[slot, part] = total.astype(BF16)
             for offset in range(1, GROUP):
                 self.hand(slot, p.other(offset)).start()
             self.result[...] = self.leave[slot, p.m]
@@ -665,7 +649,7 @@
         pl.when(jnp.logical_not(keeper))(lambda: self.hand(0, p.other(1)).wait_recv())
         for slot in range(self.home):
             self.line(slot).wait_send()
-            pl.when(p.g != p.m * self.home + slot)(lambda: self.chain(slot, True).wait_send())
+            pl.when(p.g != p.m * self.home + slot)(lambda: self.home_copy(slot).wait_send())
 
 
 CHUNKS = 4
@@ -1063,9 +1047,11 @@
     att_grad_ref,
     rows_ref,
     inverse_ref,
+    out_partial_ref,
     feed_partial_ref,
     rows_grad_ref,
     feed_result_ref,
+    out_result_ref,
     query_grad_ref,
     key_grad_ref,
     within_grad_ref,
@@ -1074,8 +1060,6 @@
     scaled_ref,
     dots_ref,
     direct_ref,
-    direct_value_ref,
-    running_ref,
     key_slots_ref,
     value_slots_ref,
     key_send,
@@ -1085,11 +1069,15 @@
     *refs,
 ):
     here = Place(groups, feed_partial_ref.shape[2])
-    here.meet()
+    here.meet(column=True)
     place, has_next, previous = here.g, here.above, here.down()
-    feed_scatter = Scatter(here, feed_partial_ref, feed_result_ref, refs)
-    feed_scatter.start()
-    pauses = Pauses(*[(functools.partial(feed_scatter.step, step),) for step in range(groups - 1)])
+    feed_refs, out_refs = several(
+        refs, len(Scatter.scratch(groups, feed_partial_ref.shape)), len(HomeScatter.scratch(groups, out_partial_ref.shape))
+    )
+    feed_scatter = Scatter(here, feed_partial_ref, feed_result_ref, feed_refs)
+    out_scatter = HomeScatter(here, out_partial_ref, out_result_ref, out_refs)
+    feed_scatter.start(out_scatter.start)
+    pauses = Pauses(*[(functools.partial(feed_scatter.step, wave),) for wave in range(1, groups)])
 
     def key_copy(hop):
         slot = hop - 1
@@ -1137,7 +1125,7 @@
 
     def hop_direct(hop, last):
         for head in range(OWN):
-            direct_value_ref[:, tile(head)] = jnp.zeros((GROUP * BLOCK, BLOCK), F32)
+            value_grad_ref[:, tile(head)] = jnp.zeros((GROUP * BLOCK, BLOCK), F32)
         for block in range(GROUP):
             first = block if last else 0
             count = GROUP - first
@@ -1151,7 +1139,7 @@
                 raw = grad.astype(BF16)
                 query_grad_ref[tile(block), tile(head)] += dot(raw, keys)
                 direct_ref[block, tile(first, count), tile(head)] = dot(raw, query, TN)
-                direct_value_ref[tile(first, count), tile(head)] += dot(
+                value_grad_ref[tile(first, count), tile(head)] += dot(
                     weights.astype(BF16), scaled_ref[tile(block), tile(head)], TN
                 )
 
@@ -1169,9 +1157,9 @@
                     direct = direct_ref[block, tile(block, GROUP - block), tile(head)]
                     grads = jnp.concatenate([direct[:BLOCK], direct[BLOCK:] + back], 0)
                 key_slots_ref[hop, :, tile(head)] = grads.astype(BF16)
-                value_slots_ref[hop, :, tile(head)] = direct_value_ref[:, tile(head)].astype(BF16)
+                value_slots_ref[hop, :, tile(head)] = value_grad_ref[:, tile(head)].astype(BF16)
             else:
-                grads = running_ref[:, tile(head)]
+                grads = key_grad_ref[:, tile(head)]
                 for block in range(GROUP - 1, -1, -1):
                     collect_map(block, head, moved_ref[hop, block, :, tile(head)], grads)
                     grads = direct_ref[block, :, tile(head)] + dot3(grads, map_ref[tile(block), tile(head)], NT)
@@ -1181,11 +1169,11 @@
         @pl.when(has_next)
         def _():
             key_copy(hop).wait_recv()
-            running_ref[...] = key_slots_ref[hop - 1].astype(F32)
+            key_grad_ref[...] = key_slots_ref[hop - 1].astype(F32)
 
         @pl.when(jnp.logical_not(has_next))
         def _():
-            running_ref[...] = jnp.zeros_like(running_ref)
+            key_grad_ref[...] = jnp.zeros_like(key_grad_ref)
 
     @pl.when(place >= hops)
     def _():
@@ -1194,12 +1182,13 @@
         key_copy(hops).start()
         value_copy(hops).start()
 
-    pauses()
-
-    def between(hop):
+    def between(hop, pause=None):
+        pl.when(place >= hop)(lambda: hop_direct(hop, False))
+        if pause is not None:
+            pause()
+
         @pl.when(place >= hop)
         def _():
-            hop_direct(hop, False)
             take(hop + 1)
             hop_chain(hop, False)
             key_copy(hop).start()
@@ -1209,13 +1198,13 @@
                 value_copy(hop + 1).wait_recv()
                 for head in range(OWN):
                     value_slots_ref[hop, :, tile(head)] = (
-                        direct_value_ref[:, tile(head)] + value_slots_ref[hop, :, tile(head)].astype(F32)
+                        value_grad_ref[:, tile(head)] + value_slots_ref[hop, :, tile(head)].astype(F32)
                     ).astype(BF16)
 
             @pl.when(jnp.logical_not(has_next))
             def _():
                 for head in range(OWN):
-                    value_slots_ref[hop, :, tile(head)] = direct_value_ref[:, tile(head)].astype(BF16)
+                    value_slots_ref[hop, :, tile(head)] = value_grad_ref[:, tile(head)].astype(BF16)
 
             value_copy(hop).start()
 
@@ -1228,11 +1217,10 @@
         lax.fori_loop(0, hops - 1, step, 0)
     else:
         for hop in range(hops - 1, 0, -1):
-            between(hop)
-            pauses()
+            between(hop, pauses)
 
     for head in range(OWN):
-        direct_value_ref[:, tile(head)] = jnp.zeros((GROUP * BLOCK, BLOCK), F32)
+        value_grad_ref[:, tile(head)] = jnp.zeros((GROUP * BLOCK, BLOCK), F32)
     for block in range(GROUP):
         wide = (BLOCK, (block + 1) * BLOCK)
         counts = row_counts(block, 0, 0, block + 1) & (iota(0, wide) + block * BLOCK >= iota(1, wide))
@@ -1244,16 +1232,17 @@
                 scores = jnp.concatenate([dot(query, keys, NT), scores], 1)
             weights, grad = pair(block, head, scores, counts, value_ref[tile(0, block + 1), tile(head)])
             within_grad_ref[tile(block), tile(head)] = grad[:, block * BLOCK :]
-            direct_value_ref[tile(0, block + 1), tile(head)] += dot(
+            value_grad_ref[tile(0, block + 1), tile(head)] += dot(
                 weights.astype(BF16), scaled_ref[tile(block), tile(head)], TN
             )
             if block:
                 raw = grad[:, : block * BLOCK].astype(BF16)
                 query_grad_ref[tile(block), tile(head)] += dot(raw, keys)
                 direct_ref[block, tile(0, block), tile(head)] = dot(raw, query, TN)
+    pauses()
     take(1)
     for head in range(OWN):
-        grads = running_ref[:, tile(head)]
+        grads = key_grad_ref[:, tile(head)]
         for block in range(GROUP - 1, 0, -1):
             key_grad_ref[tile(block), tile(head)] = grads[block * BLOCK :]
             grads = grads[: block * BLOCK]
@@ -1264,11 +1253,7 @@
     @pl.when(has_next)
     def _():
         value_copy(1).wait_recv()
-        value_grad_ref[...] = direct_value_ref[...] + value_slots_ref[0].astype(F32)
-
-    @pl.when(jnp.logical_not(has_next))
-    def _():
-        value_grad_ref[...] = direct_value_ref[...]
+        value_grad_ref[...] += value_slots_ref[0].astype(F32)
 
     def settle(hop, carry):
         @pl.when(place >= hop)
@@ -1279,30 +1264,31 @@
         return carry
 
     lax.fori_loop(1, hops + 1, settle, 0)
+    pieces = (rows_ref, inverse_ref, query_grad_ref, key_grad_ref, within_grad_ref, map_grad_ref, value_grad_ref, rows_grad_ref)
+    prepare_back_blocks(0, GROUP // 2, *pieces)
     pauses.rest()
-    prepare_back_blocks(
-        rows_ref, inverse_ref, query_grad_ref, key_grad_ref, within_grad_ref, map_grad_ref, value_grad_ref, rows_grad_ref
-    )
+    out_scatter.push()
+    prepare_back_blocks(GROUP // 2, GROUP, *pieces)
     feed_scatter.last()
+    out_scatter.last()
     feed_scatter.finish()
+    out_scatter.finish()
 
 
 def attend_back(groups, hops, *args):
     length = args[0].shape[0]
-    feed = args[-1]
+    out, feed = args[-2:]
     dma = pltpu.SemaphoreType.DMA
     return pl.pallas_call(
         functools.partial(attend_back_kernel, groups, hops),
-        out_shape=[shape(BF16, *args[-3].shape), shape(BF16, GROUP, *feed.shape[3:])],
-        in_specs=in_vmem(len(args) - 1) + anywhere(1),
-        out_specs=in_vmem(2),
+        out_shape=[shape(BF16, *args[-4].shape), shape(BF16, GROUP, *feed.shape[3:]), shape(BF16, *out.shape[3:])],
+        in_specs=in_vmem(len(args) - 2) + anywhere(2),
+        out_specs=in_vmem(3),
         scratch_shapes=[pltpu.VMEM((length, WIDE), F32)] * 5
         + [
             pltpu.VMEM((length, WIDE), BF16),
             pltpu.VMEM((OWN, length, BLOCK), F32),
             pltpu.VMEM((GROUP, length, WIDE), F32),
-            pltpu.VMEM((length, WIDE), F32),
-            pltpu.VMEM((length, WIDE), F32),
             pltpu.VMEM((hops + 1, length, WIDE), BF16),
             pltpu.VMEM((hops + 1, length, WIDE), BF16),
             dma((hops,)),
@@ -1310,7 +1296,8 @@
             dma((hops,)),
             dma((hops,)),
         ]
-        + Scatter.scratch(groups, feed.shape),
+        + Scatter.scratch(groups, feed.shape)
+        + HomeScatter.scratch(groups, out.shape),
         **communicating(2, "attend_back", 60),
     )(*args)
 
@@ -1417,7 +1404,7 @@
     total = GroupSum(here, partial_ref, sum_refs)
     whole = GroupGather(here, grad_low_ref, gather_refs)
     down = Scatter(here, down_ref, down_result_ref, down_refs)
-    pauses = Pauses(*[(functools.partial(down.step, step),) for step in range(groups - 1)])
+    pauses = Pauses(*[(functools.partial(down.step, wave),) for wave in range(1, groups)])
     total.start()
     down.start()
     for chunk in range(CHUNKS):
@@ -1457,7 +1444,6 @@
 def finish_kernel(
     groups,
     first_ref,
-    out_ref,
     normed_partial_ref,
     output_partial_ref,
     tokens_ref,
@@ -1465,21 +1451,16 @@
     grad_ref,
     gain_ref,
     first_result_ref,
-    out_result_ref,
     tokens_grad_ref,
     output_ref,
     *refs,
 ):
     here = Place(groups, first_ref.shape[2])
     here.meet()
-    first_refs, out_refs, normed_refs, output_refs = several(
-        refs, len(Scatter.scratch(groups, first_ref.shape)), len(HomeScatter.scratch(groups, out_ref.shape)), 7, 7
-    )
+    first_refs, normed_refs, output_refs = several(refs, len(Scatter.scratch(groups, first_ref.shape)), 7, 7)
     first = Scatter(here, first_ref, first_result_ref, first_refs)
-    out = HomeScatter(here, out_ref, out_result_ref, out_refs)
     normed = GroupSum(here, normed_partial_ref, normed_refs)
     output = GroupSum(here, output_partial_ref, output_refs)
-    out.start()
     first.start()
     normed.start()
     output.start()
@@ -1487,35 +1468,31 @@
         normed.pass_on(chunk)
     for chunk in range(CHUNKS):
         output.pass_on(chunk)
-    for step in range(groups - 1):
-        out.step(step)
-        first.step(step)
+    for wave in range(1, groups):
+        first.step(wave)
     for chunk in range(CHUNKS):
         back, _ = rms_back(tokens_ref[normed.at(chunk), :].astype(F32), gain_ref[...], normed.take(chunk))
         tokens_grad_ref[normed.at(chunk), :] = (grad_ref[normed.at(chunk), :] + back).astype(BF16)
     for chunk in range(CHUNKS):
         output_ref[output.at(chunk), :] = (hidden_ref[output.at(chunk), :] + output.take(chunk)).astype(BF16)
-    out.last()
     first.last()
     normed.finish()
     output.finish()
-    out.finish()
     first.finish()
 
 
-def finish(groups, first, out, normed_partial, output_partial, tokens, hidden, grad, gain):
+def finish(groups, first, normed_partial, output_partial, tokens, hidden, grad, gain):
     size, width = tokens.shape
     return pl.pallas_call(
         functools.partial(finish_kernel, groups),
-        out_shape=[shape(BF16, GROUP, *first.shape[3:]), shape(BF16, *out.shape[3:]), shape(BF16, size, width), shape(BF16, size, width)],
-        in_specs=anywhere(2) + in_vmem(6),
-        out_specs=in_vmem(4),
+        out_shape=[shape(BF16, GROUP, *first.shape[3:]), shape(BF16, size, width), shape(BF16, size, width)],
+        in_specs=anywhere(1) + in_vmem(6),
+        out_specs=in_vmem(3),
         scratch_shapes=Scatter.scratch(groups, first.shape)
-        + HomeScatter.scratch(groups, out.shape)
         + GroupSum.scratch(size, width)
         + GroupSum.scratch(size, width),
         **communicating(5, "finish"),
-    )(first, out, normed_partial, output_partial, tokens, hidden, grad, gain)
+    )(first, normed_partial, output_partial, tokens, hidden, grad, gain)
 
 
 def on_device(
@@ -1607,9 +1584,10 @@
     )
     att_grad = dot(branch_grad, out_full, NT).astype(BF16)
     feed_partial = dot(normed_two, feed_grads, TN).astype(BF16).reshape(groups, GROUP, batch, rows, -1)
-    rows_grad, feed_grad = attend_back(
+    out_partial = dot(attended_low, branch_grad, TN).astype(BF16).reshape(groups // GROUP, GROUP, batch, rows, width)
+    rows_grad, feed_grad, out_weight_grad = attend_back(
         groups, hops, query, value, within, maps, doc_query, doc_key, attended, stats, moved, values, att_grad, projected, inverse,
-        feed_partial,
+        out_partial, feed_partial,
     )
     normed_grad = dot(rows_grad, first, NT)
     gain_one_grad = jnp.sum(normed_grad * straight, axis=0)
@@ -1618,9 +1596,8 @@
     first_partial = jnp.where(lane == 4 * WIDE + OWN, gain_one_grad[:, None], first_partial)
     first_partial = jnp.where(lane == 4 * WIDE + OWN + 1, gain_two_grad[0][:, None], first_partial)
     first_partial = first_partial.astype(BF16).reshape(groups, GROUP, batch, rows, -1)
-    out_partial = dot(attended_low, branch_grad, TN).astype(BF16).reshape(groups // GROUP, GROUP, batch, rows, width)
-    first_grad, out_weight_grad, tokens_grad, output = finish(
-        groups, first_partial, out_partial, normed_grad.astype(BF16), output_partial, tokens[0], hidden, hidden_grad, gain_one
+    first_grad, tokens_grad, output = finish(
+        groups, first_partial, normed_grad.astype(BF16), output_partial, tokens[0], hidden, hidden_grad, gain_one
     )
     first_grad = first_grad.astype(F32)
     output, tokens_grad = output[None], tokens_grad[None]

time: 627 us -> 572 us (0.912)
  Pallas kernels: 532 us -> 479 us
    pallas_call x1, Pallas kernels: 112 us -> 75.3 us  [finish(): pl.pallas_call(functools.partial(finish_kernel, groups), out_shape=[shape...]
    pallas_call x1, Pallas kernels: 52.6 us -> 43 us  [branch_back(): pl.pallas_call(functools.partial(branch_back_kernel, groups), out_shape=[...]
    pallas_call x1, Pallas kernels: 136 us -> 130 us  [attend_back(): pl.pallas_call(functools.partial(attend_back_kernel, groups, hops), out_s...]
where the time goes in v3:
time: 572 us; the launch traced here: 565 us
  Pallas kernels  479 us (84%)
  matrix products  52.4 us (9%)
  local copies, waits for them, and re-layouts  22.4 us (4%)
  other arithmetic  9.16 us (2%)
    pallas_call x1, Pallas kernels, attend_back(): pl.pallas_call(functools.partial(attend_back_kernel, groups, hops), out_s...  130 us
    pallas_call x1, Pallas kernels, attend(): pl.pallas_call(functools.partial(attend_kernel, groups, hops), out_shape=...  97.5 us
    pallas_call x1, Pallas kernels, gather_first(): pl.pallas_call(functools.partial(gather_kernel, groups), out_shape=[shape...  75.3 us
    pallas_call x1, Pallas kernels, finish(): pl.pallas_call(functools.partial(finish_kernel, groups), out_shape=[shape...  75.3 us
    pallas_call x1, Pallas kernels, branch(): pl.pallas_call(functools.partial(branch_kernel, groups), out_shape=[shape...  58.4 us
    dot_general x12, matrix products, dot(): return lax.dot_general(left, right, dims, preferred_element_type=F32)  52.4 us
    pallas_call x1, Pallas kernels, branch_back(): pl.pallas_call(functools.partial(branch_back_kernel, groups), out_shape=[...  43 us

profile of v3, /device:TPU:0, one launch (start us, length us, event | category | flops | bytes accessed | tf_op | source)
XLA Modules:
  0.0 564.7 jit_solution(17716660623550955386)
XLA Ops:
  0.7 1.0 convert_element_type.127
  1.7 1.1 convert_element_type.126
  2.8 1.0 convert_element_type.129
  4.9 75.3 %gather_first.1 = (bf16[4,4,2,48,1664]{4,3,2,1,0:T(8,128)(2,1)S(1)}, bf16[512,1536]{1,0:T(8,128)(2,1)S(1)}, bf16[512,1536]{1,0:T(8,128)(2,1)S(1)}) custom-call(bf16[4,48,1664]{2,1,0:T(8,128)(2,1)S(1)} %concatenate.13.parts_ref, bf16[128,1536]{1,0:T(8,128)(2,1)S(1)} %bitcast.104, bf16[128,1536]{1,0:T(8,128)(2,1)S(1)} %bitcast.106), custom_call_target="tpu_custom_call" | custom-call | tf_op jit(solution)/shard_map/gather_first/pallas_call | solution.py:1332
  80.3 1.1 copy-done.10
  81.4 2.3 copy-done.7
  85.2 7.3 %fusion.7.rows_ref = f32[512,1664]{1,0:T(8,128)} fusion(bf16[1536,1664]{1,0:T(8,128)(2,1)} %bitcast.110, bf16[512,1536]{1,0:T(8,128)(2,1)S(1)} %get-tuple-element.42, f32[1536]{0:T(1024)S(1)} %convert_reduce_fusion, f32[512]{0:T(512)S(1)} %add_rsqrt_fusion), kind=kOutput, calls=%fused_computation.22 | convolution fusion | flops 2620391424 | bytes 10100736 | tf_op jit(solution)/shard_map/dot_general | solution.py:30
  92.5 1.2 slice.70
  94.2 0.9 copy.103.doc_query_ref
  95.7 1.6 convert_element_type.139.out_part_ref
  99.1 0.9 pad_maximum_fusion.3.feed_parts_ref
  100.0 97.5 %attend.1 = (bf16[512,384]{1,0:T(8,128)(2,1)}, bf16[512,384]{1,0:T(8,128)(2,1)}, f32[512,384]{1,0:T(8,128)}, f32[512,384]{1,0:T(8,128)}, f32[512,384]{1,0:T(8,12...) custom-call(f32[512,1664]{1,0:T(8,128)} %fusion.7.rows_ref, ...), custom_call_target="tpu_custom_call" | custom-call | tf_op jit(solution)/shard_map/attend/pallas_call | solution.py:999
  197.6 2.4 convolution_convert_fusion.4.partial_ref
  200.3 58.4 %branch.1 = (f32[128,1536]{1,0:T(8,128)S(1)}, bf16[512,1536]{1,0:T(8,128)(2,1)S(1)}, bf16[4,2,128,1536]{3,2,1,0:T(8,128)(2,1)S(1)}) custom-call(bf16[512,1536]{1,0:T(8,128)(2,1)S(1)} %convolution_convert_fusion.4.partial_ref, bf16[128,1536]{1,0:T(8,128)(2,1)S(1)} %bitcast.105, f32[1,1536]{1,0:T(1,128)S(1)} %bitcast_convert_fusion.gain_ref, ...), custom_call_target="tpu_custom_call" | custom-call | tf_op jit(solution)/shard_map/branch/pallas_call | solution.py:1388
  258.7 6.9 %fusion.14 = f32[512,2048]{1,0:T(8,128)S(1)} fusion(bf16[512,1536]{1,0:T(8,128)(2,1)S(1)} %get-tuple-element.47, bf16[1536,2048]{1,0:T(8,128)(2,1)} %bitcast.139), kind=kOutput, calls=%fused_computation.61 | convolution fusion | flops 3221225472 | bytes 12058624 | tf_op jit(solution)/shard_map/dot_general | solution.py:30
  265.7 2.5 multiply_convert_fusion.2
  268.3 3.5 convolution_convert_fusion.3.partial_ref
  271.8 3.5 convolution_convert_fusion.1
  275.3 43.0 %branch_back.1 = (f32[128,1536]{1,0:T(8,128)S(1)}, bf16[512,1536]{1,0:T(8,128)(2,1)S(1)}, f32[1,1536]{1,0:T(1,128)S(1)}, f32[1,128,1536]{2,1,0:T(8,128)S(1)}) custom-call(bf16[512,1536]{1,0:T(8,128)(2,1)S(1)} %convolution_convert_fusion.3.partial_ref, f32[128,1536]{1,0:T(8,128)S(1)} %get-tuple-element.49.hidden_ref, bf16[128,1536]{1,0:T(8,128)(2,1)S(1)} %bitcast.107, ...), custom_call_target="tpu_custom_call" | custom-call | tf_op jit(solution)/shard_map/branch_back/pallas_call | solution.py:1434
  318.3 1.7 convolution_convert_fusion.6.att_grad_ref
  320.1 1.8 convolution_convert_fusion.5
  321.9 5.5 convolution_convert_fusion
  327.4 129.7 %attend_back.1 = (bf16[512,1664]{1,0:T(8,128)(2,1)}, bf16[4,48,2048]{2,1,0:T(8,128)(2,1)}, bf16[48,1536]{1,0:T(8,128)(2,1)}) custom-call(bf16[512,384]{1,0:T(8,128)(2,1)} %get-tuple-element.51.query_ref, bf16[512,384]{1,0:T(8,128)(2,1)} %get-tuple-element.52.value_ref, f32[512,384]{1,0:T(8,128)} %get-tuple-element.53.within_ref, ...), custom_call_target="tpu_custom_call" | custom-call | tf_op jit(solution)/shard_map/attend_back/pallas_call | solution.py:1282
  457.1 7.2 %fusion.13 = (bf16[512,1536]{1,0:T(8,128)(2,1)}, bf16[1536]{0:T(1024)(128)(2,1)S(1)}) fusion(f32[512]{0:T(512)S(1)} %copy-done.24, bf16[512,1536]{1,0:T(8,128)(2,1)S(1)} %copy-done.3, bf16[512,1664]{1,0:T(8,128)(2,1)} %get-tuple-element.61, bf16[1536,1664]{1,0:T(8,128)(2,1)} %bitcast.112), kind=kOutput, calls=%fused_computation.60 | convolution fusion | flops 2621176320 | bytes 9966592 | tf_op jit(solution)/shard_map/dot_general | solution.py:30
  464.4 6.9 %select_convert_fusion = bf16[1536,1664]{1,0:T(8,128)(2,1)} fusion(bf16[512,1664]{1,0:T(8,128)(2,1)} %get-tuple-element.61, bf16[1536]{0:T(1024)(128)(2,1)S(1)} %get-tuple-element.77, bf16[1536]{0:T(1024)(128)(2,1)S(1)} %reduce.2, pred[1664]{0:T(1024)(128)(4,1)S(1)} %get-tuple-element.92, pred[1664]{0:T(1024)(128)(4,1)S(1)} %get-tuple-element.93, ...), kind=kOutput, calls=%fused_computation | convolution fusion | flops 2625503232 | bytes 8406272 | tf_op jit(solution)/shard_map/dot_general | solution.py:30
  471.2 3.0 convolution_convert_fusion.2.output_partial_ref
  474.9 75.3 %finish.1 = (bf16[4,48,1664]{2,1,0:T(8,128)(2,1)}, bf16[128,1536]{1,0:T(8,128)(2,1)}, bf16[128,1536]{1,0:T(8,128)(2,1)}) custom-call(bf16[4,4,2,48,1664]{4,3,2,1,0:T(8,128)(2,1)} %bitcast.116, bf16[512,1536]{1,0:T(8,128)(2,1)} %get-tuple-element.76.normed_partial_ref, bf16[512,1536]{1,0:T(8,128)(2,1)} %convolution_convert_fusion.2.output_partial_ref, ...), custom_call_target="tpu_custom_call" | custom-call | tf_op jit(solution)/shard_map/finish/pallas_call | solution.py:1486
  550.2 1.2 convert_element_type.159
  557.9 1.5 reshape.218
  560.6 1.5 reshape.220
  562.1 0.7 copy.137
  563.6 0.9 copy.139
  (131 shorter events, 14.6 us)
Async XLA Ops:
  0.6 3.2 copy-start.20
  0.7 3.2 copy-start.22
  0.7 3.4 copy-start.25
  0.7 3.5 copy-start.26
  0.7 3.7 copy-start.27
  1.7 3.2 copy-start
  1.7 3.2 copy-start.4
  81.4 2.3 copy-start.7
  81.4 11.1 %copy-start.2 = (bf16[512,1536]{1,0:T(8,128)(2,1)}, bf16[512,1536]{1,0:T(8,128)(2,1)S(1)}, u32[]{:S(2)}) copy-start(bf16[512,1536]{1,0:T(8,128)(2,1)S(1)} %get-tuple-element.42) | copy-start | bytes 4718596
  92.5 4.8 copy-start.13
  94.2 4.0 copy-start.14
  197.6 2.7 copy-start.15
  200.3 68.0 %slice-start = ((s8[6291456]{0:T(1024)(128)(4,1)}), s8[4194304]{0:T(1024)(128)(4,1)S(1)}, s32[]{:S(2)}) async-start(s8[6291456]{0:T(1024)(128)(4,1)} %bitcast.140), calls=%async_computation | async-start | bytes 8388608
  258.7 7.0 %copy-start.8 = (bf16[4,2,128,1536]{3,2,1,0:T(8,128)(2,1)}, bf16[4,2,128,1536]{3,2,1,0:T(8,128)(2,1)S(1)}, u32[]{:S(2)}) copy-start(bf16[4,2,128,1536]{3,2,1,0:T(8,128)(2,1)S(1)} %get-tuple-element.46) | copy-start | bytes 9437188
  258.7 16.6 %copy-start.1 = (f32[128,1536]{1,0:T(8,128)}, f32[128,1536]{1,0:T(8,128)S(1)}, u32[]{:S(2)}) copy-start(f32[128,1536]{1,0:T(8,128)S(1)} %get-tuple-element.49.hidden_ref) | copy-start | bytes 2359300
  258.7 7.0 %copy-start.11 = (bf16[512,1536]{1,0:T(8,128)(2,1)S(1)}, bf16[512,1536]{1,0:T(8,128)(2,1)}, u32[]{:S(2)}) copy-start(bf16[512,1536]{1,0:T(8,128)(2,1)} %copy-done.10) | copy-start | bytes 4718596
  258.7 9.6 %slice-start.1 = ((s8[6291456]{0:T(1024)(128)(4,1)}), s8[2097152]{0:T(1024)(128)(4,1)S(1)}, s32[]{:S(2)}) async-start(s8[6291456]{0:T(1024)(128)(4,1)} %bitcast.140), calls=%async_computation.1 | async-start | bytes 4194304
  268.2 3.5 copy-start.30
  268.2 3.5 copy-start.32
  268.2 3.5 copy-start.28
  271.8 3.5 copy-start.5
  275.3 43.0 %copy-start.12 = (bf16[1,4,2,48,1536]{4,3,2,1,0:T(8,128)(2,1)S(1)}, bf16[1,4,2,48,1536]{4,3,2,1,0:T(8,128)(2,1)}, u32[]{:S(2)}) copy-start(bf16[1,4,2,48,1536]{4,3,2,1,0:T(8,128)(2,1)} %get-tuple-element.45) | copy-start | bytes 3538948
  318.3 3.6 copy-start.6
  320.1 1.8 copy-start.33
  327.4 129.7 %copy-start.3 = (bf16[512,1536]{1,0:T(8,128)(2,1)S(1)}, bf16[512,1536]{1,0:T(8,128)(2,1)}, u32[]{:S(2)}) copy-start(bf16[512,1536]{1,0:T(8,128)(2,1)} %copy-done.2) | copy-start | bytes 4718596
  327.4 129.7 %copy-start.24 = (f32[512]{0:T(512)S(1)}, f32[512]{0:T(512)}, u32[]{:S(2)}) copy-start(f32[512]{0:T(512)} %copy-done.23) | copy-start | bytes 6148
  464.3 6.9 %copy-start.9 = (bf16[4,2,128,1536]{3,2,1,0:T(8,128)(2,1)S(1)}, bf16[4,2,128,1536]{3,2,1,0:T(8,128)(2,1)}, u32[]{:S(2)}) copy-start(bf16[4,2,128,1536]{3,2,1,0:T(8,128)(2,1)} %copy-done.8) | copy-start | bytes 9437188
  464.4 6.9 %copy-start.29 = (bf16[512,1024]{1,0:T(8,128)(2,1)S(1)}, bf16[512,1024]{1,0:T(8,128)(2,1)}, u32[]{:S(2)}) copy-start(bf16[512,1024]{1,0:T(8,128)(2,1)} %copy-done.28) | copy-start | bytes 3145732
  552.1 3.8 copy-start.21
  552.2 4.4 copy-start.16
  560.1 2.0 copy-start.19
  560.1 2.7 copy-start.18
  (4 other events, 5.3 us)

commit v4 on v3

--- a/solution.py
+++ b/solution.py
@@ -121,22 +121,19 @@
     lax.fori_loop(first, last, one_block, 0)
 
 
-def prepare_back_blocks(first, last, rows_ref, inverse_ref, query_grad_ref, key_grad_ref, within_grad_ref, map_grad_ref, value_grad_ref, out_ref):
+def prepare_back_blocks(first, last, panels_ref, extra_ref, query_grad_ref, key_grad_ref, within_grad_ref, map_grad_ref, value_grad_ref, out_ref):
     row, col = iota(0), iota(1)
 
     def one_block(block, carry):
         at = tile(block)
         rates = jnp.zeros((BLOCK, EXTRA), F32)
         for head in range(OWN):
-            query, key, value, house = [
-                rows_ref[at, pl.ds(part * WIDE + head * BLOCK, BLOCK)] for part in range(4)
-            ]
-            rate = rows_ref[at, pl.ds(4 * WIDE, EXTRA)][:, head : head + 1]
+            query, key, house, inverse = [panels_ref[part, at, tile(head)] for part in range(4)]
+            rate = extra_ref[at, :][:, head : head + 1]
             query_grad = query_grad_ref[at, tile(head)]
             key_grad = key_grad_ref[at, tile(head)]
             within_grad = within_grad_ref[at, tile(head)]
             map_grad = map_grad_ref[at, tile(head)]
-            inverse = inverse_ref[at, tile(head)]
             unit, scale = unit_of(house)
             strength = 2.0 * jax.nn.sigmoid(rate)
             unit_unit, unit_key, query_unit, query_key = products(query, key, unit)
@@ -232,17 +229,23 @@
 
 
 class Gather:
-    SEMS = 8
-
     def __init__(self, place, parts, full, sems, mixed=True):
         self.place, self.parts, self.full, self.mixed = place, parts, full, mixed
-        (self.part_send, self.part_recv, self.up_send, self.down_send, self.chain_recv, self.line_send, self.line_recv,
-         self.own_sem) = sems
+        sems = list(sems)
+        if parts is not None:
+            self.part_send, self.part_recv, self.own_sem = sems[:3]
+            sems = sems[3:]
+        if sems:
+            self.up_send, self.down_send, self.chain_recv, self.line_send, self.line_recv = sems
 
     @staticmethod
-    def scratch(groups):
+    def inside():
         dma = pltpu.SemaphoreType.DMA
-        return [dma((GROUP,)), dma((GROUP,)), dma((groups,)), dma((groups,)), dma((groups,)), dma((groups,)), dma((groups,)), dma((1,))]
+        return [dma((GROUP,)), dma((GROUP,)), dma((1,))]
+
+    @staticmethod
+    def outside(groups):
+        return [pltpu.SemaphoreType.DMA((groups,))] * 5
 
     def unit(self, group, line):
         return self.full.at[group, :, line] if self.mixed else self.full.at[group, line]
@@ -277,12 +280,14 @@
         unit = self.unit(source, p.b)
         return remote(unit, unit, self.line_send.at[source], self.line_recv.at[source], p.across())
 
-    def begin(self):
-        p = self.place
+    def settle(self):
         self.own().wait()
         if self.mixed:
             for offset in (2, 3, 1):
                 self.part(offset).wait()
+
+    def spread(self):
+        p = self.place
         pl.when(p.above)(lambda: self.chain(p.g, True).start())
         pl.when(p.below)(lambda: self.chain(p.g, False).start())
         self.across(p.g).start()
@@ -320,13 +325,19 @@
     def __init__(self, place, part, full, sems):
         self.place, self.part_ref, self.full = place, part, full
         self.home = place.groups // GROUP
-        self.part_send, self.part_recv, self.up_send, self.down_send, self.chain_recv, self.line_send, self.line_recv = sems
+        if part is not None:
+            self.part_send, self.part_recv = sems
+        else:
+            self.up_send, self.down_send, self.chain_recv, self.line_send, self.line_recv = sems
 
     @staticmethod
-    def scratch(groups):
-        home = groups // GROUP
+    def inside():
         dma = pltpu.SemaphoreType.DMA
-        return [dma((1,)), dma((GROUP,)), dma((home,)), dma((home,)), dma((home,)), dma((home,)), dma((home,))]
+        return [dma((1,)), dma((GROUP,))]
+
+    @staticmethod
+    def outside(groups):
+        return [pltpu.SemaphoreType.DMA((groups // GROUP,))] * 5
 
     def at_home(self):
         return self.place.m == self.place.g // self.home
@@ -364,7 +375,7 @@
         unit = self.full.at[slot, :, p.b]
         return remote(unit, unit, self.line_send.at[slot], self.line_recv.at[slot], p.across())
 
-    def begin(self):
+    def settle(self):
         p = self.place
 
         @pl.when(self.at_home())
@@ -372,12 +383,18 @@
             self.own().wait()
             for offset in range(1, GROUP):
                 self.taken(p.other(offset)).wait_recv()
+
+        pl.when(jnp.logical_not(self.at_home()))(lambda: self.hand().wait_send())
+
+    def spread(self):
+        p = self.place
+
+        @pl.when(self.at_home())
+        def _():
             slot = p.g % self.home
             pl.when(p.above)(lambda: self.chain(slot, True).start())
             pl.when(p.below)(lambda: self.chain(slot, False).start())
             self.across(slot).start()
-
-        pl.when(jnp.logical_not(self.at_home()))(lambda: self.hand().wait_send())
 
     def step(self, distance):
         p = self.place
@@ -467,18 +484,20 @@
         pl.when(wave > p.g)(lambda: act_up(p.groups - wave + p.g))
         pl.when(wave >= p.groups - p.g)(lambda: act_down(wave - p.groups + p.g))
 
-    def start(self, before_own=None):
-        p = self.place
-
-        def act(target):
-            self.line(target).start()
-            self.load(target).start()
-
-        for wave in range(1, p.groups):
-            self.wave(wave, act, act)
-        if before_own is not None:
-            before_own()
-        act(p.g)
+    def act(self, target):
+        self.line(target).start()
+        self.load(target).start()
+
+    def start(self):
+        self.start_far()
+        self.act(self.place.g)
+
+    def start_far(self, first=1, last=None):
+        p = self.place
+        for wave in range(first, p.groups if last is None else last + 1):
+            self.wave(wave, self.act, self.act)
+        if first > 1:
+            return
 
         @pl.when(jnp.logical_not(p.below))
         def _():
@@ -786,8 +805,8 @@
     rows_ref,
     doc_query_ref,
     doc_key_ref,
-    out_part_ref,
-    feed_parts_ref,
+    out_home_ref,
+    feed_unit_ref,
     query_ref,
     value_ref,
     within_ref,
@@ -814,11 +833,11 @@
     here = Place(groups, feed_full_ref.shape[2])
     here.meet()
     place, has_next, following = here.g, here.above, here.up()
-    home_sems, feed_sems = several(sems, len(HomeGather.scratch(groups)), len(Gather.scratch(groups)))
-    out_gather = HomeGather(here, out_part_ref, out_full_ref, home_sems)
-    feed_gather = Gather(here, feed_parts_ref, feed_full_ref, feed_sems)
-    out_gather.start()
-    feed_gather.start()
+    home_sems, feed_sems = several(sems, 5, 5)
+    out_gather = HomeGather(here, None, out_full_ref, home_sems)
+    feed_gather = Gather(here, None, feed_full_ref, feed_sems)
+    out_gather.spread()
+    feed_gather.spread()
     pauses = Pauses(
         *[
             (functools.partial(out_gather.step, distance), functools.partial(feed_gather.step, distance))
@@ -826,30 +845,13 @@
         ]
     )
     prepared = (rows_ref, query_ref, key_ref, value_ref, within_ref, map_ref, inverse_ref)
-    prepare_blocks(0, GROUP // 2, *prepared)
-    out_gather.begin()
-    feed_gather.begin()
-    prepare_blocks(GROUP // 2, GROUP, *prepared)
+    prepare_blocks(0, GROUP, *prepared)
 
     def value_copy(source, slot):
-        return pltpu.make_async_remote_copy(
-            src_ref=source,
-            dst_ref=values_ref.at[slot],
-            send_sem=value_send.at[slot],
-            recv_sem=value_recv.at[slot],
-            device_id=following,
-            device_id_type=MESH,
-        )
+        return remote(source, values_ref.at[slot], value_send.at[slot], value_recv.at[slot], following)
 
     def key_copy(slot):
-        return pltpu.make_async_remote_copy(
-            src_ref=leave_ref.at[slot],
-            dst_ref=moved_ref.at[slot + 1, 0],
-            send_sem=key_send.at[slot],
-            recv_sem=key_recv.at[slot],
-            device_id=following,
-            device_id_type=MESH,
-        )
+        return remote(leave_ref.at[slot], moved_ref.at[slot + 1, 0], key_send.at[slot], key_recv.at[slot], following)
 
     def move(keys, block, head):
         return dot2(keys, map_ref[tile(block), tile(head)]).astype(BF16)
@@ -992,9 +994,8 @@
     }
 
 
-def attend(groups, lines, hops, projected, doc_query, doc_key, out_part, feed_parts):
+def attend(groups, hops, projected, doc_query, doc_key, out_full, feed_full):
     length = projected.shape[0]
-    rows, width = out_part.shape
     dma = pltpu.SemaphoreType.DMA
     return pl.pallas_call(
         functools.partial(attend_kernel, groups, hops),
@@ -1009,8 +1010,8 @@
             shape(F32, length, BLOCK),
             shape(BF16, hops + 1, GROUP, length, WIDE),
             shape(BF16, hops, length, WIDE),
-            shape(BF16, groups // GROUP, GROUP, lines, rows, width),
-            shape(BF16, groups, GROUP, lines, rows, feed_parts.shape[2]),
+            shape(BF16, *out_full.shape),
+            shape(BF16, *feed_full.shape),
         ],
         in_specs=in_vmem(3) + anywhere(2),
         out_specs=in_vmem(10) + anywhere(2),
@@ -1025,15 +1026,22 @@
             dma((hops,)),
             dma((hops,)),
         ]
-        + HomeGather.scratch(groups)
-        + Gather.scratch(groups),
+        + HomeGather.outside(groups)
+        + Gather.outside(groups),
+        input_output_aliases={3: 10, 4: 11},
         **communicating(1, "attend"),
-    )(projected, doc_query, doc_key, out_part, feed_parts)
-
-
-def attend_back_kernel(
+    )(projected, doc_query, doc_key, out_full, feed_full)
+
+
+def back_kernel(
     groups,
     hops,
+    partial_ref,
+    hidden_ref,
+    cotangent_ref,
+    gain_ref,
+    low_ref,
+    out_ref,
     query_ref,
     value_ref,
     within_ref,
@@ -1042,16 +1050,24 @@
     doc_key_ref,
     attended_ref,
     stats_ref,
-    moved_ref,
-    values_ref,
-    att_grad_ref,
-    rows_ref,
-    inverse_ref,
-    out_partial_ref,
+    values_hbm,
+    moved_hbm,
+    rows_hbm,
+    inverse_hbm,
+    down_partial_ref,
     feed_partial_ref,
+    grad_ref,
+    down_result_ref,
     rows_grad_ref,
     feed_result_ref,
     out_result_ref,
+    grad_low_ref,
+    att_grad_ref,
+    out_partial_ref,
+    moved_ref,
+    values_ref,
+    extra_ref,
+    load_sem,
     query_grad_ref,
     key_grad_ref,
     within_grad_ref,
@@ -1060,6 +1076,7 @@
     scaled_ref,
     dots_ref,
     direct_ref,
+    panels_ref,
     key_slots_ref,
     value_slots_ref,
     key_send,
@@ -1068,38 +1085,83 @@
     value_recv,
     *refs,
 ):
-    here = Place(groups, feed_partial_ref.shape[2])
+    lines = feed_partial_ref.shape[2]
+    here = Place(groups, lines)
     here.meet(column=True)
     place, has_next, previous = here.g, here.above, here.down()
-    feed_refs, out_refs = several(
-        refs, len(Scatter.scratch(groups, feed_partial_ref.shape)), len(HomeScatter.scratch(groups, out_partial_ref.shape))
+    sum_refs, gather_refs, down_refs, feed_refs, out_refs = several(
+        refs,
+        7,
+        2,
+        len(Scatter.scratch(groups, down_partial_ref.shape)),
+        len(Scatter.scratch(groups, feed_partial_ref.shape)),
+        len(HomeScatter.scratch(groups, out_partial_ref.shape)),
     )
+    sums = GroupSum(here, partial_ref, sum_refs)
+    whole = GroupGather(here, grad_low_ref, gather_refs)
+    down = Scatter(here, down_partial_ref, down_result_ref, down_refs)
     feed_scatter = Scatter(here, feed_partial_ref, feed_result_ref, feed_refs)
     out_scatter = HomeScatter(here, out_partial_ref, out_result_ref, out_refs)
-    feed_scatter.start(out_scatter.start)
     pauses = Pauses(*[(functools.partial(feed_scatter.step, wave),) for wave in range(1, groups)])
+
+    def load(hop):
+        return pltpu.make_async_copy(moved_hbm.at[hop], moved_ref.at[hop % 2], load_sem.at[hop % 2])
+
+    def load_values(hop):
+        return pltpu.make_async_copy(values_hbm.at[hop - 1], values_ref.at[hop % 2], load_sem.at[2 + hop % 2])
+
+    short = hops > 2
+    loads = [pltpu.make_async_copy(rows_hbm.at[:, pl.ds(4 * WIDE, EXTRA)], extra_ref, load_sem.at[4])]
+    panels = direct_ref if short else panels_ref
+    for index, panel in enumerate((0, 1, 3)):
+        loads.append(pltpu.make_async_copy(rows_hbm.at[:, pl.ds(panel * WIDE, WIDE)], panels.at[index], load_sem.at[5 + index]))
+    loads.append(pltpu.make_async_copy(inverse_hbm, panels.at[3], load_sem.at[8]))
+    sums.start()
+    down.start()
+    load(hops).start()
+    load_values(hops).start()
+    if not short:
+        for copy in loads:
+            copy.start()
+    feed_scatter.start_far(1, 1)
+    for chunk in range(CHUNKS):
+        sums.pass_on(chunk)
+    for chunk in range(CHUNKS):
+        back = rms_back(hidden_ref[sums.at(chunk), :], gain_ref[...], sums.take(chunk))
+        grad = cotangent_ref[sums.at(chunk), :].astype(F32) + back
+        grad_ref[sums.at(chunk), :] = grad
+        grad_low_ref[whole.at(chunk, here.m), :] = grad.astype(BF16)
+        whole.give(chunk)
+    down.step(1)
+    for chunk in range(CHUNKS):
+        whole.pass_on(chunk)
+    if groups > 2:
+        down.step(2)
+    whole.finish()
+    att_grad_ref[...] = dot(grad_low_ref[...], out_ref[...], NT).astype(BF16)
+    turned = low_ref[...].T
+    units = out_partial_ref.shape[3]
+
+    def out_tile(at):
+        value = dot(turned, grad_low_ref[:, at])
+        for index in range(WIDE // units):
+            slot, member, line = index // (GROUP * lines), index // lines % GROUP, index % lines
+            out_partial_ref[slot, member, line, :, at] = value[index * units : (index + 1) * units].astype(BF16)
+
+    in_tiles(out_partial_ref.shape[4], out_tile)
+    out_scatter.start()
+    feed_scatter.start_far(2)
+    feed_scatter.act(here.g)
+    for wave in range(3, groups):
+        down.step(wave)
 
     def key_copy(hop):
         slot = hop - 1
-        return pltpu.make_async_remote_copy(
-            src_ref=key_slots_ref.at[hop],
-            dst_ref=key_slots_ref.at[slot],
-            send_sem=key_send.at[slot],
-            recv_sem=key_recv.at[slot],
-            device_id=previous,
-            device_id_type=MESH,
-        )
+        return remote(key_slots_ref.at[hop], key_slots_ref.at[slot], key_send.at[slot], key_recv.at[slot], previous)
 
     def value_copy(hop):
         slot = hop - 1
-        return pltpu.make_async_remote_copy(
-            src_ref=value_slots_ref.at[hop],
-            dst_ref=value_slots_ref.at[slot],
-            send_sem=value_send.at[slot],
-            recv_sem=value_recv.at[slot],
-            device_id=previous,
-            device_id_type=MESH,
-        )
+        return remote(value_slots_ref.at[hop], value_slots_ref.at[slot], value_send.at[slot], value_recv.at[slot], previous)
 
     map_grad_ref[...] = jnp.zeros_like(map_grad_ref)
     query_grad_ref[...] = jnp.zeros_like(query_grad_ref)
@@ -1132,9 +1194,9 @@
             counts = row_counts(block, hop, first, count)
             for head in range(OWN):
                 query = query_ref[tile(block), tile(head)]
-                keys = moved_ref[hop, block, tile(first, count), tile(head)]
+                keys = moved_ref[hop % 2, block, tile(first, count), tile(head)]
                 weights, grad = pair(
-                    block, head, dot(query, keys, NT), counts, values_ref[hop - 1, tile(first, count), tile(head)]
+                    block, head, dot(query, keys, NT), counts, values_ref[hop % 2, tile(first, count), tile(head)]
                 )
                 raw = grad.astype(BF16)
                 query_grad_ref[tile(block), tile(head)] += dot(raw, keys)
@@ -1152,7 +1214,7 @@
                 grads = direct_ref[GROUP - 1, tile(GROUP - 1), tile(head)]
                 for block in range(GROUP - 2, -1, -1):
                     rows = tile(block + 1, GROUP - 1 - block)
-                    collect_map(block, head, moved_ref[hop, block, rows, tile(head)], grads)
+                    collect_map(block, head, moved_ref[hop % 2, block, rows, tile(head)], grads)
                     back = dot3(grads, map_ref[tile(block), tile(head)], NT)
                     direct = direct_ref[block, tile(block, GROUP - block), tile(head)]
                     grads = jnp.concatenate([direct[:BLOCK], direct[BLOCK:] + back], 0)
@@ -1161,7 +1223,7 @@
             else:
                 grads = key_grad_ref[:, tile(head)]
                 for block in range(GROUP - 1, -1, -1):
-                    collect_map(block, head, moved_ref[hop, block, :, tile(head)], grads)
+                    collect_map(block, head, moved_ref[hop % 2, block, :, tile(head)], grads)
                     grads = direct_ref[block, :, tile(head)] + dot3(grads, map_ref[tile(block), tile(head)], NT)
                 key_slots_ref[hop, :, tile(head)] = grads.astype(BF16)
 
@@ -1174,6 +1236,11 @@
         @pl.when(jnp.logical_not(has_next))
         def _():
             key_grad_ref[...] = jnp.zeros_like(key_grad_ref)
+
+    load(hops - 1).start()
+    load_values(hops - 1).start()
+    load(hops).wait()
+    load_values(hops).wait()
 
     @pl.when(place >= hops)
     def _():
@@ -1182,7 +1249,13 @@
         key_copy(hops).start()
         value_copy(hops).start()
 
+    down.last()
+
     def between(hop, pause=None):
+        load(hop - 1).start()
+        pl.when(jnp.asarray(hop) > 1)(lambda: load_values(hop - 1).start())
+        load(hop).wait()
+        load_values(hop).wait()
         pl.when(place >= hop)(lambda: hop_direct(hop, False))
         if pause is not None:
             pause()
@@ -1219,6 +1292,7 @@
         for hop in range(hops - 1, 0, -1):
             between(hop, pauses)
 
+    load(0).wait()
     for head in range(OWN):
         value_grad_ref[:, tile(head)] = jnp.zeros((GROUP * BLOCK, BLOCK), F32)
     for block in range(GROUP):
@@ -1239,7 +1313,7 @@
                 raw = grad[:, : block * BLOCK].astype(BF16)
                 query_grad_ref[tile(block), tile(head)] += dot(raw, keys)
                 direct_ref[block, tile(0, block), tile(head)] = dot(raw, query, TN)
-    pauses()
+    out_scatter.push()
     take(1)
     for head in range(OWN):
         grads = key_grad_ref[:, tile(head)]
@@ -1264,31 +1338,58 @@
         return carry
 
     lax.fori_loop(1, hops + 1, settle, 0)
-    pieces = (rows_ref, inverse_ref, query_grad_ref, key_grad_ref, within_grad_ref, map_grad_ref, value_grad_ref, rows_grad_ref)
+    if short:
+        for copy in loads:
+            copy.start()
+    for copy in loads:
+        copy.wait()
+    pauses()
+    pieces = (panels, extra_ref, query_grad_ref, key_grad_ref, within_grad_ref, map_grad_ref, value_grad_ref, rows_grad_ref)
     prepare_back_blocks(0, GROUP // 2, *pieces)
     pauses.rest()
-    out_scatter.push()
     prepare_back_blocks(GROUP // 2, GROUP, *pieces)
     feed_scatter.last()
     out_scatter.last()
+    sums.finish()
+    down.finish()
     feed_scatter.finish()
     out_scatter.finish()
 
 
-def attend_back(groups, hops, *args):
-    length = args[0].shape[0]
-    out, feed = args[-2:]
+def back(groups, hops, partial, hidden, cotangent, gain, low, out, *args):
+    values, moved, rows, inverse, down, feed = args[-6:]
+    size, width = hidden.shape
+    length = partial.shape[0]
+    lines, units = feed.shape[2:4]
+    out_shape = (groups // GROUP, GROUP, lines, units, width)
     dma = pltpu.SemaphoreType.DMA
+    inputs = (partial, hidden, cotangent, gain, low, out) + args
     return pl.pallas_call(
-        functools.partial(attend_back_kernel, groups, hops),
-        out_shape=[shape(BF16, *args[-4].shape), shape(BF16, GROUP, *feed.shape[3:]), shape(BF16, *out.shape[3:])],
-        in_specs=in_vmem(len(args) - 2) + anywhere(2),
-        out_specs=in_vmem(3),
-        scratch_shapes=[pltpu.VMEM((length, WIDE), F32)] * 5
+        functools.partial(back_kernel, groups, hops),
+        out_shape=[
+            shape(F32, size, width),
+            shape(F32, 1, *down.shape[3:]),
+            shape(BF16, *rows.shape),
+            shape(BF16, GROUP, *feed.shape[3:]),
+            shape(BF16, units, width),
+        ],
+        in_specs=in_vmem(len(inputs) - 6) + anywhere(6),
+        out_specs=in_vmem(5),
+        scratch_shapes=[
+            pltpu.VMEM((length, width), BF16),
+            pltpu.VMEM((length, WIDE), BF16),
+            pltpu.VMEM(out_shape, BF16),
+            pltpu.VMEM((2,) + moved.shape[1:], BF16),
+            pltpu.VMEM((2,) + values.shape[1:], BF16),
+            pltpu.VMEM((length, EXTRA), F32),
+            dma((9,)),
+        ]
+        + [pltpu.VMEM((length, WIDE), F32)] * 5
         + [
             pltpu.VMEM((length, WIDE), BF16),
             pltpu.VMEM((OWN, length, BLOCK), F32),
             pltpu.VMEM((GROUP, length, WIDE), F32),
+            pltpu.VMEM((1 if hops > 2 else GROUP, BLOCK if hops > 2 else length, WIDE), F32),
             pltpu.VMEM((hops + 1, length, WIDE), BF16),
             pltpu.VMEM((hops + 1, length, WIDE), BF16),
             dma((hops,)),
@@ -1296,17 +1397,27 @@
             dma((hops,)),
             dma((hops,)),
         ]
+        + GroupSum.scratch(size, width)
+        + GroupGather.scratch()
+        + Scatter.scratch(groups, down.shape)
         + Scatter.scratch(groups, feed.shape)
-        + HomeScatter.scratch(groups, out.shape),
-        **communicating(2, "attend_back", 60),
-    )(*args)
-
-
-def gather_kernel(groups, parts_ref, tokens_ref, cotangent_ref, full_ref, tokens_all_ref, cotangent_all_ref, send, recv, local, *sems):
-    here = Place(groups, full_ref.shape[2])
+        + HomeScatter.scratch(groups, out_shape),
+        **communicating(2, "back", 60),
+    )(*inputs)
+
+
+def gather_kernel(
+    groups, first_ref, gate_ref, up_ref, out_ref, down_ref, tokens_ref, cotangent_ref, full_ref, feed_full_ref, out_full_ref,
+    down_low_ref, tokens_all_ref, cotangent_all_ref, feed_parts_ref, out_low_ref, send, recv, local, *sems
+):
+    lines = full_ref.shape[2]
+    here = Place(groups, lines)
     here.meet()
-    gather = Gather(here, parts_ref, full_ref, sems)
-    gather.start()
+    first_sems, feed_sems, out_sems = several(sems, 8, 3, 2)
+    first = Gather(here, first_ref, full_ref, first_sems)
+    feed = Gather(here, feed_parts_ref, feed_full_ref, feed_sems)
+    out = HomeGather(here, out_low_ref, out_full_ref, out_sems)
+    first.start()
     size = tokens_ref.shape[0]
     own = pl.ds(pl.multiple_of(here.m * size, size), size)
     copies = []
@@ -1318,29 +1429,60 @@
             )
     for copy in copies:
         copy.start()
-    gather.begin()
+    out_low_ref[...] = out_ref[...].astype(BF16)
+    down_low_ref[...] = down_ref[...].astype(BF16)
+    own_units = feed_parts_ref.shape[2] // 2
+    for at, weight_ref in ((0, gate_ref), (own_units, up_ref)):
+        if len(weight_ref.shape) == 3:
+            feed_parts_ref[:, :, at : at + own_units] = weight_ref[...]
+        else:
+            for member in range(GROUP):
+                for index in range(groups * lines):
+                    block = (index // lines * GROUP + member) * lines + index % lines
+                    feed_parts_ref[member, :, pl.ds(at + index * BLOCK, BLOCK)] = weight_ref[:, tile(block)].astype(BF16)
+    feed.start()
+    out.start()
+    first.settle()
+    first.spread()
     for distance in range(1, groups):
-        gather.step(distance)
+        first.step(distance)
+    feed.settle()
+    out.settle()
     for copy in copies:
         copy.wait()
-    gather.finish()
-
-
-def gather_first(groups, lines, parts, tokens, cotangent):
+    first.finish()
+
+
+def gather_first(groups, lines, first, gate, up, out, down, tokens, cotangent):
     dma = pltpu.SemaphoreType.DMA
     size, width = tokens.shape
+    rows = out.shape[0]
+    units = 2 * down.shape[0] * groups * lines
     return pl.pallas_call(
         functools.partial(gather_kernel, groups),
         out_shape=[
-            shape(BF16, groups, GROUP, lines, *parts.shape[1:]),
+            shape(BF16, groups, GROUP, lines, *first.shape[1:]),
+            shape(BF16, groups, GROUP, lines, rows, units),
+            shape(BF16, groups // GROUP, GROUP, lines, rows, width),
+            shape(BF16, *down.shape),
             shape(BF16, GROUP * size, width),
             shape(BF16, GROUP * size, width),
         ],
-        in_specs=anywhere(3),
-        out_specs=anywhere(3),
-        scratch_shapes=[dma((2, GROUP)), dma((2, GROUP)), dma((2,))] + Gather.scratch(groups),
-        **communicating(0, "gather_first", 16),
-    )(parts, tokens, cotangent)
+        in_specs=anywhere(1) + in_vmem(4) + anywhere(2),
+        out_specs=anywhere(3) + in_vmem(1) + anywhere(2),
+        scratch_shapes=[
+            pltpu.VMEM((GROUP, rows, units), BF16),
+            pltpu.VMEM((rows, width), BF16),
+            dma((2, GROUP)),
+            dma((2, GROUP)),
+            dma((2,)),
+        ]
+        + Gather.inside()
+        + Gather.outside(groups)
+        + Gather.inside()
+        + HomeGather.inside(),
+        **communicating(0, "gather_first", 24),
+    )(first, gate, up, out, down, tokens, cotangent)
 
 
 def rms_norm(values, gain):
@@ -1351,21 +1493,34 @@
     scale = lax.rsqrt(jnp.mean(values * values, axis=-1, keepdims=True) + EPSILON)
     straight = values * scale
     lifted = grad * gain
-    back = scale * (lifted - straight * jnp.mean(lifted * straight, axis=-1, keepdims=True))
-    return back, grad * straight
-
-
-def branch_kernel(groups, partial_ref, tokens_ref, gain_ref, down_ref, hidden_ref, normed_ref, down_full_ref, *refs):
+    return scale * (lifted - straight * jnp.mean(lifted * straight, axis=-1, keepdims=True))
+
+
+def in_tiles(size, act, step=2 * BLOCK):
+    def one(index, carry):
+        act(pl.ds(pl.multiple_of(index * step, step), step))
+        return carry
+
+    lax.fori_loop(0, size // step, one, 0)
+
+
+def branch_kernel(
+    groups, partial_ref, tokens_ref, gain_ref, down_ref, feed_hbm, hidden_ref, normed_ref, active_ref, gate_slope_ref, up_slope_ref,
+    down_full_ref, feed_ref, feed_sem, *refs
+):
     here = Place(groups, down_full_ref.shape[1])
     here.meet()
-    sum_refs, gather_refs, down_refs = several(refs, 7, 2, len(Gather.scratch(groups)))
+    sum_refs, gather_refs, down_refs = several(refs, 7, 2, 8)
     total = GroupSum(here, partial_ref, sum_refs)
     whole = GroupGather(here, normed_ref, gather_refs)
     down = Gather(here, down_ref, down_full_ref, down_refs, mixed=False)
     pauses = Pauses(*[(functools.partial(down.step, distance),) for distance in range(1, groups)])
     total.start()
     down.start()
-    down.begin()
+    down.settle()
+    down.spread()
+    feed_copy = pltpu.make_async_copy(feed_hbm, feed_ref, feed_sem.at[0])
+    feed_copy.start()
     for chunk in range(CHUNKS):
         total.pass_on(chunk)
     pauses()
@@ -1378,121 +1533,153 @@
     for chunk in range(CHUNKS):
         whole.pass_on(chunk)
     pauses.rest()
+    feed_copy.wait()
     whole.finish()
+    units = active_ref.shape[1]
+
+    def act(at):
+        normed = normed_ref[...]
+        gate = dot(normed, feed_ref[:, at])
+        up = dot(normed, feed_ref[:, pl.ds(pl.multiple_of(at.start + units, BLOCK), at.size)])
+        sigmoid = jax.nn.sigmoid(gate)
+        silu = gate * sigmoid
+        active_ref[:, at] = (silu * up).astype(BF16)
+        gate_slope_ref[:, at] = up * (sigmoid * (1.0 + gate * (1.0 - sigmoid)))
+        up_slope_ref[:, at] = silu
+
+    in_tiles(units, act)
     total.finish()
     down.finish()
 
 
-def branch(groups, lines, partial, tokens, gain, down):
+def branch(groups, lines, partial, tokens, gain, down, feed):
     size, width = tokens.shape
+    length, units = partial.shape[0], feed.shape[1] // 2
+    dma = pltpu.SemaphoreType.DMA
     return pl.pallas_call(
         functools.partial(branch_kernel, groups),
-        out_shape=[shape(F32, size, width), shape(BF16, GROUP * size, width), shape(BF16, groups, lines, *down.shape)],
-        in_specs=in_vmem(3) + anywhere(1),
-        out_specs=in_vmem(2) + anywhere(1),
-        scratch_shapes=GroupSum.scratch(size, width) + GroupGather.scratch() + Gather.scratch(groups),
-        **communicating(3, "branch", 32),
-    )(partial, tokens, gain, down)
-
-
-def branch_back_kernel(
-    groups, partial_ref, hidden_ref, cotangent_ref, gain_ref, down_ref, grad_ref, grad_low_ref, gain_grad_ref, down_result_ref, *refs
-):
-    here = Place(groups, down_ref.shape[2])
+        out_shape=[
+            shape(F32, size, width),
+            shape(BF16, length, width),
+            shape(BF16, length, units),
+            shape(F32, length, units),
+            shape(F32, length, units),
+            shape(BF16, groups, lines, *down.shape),
+        ],
+        in_specs=in_vmem(3) + anywhere(2),
+        out_specs=in_vmem(5) + anywhere(1),
+        scratch_shapes=[pltpu.VMEM(feed.shape, BF16), dma((1,))]
+        + GroupSum.scratch(size, width)
+        + GroupGather.scratch()
+        + Gather.inside()
+        + Gather.outside(groups),
+        **communicating(3, "branch", 48),
+    )(partial, tokens, gain, down, feed)
+
+
+def finish_kernel(groups, whole_tiles, first_partial_ref, first_hbm, rows_grad_ref, output_partial_ref, tokens_ref, hidden_ref, grad_ref,
+                  gain_ref, beta_ref, feed_result_ref, *refs):
+    lines = first_partial_ref.shape[2]
+    here = Place(groups, lines)
     here.meet()
-    sum_refs, gather_refs, down_refs = several(refs, 7, 2, len(Scatter.scratch(groups, down_ref.shape)))
-    total = GroupSum(here, partial_ref, sum_refs)
-    whole = GroupGather(here, grad_low_ref, gather_refs)
-    down = Scatter(here, down_ref, down_result_ref, down_refs)
-    pauses = Pauses(*[(functools.partial(down.step, wave),) for wave in range(1, groups)])
-    total.start()
-    down.start()
-    for chunk in range(CHUNKS):
-        total.pass_on(chunk)
-    pauses()
-    gain_grad = jnp.zeros((1, gain_ref.shape[1]), F32)
-    for chunk in range(CHUNKS):
-        back, gain_rows = rms_back(hidden_ref[total.at(chunk), :], gain_ref[...], total.take(chunk))
-        grad = cotangent_ref[total.at(chunk), :].astype(F32) + back
-        gain_grad = gain_grad + jnp.sum(gain_rows, axis=0, keepdims=True)
-        grad_ref[total.at(chunk), :] = grad
-        grad_low_ref[whole.at(chunk, here.m), :] = grad.astype(BF16)
-        whole.give(chunk)
-    gain_grad_ref[...] = gain_grad
-    pauses()
-    for chunk in range(CHUNKS):
-        whole.pass_on(chunk)
-    pauses.rest()
-    whole.finish()
-    total.finish()
-    down.last()
-    down.finish()
-
-
-def branch_back(groups, partial, hidden, cotangent, gain, down):
-    size, width = hidden.shape
-    return pl.pallas_call(
-        functools.partial(branch_back_kernel, groups),
-        out_shape=[shape(F32, size, width), shape(BF16, GROUP * size, width), shape(F32, 1, width), shape(F32, 1, *down.shape[3:])],
-        in_specs=in_vmem(4) + anywhere(1),
-        out_specs=in_vmem(4),
-        scratch_shapes=GroupSum.scratch(size, width) + GroupGather.scratch() + Scatter.scratch(groups, down.shape),
-        **communicating(4, "branch_back", 48),
-    )(partial, hidden, cotangent, gain, down)
-
-
-def finish_kernel(
-    groups,
-    first_ref,
-    normed_partial_ref,
-    output_partial_ref,
-    tokens_ref,
-    hidden_ref,
-    grad_ref,
-    gain_ref,
-    first_result_ref,
-    tokens_grad_ref,
-    output_ref,
-    *refs,
-):
-    here = Place(groups, first_ref.shape[2])
-    here.meet()
-    first_refs, normed_refs, output_refs = several(refs, len(Scatter.scratch(groups, first_ref.shape)), 7, 7)
-    first = Scatter(here, first_ref, first_result_ref, first_refs)
+    weights, (query_out, key_out, value_out, house_out, extra_ref, sums_ref, tokens_grad_ref, output_ref), refs = (
+        refs[:6], refs[6:14], refs[14:]
+    )
+    if whole_tiles:
+        gate_out, up_out = refs[:2]
+        refs = refs[2:]
+    first_result_ref, first_full_ref, normed_partial_ref, first_sem = refs[:4]
+    first_refs, normed_refs, output_refs = several(refs[4:], len(Scatter.scratch(groups, first_partial_ref.shape)), 7, 7)
+    first = Scatter(here, first_partial_ref, first_result_ref, first_refs)
     normed = GroupSum(here, normed_partial_ref, normed_refs)
     output = GroupSum(here, output_partial_ref, output_refs)
     first.start()
-    normed.start()
+    first_copy = pltpu.make_async_copy(first_hbm, first_full_ref, first_sem.at[0])
+    first_copy.start()
     output.start()
     for chunk in range(CHUNKS):
+        output.pass_on(chunk)
+    first_copy.wait()
+
+    def normed_tile(at):
+        normed_partial_ref[:, at] = dot(rows_grad_ref[...], first_full_ref[at, :], NT).astype(BF16)
+
+    in_tiles(normed_partial_ref.shape[1], normed_tile)
+    normed.start()
+    for chunk in range(CHUNKS):
         normed.pass_on(chunk)
-    for chunk in range(CHUNKS):
-        output.pass_on(chunk)
-    for wave in range(1, groups):
-        first.step(wave)
-    for chunk in range(CHUNKS):
-        back, _ = rms_back(tokens_ref[normed.at(chunk), :].astype(F32), gain_ref[...], normed.take(chunk))
-        tokens_grad_ref[normed.at(chunk), :] = (grad_ref[normed.at(chunk), :] + back).astype(BF16)
+    first.step(1)
+    rows = sums_ref.shape[0]
+    sums_ref[...] = jnp.zeros_like(sums_ref)
+    lane = iota(1, (rows, BLOCK))
+    if whole_tiles:
+        units = feed_result_ref.shape[2] // 2
+        feed_sum = jnp.zeros((rows, BLOCK), F32)
+        for at, weight_ref, target_ref in ((0, weights[4], gate_out), (units, weights[5], up_out)):
+            for member in range(GROUP):
+                for index in range(groups * lines):
+                    block = (index // lines * GROUP + member) * lines + index % lines
+                    value = feed_result_ref[member, :, pl.ds(at + index * BLOCK, BLOCK)].astype(F32)
+                    target_ref[:, tile(block)] = value
+                    feed_sum = feed_sum + value * weight_ref[:, tile(block)].astype(BF16).astype(F32)
+        sums_ref[...] = jnp.where(lane == 1, jnp.sum(feed_sum, axis=1, keepdims=True), sums_ref[...])
+    if groups > 2:
+        first.step(2)
     for chunk in range(CHUNKS):
         output_ref[output.at(chunk), :] = (hidden_ref[output.at(chunk), :] + output.take(chunk)).astype(BF16)
-    first.last()
+    for chunk in range(CHUNKS):
+        back = rms_back(tokens_ref[normed.at(chunk), :].astype(F32), gain_ref[...], normed.take(chunk))
+        tokens_grad_ref[normed.at(chunk), :] = (grad_ref[normed.at(chunk), :] + back).astype(BF16)
+    for wave in range(3, groups):
+        first.step(wave)
     normed.finish()
     output.finish()
+    first.last()
     first.finish()
-
-
-def finish(groups, first, normed_partial, output_partial, tokens, hidden, grad, gain):
+    first_sum = jnp.zeros((rows, WIDE), F32)
+    extra_sum = jnp.zeros((rows, EXTRA), F32)
+    for member in range(GROUP):
+        for part, target_ref in enumerate((query_out, key_out, value_out, house_out)):
+            value = first_result_ref[member, :, pl.ds(part * WIDE, WIDE)].astype(F32)
+            at = pl.ds(member * WIDE, WIDE)
+            target_ref[:, at] = value
+            first_sum = first_sum + value * weights[part][:, at].astype(BF16).astype(F32)
+        extra = first_result_ref[member, :, pl.ds(4 * WIDE, EXTRA)].astype(F32)
+        extra_ref[member] = extra
+        extra_sum = extra_sum + extra * beta_ref[member].astype(F32)
+    total = jnp.sum(first_sum, axis=1, keepdims=True) + jnp.sum(extra_sum, axis=1, keepdims=True)
+    sums_ref[...] = jnp.where(lane == 0, total, sums_ref[...])
+
+
+def finish(groups, whole_tiles, first_partial, first, rows_grad, output_partial, tokens, hidden, grad, gain, beta, feed_result, weights):
     size, width = tokens.shape
+    length = rows_grad.shape[0]
+    rows = weights[0].shape[0]
+    dma = pltpu.SemaphoreType.DMA
+    out = [shape(F32, rows, width)] * 4 + [
+        shape(F32, GROUP, rows, EXTRA),
+        shape(F32, rows, BLOCK),
+        shape(BF16, size, width),
+        shape(BF16, size, width),
+    ]
+    if whole_tiles:
+        out = out + [shape(F32, *weights[4].shape)] * 2
     return pl.pallas_call(
-        functools.partial(finish_kernel, groups),
-        out_shape=[shape(BF16, GROUP, *first.shape[3:]), shape(BF16, size, width), shape(BF16, size, width)],
-        in_specs=anywhere(1) + in_vmem(6),
-        out_specs=in_vmem(3),
-        scratch_shapes=Scatter.scratch(groups, first.shape)
+        functools.partial(finish_kernel, groups, whole_tiles),
+        out_shape=out,
+        in_specs=anywhere(2) + in_vmem(8 + len(weights)),
+        out_specs=in_vmem(len(out)),
+        scratch_shapes=[
+            pltpu.VMEM((GROUP,) + first_partial.shape[3:], BF16),
+            pltpu.VMEM(first.shape, BF16),
+            pltpu.VMEM((length, width), BF16),
+            dma((1,)),
+        ]
+        + Scatter.scratch(groups, first_partial.shape)
         + GroupSum.scratch(size, width)
         + GroupSum.scratch(size, width),
         **communicating(5, "finish"),
-    )(first, normed_partial, output_partial, tokens, hidden, grad, gain)
+    )(first_partial, first, rows_grad, output_partial, tokens, hidden, grad, gain, beta, feed_result, *weights)
 
 
 def on_device(
@@ -1536,8 +1723,11 @@
         parts = weight.astype(BF16).reshape(rows, groups, GROUP, batch, hidden_rows)
         return jnp.transpose(parts, (2, 0, 1, 3, 4)).reshape(GROUP, rows, hidden_own)
 
-    feed_parts = jnp.concatenate([unit_columns(gate_weight), unit_columns(up_weight)], 2)
-    first, tokens_all, cotangent_all = gather_first(groups, batch, first_parts, tokens[0], cotangent[0])
+    whole_tiles = hidden_rows == BLOCK
+    feed_weights = (gate_weight, up_weight) if whole_tiles else (unit_columns(gate_weight), unit_columns(up_weight))
+    first, feed, out_full, down_low, tokens_all, cotangent_all = gather_first(
+        groups, batch, first_parts, *feed_weights, out_weight, down_weight, tokens[0], cotangent[0]
+    )
     first = first.reshape(width, -1)
 
     extra = first[:, 4 * WIDE :]
@@ -1554,82 +1744,64 @@
     )[:, None, :]
     doc_query = lax.dynamic_index_in_dim(docs, place, 0, keepdims=False)[:, None]
 
-    tokens_wide = tokens_all.astype(F32)
-    straight = tokens_wide * lax.rsqrt(jnp.mean(tokens_wide * tokens_wide, axis=-1, keepdims=True) + EPSILON)
-    normed = (straight * gain_one).astype(BF16)
+    normed = rms_norm(tokens_all.astype(F32), gain_one).astype(BF16)
     projected = dot(normed, first)
     (query, value, within, maps, inverse, attended, attended_low, stats, moved, values, out_full, feed) = attend(
-        groups, batch, hops, projected, doc_query, doc_key, out_weight.astype(BF16), feed_parts
+        groups, hops, projected, doc_query, doc_key, out_full, feed
     )
     out_full = out_full.reshape(WIDE, width)
     feed = feed.reshape(width, -1)
-    hidden, normed_two, down_full = branch(
-        groups, batch, dot(attended_low, out_full).astype(BF16), tokens[0], gain_two, down_weight.astype(BF16)
+    hidden, normed_two, active, gate_slope, up_slope, down_full = branch(
+        groups, batch, dot(attended_low, out_full).astype(BF16), tokens[0], gain_two, down_low, feed
     )
     down_full = down_full.reshape(hidden_own, width)
-    both = dot(normed_two, feed)
-    gate, up = both[:, :hidden_own], both[:, hidden_own:]
-    sigmoid = jax.nn.sigmoid(gate)
-    silu = gate * sigmoid
-    active = (silu * up).astype(BF16)
+    active_grad = dot(cotangent_all, down_full, NT)
+    feed_grads = jnp.concatenate([(active_grad * gate_slope).astype(BF16), (active_grad * up_slope).astype(BF16)], 1)
+    down_partial = dot(active, cotangent_all, TN).astype(BF16).reshape(groups, 1, batch, hidden_rows, width)
+    feed_partial = dot(normed_two, feed_grads, TN).astype(BF16).reshape(groups, GROUP, batch, rows, -1)
+    hidden_grad, down_weight_grad, rows_grad, feed_grad, out_weight_grad = back(
+        groups, hops, dot(feed_grads, feed, NT).astype(BF16), hidden, cotangent[0], gain_two, attended_low, out_full, query, value,
+        within, maps, doc_query, doc_key, attended, stats, values, moved, projected, inverse, down_partial, feed_partial,
+    )
     output_partial = dot(active, down_full).astype(BF16)
-
-    active_grad = dot(cotangent_all, down_full, NT)
-    gate_grad = (active_grad * up * (sigmoid * (1.0 + gate * (1.0 - sigmoid)))).astype(BF16)
-    up_grad = (active_grad * silu).astype(BF16)
-    feed_grads = jnp.concatenate([gate_grad, up_grad], 1)
-    down_partial = dot(active, cotangent_all, TN).astype(BF16).reshape(groups, 1, batch, hidden_rows, width)
-    hidden_grad, branch_grad, gain_two_grad, down_weight_grad = branch_back(
-        groups, dot(feed_grads, feed, NT).astype(BF16), hidden, cotangent[0], gain_two, down_partial
+    first_partial = dot(normed, rows_grad, TN).astype(BF16).reshape(groups, GROUP, batch, rows, -1)
+    beta_parts = jnp.pad(columns(beta_weight), ((0, 0), (0, 0), (0, EXTRA - OWN)))
+    weights = (query_weight, key_weight, value_weight, house_weight) + feed_weights
+    results = finish(
+        groups, whole_tiles, first_partial, first, rows_grad, output_partial, tokens[0], hidden, hidden_grad, gain_one, beta_parts, feed_grad,
+        weights,
     )
-    att_grad = dot(branch_grad, out_full, NT).astype(BF16)
-    feed_partial = dot(normed_two, feed_grads, TN).astype(BF16).reshape(groups, GROUP, batch, rows, -1)
-    out_partial = dot(attended_low, branch_grad, TN).astype(BF16).reshape(groups // GROUP, GROUP, batch, rows, width)
-    rows_grad, feed_grad, out_weight_grad = attend_back(
-        groups, hops, query, value, within, maps, doc_query, doc_key, attended, stats, moved, values, att_grad, projected, inverse,
-        out_partial, feed_partial,
-    )
-    normed_grad = dot(rows_grad, first, NT)
-    gain_one_grad = jnp.sum(normed_grad * straight, axis=0)
-    first_partial = dot(normed, rows_grad, TN)
-    lane = iota(1, (1, first_partial.shape[1]))
-    first_partial = jnp.where(lane == 4 * WIDE + OWN, gain_one_grad[:, None], first_partial)
-    first_partial = jnp.where(lane == 4 * WIDE + OWN + 1, gain_two_grad[0][:, None], first_partial)
-    first_partial = first_partial.astype(BF16).reshape(groups, GROUP, batch, rows, -1)
-    first_grad, tokens_grad, output = finish(
-        groups, first_partial, normed_grad.astype(BF16), output_partial, tokens[0], hidden, hidden_grad, gain_one
-    )
-    first_grad = first_grad.astype(F32)
+    query_weight_grad, key_weight_grad, value_weight_grad, house_weight_grad, extra_grad, sums, tokens_grad, output = results[:8]
     output, tokens_grad = output[None], tokens_grad[None]
     out_weight_grad = out_weight_grad.astype(F32)
     down_weight_grad = down_weight_grad[0]
-
-    def whole_columns(parts):
-        return jnp.transpose(parts, (1, 0, 2)).reshape(rows, -1)
-
-    query_weight_grad, key_weight_grad, value_weight_grad, house_weight_grad = [
-        whole_columns(first_grad[:, :, part * WIDE : (part + 1) * WIDE]) for part in range(4)
-    ]
-    beta_weight_grad = whole_columns(first_grad[:, :, 4 * WIDE : 4 * WIDE + OWN])
-    gains_grad = jnp.sum(first_grad[:, :, 4 * WIDE + OWN : 4 * WIDE + OWN + 2], axis=0)
+    beta_weight_grad = jnp.transpose(extra_grad[:, :, :OWN], (1, 0, 2)).reshape(rows, -1)
 
     def unit_whole(parts):
         parts = parts.astype(F32).reshape(GROUP, rows, groups, batch, hidden_rows)
         return jnp.transpose(parts, (1, 2, 0, 3, 4)).reshape(rows, -1)
 
-    gate_weight_grad = unit_whole(feed_grad[:, :, :hidden_own])
-    up_weight_grad = unit_whole(feed_grad[:, :, hidden_own:])
+    norm_gain_grad = sums[:, 0] / norm_gain.astype(BF16).astype(F32)
+    if whole_tiles:
+        gate_weight_grad, up_weight_grad = results[8:]
+        feed_sum = sums[:, 1]
+    else:
+        gate_weight_grad, up_weight_grad = unit_whole(feed_grad[:, :, :hidden_own]), unit_whole(feed_grad[:, :, hidden_own:])
+        feed_sum = jnp.sum(gate_weight_grad * gate_weight.astype(BF16).astype(F32), axis=1) + jnp.sum(
+            up_weight_grad * up_weight.astype(BF16).astype(F32), axis=1
+        )
+    ffn_gain_grad = feed_sum / ffn_gain.astype(BF16).astype(F32)
     return (
         output,
         tokens_grad,
-        gains_grad[:, 0],
+        norm_gain_grad,
         query_weight_grad,
         key_weight_grad,
         value_weight_grad,
         house_weight_grad,
         beta_weight_grad,
         out_weight_grad,
-        gains_grad[:, 1],
+        ffn_gain_grad,
         gate_weight_grad,
         up_weight_grad,
         down_weight_grad,

time: 572 us -> 538 us (0.941)
  matrix products: 52.4 us -> 36.6 us
  Pallas kernels: 479 us -> 465 us
    dot_general x12 -> x8, matrix products: 52.4 us -> 36.6 us  [dot(): return lax.dot_general(left, right, dims, preferred_element_type=F32)]
    pallas_call x3 -> x2, Pallas kernels: 248 us -> 238 us  [the longest x1 160 us: back(): pl.pallas_call(functools.partial(back_kernel, groups, hops), out_shape=[s...]
    reshape x17 -> x1, local copies, waits for them, and re-layouts: 10.4 us -> 0.62 us  [on_device(): jnp.transpose(extra_grad[:, :, :OWN], (1, 0, 2)).reshape(rows, -1)]
    pallas_call x1, Pallas kernels: 97.5 us -> 89.3 us  [attend(): pl.pallas_call(functools.partial(attend_kernel, groups, hops), out_shape=...]
where the time goes in v4:
time: 538 us; the launch traced here: 530 us
  Pallas kernels  465 us (86%)
  matrix products  36.6 us (7%)
  local copies, waits for them, and re-layouts  21.1 us (4%)
  other arithmetic  5.99 us (1%)
    pallas_call x1, Pallas kernels, back(): pl.pallas_call(functools.partial(back_kernel, groups, hops), out_shape=[s...  160 us
    pallas_call x1, Pallas kernels, attend(): pl.pallas_call(functools.partial(attend_kernel, groups, hops), out_shape=...  89.3 us
    pallas_call x1, Pallas kernels, finish(): pl.pallas_call(functools.partial(finish_kernel, groups, whole_tiles), out...  77.3 us
    pallas_call x1, Pallas kernels, gather_first(): pl.pallas_call(functools.partial(gather_kernel, groups), out_shape=[shape...  75.4 us
    pallas_call x1, Pallas kernels, branch(): pl.pallas_call(functools.partial(branch_kernel, groups), out_shape=[shape...  62.8 us
    dot_general x8, matrix products, dot(): return lax.dot_general(left, right, dims, preferred_element_type=F32)  36.6 us
    unnamed x76, local copies, waits for them, and re-layouts  11.3 us

profile of v4, /device:TPU:0, one launch (start us, length us, event | category | flops | bytes accessed | tf_op | source)
XLA Modules:
  0.0 530.4 jit_solution(13566454375646148082)
XLA Ops:
  0.7 1.0 convert_element_type.109
  1.8 1.1 convert_element_type.108
  2.9 1.0 convert_element_type.111
  6.0 1.1 concatenate.10.first_ref
  7.1 1.1 copy-done.12
  8.3 1.0 copy-done.13
  9.2 75.4 %gather_first.1 = (bf16[4,4,2,48,1664]{4,3,2,1,0:T(8,128)(2,1)S(1)}, bf16[4,4,2,48,2048]{4,3,2,1,0:T(8,128)(2,1)S(1)}, bf16[1,4,2,48,1536]{4,3,2,1,0:T(8,128)(2,...) custom-call(bf16[4,48,1664]{2,1,0:T(8,128)(2,1)S(1)} %concatenate.10.first_ref, ...), custom_call_target="tpu_custom_call" | custom-call | tf_op jit(solution)/shard_map/gather_first/pallas_call | solution.py:1461
  85.6 5.6 %fusion.4.rows_ref.rows_hbm = f32[512,1664]{1,0:T(8,128)} fusion(bf16[1536,1664]{1,0:T(8,128)(2,1)S(1)} %bitcast.75, bf16[512,1536]{1,0:T(8,128)(2,1)S(1)} %get-tuple-element.52, f32[1536]{0:T(1024)S(1)} %get-tuple-element.92, f32[512]{0:T(512)S(1)} %add_rsqrt_fusion), kind=kOutput, calls=%fused_computation.16 | convolution fusion | flops 2620391424 | bytes 10100736 | tf_op jit(solution)/shard_map/dot_general | solution.py:30
  91.3 1.2 slice.34
  92.9 0.9 copy.62.doc_query_ref
  94.3 89.3 %attend.1 = (bf16[512,384]{1,0:T(8,128)(2,1)}, bf16[512,384]{1,0:T(8,128)(2,1)}, f32[512,384]{1,0:T(8,128)}, f32[512,384]{1,0:T(8,128)}, f32[512,384]{1,0:T(8,12...) custom-call(f32[512,1664]{1,0:T(8,128)} %fusion.4.rows_ref.rows_hbm,, ...), custom_call_target="tpu_custom_call", output_to_operand_aliasing={{10}: (3, {}), {11}: (4, {})} | custom-call | tf_op jit(solution)/shard_map/attend/pallas_call | solution.py:1000
  183.7 2.4 convolution_convert_fusion.5.partial_ref
  186.1 62.8 %branch.1 = (f32[128,1536]{1,0:T(8,128)S(1)}, bf16[512,1536]{1,0:T(8,128)(2,1)S(1)}, bf16[512,1024]{1,0:T(8,128)(2,1)S(1)}, f32[512,1024]{1,0:T(8,128)}, f32[512...) custom-call(bf16[512,1536]{1,0:T(8,128)(2,1)S(1)} %convolution_convert_fusion.5.partial_ref, ...), custom_call_target="tpu_custom_call" | custom-call | tf_op jit(solution)/shard_map/branch/pallas_call | solution.py:1559
  249.0 5.3 multiply_convert_fusion.1
  254.4 4.6 convolution_convert_fusion.4.partial_ref
  259.0 3.5 convolution_convert_fusion.2
  262.5 5.5 %convolution_convert_fusion.1 = bf16[1536,2048]{1,0:T(8,128)(2,1)} fusion(bf16[512,1536]{1,0:T(8,128)(2,1)S(1)} %get-tuple-element.75, bf16[512,1024]{1,0:T(8,128)(2,1)S(1)} %get-tuple-element.96, bf16[512,1024]{1,0:T(8,128)(2,1)S(1)} %get-tuple-element.95), kind=kOutput, calls=%fused_computation.1 | convolution fusion | flops 3228565504 | bytes 9961472 | tf_op jit(solution)/shard_map/dot_general | solution.py:30
  268.0 160.2 %back.1 = (f32[128,1536]{1,0:T(8,128)}, f32[1,128,1536]{2,1,0:T(8,128)}, bf16[512,1664]{1,0:T(8,128)(2,1)}, bf16[4,48,2048]{2,1,0:T(8,128)(2,1)}, bf16[48,1536]{1,0:T(8,128)(2,1)}) custom-call(bf16[512,1536]{1,0:T(8,128)(2,1)} %convolution_convert_fusion.4.partial_ref, f32[128,1536]{1,0:T(8,128)} %copy-done.6, bf16[128,1536]{1,0:T(8,128)(2,1)} %bitcast.81, ...), custom_call_target="tpu_custom_call" | custom-call | tf_op jit(solution)/shard_map/back/pallas_call | solution.py:1367
  428.3 6.6 %convolution_convert_fusion = bf16[1536,1664]{1,0:T(8,128)(2,1)} fusion(bf16[512,1664]{1,0:T(8,128)(2,1)} %get-tuple-element.76.rows_grad_ref, bf16[512,1536]{1,0:T(8,128)(2,1)S(1)} %copy-done.8, f32[1536]{0:T(1024)S(1)} %get-tuple-element.92, f32[512]{0:T(512)S(1)} %add_rsqrt_fusion), kind=kOutput, calls=%fused_computation | convolution fusion | flops 2622947328 | bytes 8396800 | tf_op jit(solution)/shard_map/dot_general | solution.py:30
  434.9 3.1 convolution_convert_fusion.3.output_partial_ref
  439.2 77.3 %finish.1 = (f32[48,1536]{1,0:T(8,128)}, f32[48,1536]{1,0:T(8,128)}, f32[48,1536]{1,0:T(8,128)}, f32[48,1536]{1,0:T(8,128)}, f32[4,48,128]{2,1,0:T(8,128)}, /*in...) custom-call(bf16[4,4,2,48,1664]{4,3,2,1,0:T(8,128)(2,1)} %bitcast.84, ...), custom_call_target="tpu_custom_call" | custom-call | tf_op jit(solution)/shard_map/finish/pallas_call | solution.py:1667
  516.5 1.0 slice_reduce_fusion
  518.1 0.9 slice_bitcast_fusion
  519.7 0.7 convert_element_type.134
  520.9 1.8 copy.88
  522.7 1.8 copy.89
  524.5 0.7 copy.90
  525.2 0.7 copy.91
  525.9 0.7 copy.92
  527.3 0.9 copy.94
  528.2 0.9 copy.95
  529.1 0.9 copy.96
  (99 shorter events, 7.8 us)
Async XLA Ops:
  0.6 3.3 copy-start.16
  0.7 4.0 copy-start.27
  0.7 4.2 copy-start.28
  0.7 4.3 copy-start.30
  0.7 4.4 copy-start.29
  1.7 5.4 %copy-start.3 = (bf16[1,128,1536]{2,1,0:T(8,128)(2,1)S(1)}, bf16[1,128,1536]{2,1,0:T(8,128)(2,1)}, u32[]{:S(2)}) copy-start(bf16[1,128,1536]{2,1,0:T(8,128)(2,1)} %param.14) | copy-start | bytes 1179652
  1.7 5.4 %copy-start.4 = (f32[48,4096]{1,0:T(8,128)S(1)}, f32[48,4096]{1,0:T(8,128)}, u32[]{:S(2)}) copy-start(f32[48,4096]{1,0:T(8,128)} %refs_4_.1) | copy-start | bytes 2359300
  1.7 5.4 %copy-start.5 = (f32[48,4096]{1,0:T(8,128)S(1)}, f32[48,4096]{1,0:T(8,128)}, u32[]{:S(2)}) copy-start(f32[48,4096]{1,0:T(8,128)} %refs_5_.1) | copy-start | bytes 2359300
  1.8 5.4 %copy-start.11 = (bf16[1,128,1536]{2,1,0:T(8,128)(2,1)S(1)}, bf16[1,128,1536]{2,1,0:T(8,128)(2,1)}, u32[]{:S(2)}) copy-start(bf16[1,128,1536]{2,1,0:T(8,128)(2,1)} %param.27) | copy-start | bytes 1179652
  4.8 2.3 copy-start.20
  7.1 1.1 copy-start.12
  84.7 6.6 %copy-start = (bf16[4,4,2,48,2048]{4,3,2,1,0:T(8,128)(2,1)}, bf16[4,4,2,48,2048]{4,3,2,1,0:T(8,128)(2,1)S(1)}, u32[]{:S(2)}) copy-start(bf16[4,4,2,48,2048]{4,3,2,1,0:T(8,128)(2,1)S(1)} %get-tuple-element.56.feed_unit_ref) | copy-start | bytes 18874372
  84.7 6.6 %copy-start.1 = (bf16[1,4,2,48,1536]{4,3,2,1,0:T(8,128)(2,1)}, bf16[1,4,2,48,1536]{4,3,2,1,0:T(8,128)(2,1)S(1)}, u32[]{:S(2)}) copy-start(bf16[1,4,2,48,1536]{4,3,2,1,0:T(8,128)(2,1)S(1)} %get-tuple-element.55.out_home_ref) | copy-start | bytes 3538948
  84.7 6.6 %copy-start.2 = (bf16[4,4,2,48,1664]{4,3,2,1,0:T(8,128)(2,1)}, bf16[4,4,2,48,1664]{4,3,2,1,0:T(8,128)(2,1)S(1)}, u32[]{:S(2)}) copy-start(bf16[4,4,2,48,1664]{4,3,2,1,0:T(8,128)(2,1)S(1)} %get-tuple-element.53) | copy-start | bytes 15335428
  84.7 6.6 %copy-start.7 = (bf16[512,1536]{1,0:T(8,128)(2,1)}, bf16[512,1536]{1,0:T(8,128)(2,1)S(1)}, u32[]{:S(2)}) copy-start(bf16[512,1536]{1,0:T(8,128)(2,1)S(1)} %get-tuple-element.52) | copy-start | bytes 4718596
  84.7 6.6 %copy-start.9 = (bf16[512,1536]{1,0:T(8,128)(2,1)}, bf16[512,1536]{1,0:T(8,128)(2,1)S(1)}, u32[]{:S(2)}) copy-start(bf16[512,1536]{1,0:T(8,128)(2,1)S(1)} %get-tuple-element.54) | copy-start | bytes 4718596
  186.1 62.9 %copy-start.14 = (f32[1,1536]{1,0:T(1,128)}, f32[1,1536]{1,0:T(1,128)S(1)}, u32[]{:S(2)}) copy-start(f32[1,1536]{1,0:T(1,128)S(1)} %reshape.142.gain_ref) | copy-start | bytes 18436
  186.1 62.9 %copy-start.10 = (bf16[512,1536]{1,0:T(8,128)(2,1)S(1)}, bf16[512,1536]{1,0:T(8,128)(2,1)}, u32[]{:S(2)}) copy-start(bf16[512,1536]{1,0:T(8,128)(2,1)} %copy-done.9) | copy-start | bytes 4718596
  186.1 68.2 %slice-start = ((s8[6291456]{0:T(1024)(128)(4,1)}), s8[2097152]{0:T(1024)(128)(4,1)S(1)}, s32[]{:S(2)}) async-start(s8[6291456]{0:T(1024)(128)(4,1)} %bitcast.69), calls=%async_computation | async-start | bytes 4194304
  249.0 5.3 %copy-start.6 = (f32[128,1536]{1,0:T(8,128)}, f32[128,1536]{1,0:T(8,128)S(1)}, u32[]{:S(2)}) copy-start(f32[128,1536]{1,0:T(8,128)S(1)} %get-tuple-element.64.hidden_ref) | copy-start | bytes 2359300
  249.0 5.3 %slice-start.1 = ((s8[6291456]{0:T(1024)(128)(4,1)}), s8[4194304]{0:T(1024)(128)(4,1)S(1)}, s32[]{:S(2)}) async-start(s8[6291456]{0:T(1024)(128)(4,1)} %bitcast.69), calls=%async_computation.1 | async-start | bytes 8388608
  268.0 160.2 %copy-start.8 = (bf16[512,1536]{1,0:T(8,128)(2,1)S(1)}, bf16[512,1536]{1,0:T(8,128)(2,1)}, u32[]{:S(2)}) copy-start(bf16[512,1536]{1,0:T(8,128)(2,1)} %copy-done.7) | copy-start | bytes 4718596
  428.2 6.6 %copy-start.15 = (bf16[4,2,128,1536]{3,2,1,0:T(8,128)(2,1)S(1)}, bf16[4,2,128,1536]{3,2,1,0:T(8,128)(2,1)}, u32[]{:S(2)}) copy-start(bf16[4,2,128,1536]{3,2,1,0:T(8,128)(2,1)} %get-tuple-element.61) | copy-start | bytes 9437188
  434.9 3.7 copy-start.21
  439.2 80.5 %copy-start.26 = (bf16[48,1536]{1,0:T(8,128)(2,1)S(1)}, bf16[48,1536]{1,0:T(8,128)(2,1)}, u32[]{:S(2)}) copy-start(bf16[48,1536]{1,0:T(8,128)(2,1)} %get-tuple-element.87) | copy-start | bytes 442372
  516.5 8.0 %copy-start.25 = (f32[48,1536]{1,0:T(8,128)S(1)}, f32[48,1536]{1,0:T(8,128)}, u32[]{:S(2)}) copy-start(f32[48,1536]{1,0:T(8,128)} %get-tuple-element.121) | copy-start | bytes 884740
  516.5 8.7 %copy-start.24 = (f32[48,1536]{1,0:T(8,128)S(1)}, f32[48,1536]{1,0:T(8,128)}, u32[]{:S(2)}) copy-start(f32[48,1536]{1,0:T(8,128)} %get-tuple-element.122) | copy-start | bytes 884740
  516.5 9.4 %copy-start.23 = (f32[48,1536]{1,0:T(8,128)S(1)}, f32[48,1536]{1,0:T(8,128)}, u32[]{:S(2)}) copy-start(f32[48,1536]{1,0:T(8,128)} %get-tuple-element.123) | copy-start | bytes 884740
  516.5 10.1 %copy-start.22 = (f32[48,1536]{1,0:T(8,128)S(1)}, f32[48,1536]{1,0:T(8,128)}, u32[]{:S(2)}) copy-start(f32[48,1536]{1,0:T(8,128)} %get-tuple-element.124) | copy-start | bytes 884740
  519.7 7.7 %copy-start.19 = (f32[48,4096]{1,0:T(8,128)S(1)}, f32[48,4096]{1,0:T(8,128)}, u32[]{:S(2)}) copy-start(f32[48,4096]{1,0:T(8,128)} %get-tuple-element.128) | copy-start | bytes 2359300
  524.5 3.8 copy-start.18
  525.9 3.2 copy-start.17
  (1 other events, 1.0 us)

commit v5 on v4

--- a/solution.py
+++ b/solution.py
@@ -325,19 +325,12 @@
     def __init__(self, place, part, full, sems):
         self.place, self.part_ref, self.full = place, part, full
         self.home = place.groups // GROUP
-        if part is not None:
-            self.part_send, self.part_recv = sems
-        else:
-            self.up_send, self.down_send, self.chain_recv, self.line_send, self.line_recv = sems
+        self.part_send, self.part_recv, self.up_send, self.down_send, self.chain_recv = sems
 
     @staticmethod
-    def inside():
+    def scratch(groups):
         dma = pltpu.SemaphoreType.DMA
-        return [dma((1,)), dma((GROUP,))]
-
-    @staticmethod
-    def outside(groups):
-        return [pltpu.SemaphoreType.DMA((groups // GROUP,))] * 5
+        return [dma((1,)), dma((GROUP,))] + [dma((groups // GROUP,))] * 3
 
     def at_home(self):
         return self.place.m == self.place.g // self.home
@@ -370,12 +363,7 @@
         sems = self.up_send if up else self.down_send
         return remote(unit, unit, sems.at[slot], self.chain_recv.at[slot], p.up() if up else p.down())
 
-    def across(self, slot):
-        p = self.place
-        unit = self.full.at[slot, :, p.b]
-        return remote(unit, unit, self.line_send.at[slot], self.line_recv.at[slot], p.across())
-
-    def settle(self):
+    def spread(self):
         p = self.place
 
         @pl.when(self.at_home())
@@ -383,18 +371,9 @@
             self.own().wait()
             for offset in range(1, GROUP):
                 self.taken(p.other(offset)).wait_recv()
-
-        pl.when(jnp.logical_not(self.at_home()))(lambda: self.hand().wait_send())
-
-    def spread(self):
-        p = self.place
-
-        @pl.when(self.at_home())
-        def _():
             slot = p.g % self.home
             pl.when(p.above)(lambda: self.chain(slot, True).start())
             pl.when(p.below)(lambda: self.chain(slot, False).start())
-            self.across(slot).start()
 
     def step(self, distance):
         p = self.place
@@ -405,21 +384,27 @@
             def _():
                 self.chain(slot, True).wait_recv()
                 pl.when(p.above)(lambda: self.chain(slot, True).start())
-                self.across(slot).start()
 
             @pl.when(source - p.g == distance)
             def _():
                 self.chain(slot, False).wait_recv()
                 pl.when(p.below)(lambda: self.chain(slot, False).start())
-                self.across(slot).start()
 
     def finish(self):
         p = self.place
+        pl.when(jnp.logical_not(self.at_home()))(lambda: self.hand().wait_send())
         for slot in range(self.home):
             source = p.m * self.home + slot
-            self.across(slot).wait()
             pl.when(p.above & (p.g >= source))(lambda: self.chain(slot, True).wait_send())
             pl.when(p.below & (p.g <= source))(lambda: self.chain(slot, False).wait_send())
+
+
+def home_lines(place, full, send, recv):
+    copies = []
+    for slot in range(place.groups // GROUP):
+        unit = full.at[slot, :, place.b]
+        copies.append(remote(unit, unit, send.at[slot], recv.at[slot], place.across()))
+    return copies
 
 
 class Scatter:
@@ -569,72 +554,77 @@
                 self.hand(offset).wait()
 
 
+class LineSum:
+    def __init__(self, place, partial, result, refs):
+        self.place, self.partial, self.result = place, partial, result
+        self.land, self.mine_sem, self.send, self.recv = refs
+
+    @staticmethod
+    def scratch(groups, shape):
+        home = groups // GROUP
+        return [pltpu.VMEM((home, GROUP) + tuple(shape[3:]), BF16)] + [pltpu.SemaphoreType.DMA((home,))] * 3
+
+    def load(self, slot):
+        return pltpu.make_async_copy(self.partial.at[slot, :, self.place.b], self.result.at[slot], self.mine_sem.at[slot])
+
+    def line(self, slot):
+        p = self.place
+        return remote(self.partial.at[slot, :, 1 - p.b], self.land.at[slot], self.send.at[slot], self.recv.at[slot], p.across())
+
+    def start(self):
+        for slot in range(self.partial.shape[0]):
+            self.line(slot).start()
+            self.load(slot).start()
+
+    def finish(self):
+        for slot in range(self.partial.shape[0]):
+            self.load(slot).wait()
+            self.line(slot).wait()
+            for part in range(GROUP):
+                total = self.result[slot, part].astype(F32) + self.land[slot, part].astype(F32)
+                self.result[slot, part] = total.astype(BF16)
+
+
 class HomeScatter:
     def __init__(self, place, partial, result, refs):
         self.place, self.partial, self.result = place, partial, result
-        (self.land, self.home_land, self.leave, self.mine_sem, self.line_send, self.line_recv, self.home_send, self.home_recv,
-         self.part_send, self.part_recv) = refs
+        self.home_land, self.leave, self.home_send, self.home_recv, self.part_send, self.part_recv = refs
         self.home = place.groups // GROUP
 
     @staticmethod
     def scratch(groups, shape):
         dma = pltpu.SemaphoreType.DMA
-        home = groups // GROUP
-        unit = (GROUP,) + tuple(shape[3:])
+        unit = tuple(shape[1:])
         return [
-            pltpu.VMEM((home,) + unit, BF16),
             pltpu.VMEM((groups - 1,) + unit, BF16),
-            pltpu.VMEM((home,) + unit, BF16),
-            dma((home,)),
-            dma((home,)),
-            dma((home,)),
-            dma((home,)),
+            pltpu.VMEM(unit, BF16),
+            dma((shape[0],)),
             dma((groups - 1,)),
             dma((GROUP,)),
             dma((1,)),
         ]
 
-    def load(self, slot):
-        return pltpu.make_async_copy(self.partial.at[slot, :, self.place.b], self.leave.at[slot], self.mine_sem.at[slot])
-
-    def line(self, slot):
-        p = self.place
-        return remote(self.partial.at[slot, :, 1 - p.b], self.land.at[slot], self.line_send.at[slot], self.line_recv.at[slot], p.across())
-
-    def start(self):
-        for slot in range(self.home):
-            self.line(slot).start()
-            self.load(slot).start()
-
     def home_copy(self, slot):
         p = self.place
         target = p.m * self.home + slot
         index = (p.g - target + p.groups - 1) % p.groups
         return remote(
-            self.leave.at[slot], self.home_land.at[index], self.home_send.at[slot], self.home_recv.at[index], p.column(target)
+            self.partial.at[slot], self.home_land.at[index], self.home_send.at[slot], self.home_recv.at[index], p.column(target)
         )
 
     def landed(self, index):
         p = self.place
-        return remote(self.leave.at[0], self.home_land.at[index], self.home_send.at[0], self.home_recv.at[index], p.across())
-
-    def push(self):
+        return remote(self.leave, self.home_land.at[index], self.home_send.at[0], self.home_recv.at[index], p.across())
+
+    def start(self):
         p = self.place
         for slot in range(self.home):
-
-            @pl.when(p.g != p.m * self.home + slot)
-            def _():
-                self.load(slot).wait()
-                self.line(slot).wait_recv()
-                for part in range(GROUP):
-                    total = self.leave[slot, part].astype(F32) + self.land[slot, part].astype(F32)
-                    self.leave[slot, part] = total.astype(BF16)
-                self.home_copy(slot).start()
-
-    def hand(self, slot, other):
+            pl.when(p.g != p.m * self.home + slot)(lambda: self.home_copy(slot).start())
+
+    def hand(self, other):
         p = self.place
         return remote(
-            self.leave.at[slot, other], self.result, self.part_send.at[other], self.part_recv.at[0], {"g": p.g, "m": other, "b": p.b}
+            self.leave.at[other], self.result, self.part_send.at[other], self.part_recv.at[0], {"g": p.g, "m": other, "b": p.b}
         )
 
     def last(self):
@@ -642,19 +632,16 @@
 
         @pl.when(p.m == p.g // self.home)
         def _():
-            slot = p.g % self.home
-            self.load(slot).wait()
-            self.line(slot).wait_recv()
             for index in range(p.groups - 1):
                 self.landed(index).wait_recv()
             for part in range(GROUP):
-                total = self.leave[slot, part].astype(F32) + self.land[slot, part].astype(F32)
+                total = self.partial[p.g % self.home, part].astype(F32)
                 for index in range(p.groups - 1):
                     total = total + self.home_land[index, part].astype(F32)
-                self.leave[slot, part] = total.astype(BF16)
+                self.leave[part] = total.astype(BF16)
             for offset in range(1, GROUP):
-                self.hand(slot, p.other(offset)).start()
-            self.result[...] = self.leave[slot, p.m]
+                self.hand(p.other(offset)).start()
+            self.result[...] = self.leave[p.m]
 
     def finish(self):
         p = self.place
@@ -663,11 +650,10 @@
         @pl.when(keeper)
         def _():
             for offset in range(1, GROUP):
-                self.hand(p.g % self.home, p.other(offset)).wait_send()
-
-        pl.when(jnp.logical_not(keeper))(lambda: self.hand(0, p.other(1)).wait_recv())
+                self.hand(p.other(offset)).wait_send()
+
+        pl.when(jnp.logical_not(keeper))(lambda: self.hand(p.other(1)).wait_recv())
         for slot in range(self.home):
-            self.line(slot).wait_send()
             pl.when(p.g != p.m * self.home + slot)(lambda: self.home_copy(slot).wait_send())
 
 
@@ -833,14 +819,15 @@
     here = Place(groups, feed_full_ref.shape[2])
     here.meet()
     place, has_next, following = here.g, here.above, here.up()
-    home_sems, feed_sems = several(sems, 5, 5)
-    out_gather = HomeGather(here, None, out_full_ref, home_sems)
+    home_sems, feed_sems = several(sems, 2, 5)
+    out_copies = home_lines(here, out_full_ref, *home_sems)
     feed_gather = Gather(here, None, feed_full_ref, feed_sems)
-    out_gather.spread()
     feed_gather.spread()
+    for copy in out_copies:
+        copy.start()
     pauses = Pauses(
         *[
-            (functools.partial(out_gather.step, distance), functools.partial(feed_gather.step, distance))
+            (functools.partial(feed_gather.step, distance),)
             for distance in range(1, groups)
         ]
     )
@@ -971,7 +958,8 @@
 
     lax.fori_loop(0, hops, settle, 0)
     pauses.rest()
-    out_gather.finish()
+    for copy in out_copies:
+        copy.wait()
     feed_gather.finish()
 
 
@@ -1026,7 +1014,7 @@
             dma((hops,)),
             dma((hops,)),
         ]
-        + HomeGather.outside(groups)
+        + [dma((groups // GROUP,))] * 2
         + Gather.outside(groups),
         input_output_aliases={3: 10, 4: 11},
         **communicating(1, "attend"),
@@ -1087,7 +1075,7 @@
 ):
     lines = feed_partial_ref.shape[2]
     here = Place(groups, lines)
-    here.meet(column=True)
+    here.meet()
     place, has_next, previous = here.g, here.above, here.down()
     sum_refs, gather_refs, down_refs, feed_refs, out_refs = several(
         refs,
@@ -1095,13 +1083,13 @@
         2,
         len(Scatter.scratch(groups, down_partial_ref.shape)),
         len(Scatter.scratch(groups, feed_partial_ref.shape)),
-        len(HomeScatter.scratch(groups, out_partial_ref.shape)),
+        len(LineSum.scratch(groups, out_partial_ref.shape)),
     )
     sums = GroupSum(here, partial_ref, sum_refs)
     whole = GroupGather(here, grad_low_ref, gather_refs)
     down = Scatter(here, down_partial_ref, down_result_ref, down_refs)
     feed_scatter = Scatter(here, feed_partial_ref, feed_result_ref, feed_refs)
-    out_scatter = HomeScatter(here, out_partial_ref, out_result_ref, out_refs)
+    out_lines = LineSum(here, out_partial_ref, out_result_ref, out_refs)
     pauses = Pauses(*[(functools.partial(feed_scatter.step, wave),) for wave in range(1, groups)])
 
     def load(hop):
@@ -1149,7 +1137,7 @@
             out_partial_ref[slot, member, line, :, at] = value[index * units : (index + 1) * units].astype(BF16)
 
     in_tiles(out_partial_ref.shape[4], out_tile)
-    out_scatter.start()
+    out_lines.start()
     feed_scatter.start_far(2)
     feed_scatter.act(here.g)
     for wave in range(3, groups):
@@ -1313,7 +1301,6 @@
                 raw = grad[:, : block * BLOCK].astype(BF16)
                 query_grad_ref[tile(block), tile(head)] += dot(raw, keys)
                 direct_ref[block, tile(0, block), tile(head)] = dot(raw, query, TN)
-    out_scatter.push()
     take(1)
     for head in range(OWN):
         grads = key_grad_ref[:, tile(head)]
@@ -1348,12 +1335,11 @@
     prepare_back_blocks(0, GROUP // 2, *pieces)
     pauses.rest()
     prepare_back_blocks(GROUP // 2, GROUP, *pieces)
+    out_lines.finish()
     feed_scatter.last()
-    out_scatter.last()
     sums.finish()
     down.finish()
     feed_scatter.finish()
-    out_scatter.finish()
 
 
 def back(groups, hops, partial, hidden, cotangent, gain, low, out, *args):
@@ -1371,7 +1357,7 @@
             shape(F32, 1, *down.shape[3:]),
             shape(BF16, *rows.shape),
             shape(BF16, GROUP, *feed.shape[3:]),
-            shape(BF16, units, width),
+            shape(BF16, groups // GROUP, GROUP, units, width),
         ],
         in_specs=in_vmem(len(inputs) - 6) + anywhere(6),
         out_specs=in_vmem(5),
@@ -1401,7 +1387,7 @@
         + GroupGather.scratch()
         + Scatter.scratch(groups, down.shape)
         + Scatter.scratch(groups, feed.shape)
-        + HomeScatter.scratch(groups, out_shape),
+        + LineSum.scratch(groups, out_shape),
         **communicating(2, "back", 60),
     )(*inputs)
 
@@ -1413,11 +1399,13 @@
     lines = full_ref.shape[2]
     here = Place(groups, lines)
     here.meet()
-    first_sems, feed_sems, out_sems = several(sems, 8, 3, 2)
+    first_sems, feed_sems, out_sems = several(sems, 8, 3, 5)
     first = Gather(here, first_ref, full_ref, first_sems)
     feed = Gather(here, feed_parts_ref, feed_full_ref, feed_sems)
     out = HomeGather(here, out_low_ref, out_full_ref, out_sems)
     first.start()
+    out_low_ref[...] = out_ref[...].astype(BF16)
+    out.start()
     size = tokens_ref.shape[0]
     own = pl.ds(pl.multiple_of(here.m * size, size), size)
     copies = []
@@ -1429,7 +1417,6 @@
             )
     for copy in copies:
         copy.start()
-    out_low_ref[...] = out_ref[...].astype(BF16)
     down_low_ref[...] = down_ref[...].astype(BF16)
     own_units = feed_parts_ref.shape[2] // 2
     for at, weight_ref in ((0, gate_ref), (own_units, up_ref)):
@@ -1441,13 +1428,14 @@
                     block = (index // lines * GROUP + member) * lines + index % lines
                     feed_parts_ref[member, :, pl.ds(at + index * BLOCK, BLOCK)] = weight_ref[:, tile(block)].astype(BF16)
     feed.start()
-    out.start()
     first.settle()
     first.spread()
+    out.spread()
     for distance in range(1, groups):
         first.step(distance)
+        out.step(distance)
     feed.settle()
-    out.settle()
+    out.finish()
     for copy in copies:
         copy.wait()
     first.finish()
@@ -1480,7 +1468,7 @@
         + Gather.inside()
         + Gather.outside(groups)
         + Gather.inside()
-        + HomeGather.inside(),
+        + HomeGather.scratch(groups),
         **communicating(0, "gather_first", 24),
     )(first, gate, up, out, down, tokens, cotangent)
 
@@ -1577,109 +1565,133 @@
     )(partial, tokens, gain, down, feed)
 
 
-def finish_kernel(groups, whole_tiles, first_partial_ref, first_hbm, rows_grad_ref, output_partial_ref, tokens_ref, hidden_ref, grad_ref,
-                  gain_ref, beta_ref, feed_result_ref, *refs):
-    lines = first_partial_ref.shape[2]
-    here = Place(groups, lines)
-    here.meet()
-    weights, (query_out, key_out, value_out, house_out, extra_ref, sums_ref, tokens_grad_ref, output_ref), refs = (
-        refs[:6], refs[6:14], refs[14:]
+def finish_kernel(
+    groups, first_partial_ref, first_hbm, down_hbm, rows_grad_ref, active_ref, out_lines_ref, tokens_ref, hidden_ref, grad_ref, gain_ref,
+    first_result_ref, out_result_ref, tokens_grad_ref, output_ref, first_full_ref, down_full_ref, normed_partial_ref,
+    output_partial_ref, load_sem, *refs
+):
+    here = Place(groups, first_partial_ref.shape[2])
+    here.meet(column=True)
+    first_refs, out_refs, normed_refs, output_refs = several(
+        refs, len(Scatter.scratch(groups, first_partial_ref.shape)), len(HomeScatter.scratch(groups, out_lines_ref.shape)), 7, 7
     )
-    if whole_tiles:
-        gate_out, up_out = refs[:2]
-        refs = refs[2:]
-    first_result_ref, first_full_ref, normed_partial_ref, first_sem = refs[:4]
-    first_refs, normed_refs, output_refs = several(refs[4:], len(Scatter.scratch(groups, first_partial_ref.shape)), 7, 7)
     first = Scatter(here, first_partial_ref, first_result_ref, first_refs)
+    out = HomeScatter(here, out_lines_ref, out_result_ref, out_refs)
     normed = GroupSum(here, normed_partial_ref, normed_refs)
     output = GroupSum(here, output_partial_ref, output_refs)
     first.start()
-    first_copy = pltpu.make_async_copy(first_hbm, first_full_ref, first_sem.at[0])
+    first_copy = pltpu.make_async_copy(first_hbm, first_full_ref, load_sem.at[0])
+    down_copy = pltpu.make_async_copy(down_hbm, down_full_ref, load_sem.at[1])
     first_copy.start()
+    down_copy.start()
+    out.start()
+    first_copy.wait()
+
+    def normed_tile(at):
+        normed_partial_ref[:, at] = dot(rows_grad_ref[...], first_full_ref[at, :], NT).astype(BF16)
+
+    in_tiles(normed_partial_ref.shape[1], normed_tile)
+    normed.start()
+    down_copy.wait()
+    for chunk in range(CHUNKS):
+        normed.pass_on(chunk)
+
+    def output_tile(at):
+        output_partial_ref[:, at] = dot(active_ref[...], down_full_ref[:, at]).astype(BF16)
+
+    in_tiles(output_partial_ref.shape[1], output_tile)
     output.start()
+    first.step(1)
     for chunk in range(CHUNKS):
         output.pass_on(chunk)
-    first_copy.wait()
-
-    def normed_tile(at):
-        normed_partial_ref[:, at] = dot(rows_grad_ref[...], first_full_ref[at, :], NT).astype(BF16)
-
-    in_tiles(normed_partial_ref.shape[1], normed_tile)
-    normed.start()
     for chunk in range(CHUNKS):
-        normed.pass_on(chunk)
-    first.step(1)
-    rows = sums_ref.shape[0]
-    sums_ref[...] = jnp.zeros_like(sums_ref)
-    lane = iota(1, (rows, BLOCK))
-    if whole_tiles:
-        units = feed_result_ref.shape[2] // 2
+        back = rms_back(tokens_ref[normed.at(chunk), :].astype(F32), gain_ref[...], normed.take(chunk))
+        tokens_grad_ref[normed.at(chunk), :] = (grad_ref[normed.at(chunk), :] + back).astype(BF16)
+    if groups > 2:
+        first.step(2)
+    for chunk in range(CHUNKS):
+        output_ref[output.at(chunk), :] = (hidden_ref[output.at(chunk), :] + output.take(chunk)).astype(BF16)
+    for wave in range(3, groups):
+        first.step(wave)
+    out.last()
+    normed.finish()
+    output.finish()
+    first.last()
+    out.finish()
+    first.finish()
+
+
+def finish(groups, first_partial, first, down, rows_grad, active, out_lines, tokens, hidden, grad, gain):
+    size, width = tokens.shape
+    length = rows_grad.shape[0]
+    return pl.pallas_call(
+        functools.partial(finish_kernel, groups),
+        out_shape=[
+            shape(BF16, GROUP, *first_partial.shape[3:]),
+            shape(BF16, *out_lines.shape[2:]),
+            shape(BF16, size, width),
+            shape(BF16, size, width),
+        ],
+        in_specs=anywhere(3) + in_vmem(7),
+        out_specs=in_vmem(4),
+        scratch_shapes=[
+            pltpu.VMEM(first.shape, BF16),
+            pltpu.VMEM(down.shape, BF16),
+            pltpu.VMEM((length, width), BF16),
+            pltpu.VMEM((length, width), BF16),
+            pltpu.SemaphoreType.DMA((2,)),
+        ]
+        + Scatter.scratch(groups, first_partial.shape)
+        + HomeScatter.scratch(groups, out_lines.shape)
+        + GroupSum.scratch(size, width)
+        + GroupSum.scratch(size, width),
+        **communicating(5, "finish"),
+    )(first_partial, first, down, rows_grad, active, out_lines, tokens, hidden, grad, gain)
+
+
+def layout_kernel(groups, lines, first_ref, feed_ref, out_ref, beta_ref, gains_ref, *refs):
+    weights, targets = refs[:6], refs[6:]
+    query_out, key_out, value_out, house_out, out_out, norm_gain_out = targets[:6]
+    rows = gains_ref.shape[0]
+    first_sum = jnp.zeros((rows, WIDE), F32)
+    extra_sum = jnp.zeros((rows, EXTRA), F32)
+    for member in range(GROUP):
+        for part, target_ref in enumerate((query_out, key_out, value_out, house_out)):
+            value = first_ref[member, :, pl.ds(part * WIDE, WIDE)].astype(F32)
+            at = pl.ds(member * WIDE, WIDE)
+            target_ref[:, at] = value
+            first_sum = first_sum + value * weights[part][:, at].astype(BF16).astype(F32)
+        extra_sum = extra_sum + first_ref[member, :, pl.ds(4 * WIDE, EXTRA)].astype(F32) * beta_ref[member].astype(F32)
+    total = jnp.sum(first_sum, axis=1, keepdims=True) + jnp.sum(extra_sum, axis=1, keepdims=True)
+    norm_gain_out[...] = total / gains_ref[:, 0:1]
+    out_out[...] = out_ref[...].astype(F32)
+    if len(targets) > 6:
+        gate_out, up_out, ffn_gain_out = targets[6:]
+        units = feed_ref.shape[2] // 2
         feed_sum = jnp.zeros((rows, BLOCK), F32)
         for at, weight_ref, target_ref in ((0, weights[4], gate_out), (units, weights[5], up_out)):
             for member in range(GROUP):
                 for index in range(groups * lines):
                     block = (index // lines * GROUP + member) * lines + index % lines
-                    value = feed_result_ref[member, :, pl.ds(at + index * BLOCK, BLOCK)].astype(F32)
+                    value = feed_ref[member, :, pl.ds(at + index * BLOCK, BLOCK)].astype(F32)
                     target_ref[:, tile(block)] = value
                     feed_sum = feed_sum + value * weight_ref[:, tile(block)].astype(BF16).astype(F32)
-        sums_ref[...] = jnp.where(lane == 1, jnp.sum(feed_sum, axis=1, keepdims=True), sums_ref[...])
-    if groups > 2:
-        first.step(2)
-    for chunk in range(CHUNKS):
-        output_ref[output.at(chunk), :] = (hidden_ref[output.at(chunk), :] + output.take(chunk)).astype(BF16)
-    for chunk in range(CHUNKS):
-        back = rms_back(tokens_ref[normed.at(chunk), :].astype(F32), gain_ref[...], normed.take(chunk))
-        tokens_grad_ref[normed.at(chunk), :] = (grad_ref[normed.at(chunk), :] + back).astype(BF16)
-    for wave in range(3, groups):
-        first.step(wave)
-    normed.finish()
-    output.finish()
-    first.last()
-    first.finish()
-    first_sum = jnp.zeros((rows, WIDE), F32)
-    extra_sum = jnp.zeros((rows, EXTRA), F32)
-    for member in range(GROUP):
-        for part, target_ref in enumerate((query_out, key_out, value_out, house_out)):
-            value = first_result_ref[member, :, pl.ds(part * WIDE, WIDE)].astype(F32)
-            at = pl.ds(member * WIDE, WIDE)
-            target_ref[:, at] = value
-            first_sum = first_sum + value * weights[part][:, at].astype(BF16).astype(F32)
-        extra = first_result_ref[member, :, pl.ds(4 * WIDE, EXTRA)].astype(F32)
-        extra_ref[member] = extra
-        extra_sum = extra_sum + extra * beta_ref[member].astype(F32)
-    total = jnp.sum(first_sum, axis=1, keepdims=True) + jnp.sum(extra_sum, axis=1, keepdims=True)
-    sums_ref[...] = jnp.where(lane == 0, total, sums_ref[...])
-
-
-def finish(groups, whole_tiles, first_partial, first, rows_grad, output_partial, tokens, hidden, grad, gain, beta, feed_result, weights):
-    size, width = tokens.shape
-    length = rows_grad.shape[0]
-    rows = weights[0].shape[0]
-    dma = pltpu.SemaphoreType.DMA
-    out = [shape(F32, rows, width)] * 4 + [
-        shape(F32, GROUP, rows, EXTRA),
-        shape(F32, rows, BLOCK),
-        shape(BF16, size, width),
-        shape(BF16, size, width),
-    ]
+        ffn_gain_out[...] = jnp.sum(feed_sum, axis=1, keepdims=True) / gains_ref[:, 1:2]
+
+
+def layout(groups, lines, whole_tiles, first, feed, out, beta, gains, weights):
+    rows, width = out.shape
+    outs = [shape(F32, rows, width)] * 5 + [shape(F32, rows, 1)]
     if whole_tiles:
-        out = out + [shape(F32, *weights[4].shape)] * 2
+        outs = outs + [shape(F32, *weights[4].shape)] * 2 + [shape(F32, rows, 1)]
     return pl.pallas_call(
-        functools.partial(finish_kernel, groups, whole_tiles),
-        out_shape=out,
-        in_specs=anywhere(2) + in_vmem(8 + len(weights)),
-        out_specs=in_vmem(len(out)),
-        scratch_shapes=[
-            pltpu.VMEM((GROUP,) + first_partial.shape[3:], BF16),
-            pltpu.VMEM(first.shape, BF16),
-            pltpu.VMEM((length, width), BF16),
-            dma((1,)),
-        ]
-        + Scatter.scratch(groups, first_partial.shape)
-        + GroupSum.scratch(size, width)
-        + GroupSum.scratch(size, width),
-        **communicating(5, "finish"),
-    )(first_partial, first, rows_grad, output_partial, tokens, hidden, grad, gain, beta, feed_result, *weights)
+        functools.partial(layout_kernel, groups, lines),
+        out_shape=outs,
+        in_specs=in_vmem(5 + len(weights)),
+        out_specs=in_vmem(len(outs)),
+        compiler_params=pltpu.CompilerParams(vmem_limit_bytes=32 << 20),
+        name="layout",
+    )(first, feed, out, beta, gains, *weights)
 
 
 def on_device(
@@ -1759,42 +1771,40 @@
     feed_grads = jnp.concatenate([(active_grad * gate_slope).astype(BF16), (active_grad * up_slope).astype(BF16)], 1)
     down_partial = dot(active, cotangent_all, TN).astype(BF16).reshape(groups, 1, batch, hidden_rows, width)
     feed_partial = dot(normed_two, feed_grads, TN).astype(BF16).reshape(groups, GROUP, batch, rows, -1)
-    hidden_grad, down_weight_grad, rows_grad, feed_grad, out_weight_grad = back(
+    hidden_grad, down_weight_grad, rows_grad, feed_grad, out_lines = back(
         groups, hops, dot(feed_grads, feed, NT).astype(BF16), hidden, cotangent[0], gain_two, attended_low, out_full, query, value,
         within, maps, doc_query, doc_key, attended, stats, values, moved, projected, inverse, down_partial, feed_partial,
     )
-    output_partial = dot(active, down_full).astype(BF16)
     first_partial = dot(normed, rows_grad, TN).astype(BF16).reshape(groups, GROUP, batch, rows, -1)
     beta_parts = jnp.pad(columns(beta_weight), ((0, 0), (0, 0), (0, EXTRA - OWN)))
     weights = (query_weight, key_weight, value_weight, house_weight) + feed_weights
-    results = finish(
-        groups, whole_tiles, first_partial, first, rows_grad, output_partial, tokens[0], hidden, hidden_grad, gain_one, beta_parts, feed_grad,
-        weights,
+    first_grad, out_grad, tokens_grad, output = finish(
+        groups, first_partial, first, down_full, rows_grad, active, out_lines, tokens[0], hidden, hidden_grad, gain_one
     )
-    query_weight_grad, key_weight_grad, value_weight_grad, house_weight_grad, extra_grad, sums, tokens_grad, output = results[:8]
+    gains = jnp.stack([norm_gain, ffn_gain], 1).astype(BF16).astype(F32)
+    results = layout(groups, batch, whole_tiles, first_grad, feed_grad, out_grad, beta_parts, gains, weights)
+    query_weight_grad, key_weight_grad, value_weight_grad, house_weight_grad, out_weight_grad, norm_gain_grad = results[:6]
     output, tokens_grad = output[None], tokens_grad[None]
-    out_weight_grad = out_weight_grad.astype(F32)
     down_weight_grad = down_weight_grad[0]
-    beta_weight_grad = jnp.transpose(extra_grad[:, :, :OWN], (1, 0, 2)).reshape(rows, -1)
+    beta_weight_grad = jnp.transpose(first_grad[:, :, 4 * WIDE : 4 * WIDE + OWN].astype(F32), (1, 0, 2)).reshape(rows, -1)
 
     def unit_whole(parts):
         parts = parts.astype(F32).reshape(GROUP, rows, groups, batch, hidden_rows)
         return jnp.transpose(parts, (1, 2, 0, 3, 4)).reshape(rows, -1)
 
-    norm_gain_grad = sums[:, 0] / norm_gain.astype(BF16).astype(F32)
     if whole_tiles:
-        gate_weight_grad, up_weight_grad = results[8:]
-        feed_sum = sums[:, 1]
+        gate_weight_grad, up_weight_grad, ffn_gain_grad = results[6:]
+        ffn_gain_grad = ffn_gain_grad[:, 0]
     else:
         gate_weight_grad, up_weight_grad = unit_whole(feed_grad[:, :, :hidden_own]), unit_whole(feed_grad[:, :, hidden_own:])
         feed_sum = jnp.sum(gate_weight_grad * gate_weight.astype(BF16).astype(F32), axis=1) + jnp.sum(
             up_weight_grad * up_weight.astype(BF16).astype(F32), axis=1
         )
-    ffn_gain_grad = feed_sum / ffn_gain.astype(BF16).astype(F32)
+        ffn_gain_grad = feed_sum / gains[:, 1]
     return (
         output,
         tokens_grad,
-        norm_gain_grad,
+        norm_gain_grad[:, 0],
         query_weight_grad,
         key_weight_grad,
         value_weight_grad,

time: 538 us -> 503 us (0.935)
  Pallas kernels: 465 us -> 436 us
    pallas_call x1, Pallas kernels: 160 us -> 142 us  [back(): pl.pallas_call(functools.partial(back_kernel, groups, hops), out_shape=[s...]
    pallas_call x1, Pallas kernels: 62.8 us -> 48.4 us  [branch(): pl.pallas_call(functools.partial(branch_kernel, groups), out_shape=[shape...]
    dot_general x8 -> x7, matrix products: 36.6 us -> 33.9 us  [dot(): return lax.dot_general(left, right, dims, preferred_element_type=F32)]
    unnamed x76 -> x72, local copies, waits for them, and re-layouts: 11.3 us -> 8.74 us
    pallas_call x1 -> x2, Pallas kernels: 77.3 us -> 77.1 us  [the longest x1 75 us: finish(): pl.pallas_call(functools.partial(finish_kernel, groups), out_shape=[shape...]
where the time goes in v5:
time: 503 us; the launch traced here: 494 us
  Pallas kernels  436 us (87%)
  matrix products  33.9 us (7%)
  local copies, waits for them, and re-layouts  16.1 us (3%)
  other arithmetic  6.27 us (1%)
    pallas_call x1, Pallas kernels, back(): pl.pallas_call(functools.partial(back_kernel, groups, hops), out_shape=[s...  142 us
    pallas_call x1, Pallas kernels, attend(): pl.pallas_call(functools.partial(attend_kernel, groups, hops), out_shape=...  90.6 us
    pallas_call x1, Pallas kernels, gather_first(): pl.pallas_call(functools.partial(gather_kernel, groups), out_shape=[shape...  77.9 us
    pallas_call x1, Pallas kernels, finish(): pl.pallas_call(functools.partial(finish_kernel, groups), out_shape=[shape...  75 us
    pallas_call x1, Pallas kernels, branch(): pl.pallas_call(functools.partial(branch_kernel, groups), out_shape=[shape...  48.4 us
    dot_general x7, matrix products, dot(): return lax.dot_general(left, right, dims, preferred_element_type=F32)  33.9 us

profile of v5, /device:TPU:0, one launch (start us, length us, event | category | flops | bytes accessed | tf_op | source)
XLA Modules:
  0.0 493.7 jit_solution(2043166028508324460)
XLA Ops:
  0.7 1.0 convert_element_type.100
  1.8 1.1 convert_element_type.99
  2.9 1.0 convert_element_type.102
  4.0 0.7 bitcast_bitcast_fusion
  5.3 0.6 pad.13
  6.0 1.1 concatenate.10.first_ref
  7.1 1.1 copy-done.18
  8.3 1.0 copy-done.21
  9.2 77.9 %gather_first.1 = (bf16[4,4,2,48,1664]{4,3,2,1,0:T(8,128)(2,1)S(1)}, bf16[4,4,2,48,2048]{4,3,2,1,0:T(8,128)(2,1)S(1)}, bf16[1,4,2,48,1536]{4,3,2,1,0:T(8,128)(2,...) custom-call(bf16[4,48,1664]{2,1,0:T(8,128)(2,1)S(1)} %concatenate.10.first_ref, ...), custom_call_target="tpu_custom_call" | custom-call | tf_op jit(solution)/shard_map/gather_first/pallas_call | solution.py:1449
  88.1 5.7 %fusion.4.rows_ref.rows_hbm = f32[512,1664]{1,0:T(8,128)} fusion(bf16[1536,1664]{1,0:T(8,128)(2,1)S(1)} %bitcast.73, bf16[512,1536]{1,0:T(8,128)(2,1)S(1)} %get-tuple-element.55, f32[1536]{0:T(1024)S(1)} %get-tuple-element.98, f32[512]{0:T(512)S(1)} %add_rsqrt_fusion), kind=kOutput, calls=%fused_computation.15 | convolution fusion | flops 2620391424 | bytes 10100736 | tf_op jit(solution)/shard_map/dot_general | solution.py:30
  93.8 1.2 slice.26
  95.4 0.9 copy.79.doc_query_ref
  96.9 90.6 %attend.1 = (bf16[512,384]{1,0:T(8,128)(2,1)}, bf16[512,384]{1,0:T(8,128)(2,1)}, f32[512,384]{1,0:T(8,128)}, f32[512,384]{1,0:T(8,128)}, f32[512,384]{1,0:T(8,12...) custom-call(f32[512,1664]{1,0:T(8,128)} %fusion.4.rows_ref.rows_hbm,, ...), custom_call_target="tpu_custom_call", output_to_operand_aliasing={{10}: (3, {}), {11}: (4, {})} | custom-call | tf_op jit(solution)/shard_map/attend/pallas_call | solution.py:988
  187.4 2.4 convolution_convert_fusion.4.partial_ref
  189.9 48.4 %branch.1 = (f32[128,1536]{1,0:T(8,128)S(1)}, bf16[512,1536]{1,0:T(8,128)(2,1)S(1)}, bf16[512,1024]{1,0:T(8,128)(2,1)S(1)}, f32[512,1024]{1,0:T(8,128)}, f32[512...) custom-call(bf16[512,1536]{1,0:T(8,128)(2,1)S(1)} %convolution_convert_fusion.4.partial_ref, ...), custom_call_target="tpu_custom_call" | custom-call | tf_op jit(solution)/shard_map/branch/pallas_call | solution.py:1547
  238.3 5.7 %multiply_convert_fusion.1 = (bf16[512,1024]{1,0:T(8,128)(2,1)S(1)}, bf16[512,1024]{1,0:T(8,128)(2,1)S(1)}) fusion(f32[512,1024]{1,0:T(8,128)} %get-tuple-element.65, f32[512,1024]{1,0:T(8,128)} %get-tuple-element.66, bf16[512,1536]{1,0:T(8,128)(2,1)S(1)} %copy-done.10, bf16[1024,1536]{1,0:T(8,128)(2,1)} %bitcast.81), kind=kOutput, calls=%fused_computation.12 | convolution fusion | flops 1612709888 | bytes 11010048 | tf_op jit(solution)/shard_map/dot_general | solution.py:30
  244.0 4.7 convolution_convert_fusion.3.partial_ref
  248.7 3.5 convolution_convert_fusion.2
  252.3 5.5 %convolution_convert_fusion.1 = bf16[1536,2048]{1,0:T(8,128)(2,1)} fusion(bf16[512,1536]{1,0:T(8,128)(2,1)S(1)} %get-tuple-element.78, bf16[512,1024]{1,0:T(8,128)(2,1)S(1)} %get-tuple-element.100, bf16[512,1024]{1,0:T(8,128)(2,1)S(1)} %get-tuple-element.99), kind=kOutput, calls=%fused_computation.1 | convolution fusion | flops 3228565504 | bytes 9961472 | tf_op jit(solution)/shard_map/dot_general | solution.py:30
  257.8 141.8 %back.1 = (f32[128,1536]{1,0:T(8,128)}, f32[1,128,1536]{2,1,0:T(8,128)}, bf16[512,1664]{1,0:T(8,128)(2,1)}, bf16[4,48,2048]{2,1,0:T(8,128)(2,1)}, bf16[1,4,48,1536]{3,2,1,0:T(8,128)(2,1)}) custom-call(bf16[512,1536]{1,0:T(8,128)(2,1)} %convolution_convert_fusion.3.partial_ref, f32[128,1536]{1,0:T(8,128)} %copy-done.4, bf16[128,1536]{1,0:T(8,128)(2,1)} %bitcast.79, ...), custom_call_target="tpu_custom_call" | custom-call | tf_op jit(solution)/shard_map/back/pallas_call | solution.py:1353
  399.6 6.5 %convolution_convert_fusion = bf16[1536,1664]{1,0:T(8,128)(2,1)} fusion(bf16[512,1664]{1,0:T(8,128)(2,1)} %get-tuple-element.79.rows_grad_ref, bf16[512,1536]{1,0:T(8,128)(2,1)S(1)} %copy-done.8, f32[1536]{0:T(1024)S(1)} %get-tuple-element.98, f32[512]{0:T(512)S(1)} %add_rsqrt_fusion), kind=kOutput, calls=%fused_computation | convolution fusion | flops 2622947328 | bytes 8396800 | tf_op jit(solution)/shard_map/dot_general | solution.py:30
  406.7 75.0 %finish.1 = (bf16[4,48,1664]{2,1,0:T(8,128)(2,1)}, bf16[48,1536]{1,0:T(8,128)(2,1)}, bf16[128,1536]{1,0:T(8,128)(2,1)}, bf16[128,1536]{1,0:T(8,128)(2,1)}) custom-call(bf16[4,4,2,48,1664]{4,3,2,1,0:T(8,128)(2,1)} %bitcast.84, bf16[1536,1664]{1,0:T(8,128)(2,1)} %bitcast.75, bf16[1024,1536]{1,0:T(8,128)(2,1)} %bitcast.82, ...), custom_call_target="tpu_custom_call" | custom-call | tf_op jit(solution)/shard_map/finish/pallas_call | solution.py:1627
  482.0 1.1 copy-done.19
  483.1 1.1 copy-done.20
  484.2 0.9 copy-done.22
  485.1 2.0 layout.1
  487.1 0.6 reduce.3
  487.7 0.8 convert_bitcast_fusion
  489.3 0.6 reduce.4
  489.9 1.8 copy.100
  491.6 0.7 copy.101
  492.4 0.9 copy.102
  (94 shorter events, 4.2 us)
Async XLA Ops:
  0.6 3.3 copy-start.15
  0.7 4.0 copy-start.28
  0.7 4.2 copy-start.31
  0.7 4.3 copy-start.29
  0.7 4.3 copy-start.30
  1.7 5.4 %copy-start.3 = (bf16[1,128,1536]{2,1,0:T(8,128)(2,1)S(1)}, bf16[1,128,1536]{2,1,0:T(8,128)(2,1)}, u32[]{:S(2)}) copy-start(bf16[1,128,1536]{2,1,0:T(8,128)(2,1)} %param.14) | copy-start | bytes 1179652
  1.7 5.4 %copy-start.5 = (f32[48,4096]{1,0:T(8,128)S(1)}, f32[48,4096]{1,0:T(8,128)}, u32[]{:S(2)}) copy-start(f32[48,4096]{1,0:T(8,128)} %refs_4_.1) | copy-start | bytes 2359300
  1.7 5.4 %copy-start.6 = (f32[48,4096]{1,0:T(8,128)S(1)}, f32[48,4096]{1,0:T(8,128)}, u32[]{:S(2)}) copy-start(f32[48,4096]{1,0:T(8,128)} %refs_5_.1) | copy-start | bytes 2359300
  1.8 5.4 %copy-start.11 = (bf16[1,128,1536]{2,1,0:T(8,128)(2,1)S(1)}, bf16[1,128,1536]{2,1,0:T(8,128)(2,1)}, u32[]{:S(2)}) copy-start(bf16[1,128,1536]{2,1,0:T(8,128)(2,1)} %param.27) | copy-start | bytes 1179652
  4.8 2.3 copy-start.25
  7.1 1.1 copy-start.18
  87.1 6.6 %copy-start = (bf16[4,4,2,48,2048]{4,3,2,1,0:T(8,128)(2,1)}, bf16[4,4,2,48,2048]{4,3,2,1,0:T(8,128)(2,1)S(1)}, u32[]{:S(2)}) copy-start(bf16[4,4,2,48,2048]{4,3,2,1,0:T(8,128)(2,1)S(1)} %get-tuple-element.59.feed_unit_ref) | copy-start | bytes 18874372
  87.1 6.6 %copy-start.1 = (bf16[1,4,2,48,1536]{4,3,2,1,0:T(8,128)(2,1)}, bf16[1,4,2,48,1536]{4,3,2,1,0:T(8,128)(2,1)S(1)}, u32[]{:S(2)}) copy-start(bf16[1,4,2,48,1536]{4,3,2,1,0:T(8,128)(2,1)S(1)} %get-tuple-element.58.out_home_ref) | copy-start | bytes 3538948
  87.1 6.6 %copy-start.2 = (bf16[4,4,2,48,1664]{4,3,2,1,0:T(8,128)(2,1)}, bf16[4,4,2,48,1664]{4,3,2,1,0:T(8,128)(2,1)S(1)}, u32[]{:S(2)}) copy-start(bf16[4,4,2,48,1664]{4,3,2,1,0:T(8,128)(2,1)S(1)} %get-tuple-element.56) | copy-start | bytes 15335428
  87.1 6.6 %copy-start.7 = (bf16[512,1536]{1,0:T(8,128)(2,1)}, bf16[512,1536]{1,0:T(8,128)(2,1)S(1)}, u32[]{:S(2)}) copy-start(bf16[512,1536]{1,0:T(8,128)(2,1)S(1)} %get-tuple-element.55) | copy-start | bytes 4718596
  87.2 6.6 %copy-start.9 = (bf16[512,1536]{1,0:T(8,128)(2,1)}, bf16[512,1536]{1,0:T(8,128)(2,1)S(1)}, u32[]{:S(2)}) copy-start(bf16[512,1536]{1,0:T(8,128)(2,1)S(1)} %get-tuple-element.57) | copy-start | bytes 4718596
  189.8 48.5 %copy-start.23 = (f32[1,1536]{1,0:T(1,128)}, f32[1,1536]{1,0:T(1,128)S(1)}, u32[]{:S(2)}) copy-start(f32[1,1536]{1,0:T(1,128)S(1)} %reshape.146.gain_ref) | copy-start | bytes 18436
  189.8 48.5 %copy-start.10 = (bf16[512,1536]{1,0:T(8,128)(2,1)S(1)}, bf16[512,1536]{1,0:T(8,128)(2,1)}, u32[]{:S(2)}) copy-start(bf16[512,1536]{1,0:T(8,128)(2,1)} %copy-done.9) | copy-start | bytes 4718596
  189.9 54.2 %slice-start = ((s8[6291456]{0:T(1024)(128)(4,1)}), s8[2097152]{0:T(1024)(128)(4,1)S(1)}, s32[]{:S(2)}) async-start(s8[6291456]{0:T(1024)(128)(4,1)} %bitcast.67), calls=%async_computation | async-start | bytes 4194304
  238.3 5.7 %copy-start.4 = (f32[128,1536]{1,0:T(8,128)}, f32[128,1536]{1,0:T(8,128)S(1)}, u32[]{:S(2)}) copy-start(f32[128,1536]{1,0:T(8,128)S(1)} %get-tuple-element.67.hidden_ref) | copy-start | bytes 2359300
  238.3 10.4 %copy-start.17 = (bf16[512,1024]{1,0:T(8,128)(2,1)}, bf16[512,1024]{1,0:T(8,128)(2,1)S(1)}, u32[]{:S(2)}) copy-start(bf16[512,1024]{1,0:T(8,128)(2,1)S(1)} %get-tuple-element.77.active_ref) | copy-start | bytes 3145732
  238.3 5.7 %slice-start.1 = ((s8[6291456]{0:T(1024)(128)(4,1)}), s8[4194304]{0:T(1024)(128)(4,1)S(1)}, s32[]{:S(2)}) async-start(s8[6291456]{0:T(1024)(128)(4,1)} %bitcast.67), calls=%async_computation.1 | async-start | bytes 8388608
  257.8 141.8 %copy-start.8 = (bf16[512,1536]{1,0:T(8,128)(2,1)S(1)}, bf16[512,1536]{1,0:T(8,128)(2,1)}, u32[]{:S(2)}) copy-start(bf16[512,1536]{1,0:T(8,128)(2,1)} %copy-done.7) | copy-start | bytes 4718596
  406.7 75.1 %copy-start.26 = (bf16[48,4,3]{2,0,1:T(8,128)(2,1)S(1)}, bf16[48,4,3]{2,0,1:T(8,128)(2,1)}, u32[]{:S(2)}) copy-start(bf16[48,4,3]{2,0,1:T(8,128)(2,1)} %copy-done.25) | copy-start | bytes 3460
  406.7 75.2 %copy-start.12 = (f32[48,1536]{1,0:T(8,128)S(1)}, f32[48,1536]{1,0:T(8,128)}, u32[]{:S(2)}) copy-start(f32[48,1536]{1,0:T(8,128)} %refs_1_.1) | copy-start | bytes 884740
  406.7 75.2 %copy-start.13 = (f32[48,1536]{1,0:T(8,128)S(1)}, f32[48,1536]{1,0:T(8,128)}, u32[]{:S(2)}) copy-start(f32[48,1536]{1,0:T(8,128)} %refs_0_.1) | copy-start | bytes 884740
  406.7 75.2 %copy-start.14 = (f32[48,1536]{1,0:T(8,128)S(1)}, f32[48,1536]{1,0:T(8,128)}, u32[]{:S(2)}) copy-start(f32[48,1536]{1,0:T(8,128)} %refs_3_.1) | copy-start | bytes 884740
  406.7 75.2 %copy-start.16 = (f32[48,1536]{1,0:T(8,128)S(1)}, f32[48,1536]{1,0:T(8,128)}, u32[]{:S(2)}) copy-start(f32[48,1536]{1,0:T(8,128)} %refs_2_.1) | copy-start | bytes 884740
  482.0 1.1 copy-start.19
  483.1 1.1 copy-start.20
  485.1 6.6 %copy-start.27 = (bf16[128,1536]{1,0:T(8,128)(2,1)S(1)}, bf16[128,1536]{1,0:T(8,128)(2,1)}, u32[]{:S(2)}) copy-start(bf16[128,1536]{1,0:T(8,128)(2,1)} %get-tuple-element.83) | copy-start | bytes 1179652
  487.1 5.3 %copy-start.24 = (f32[1,128,1536]{2,1,0:T(8,128)S(1)}, f32[1,128,1536]{2,1,0:T(8,128)}, u32[]{:S(2)}) copy-start(f32[1,128,1536]{2,1,0:T(8,128)} %get-tuple-element.96) | copy-start | bytes 2359300
  (2 other events, 1.9 us)

commit v6 on v5

--- a/solution.py
+++ b/solution.py
@@ -408,8 +408,8 @@
 
 
 class Scatter:
-    def __init__(self, place, partial, result, refs):
-        self.place, self.partial, self.result = place, partial, result
+    def __init__(self, place, partial, result, refs, make=None):
+        self.place, self.partial, self.result, self.make = place, partial, result, make
         (self.land, self.chain_land, self.leave, self.mine_sem, self.line_send, self.line_recv, self.chain_send,
          self.chain_recv, self.part_send, self.part_recv) = refs
         self.parts = partial.shape[1]
@@ -470,6 +470,8 @@
         pl.when(wave >= p.groups - p.g)(lambda: act_down(wave - p.groups + p.g))
 
     def act(self, target):
+        if self.make is not None:
+            self.make(target)
         self.line(target).start()
         self.load(target).start()
 
@@ -479,8 +481,16 @@
 
     def start_far(self, first=1, last=None):
         p = self.place
-        for wave in range(first, p.groups if last is None else last + 1):
-            self.wave(wave, self.act, self.act)
+        if self.make is None:
+            for wave in range(first, p.groups if last is None else last + 1):
+                self.wave(wave, self.act, self.act)
+        else:
+
+            def one(wave, carry):
+                self.wave(wave, self.act, self.act)
+                return carry
+
+            lax.fori_loop(1, p.groups, one, 0)
         if first > 1:
             return
 
@@ -1393,17 +1403,31 @@
 
 
 def gather_kernel(
-    groups, first_ref, gate_ref, up_ref, out_ref, down_ref, tokens_ref, cotangent_ref, full_ref, feed_full_ref, out_full_ref,
-    down_low_ref, tokens_all_ref, cotangent_all_ref, feed_parts_ref, out_low_ref, send, recv, local, *sems
+    groups, query_ref, key_ref, value_ref, house_ref, extra_ref, gate_hbm, up_hbm, out_hbm, down_hbm, tokens_ref, cotangent_ref,
+    full_ref, feed_full_ref, out_full_ref, down_low_ref, tokens_all_ref, cotangent_all_ref, first_ref, feed_parts_ref, out_low_ref,
+    gate_ref, up_ref, out_ref, down_ref, load_sem, send, recv, local, *sems
 ):
     lines = full_ref.shape[2]
     here = Place(groups, lines)
+    loads = [
+        pltpu.make_async_copy(source, target, load_sem.at[index])
+        for index, (source, target) in enumerate(
+            ((out_hbm, out_ref), (gate_hbm, gate_ref), (up_hbm, up_ref), (down_hbm, down_ref))
+        )
+    ]
+    for copy in loads:
+        copy.start()
+    for member in range(GROUP):
+        for part, weight_ref in enumerate((query_ref, key_ref, value_ref, house_ref)):
+            first_ref[member, :, pl.ds(part * WIDE, WIDE)] = weight_ref[:, pl.ds(member * WIDE, WIDE)].astype(BF16)
+        first_ref[member, :, pl.ds(4 * WIDE, EXTRA)] = extra_ref[member]
     here.meet()
     first_sems, feed_sems, out_sems = several(sems, 8, 3, 5)
     first = Gather(here, first_ref, full_ref, first_sems)
     feed = Gather(here, feed_parts_ref, feed_full_ref, feed_sems)
     out = HomeGather(here, out_low_ref, out_full_ref, out_sems)
     first.start()
+    loads[0].wait()
     out_low_ref[...] = out_ref[...].astype(BF16)
     out.start()
     size = tokens_ref.shape[0]
@@ -1417,6 +1441,8 @@
             )
     for copy in copies:
         copy.start()
+    for copy in loads[1:]:
+        copy.wait()
     down_low_ref[...] = down_ref[...].astype(BF16)
     own_units = feed_parts_ref.shape[2] // 2
     for at, weight_ref in ((0, gate_ref), (own_units, up_ref)):
@@ -1441,7 +1467,7 @@
     first.finish()
 
 
-def gather_first(groups, lines, first, gate, up, out, down, tokens, cotangent):
+def gather_first(groups, lines, first, extra, gate, up, out, down, tokens, cotangent):
     dma = pltpu.SemaphoreType.DMA
     size, width = tokens.shape
     rows = out.shape[0]
@@ -1449,18 +1475,24 @@
     return pl.pallas_call(
         functools.partial(gather_kernel, groups),
         out_shape=[
-            shape(BF16, groups, GROUP, lines, *first.shape[1:]),
+            shape(BF16, groups, GROUP, lines, rows, 4 * WIDE + EXTRA),
             shape(BF16, groups, GROUP, lines, rows, units),
             shape(BF16, groups // GROUP, GROUP, lines, rows, width),
             shape(BF16, *down.shape),
             shape(BF16, GROUP * size, width),
             shape(BF16, GROUP * size, width),
         ],
-        in_specs=anywhere(1) + in_vmem(4) + anywhere(2),
+        in_specs=in_vmem(5) + anywhere(6),
         out_specs=anywhere(3) + in_vmem(1) + anywhere(2),
         scratch_shapes=[
+            pltpu.VMEM((GROUP, rows, 4 * WIDE + EXTRA), BF16),
             pltpu.VMEM((GROUP, rows, units), BF16),
             pltpu.VMEM((rows, width), BF16),
+            pltpu.VMEM(gate.shape, gate.dtype),
+            pltpu.VMEM(up.shape, up.dtype),
+            pltpu.VMEM(out.shape, F32),
+            pltpu.VMEM(down.shape, F32),
+            dma((4,)),
             dma((2, GROUP)),
             dma((2, GROUP)),
             dma((2,)),
@@ -1469,8 +1501,8 @@
         + Gather.outside(groups)
         + Gather.inside()
         + HomeGather.scratch(groups),
-        **communicating(0, "gather_first", 24),
-    )(first, gate, up, out, down, tokens, cotangent)
+        **communicating(0, "gather_first", 60),
+    )(*first, extra, gate, up, out, down, tokens, cotangent)
 
 
 def rms_norm(values, gain):
@@ -1566,25 +1598,44 @@
 
 
 def finish_kernel(
-    groups, first_partial_ref, first_hbm, down_hbm, rows_grad_ref, active_ref, out_lines_ref, tokens_ref, hidden_ref, grad_ref, gain_ref,
+    groups, first_partial_ref, wide_hbm, first_hbm, down_hbm, rows_grad_ref, active_ref, out_lines_ref, tokens_ref, hidden_ref, grad_ref, gain_ref,
     first_result_ref, out_result_ref, tokens_grad_ref, output_ref, first_full_ref, down_full_ref, normed_partial_ref,
-    output_partial_ref, load_sem, *refs
+    output_partial_ref, wide_ref, normed_ref, made_ref, load_sem, *refs
 ):
-    here = Place(groups, first_partial_ref.shape[2])
+    lines, rows = first_partial_ref.shape[2:4]
+    here = Place(groups, lines)
+    made = rows % 16 == 0
+    if made:
+        first_partial_ref = made_ref
+    wide_copy = pltpu.make_async_copy(wide_hbm, wide_ref, load_sem.at[2])
+    wide_copy.start()
     here.meet(column=True)
+
+    def make(target):
+        span = GROUP * lines * rows
+        left = normed_ref[:, pl.ds(pl.multiple_of(target * span, BLOCK), span)].T
+        for at, size in [(part * WIDE, WIDE) for part in range(4)] + [(4 * WIDE, EXTRA)]:
+            value = dot(left, rows_grad_ref[:, pl.ds(at, size)])
+            for index in range(GROUP * lines):
+                made_ref[target, index // lines, index % lines, :, pl.ds(at, size)] = value[index * rows : (index + 1) * rows].astype(BF16)
+
     first_refs, out_refs, normed_refs, output_refs = several(
         refs, len(Scatter.scratch(groups, first_partial_ref.shape)), len(HomeScatter.scratch(groups, out_lines_ref.shape)), 7, 7
     )
-    first = Scatter(here, first_partial_ref, first_result_ref, first_refs)
+    first = Scatter(here, first_partial_ref, first_result_ref, first_refs, make if made else None)
     out = HomeScatter(here, out_lines_ref, out_result_ref, out_refs)
     normed = GroupSum(here, normed_partial_ref, normed_refs)
     output = GroupSum(here, output_partial_ref, output_refs)
-    first.start()
     first_copy = pltpu.make_async_copy(first_hbm, first_full_ref, load_sem.at[0])
     down_copy = pltpu.make_async_copy(down_hbm, down_full_ref, load_sem.at[1])
     first_copy.start()
     down_copy.start()
+    wide_copy.wait()
     out.start()
+    if made:
+        for block in range(GROUP):
+            normed_ref[tile(block), :] = rms_norm(wide_ref[tile(block), :].astype(F32), gain_ref[...]).astype(BF16)
+    first.start()
     first_copy.wait()
 
     def normed_tile(at):
@@ -1621,9 +1672,10 @@
     first.finish()
 
 
-def finish(groups, first_partial, first, down, rows_grad, active, out_lines, tokens, hidden, grad, gain):
+def finish(groups, first_partial, wide, first, down, rows_grad, active, out_lines, tokens, hidden, grad, gain):
     size, width = tokens.shape
     length = rows_grad.shape[0]
+    made = first_partial.shape if first_partial.shape[3] % 16 == 0 else (1, 1, 1, 16, BLOCK)
     return pl.pallas_call(
         functools.partial(finish_kernel, groups),
         out_shape=[
@@ -1632,27 +1684,37 @@
             shape(BF16, size, width),
             shape(BF16, size, width),
         ],
-        in_specs=anywhere(3) + in_vmem(7),
+        in_specs=anywhere(4) + in_vmem(7),
         out_specs=in_vmem(4),
         scratch_shapes=[
             pltpu.VMEM(first.shape, BF16),
             pltpu.VMEM(down.shape, BF16),
             pltpu.VMEM((length, width), BF16),
             pltpu.VMEM((length, width), BF16),
-            pltpu.SemaphoreType.DMA((2,)),
+            pltpu.VMEM(wide.shape, BF16),
+            pltpu.VMEM(wide.shape, BF16),
+            pltpu.VMEM(made, BF16),
+            pltpu.SemaphoreType.DMA((3,)),
         ]
         + Scatter.scratch(groups, first_partial.shape)
         + HomeScatter.scratch(groups, out_lines.shape)
         + GroupSum.scratch(size, width)
         + GroupSum.scratch(size, width),
         **communicating(5, "finish"),
-    )(first_partial, first, down, rows_grad, active, out_lines, tokens, hidden, grad, gain)
-
-
-def layout_kernel(groups, lines, first_ref, feed_ref, out_ref, beta_ref, gains_ref, *refs):
+    )(first_partial, wide, first, down, rows_grad, active, out_lines, tokens, hidden, grad, gain)
+
+
+def layout_kernel(groups, lines, first_ref, feed_ref, out_ref, beta_ref, gains_ref, down_ref, tokens_ref, result_ref, *refs):
     weights, targets = refs[:6], refs[6:]
-    query_out, key_out, value_out, house_out, out_out, norm_gain_out = targets[:6]
-    rows = gains_ref.shape[0]
+    query_out, key_out, value_out, house_out, out_out, down_out, tokens_out, result_out, norm_gain_out, beta_out = targets[:10]
+    rows = gains_ref.shape[1]
+    down_out[...] = down_ref[0]
+    tokens_out[...] = tokens_ref[...]
+    result_out[...] = result_ref[...]
+
+    def as_row(column):
+        return jnp.broadcast_to(column, (rows, BLOCK)).T[0:1, :]
+
     first_sum = jnp.zeros((rows, WIDE), F32)
     extra_sum = jnp.zeros((rows, EXTRA), F32)
     for member in range(GROUP):
@@ -1661,12 +1723,14 @@
             at = pl.ds(member * WIDE, WIDE)
             target_ref[:, at] = value
             first_sum = first_sum + value * weights[part][:, at].astype(BF16).astype(F32)
-        extra_sum = extra_sum + first_ref[member, :, pl.ds(4 * WIDE, EXTRA)].astype(F32) * beta_ref[member].astype(F32)
+        extra = first_ref[member, :, pl.ds(4 * WIDE, EXTRA)].astype(F32)
+        extra_sum = extra_sum + extra * beta_ref[member].astype(F32)
+        beta_out[member] = extra.T[0:OWN, :]
     total = jnp.sum(first_sum, axis=1, keepdims=True) + jnp.sum(extra_sum, axis=1, keepdims=True)
-    norm_gain_out[...] = total / gains_ref[:, 0:1]
+    norm_gain_out[...] = as_row(total) / gains_ref[0:1, :]
     out_out[...] = out_ref[...].astype(F32)
-    if len(targets) > 6:
-        gate_out, up_out, ffn_gain_out = targets[6:]
+    if len(targets) > 10:
+        gate_out, up_out, ffn_gain_out = targets[10:]
         units = feed_ref.shape[2] // 2
         feed_sum = jnp.zeros((rows, BLOCK), F32)
         for at, weight_ref, target_ref in ((0, weights[4], gate_out), (units, weights[5], up_out)):
@@ -1676,22 +1740,28 @@
                     value = feed_ref[member, :, pl.ds(at + index * BLOCK, BLOCK)].astype(F32)
                     target_ref[:, tile(block)] = value
                     feed_sum = feed_sum + value * weight_ref[:, tile(block)].astype(BF16).astype(F32)
-        ffn_gain_out[...] = jnp.sum(feed_sum, axis=1, keepdims=True) / gains_ref[:, 1:2]
-
-
-def layout(groups, lines, whole_tiles, first, feed, out, beta, gains, weights):
+        ffn_gain_out[...] = as_row(jnp.sum(feed_sum, axis=1, keepdims=True)) / gains_ref[1:2, :]
+
+
+def layout(groups, lines, whole_tiles, first, feed, out, beta, gains, down, tokens, result, weights):
     rows, width = out.shape
-    outs = [shape(F32, rows, width)] * 5 + [shape(F32, rows, 1)]
+    outs = [shape(F32, rows, width)] * 5 + [
+        shape(F32, *down.shape[1:]),
+        shape(BF16, *tokens.shape),
+        shape(BF16, *tokens.shape),
+        shape(F32, 1, rows),
+        shape(F32, GROUP, OWN, rows),
+    ]
     if whole_tiles:
-        outs = outs + [shape(F32, *weights[4].shape)] * 2 + [shape(F32, rows, 1)]
+        outs = outs + [shape(F32, *weights[4].shape)] * 2 + [shape(F32, 1, rows)]
     return pl.pallas_call(
         functools.partial(layout_kernel, groups, lines),
         out_shape=outs,
-        in_specs=in_vmem(5 + len(weights)),
+        in_specs=in_vmem(8 + len(weights)),
         out_specs=in_vmem(len(outs)),
-        compiler_params=pltpu.CompilerParams(vmem_limit_bytes=32 << 20),
+        compiler_params=pltpu.CompilerParams(vmem_limit_bytes=60 << 20),
         name="layout",
-    )(first, feed, out, beta, gains, *weights)
+    )(first, feed, out, beta, gains, down, tokens, result, *weights)
 
 
 def on_device(
@@ -1727,9 +1797,7 @@
     same = jnp.concatenate([norm_gain.astype(BF16)[:, None], ffn_gain.astype(BF16)[:, None], docs], 1)
     same = jnp.broadcast_to(same[None], (GROUP,) + same.shape)
     same = jnp.pad(same, ((0, 0), (0, 0), (0, EXTRA - OWN - same.shape[2])))
-    first_parts = jnp.concatenate(
-        [columns(w) for w in (query_weight, key_weight, value_weight, house_weight, beta_weight)] + [same], 2
-    )
+    extra = jnp.concatenate([columns(beta_weight), same], 2)
 
     def unit_columns(weight):
         parts = weight.astype(BF16).reshape(rows, groups, GROUP, batch, hidden_rows)
@@ -1738,7 +1806,7 @@
     whole_tiles = hidden_rows == BLOCK
     feed_weights = (gate_weight, up_weight) if whole_tiles else (unit_columns(gate_weight), unit_columns(up_weight))
     first, feed, out_full, down_low, tokens_all, cotangent_all = gather_first(
-        groups, batch, first_parts, *feed_weights, out_weight, down_weight, tokens[0], cotangent[0]
+        groups, batch, (query_weight, key_weight, value_weight, house_weight), extra, *feed_weights, out_weight, down_weight, tokens[0], cotangent[0]
     )
     first = first.reshape(width, -1)
 
@@ -1775,36 +1843,41 @@
         groups, hops, dot(feed_grads, feed, NT).astype(BF16), hidden, cotangent[0], gain_two, attended_low, out_full, query, value,
         within, maps, doc_query, doc_key, attended, stats, values, moved, projected, inverse, down_partial, feed_partial,
     )
-    first_partial = dot(normed, rows_grad, TN).astype(BF16).reshape(groups, GROUP, batch, rows, -1)
+    partial_shape = (groups, GROUP, batch, rows, rows_grad.shape[1])
+    if rows % 16 == 0:
+        first_partial = first.reshape(partial_shape)
+    else:
+        first_partial = dot(normed, rows_grad, TN).astype(BF16).reshape(partial_shape)
     beta_parts = jnp.pad(columns(beta_weight), ((0, 0), (0, 0), (0, EXTRA - OWN)))
     weights = (query_weight, key_weight, value_weight, house_weight) + feed_weights
     first_grad, out_grad, tokens_grad, output = finish(
-        groups, first_partial, first, down_full, rows_grad, active, out_lines, tokens[0], hidden, hidden_grad, gain_one
+        groups, first_partial, tokens_all, first, down_full, rows_grad, active, out_lines, tokens[0], hidden, hidden_grad, gain_one
     )
-    gains = jnp.stack([norm_gain, ffn_gain], 1).astype(BF16).astype(F32)
-    results = layout(groups, batch, whole_tiles, first_grad, feed_grad, out_grad, beta_parts, gains, weights)
-    query_weight_grad, key_weight_grad, value_weight_grad, house_weight_grad, out_weight_grad, norm_gain_grad = results[:6]
+    gains = jnp.stack([norm_gain, ffn_gain]).astype(BF16).astype(F32)
+    results = layout(
+        groups, batch, whole_tiles, first_grad, feed_grad, out_grad, beta_parts, gains, down_weight_grad, tokens_grad, output, weights
+    )
+    query_weight_grad, key_weight_grad, value_weight_grad, house_weight_grad, out_weight_grad, down_weight_grad = results[:6]
+    tokens_grad, output, norm_gain_grad, beta_weight_grad = results[6:10]
     output, tokens_grad = output[None], tokens_grad[None]
-    down_weight_grad = down_weight_grad[0]
-    beta_weight_grad = jnp.transpose(first_grad[:, :, 4 * WIDE : 4 * WIDE + OWN].astype(F32), (1, 0, 2)).reshape(rows, -1)
-
+    beta_weight_grad = beta_weight_grad.reshape(-1, rows).T
     def unit_whole(parts):
         parts = parts.astype(F32).reshape(GROUP, rows, groups, batch, hidden_rows)
         return jnp.transpose(parts, (1, 2, 0, 3, 4)).reshape(rows, -1)
 
     if whole_tiles:
-        gate_weight_grad, up_weight_grad, ffn_gain_grad = results[6:]
-        ffn_gain_grad = ffn_gain_grad[:, 0]
+        gate_weight_grad, up_weight_grad, ffn_gain_grad = results[10:]
+        ffn_gain_grad = ffn_gain_grad[0]
     else:
         gate_weight_grad, up_weight_grad = unit_whole(feed_grad[:, :, :hidden_own]), unit_whole(feed_grad[:, :, hidden_own:])
         feed_sum = jnp.sum(gate_weight_grad * gate_weight.astype(BF16).astype(F32), axis=1) + jnp.sum(
             up_weight_grad * up_weight.astype(BF16).astype(F32), axis=1
         )
-        ffn_gain_grad = feed_sum / gains[:, 1]
+        ffn_gain_grad = feed_sum / gains[1]
     return (
         output,
         tokens_grad,
-        norm_gain_grad[:, 0],
+        norm_gain_grad[0],
         query_weight_grad,
         key_weight_grad,
         value_weight_grad,

time: 503 us -> 494 us (0.982)
  local copies, waits for them, and re-layouts: 16.1 us -> 5.43 us
  Pallas kernels: 436 us -> 443 us
    unnamed x72 -> x19, local copies, waits for them, and re-layouts: 8.74 us -> 0.05 us
    dot_general x7 -> x6, matrix products: 33.9 us -> 29.1 us  [dot(): return lax.dot_general(left, right, dims, preferred_element_type=F32)]
where the time goes in v6:
time: 494 us; the launch traced here: 486 us
  Pallas kernels  443 us (90%)
  matrix products  29.1 us (6%)
  other arithmetic  7.25 us (1%)
  local copies, waits for them, and re-layouts  5.43 us (1%)
    pallas_call x1, Pallas kernels, back(): pl.pallas_call(functools.partial(back_kernel, groups, hops), out_shape=[s...  142 us
    pallas_call x1, Pallas kernels, attend(): pl.pallas_call(functools.partial(attend_kernel, groups, hops), out_shape=...  90.3 us
    pallas_call x1, Pallas kernels, gather_first(): pl.pallas_call(functools.partial(gather_kernel, groups), out_shape=[shape...  81 us
    pallas_call x1, Pallas kernels, finish(): pl.pallas_call(functools.partial(finish_kernel, groups), out_shape=[shape...  76.9 us
    pallas_call x1, Pallas kernels, branch(): pl.pallas_call(functools.partial(branch_kernel, groups), out_shape=[shape...  48.3 us
    dot_general x6, matrix products, dot(): return lax.dot_general(left, right, dims, preferred_element_type=F32)  29.1 us

profile of v6, /device:TPU:0, one launch (start us, length us, event | category | flops | bytes accessed | tf_op | source)
XLA Modules:
  0.0 486.4 jit_solution(11654321150486308048)
XLA Ops:
  0.7 0.7 convert_bitcast_fusion
  1.3 0.7 convert_bitcast_fusion.1
  2.0 0.6 maximum_convert_fusion.gains_ref
  2.6 0.7 convert_element_type.83
  3.3 0.1 reshape.107
  3.4 0.1 copy.46
  3.5 0.1 copy.45
  3.6 0.1 pad_maximum_fusion.3
  3.7 0.1 copy.44
  3.9 0.7 fusion.11
  4.6 81.0 %gather_first.1 = (bf16[4,4,2,48,1664]{4,3,2,1,0:T(8,128)(2,1)}, bf16[4,4,2,48,2048]{4,3,2,1,0:T(8,128)(2,1)}, bf16[1,4,2,48,1536]{4,3,2,1,0:T(8,128)(2,1)}, bf1...) custom-call(f32[48,1536]{1,0:T(8,128)} %refs_0_.1, f32[48,1536]{1,0:T(8,128)} %refs_1_.1, ...), custom_call_target="tpu_custom_call" | custom-call | tf_op jit(solution)/shard_map/gather_first/pallas_call | solution.py:1475
  85.6 1.9 fusion
  87.5 1.9 convert_reduce_fusion
  89.4 0.6 reshape.123.gain_ref
  90.0 1.2 slice.22
  91.2 0.3 reshape.109
  91.6 0.6 broadcast_in_dim.38.doc_key_ref
  92.2 0.9 copy.48.doc_query_ref
  93.1 7.3 %fusion.3.rows_ref.rows_hbm = f32[512,1664]{1,0:T(8,128)} fusion(bf16[1536,1664]{1,0:T(8,128)(2,1)} %bitcast.51, bf16[512,1536]{1,0:T(8,128)(2,1)S(1)} %copy-done.5, f32[1536]{0:T(1024)S(1)} %get-tuple-element.106, f32[512]{0:T(512)S(1)} %add_rsqrt_fusion), kind=kOutput, calls=%fused_computation.12 | convolution fusion | flops 2620391424 | bytes 10100736 | tf_op jit(solution)/shard_map/dot_general | solution.py:30
  100.4 90.3 %attend.1 = (bf16[512,384]{1,0:T(8,128)(2,1)}, bf16[512,384]{1,0:T(8,128)(2,1)}, f32[512,384]{1,0:T(8,128)}, f32[512,384]{1,0:T(8,128)}, f32[512,384]{1,0:T(8,12...) custom-call(f32[512,1664]{1,0:T(8,128)} %fusion.3.rows_ref.rows_hbm,, ...), custom_call_target="tpu_custom_call", output_to_operand_aliasing={{10}: (3, {}), {11}: (4, {})} | custom-call | tf_op jit(solution)/shard_map/attend/pallas_call | solution.py:998
  190.7 0.0 copy-start
  190.7 2.4 convolution_convert_fusion.3.partial_ref
  193.2 48.3 %branch.1 = (f32[128,1536]{1,0:T(8,128)S(1)}, bf16[512,1536]{1,0:T(8,128)(2,1)S(1)}, bf16[512,1024]{1,0:T(8,128)(2,1)S(1)}, f32[512,1024]{1,0:T(8,128)}, f32[512...) custom-call(bf16[512,1536]{1,0:T(8,128)(2,1)S(1)} %convolution_convert_fusion.3.partial_ref, ...), custom_call_target="tpu_custom_call" | custom-call | tf_op jit(solution)/shard_map/branch/pallas_call | solution.py:1579
  241.5 0.0 copy-start.1
  241.6 5.7 %multiply_convert_fusion.1 = (bf16[512,1024]{1,0:T(8,128)(2,1)S(1)}, bf16[512,1024]{1,0:T(8,128)(2,1)S(1)}) fusion(f32[512,1024]{1,0:T(8,128)} %get-tuple-element.69, f32[512,1024]{1,0:T(8,128)} %get-tuple-element.70, bf16[512,1536]{1,0:T(8,128)(2,1)S(1)} %copy-done.6, bf16[1024,1536]{1,0:T(8,128)(2,1)} %bitcast.57), kind=kOutput, calls=%fused_computation.11 | convolution fusion | flops 1612709888 | bytes 11010048 | tf_op jit(solution)/shard_map/dot_general | solution.py:30
  247.3 4.6 convolution_convert_fusion.2.partial_ref
  251.9 3.5 convolution_convert_fusion.1
  255.5 5.5 %convolution_convert_fusion = bf16[1536,2048]{1,0:T(8,128)(2,1)} fusion(bf16[512,1536]{1,0:T(8,128)(2,1)S(1)} %get-tuple-element.82, bf16[512,1024]{1,0:T(8,128)(2,1)S(1)} %get-tuple-element.108, bf16[512,1024]{1,0:T(8,128)(2,1)S(1)} %get-tuple-element.107), kind=kOutput, calls=%fused_computation | convolution fusion | flops 3228565504 | bytes 9961472 | tf_op jit(solution)/shard_map/dot_general | solution.py:30
  261.0 141.7 %back.1 = (f32[128,1536]{1,0:T(8,128)}, f32[1,128,1536]{2,1,0:T(8,128)}, bf16[512,1664]{1,0:T(8,128)(2,1)}, bf16[4,48,2048]{2,1,0:T(8,128)(2,1)}, bf16[1,4,48,1536]{3,2,1,0:T(8,128)(2,1)}) custom-call(bf16[512,1536]{1,0:T(8,128)(2,1)} %convolution_convert_fusion.2.partial_ref, f32[128,1536]{1,0:T(8,128)} %copy-done.1, bf16[128,1536]{1,0:T(8,128)(2,1)} %bitcast.64, ...), custom_call_target="tpu_custom_call" | custom-call | tf_op jit(solution)/shard_map/back/pallas_call | solution.py:1363
  402.7 76.9 %finish.1 = (bf16[4,48,1664]{2,1,0:T(8,128)(2,1)}, bf16[48,1536]{1,0:T(8,128)(2,1)}, bf16[128,1536]{1,0:T(8,128)(2,1)}, bf16[128,1536]{1,0:T(8,128)(2,1)}) custom-call(bf16[4,4,2,48,1664]{4,3,2,1,0:T(8,128)(2,1)} %get-tuple-element.59.first_partial_ref, bf16[512,1536]{1,0:T(8,128)(2,1)} %get-tuple-element.60.wide_hbm, bf16[1536,1664]{1,0:T(8,128)(2,1)} %bitcast.52, ...), custom_call_target="tpu_custom_call" | custom-call | tf_op jit(solution)/shard_map/finish/pallas_call | solution.py:1679
  479.6 5.0 %layout.1 = (f32[48,1536]{1,0:T(8,128)}, f32[48,1536]{1,0:T(8,128)}, f32[48,1536]{1,0:T(8,128)}, f32[48,1536]{1,0:T(8,128)}, f32[48,1536]{1,0:T(8,128)}, /*index...) custom-call(bf16[4,48,1664]{2,1,0:T(8,128)(2,1)} %get-tuple-element., ...), custom_call_target="tpu_custom_call" | custom-call | tf_op jit(solution)/shard_map/layout/pallas_call | solution.py:1757
  484.6 1.3 reshape.118
  (27 shorter events, 0.1 us)
Async XLA Ops:
  85.6 7.5 %copy-start.5 = (bf16[512,1536]{1,0:T(8,128)(2,1)S(1)}, bf16[512,1536]{1,0:T(8,128)(2,1)}, u32[]{:S(2)}) copy-start(bf16[512,1536]{1,0:T(8,128)(2,1)} %get-tuple-element.60.wide_hbm) | copy-start | bytes 4718596
  89.4 103.7 %copy-start.4 = (f32[1,1536]{1,0:T(1,128)}, f32[1,1536]{1,0:T(1,128)S(1)}, u32[]{:S(2)}) copy-start(f32[1,1536]{1,0:T(1,128)S(1)} %reshape.122.gain_ref) | copy-start | bytes 18436
  190.7 2.5 copy-start
  190.7 2.5 copy-start.3
  193.2 48.4 %copy-start.6 = (bf16[512,1536]{1,0:T(8,128)(2,1)S(1)}, bf16[512,1536]{1,0:T(8,128)(2,1)}, u32[]{:S(2)}) copy-start(bf16[512,1536]{1,0:T(8,128)(2,1)} %get-tuple-element.68) | copy-start | bytes 4718596
  193.2 54.1 %slice-start = ((s8[6291456]{0:T(1024)(128)(4,1)}), s8[2097152]{0:T(1024)(128)(4,1)S(1)}, s32[]{:S(2)}) async-start(s8[6291456]{0:T(1024)(128)(4,1)} %bitcast.54), calls=%async_computation | async-start | bytes 4194304
  241.5 5.7 %copy-start.1 = (f32[128,1536]{1,0:T(8,128)}, f32[128,1536]{1,0:T(8,128)S(1)}, u32[]{:S(2)}) copy-start(f32[128,1536]{1,0:T(8,128)S(1)} %get-tuple-element.71.hidden_ref) | copy-start | bytes 2359300
  241.6 10.4 %copy-start.2 = (bf16[512,1024]{1,0:T(8,128)(2,1)}, bf16[512,1024]{1,0:T(8,128)(2,1)S(1)}, u32[]{:S(2)}) copy-start(bf16[512,1024]{1,0:T(8,128)(2,1)S(1)} %get-tuple-element.81.active_ref) | copy-start | bytes 3145732
  241.6 5.7 %slice-start.1 = ((s8[6291456]{0:T(1024)(128)(4,1)}), s8[4194304]{0:T(1024)(128)(4,1)S(1)}, s32[]{:S(2)}) async-start(s8[6291456]{0:T(1024)(128)(4,1)} %bitcast.54), calls=%async_computation.1 | async-start | bytes 8388608

commit v7 on v6

--- a/solution.py
+++ b/solution.py
@@ -490,7 +490,7 @@
                 self.wave(wave, self.act, self.act)
                 return carry
 
-            lax.fori_loop(1, p.groups, one, 0)
+            lax.fori_loop(first, p.groups if last is None else last + 1, one, 0)
         if first > 1:
             return
 
@@ -798,11 +798,14 @@
 def attend_kernel(
     groups,
     hops,
-    rows_ref,
+    tokens_hbm,
+    first_hbm,
+    gain_ref,
     doc_query_ref,
     doc_key_ref,
     out_home_ref,
     feed_unit_ref,
+    rows_ref,
     query_ref,
     value_ref,
     within_ref,
@@ -815,6 +818,10 @@
     values_ref,
     out_full_ref,
     feed_full_ref,
+    tokens_ref,
+    first_ref,
+    normed_ref,
+    load_sem,
     key_ref,
     leave_ref,
     top_ref,
@@ -827,6 +834,10 @@
     *sems,
 ):
     here = Place(groups, feed_full_ref.shape[2])
+    tokens_load = pltpu.make_async_copy(tokens_hbm, tokens_ref, load_sem.at[0])
+    first_load = pltpu.make_async_copy(first_hbm, first_ref, load_sem.at[1])
+    tokens_load.start()
+    first_load.start()
     here.meet()
     place, has_next, following = here.g, here.above, here.up()
     home_sems, feed_sems = several(sems, 2, 5)
@@ -842,7 +853,15 @@
         ]
     )
     prepared = (rows_ref, query_ref, key_ref, value_ref, within_ref, map_ref, inverse_ref)
-    prepare_blocks(0, GROUP, *prepared)
+    tokens_load.wait()
+    for block in range(GROUP):
+        normed_ref[tile(block), :] = rms_norm(tokens_ref[tile(block), :].astype(F32), gain_ref[...]).astype(BF16)
+    first_load.wait()
+    for at, size in [(part * WIDE, WIDE) for part in range(4)] + [(4 * WIDE, EXTRA)]:
+        rows_ref[:, pl.ds(at, size)] = dot(normed_ref[...], first_ref[:, pl.ds(at, size)])
+    prepare_blocks(0, GROUP // 2, *prepared)
+    pauses()
+    prepare_blocks(GROUP // 2, GROUP, *prepared)
 
     def value_copy(source, slot):
         return remote(source, values_ref.at[slot], value_send.at[slot], value_recv.at[slot], following)
@@ -865,7 +884,6 @@
         key_copy(0).start()
         value_copy(value_ref, 0).start()
 
-    pauses()
 
     def row_counts(block, hop, first, count):
         return doc_query_ref[tile(block), :] == doc_key_ref[hop, :, tile(first, count)]
@@ -992,12 +1010,13 @@
     }
 
 
-def attend(groups, hops, projected, doc_query, doc_key, out_full, feed_full):
-    length = projected.shape[0]
+def attend(groups, hops, tokens, first, gain, doc_query, doc_key, out_full, feed_full):
+    length = tokens.shape[0]
     dma = pltpu.SemaphoreType.DMA
     return pl.pallas_call(
         functools.partial(attend_kernel, groups, hops),
         out_shape=[
+            shape(F32, length, first.shape[1]),
             shape(BF16, length, WIDE),
             shape(BF16, length, WIDE),
             shape(F32, length, WIDE),
@@ -1011,9 +1030,13 @@
             shape(BF16, *out_full.shape),
             shape(BF16, *feed_full.shape),
         ],
-        in_specs=in_vmem(3) + anywhere(2),
-        out_specs=in_vmem(10) + anywhere(2),
+        in_specs=anywhere(2) + in_vmem(3) + anywhere(2),
+        out_specs=in_vmem(11) + anywhere(2),
         scratch_shapes=[
+            pltpu.VMEM(tokens.shape, BF16),
+            pltpu.VMEM(first.shape, BF16),
+            pltpu.VMEM(tokens.shape, BF16),
+            dma((2,)),
             pltpu.VMEM((length, WIDE), BF16),
             pltpu.VMEM((hops, length, WIDE), BF16),
             pltpu.VMEM((OWN, length, BLOCK), F32),
@@ -1026,9 +1049,13 @@
         ]
         + [dma((groups // GROUP,))] * 2
         + Gather.outside(groups),
-        input_output_aliases={3: 10, 4: 11},
+        input_output_aliases={5: 11, 6: 12},
         **communicating(1, "attend"),
-    )(projected, doc_query, doc_key, out_full, feed_full)
+    )(tokens, first, gain, doc_query, doc_key, out_full, feed_full)
+
+
+def made_feed(groups, rows):
+    return groups == GROUP and rows % 16 == 0
 
 
 def back_kernel(
@@ -1054,6 +1081,8 @@
     inverse_hbm,
     down_partial_ref,
     feed_partial_ref,
+    normed_hbm,
+    feed_grads_hbm,
     grad_ref,
     down_result_ref,
     rows_grad_ref,
@@ -1065,6 +1094,9 @@
     moved_ref,
     values_ref,
     extra_ref,
+    normed_ref,
+    feed_grads_ref,
+    made_ref,
     load_sem,
     query_grad_ref,
     key_grad_ref,
@@ -1074,7 +1106,6 @@
     scaled_ref,
     dots_ref,
     direct_ref,
-    panels_ref,
     key_slots_ref,
     value_slots_ref,
     key_send,
@@ -1083,8 +1114,27 @@
     value_recv,
     *refs,
 ):
-    lines = feed_partial_ref.shape[2]
+    lines, rows = feed_partial_ref.shape[2:4]
     here = Place(groups, lines)
+    make = None
+    if made_feed(groups, rows):
+        normed_load = pltpu.make_async_copy(normed_hbm, normed_ref, load_sem.at[9])
+        feed_load = pltpu.make_async_copy(feed_grads_hbm, feed_grads_ref, load_sem.at[10])
+        feed_partial_ref = made_ref
+        normed_load.start()
+        feed_load.start()
+
+        def make(target):
+            span = GROUP * lines * rows
+            left = normed_ref[:, pl.ds(pl.multiple_of(target * span, BLOCK), span)].T
+
+            def one(at):
+                value = dot(left, feed_grads_ref[:, at])
+                for index in range(GROUP * lines):
+                    made_ref[target, index // lines, index % lines, :, at] = value[index * rows : (index + 1) * rows].astype(BF16)
+
+            in_tiles(feed_grads_ref.shape[1], one, 4 * BLOCK)
+
     here.meet()
     place, has_next, previous = here.g, here.above, here.down()
     sum_refs, gather_refs, down_refs, feed_refs, out_refs = several(
@@ -1098,7 +1148,7 @@
     sums = GroupSum(here, partial_ref, sum_refs)
     whole = GroupGather(here, grad_low_ref, gather_refs)
     down = Scatter(here, down_partial_ref, down_result_ref, down_refs)
-    feed_scatter = Scatter(here, feed_partial_ref, feed_result_ref, feed_refs)
+    feed_scatter = Scatter(here, feed_partial_ref, feed_result_ref, feed_refs, make)
     out_lines = LineSum(here, out_partial_ref, out_result_ref, out_refs)
     pauses = Pauses(*[(functools.partial(feed_scatter.step, wave),) for wave in range(1, groups)])
 
@@ -1108,19 +1158,17 @@
     def load_values(hop):
         return pltpu.make_async_copy(values_hbm.at[hop - 1], values_ref.at[hop % 2], load_sem.at[2 + hop % 2])
 
-    short = hops > 2
     loads = [pltpu.make_async_copy(rows_hbm.at[:, pl.ds(4 * WIDE, EXTRA)], extra_ref, load_sem.at[4])]
-    panels = direct_ref if short else panels_ref
     for index, panel in enumerate((0, 1, 3)):
-        loads.append(pltpu.make_async_copy(rows_hbm.at[:, pl.ds(panel * WIDE, WIDE)], panels.at[index], load_sem.at[5 + index]))
-    loads.append(pltpu.make_async_copy(inverse_hbm, panels.at[3], load_sem.at[8]))
+        loads.append(pltpu.make_async_copy(rows_hbm.at[:, pl.ds(panel * WIDE, WIDE)], direct_ref.at[index], load_sem.at[5 + index]))
+    loads.append(pltpu.make_async_copy(inverse_hbm, direct_ref.at[3], load_sem.at[8]))
     sums.start()
     down.start()
     load(hops).start()
     load_values(hops).start()
-    if not short:
-        for copy in loads:
-            copy.start()
+    if make is not None:
+        normed_load.wait()
+        feed_load.wait()
     feed_scatter.start_far(1, 1)
     for chunk in range(CHUNKS):
         sums.pass_on(chunk)
@@ -1335,13 +1383,12 @@
         return carry
 
     lax.fori_loop(1, hops + 1, settle, 0)
-    if short:
-        for copy in loads:
-            copy.start()
+    for copy in loads:
+        copy.start()
     for copy in loads:
         copy.wait()
     pauses()
-    pieces = (panels, extra_ref, query_grad_ref, key_grad_ref, within_grad_ref, map_grad_ref, value_grad_ref, rows_grad_ref)
+    pieces = (direct_ref, extra_ref, query_grad_ref, key_grad_ref, within_grad_ref, map_grad_ref, value_grad_ref, rows_grad_ref)
     prepare_back_blocks(0, GROUP // 2, *pieces)
     pauses.rest()
     prepare_back_blocks(GROUP // 2, GROUP, *pieces)
@@ -1353,7 +1400,7 @@
 
 
 def back(groups, hops, partial, hidden, cotangent, gain, low, out, *args):
-    values, moved, rows, inverse, down, feed = args[-6:]
+    values, moved, rows, inverse, down, feed, normed, feed_grads = args[-8:]
     size, width = hidden.shape
     length = partial.shape[0]
     lines, units = feed.shape[2:4]
@@ -1369,7 +1416,7 @@
             shape(BF16, GROUP, *feed.shape[3:]),
             shape(BF16, groups // GROUP, GROUP, units, width),
         ],
-        in_specs=in_vmem(len(inputs) - 6) + anywhere(6),
+        in_specs=in_vmem(len(inputs) - 8) + anywhere(8),
         out_specs=in_vmem(5),
         scratch_shapes=[
             pltpu.VMEM((length, width), BF16),
@@ -1378,14 +1425,16 @@
             pltpu.VMEM((2,) + moved.shape[1:], BF16),
             pltpu.VMEM((2,) + values.shape[1:], BF16),
             pltpu.VMEM((length, EXTRA), F32),
-            dma((9,)),
+            pltpu.VMEM(normed.shape if made_feed(groups, units) else (16, BLOCK), BF16),
+            pltpu.VMEM(feed_grads.shape if made_feed(groups, units) else (16, BLOCK), BF16),
+            pltpu.VMEM(feed.shape if made_feed(groups, units) else (1, 1, 1, 16, BLOCK), BF16),
+            dma((11,)),
         ]
         + [pltpu.VMEM((length, WIDE), F32)] * 5
         + [
             pltpu.VMEM((length, WIDE), BF16),
             pltpu.VMEM((OWN, length, BLOCK), F32),
             pltpu.VMEM((GROUP, length, WIDE), F32),
-            pltpu.VMEM((1 if hops > 2 else GROUP, BLOCK if hops > 2 else length, WIDE), F32),
             pltpu.VMEM((hops + 1, length, WIDE), BF16),
             pltpu.VMEM((hops + 1, length, WIDE), BF16),
             dma((hops,)),
@@ -1824,10 +1873,8 @@
     )[:, None, :]
     doc_query = lax.dynamic_index_in_dim(docs, place, 0, keepdims=False)[:, None]
 
-    normed = rms_norm(tokens_all.astype(F32), gain_one).astype(BF16)
-    projected = dot(normed, first)
-    (query, value, within, maps, inverse, attended, attended_low, stats, moved, values, out_full, feed) = attend(
-        groups, hops, projected, doc_query, doc_key, out_full, feed
+    (projected, query, value, within, maps, inverse, attended, attended_low, stats, moved, values, out_full, feed) = attend(
+        groups, hops, tokens_all, first, gain_one, doc_query, doc_key, out_full, feed
     )
     out_full = out_full.reshape(WIDE, width)
     feed = feed.reshape(width, -1)
@@ -1838,15 +1885,20 @@
     active_grad = dot(cotangent_all, down_full, NT)
     feed_grads = jnp.concatenate([(active_grad * gate_slope).astype(BF16), (active_grad * up_slope).astype(BF16)], 1)
     down_partial = dot(active, cotangent_all, TN).astype(BF16).reshape(groups, 1, batch, hidden_rows, width)
-    feed_partial = dot(normed_two, feed_grads, TN).astype(BF16).reshape(groups, GROUP, batch, rows, -1)
+    if made_feed(groups, rows):
+        feed_partial = feed.reshape(groups, GROUP, batch, rows, -1)
+    else:
+        feed_partial = dot(normed_two, feed_grads, TN).astype(BF16).reshape(groups, GROUP, batch, rows, -1)
     hidden_grad, down_weight_grad, rows_grad, feed_grad, out_lines = back(
         groups, hops, dot(feed_grads, feed, NT).astype(BF16), hidden, cotangent[0], gain_two, attended_low, out_full, query, value,
         within, maps, doc_query, doc_key, attended, stats, values, moved, projected, inverse, down_partial, feed_partial,
+        normed_two, feed_grads,
     )
     partial_shape = (groups, GROUP, batch, rows, rows_grad.shape[1])
     if rows % 16 == 0:
         first_partial = first.reshape(partial_shape)
     else:
+        normed = rms_norm(tokens_all.astype(F32), gain_one).astype(BF16)
         first_partial = dot(normed, rows_grad, TN).astype(BF16).reshape(partial_shape)
     beta_parts = jnp.pad(columns(beta_weight), ((0, 0), (0, 0), (0, EXTRA - OWN)))
     weights = (query_weight, key_weight, value_weight, house_weight) + feed_weights

time: 494 us -> 484 us (0.980)
  matrix products: 29.1 us -> 16.8 us
  Pallas kernels: 443 us -> 448 us
    dot_general x6 -> x4, matrix products: 29.1 us -> 16.8 us  [dot(): return lax.dot_general(left, right, dims, preferred_element_type=F32)]
where the time goes in v7:
time: 484 us; the launch traced here: 478 us
  Pallas kernels  448 us (93%)
  matrix products  16.8 us (3%)
  other arithmetic  6.66 us (1%)
  local copies, waits for them, and re-layouts  5.43 us (1%)
    pallas_call x1, Pallas kernels, back(): pl.pallas_call(functools.partial(back_kernel, groups, hops), out_shape=[s...  144 us
    pallas_call x1, Pallas kernels, attend(): pl.pallas_call(functools.partial(attend_kernel, groups, hops), out_shape=...  90.4 us
    pallas_call x1, Pallas kernels, gather_first(): pl.pallas_call(functools.partial(gather_kernel, groups), out_shape=[shape...  81 us
    pallas_call x1, Pallas kernels, finish(): pl.pallas_call(functools.partial(finish_kernel, groups), out_shape=[shape...  80 us
    pallas_call x1, Pallas kernels, branch(): pl.pallas_call(functools.partial(branch_kernel, groups), out_shape=[shape...  47.7 us
    dot_general x4, matrix products, dot(): return lax.dot_general(left, right, dims, preferred_element_type=F32)  16.8 us

profile of v7, /device:TPU:0, one launch (start us, length us, event | category | flops | bytes accessed | tf_op | source)
XLA Modules:
  0.0 477.9 jit_solution(7557800287979986756)
XLA Ops:
  0.7 0.7 convert_bitcast_fusion
  1.3 0.7 convert_bitcast_fusion.1
  2.0 0.6 maximum_convert_fusion.gains_ref
  2.6 0.7 convert_element_type.68
  3.3 0.1 reshape.93
  3.4 0.1 copy.46
  3.5 0.1 copy.45
  3.6 0.1 pad_maximum_fusion.1
  3.7 0.1 copy.44
  3.9 0.7 fusion.2
  4.6 81.0 %gather_first.1 = (bf16[4,4,2,48,1664]{4,3,2,1,0:T(8,128)(2,1)}, bf16[4,4,2,48,2048]{4,3,2,1,0:T(8,128)(2,1)}, bf16[1,4,2,48,1536]{4,3,2,1,0:T(8,128)(2,1)}, bf1...) custom-call(f32[48,1536]{1,0:T(8,128)} %refs_0_.1, f32[48,1536]{1,0:T(8,128)} %refs_1_.1, ...), custom_call_target="tpu_custom_call" | custom-call | tf_op jit(solution)/shard_map/gather_first/pallas_call | solution.py:1524
  85.6 1.7 convert_reduce_fusion
  87.3 0.0 copy-start.5
  87.3 0.6 reshape.104.gain_ref
  87.9 1.2 slice.22
  89.1 0.3 reshape.95
  89.5 0.6 broadcast_in_dim.37.doc_key_ref
  90.1 0.9 copy.48.doc_query_ref
  91.0 90.4 %attend.1 = (f32[512,1664]{1,0:T(8,128)}, bf16[512,384]{1,0:T(8,128)(2,1)}, bf16[512,384]{1,0:T(8,128)(2,1)}, f32[512,384]{1,0:T(8,128)}, f32[512,384]{1,0:T(8,1...) custom-call(bf16[512,1536]{1,0:T(8,128)(2,1)} %get-tuple-element.61., ...), custom_call_target="tpu_custom_call", output_to_operand_aliasing={{11}: (5, {}), {12}: (6, {})} | custom-call | tf_op jit(solution)/shard_map/attend/pallas_call | solution.py:1016
  181.3 0.0 copy-start
  181.4 2.4 convolution_convert_fusion.2.partial_ref
  183.8 47.7 %branch.1 = (f32[128,1536]{1,0:T(8,128)S(1)}, bf16[512,1536]{1,0:T(8,128)(2,1)S(1)}, bf16[512,1024]{1,0:T(8,128)(2,1)S(1)}, f32[512,1024]{1,0:T(8,128)}, f32[512...) custom-call(bf16[512,1536]{1,0:T(8,128)(2,1)S(1)} %convolution_convert_fusion.2.partial_ref, ...), custom_call_target="tpu_custom_call" | custom-call | tf_op jit(solution)/shard_map/branch/pallas_call | solution.py:1628
  231.5 0.0 copy-start.1
  231.6 0.0 slice-start.1
  231.6 6.2 %multiply_convert_fusion.1 = (bf16[512,1024]{1,0:T(8,128)(2,1)S(1)}, bf16[512,1024]{1,0:T(8,128)(2,1)S(1)}) fusion(f32[512,1024]{1,0:T(8,128)} %get-tuple-element.70, f32[512,1024]{1,0:T(8,128)} %get-tuple-element.71, bf16[512,1536]{1,0:T(8,128)(2,1)S(1)} %copy-done.6, bf16[1024,1536]{1,0:T(8,128)(2,1)} %bitcast.54), kind=kOutput, calls=%fused_computation.5 | convolution fusion | flops 1612709888 | bytes 11010048 | tf_op jit(solution)/shard_map/dot_general | solution.py:30
  237.9 4.6 convolution_convert_fusion.1.partial_ref
  242.5 1.5 pad_maximum_fusion.feed_grads_hbm
  244.0 3.5 convolution_convert_fusion
  247.5 143.6 %back.1 = (f32[128,1536]{1,0:T(8,128)}, f32[1,128,1536]{2,1,0:T(8,128)}, bf16[512,1664]{1,0:T(8,128)(2,1)}, bf16[4,48,2048]{2,1,0:T(8,128)(2,1)}, bf16[1,4,48,1536]{3,2,1,0:T(8,128)(2,1)}) custom-call(bf16[512,1536]{1,0:T(8,128)(2,1)} %convolution_convert_fusion.1.partial_ref, f32[128,1536]{1,0:T(8,128)} %copy-done.1, bf16[128,1536]{1,0:T(8,128)(2,1)} %bitcast.60, ...), custom_call_target="tpu_custom_call" | custom-call | tf_op jit(solution)/shard_map/back/pallas_call | solution.py:1410
  391.1 80.0 %finish.1 = (bf16[4,48,1664]{2,1,0:T(8,128)(2,1)}, bf16[48,1536]{1,0:T(8,128)(2,1)}, bf16[128,1536]{1,0:T(8,128)(2,1)}, bf16[128,1536]{1,0:T(8,128)(2,1)}) custom-call(bf16[4,4,2,48,1664]{4,3,2,1,0:T(8,128)(2,1)} %get-tuple-element.60.first_partial_ref, bf16[512,1536]{1,0:T(8,128)(2,1)} %get-tuple-element.61.tokens_hbm.wide_hbm, ...), custom_call_target="tpu_custom_call" | custom-call | tf_op jit(solution)/shard_map/finish/pallas_call | solution.py:1728
  471.1 5.0 %layout.1 = (f32[48,1536]{1,0:T(8,128)}, f32[48,1536]{1,0:T(8,128)}, f32[48,1536]{1,0:T(8,128)}, f32[48,1536]{1,0:T(8,128)}, f32[48,1536]{1,0:T(8,128)}, /*index...) custom-call(bf16[4,48,1664]{2,1,0:T(8,128)(2,1)} %get-tuple-element., ...), custom_call_target="tpu_custom_call" | custom-call | tf_op jit(solution)/shard_map/layout/pallas_call | solution.py:1806
  476.2 1.3 reshape.103
  (24 shorter events, 0.1 us)
Async XLA Ops:
  87.3 96.5 %copy-start.5 = (f32[1,1536]{1,0:T(1,128)}, f32[1,1536]{1,0:T(1,128)S(1)}, u32[]{:S(2)}) copy-start(f32[1,1536]{1,0:T(1,128)S(1)} %reshape.107.gain_ref) | copy-start | bytes 18436
  181.3 2.5 copy-start
  181.4 2.5 copy-start.4
  183.8 47.7 %copy-start.6 = (bf16[512,1536]{1,0:T(8,128)(2,1)S(1)}, bf16[512,1536]{1,0:T(8,128)(2,1)}, u32[]{:S(2)}) copy-start(bf16[512,1536]{1,0:T(8,128)(2,1)} %get-tuple-element.69) | copy-start | bytes 4718596
  183.8 54.0 %slice-start = ((s8[6291456]{0:T(1024)(128)(4,1)}), s8[4194304]{0:T(1024)(128)(4,1)S(1)}, s32[]{:S(2)}) async-start(s8[6291456]{0:T(1024)(128)(4,1)} %bitcast.47), calls=%async_computation | async-start | bytes 8388608
  231.5 6.3 %copy-start.1 = (f32[128,1536]{1,0:T(8,128)}, f32[128,1536]{1,0:T(8,128)S(1)}, u32[]{:S(2)}) copy-start(f32[128,1536]{1,0:T(8,128)S(1)} %get-tuple-element.72.hidden_ref) | copy-start | bytes 2359300
  231.5 6.3 %copy-start.2 = (bf16[512,1536]{1,0:T(8,128)(2,1)}, bf16[512,1536]{1,0:T(8,128)(2,1)S(1)}, u32[]{:S(2)}) copy-start(bf16[512,1536]{1,0:T(8,128)(2,1)S(1)} %get-tuple-element.84.normed_hbm) | copy-start | bytes 4718596
  231.6 12.5 %copy-start.3 = (bf16[512,1024]{1,0:T(8,128)(2,1)}, bf16[512,1024]{1,0:T(8,128)(2,1)S(1)}, u32[]{:S(2)}) copy-start(bf16[512,1024]{1,0:T(8,128)(2,1)S(1)} %get-tuple-element.83.active_ref) | copy-start | bytes 3145732
  231.6 6.3 %slice-start.1 = ((s8[6291456]{0:T(1024)(128)(4,1)}), s8[2097152]{0:T(1024)(128)(4,1)S(1)}, s32[]{:S(2)}) async-start(s8[6291456]{0:T(1024)(128)(4,1)} %bitcast.47), calls=%async_computation.1 | async-start | bytes 4194304

commit v8 on v7

--- a/solution.py
+++ b/solution.py
@@ -1574,8 +1574,8 @@
 
 
 def branch_kernel(
-    groups, partial_ref, tokens_ref, gain_ref, down_ref, feed_hbm, hidden_ref, normed_ref, active_ref, gate_slope_ref, up_slope_ref,
-    down_full_ref, feed_ref, feed_sem, *refs
+    groups, partial_ref, tokens_ref, gain_ref, down_ref, feed_hbm, cotangent_hbm, hidden_ref, normed_ref, active_ref, feed_grads_ref,
+    down_full_ref, gate_slope_ref, up_slope_ref, cotangent_ref, down_rows_ref, feed_ref, feed_sem, *refs
 ):
     here = Place(groups, down_full_ref.shape[1])
     here.meet()
@@ -1590,6 +1590,8 @@
     down.spread()
     feed_copy = pltpu.make_async_copy(feed_hbm, feed_ref, feed_sem.at[0])
     feed_copy.start()
+    cotangent_copy = pltpu.make_async_copy(cotangent_hbm, cotangent_ref, feed_sem.at[1])
+    cotangent_copy.start()
     for chunk in range(CHUNKS):
         total.pass_on(chunk)
     pauses()
@@ -1618,10 +1620,21 @@
 
     in_tiles(units, act)
     total.finish()
+    cotangent_copy.wait()
     down.finish()
-
-
-def branch(groups, lines, partial, tokens, gain, down, feed):
+    down_copy = pltpu.make_async_copy(down_full_ref, down_rows_ref, feed_sem.at[2])
+    down_copy.start()
+    down_copy.wait()
+    down_rows = down_rows_ref[...].reshape(units, down_rows_ref.shape[3])
+    step = 2 * BLOCK
+    for index in range(units // step):
+        at = pl.ds(index * step, step)
+        grad = dot(cotangent_ref[...], down_rows[index * step : (index + 1) * step], NT)
+        feed_grads_ref[:, at] = (grad * gate_slope_ref[:, at]).astype(BF16)
+        feed_grads_ref[:, pl.ds(units + index * step, step)] = (grad * up_slope_ref[:, at]).astype(BF16)
+
+
+def branch(groups, lines, partial, tokens, gain, down, feed, cotangent):
     size, width = tokens.shape
     length, units = partial.shape[0], feed.shape[1] // 2
     dma = pltpu.SemaphoreType.DMA
@@ -1631,19 +1644,25 @@
             shape(F32, size, width),
             shape(BF16, length, width),
             shape(BF16, length, units),
-            shape(F32, length, units),
-            shape(F32, length, units),
+            shape(BF16, length, 2 * units),
             shape(BF16, groups, lines, *down.shape),
         ],
-        in_specs=in_vmem(3) + anywhere(2),
-        out_specs=in_vmem(5) + anywhere(1),
-        scratch_shapes=[pltpu.VMEM(feed.shape, BF16), dma((1,))]
+        in_specs=in_vmem(3) + anywhere(3),
+        out_specs=in_vmem(4) + anywhere(1),
+        scratch_shapes=[
+            pltpu.VMEM((length, units), F32),
+            pltpu.VMEM((length, units), F32),
+            pltpu.VMEM(cotangent.shape, BF16),
+            pltpu.VMEM((groups, lines) + down.shape, BF16),
+            pltpu.VMEM(feed.shape, BF16),
+            dma((3,)),
+        ]
         + GroupSum.scratch(size, width)
         + GroupGather.scratch()
         + Gather.inside()
         + Gather.outside(groups),
         **communicating(3, "branch", 48),
-    )(partial, tokens, gain, down, feed)
+    )(partial, tokens, gain, down, feed, cotangent)
 
 
 def finish_kernel(
@@ -1878,12 +1897,10 @@
     )
     out_full = out_full.reshape(WIDE, width)
     feed = feed.reshape(width, -1)
-    hidden, normed_two, active, gate_slope, up_slope, down_full = branch(
-        groups, batch, dot(attended_low, out_full).astype(BF16), tokens[0], gain_two, down_low, feed
+    hidden, normed_two, active, feed_grads, down_full = branch(
+        groups, batch, dot(attended_low, out_full).astype(BF16), tokens[0], gain_two, down_low, feed, cotangent_all
     )
     down_full = down_full.reshape(hidden_own, width)
-    active_grad = dot(cotangent_all, down_full, NT)
-    feed_grads = jnp.concatenate([(active_grad * gate_slope).astype(BF16), (active_grad * up_slope).astype(BF16)], 1)
     down_partial = dot(active, cotangent_all, TN).astype(BF16).reshape(groups, 1, batch, hidden_rows, width)
     if made_feed(groups, rows):
         feed_partial = feed.reshape(groups, GROUP, batch, rows, -1)

time: 484 us -> 483 us (level)
    dot_general x4 -> x3, matrix products: 16.8 us -> 13.5 us  [dot(): return lax.dot_general(left, right, dims, preferred_element_type=F32)]
where the time goes in v8:
time: 483 us; the launch traced here: 476 us
  Pallas kernels  451 us (93%)
  matrix products  13.5 us (3%)
  local copies, waits for them, and re-layouts  5.43 us (1%)
  other arithmetic  5.17 us (1%)
    pallas_call x1, Pallas kernels, back(): pl.pallas_call(functools.partial(back_kernel, groups, hops), out_shape=[s...  144 us
    pallas_call x1, Pallas kernels, attend(): pl.pallas_call(functools.partial(attend_kernel, groups, hops), out_shape=...  90.3 us
    pallas_call x1, Pallas kernels, gather_first(): pl.pallas_call(functools.partial(gather_kernel, groups), out_shape=[shape...  81 us
    pallas_call x1, Pallas kernels, finish(): pl.pallas_call(functools.partial(finish_kernel, groups), out_shape=[shape...  80.2 us
    pallas_call x1, Pallas kernels, branch(): pl.pallas_call(functools.partial(branch_kernel, groups), out_shape=[shape...  50.7 us
    dot_general x3, matrix products, dot(): return lax.dot_general(left, right, dims, preferred_element_type=F32)  13.5 us

profile of v8, /device:TPU:0, one launch (start us, length us, event | category | flops | bytes accessed | tf_op | source)
XLA Modules:
  0.0 476.3 jit_solution(5856585107854776898)
XLA Ops:
  0.7 0.7 convert_bitcast_fusion
  1.3 0.7 convert_bitcast_fusion.1
  2.0 0.6 maximum_convert_fusion.gains_ref
  2.6 0.7 convert_element_type.62
  3.3 0.1 reshape.93
  3.4 0.1 copy.46
  3.5 0.1 copy.45
  3.7 0.1 pad_maximum_fusion
  3.8 0.1 copy.44
  3.9 0.7 fusion.2
  4.6 81.0 %gather_first.1 = (bf16[4,4,2,48,1664]{4,3,2,1,0:T(8,128)(2,1)}, bf16[4,4,2,48,2048]{4,3,2,1,0:T(8,128)(2,1)}, bf16[1,4,2,48,1536]{4,3,2,1,0:T(8,128)(2,1)}, bf1...) custom-call(f32[48,1536]{1,0:T(8,128)} %refs_0_.1, f32[48,1536]{1,0:T(8,128)} %refs_1_.1, ...), custom_call_target="tpu_custom_call" | custom-call | tf_op jit(solution)/shard_map/gather_first/pallas_call | solution.py:1524
  85.6 1.7 convert_reduce_fusion
  87.3 0.0 copy-start.5
  87.3 0.6 reshape.104.gain_ref
  87.9 1.2 slice.22
  89.1 0.3 reshape.95
  89.5 0.6 broadcast_in_dim.37.doc_key_ref
  90.1 0.9 copy.48.doc_query_ref
  91.0 90.3 %attend.1 = (f32[512,1664]{1,0:T(8,128)}, bf16[512,384]{1,0:T(8,128)(2,1)}, bf16[512,384]{1,0:T(8,128)(2,1)}, f32[512,384]{1,0:T(8,128)}, f32[512,384]{1,0:T(8,1...) custom-call(bf16[512,1536]{1,0:T(8,128)(2,1)} %get-tuple-element.60., ...), custom_call_target="tpu_custom_call", output_to_operand_aliasing={{11}: (5, {}), {12}: (6, {})} | custom-call | tf_op jit(solution)/shard_map/attend/pallas_call | solution.py:1016
  181.3 0.0 copy-start
  181.3 0.0 slice-start
  181.3 2.5 convolution_convert_fusion.2.partial_ref
  183.8 0.0 slice-start.1
  183.9 50.7 %branch.1 = (f32[128,1536]{1,0:T(8,128)S(1)}, bf16[512,1536]{1,0:T(8,128)(2,1)S(1)}, bf16[512,1024]{1,0:T(8,128)(2,1)S(1)}, bf16[512,2048]{1,0:T(8,128)(2,1)}, bf16[4,2,128,1536]{3,2,1,0:T(8,128)(2,1)}) custom-call(bf16[512,1536]{1,0:T(8,128)(2,1)S(1)} %convolution_convert_fusion.2.partial_ref, bf16[128,1536]{1,0:T(8,128)(2,1)S(1)} %bitcast.44, ...), custom_call_target="tpu_custom_call" | custom-call | tf_op jit(solution)/shard_map/branch/pallas_call | solution.py:1641
  234.6 0.0 copy-start.1
  234.6 7.5 %convolution_convert_fusion.1.partial_ref = bf16[512,1536]{1,0:T(8,128)(2,1)} fusion(bf16[512,2048]{1,0:T(8,128)(2,1)} %get-tuple-element.69.feed_grads_hbm, bf16[1536,2048]{1,0:T(8,128)(2,1)S(1)} %bitcast.48), kind=kOutput, calls=%fused_computation.1 | convolution fusion | flops 3222011904 | bytes 9961472 | tf_op jit(solution)/shard_map/dot_general | solution.py:30
  242.1 0.0 copy-done.3
  242.1 3.6 convolution_convert_fusion
  245.7 143.6 %back.1 = (f32[128,1536]{1,0:T(8,128)}, f32[1,128,1536]{2,1,0:T(8,128)}, bf16[512,1664]{1,0:T(8,128)(2,1)}, bf16[4,48,2048]{2,1,0:T(8,128)(2,1)}, bf16[1,4,48,1536]{3,2,1,0:T(8,128)(2,1)}) custom-call(bf16[512,1536]{1,0:T(8,128)(2,1)} %convolution_convert_fusion.1.partial_ref, f32[128,1536]{1,0:T(8,128)} %copy-done.1, bf16[128,1536]{1,0:T(8,128)(2,1)} %bitcast.58, ...), custom_call_target="tpu_custom_call" | custom-call | tf_op jit(solution)/shard_map/back/pallas_call | solution.py:1410
  389.2 80.2 %finish.1 = (bf16[4,48,1664]{2,1,0:T(8,128)(2,1)}, bf16[48,1536]{1,0:T(8,128)(2,1)}, bf16[128,1536]{1,0:T(8,128)(2,1)}, bf16[128,1536]{1,0:T(8,128)(2,1)}) custom-call(bf16[4,4,2,48,1664]{4,3,2,1,0:T(8,128)(2,1)} %get-tuple-element.59.first_partial_ref, bf16[512,1536]{1,0:T(8,128)(2,1)} %get-tuple-element.60.tokens_hbm.wide_hbm, ...), custom_call_target="tpu_custom_call" | custom-call | tf_op jit(solution)/shard_map/finish/pallas_call | solution.py:1747
  469.5 5.0 %layout.1 = (f32[48,1536]{1,0:T(8,128)}, f32[48,1536]{1,0:T(8,128)}, f32[48,1536]{1,0:T(8,128)}, f32[48,1536]{1,0:T(8,128)}, f32[48,1536]{1,0:T(8,128)}, /*index...) custom-call(bf16[4,48,1664]{2,1,0:T(8,128)(2,1)} %get-tuple-element., ...), custom_call_target="tpu_custom_call" | custom-call | tf_op jit(solution)/shard_map/layout/pallas_call | solution.py:1825
  474.5 1.3 reshape.103
  (22 shorter events, 0.1 us)
Async XLA Ops:
  87.3 96.5 %copy-start.5 = (f32[1,1536]{1,0:T(1,128)}, f32[1,1536]{1,0:T(1,128)S(1)}, u32[]{:S(2)}) copy-start(f32[1,1536]{1,0:T(1,128)S(1)} %reshape.107.gain_ref) | copy-start | bytes 18436
  181.3 2.6 copy-start
  181.3 2.6 copy-start.4
  181.3 53.3 %slice-start = ((s8[6291456]{0:T(1024)(128)(4,1)}), s8[4194304]{0:T(1024)(128)(4,1)S(1)}, s32[]{:S(2)}) async-start(s8[6291456]{0:T(1024)(128)(4,1)} %bitcast.46), calls=%async_computation | async-start | bytes 8388608
  183.8 50.8 %slice-start.1 = ((s8[6291456]{0:T(1024)(128)(4,1)}), s8[2097152]{0:T(1024)(128)(4,1)S(1)}, s32[]{:S(2)}) async-start(s8[6291456]{0:T(1024)(128)(4,1)} %bitcast.46), calls=%async_computation.1 | async-start | bytes 4194304
  234.6 7.5 %copy-start.1 = (f32[128,1536]{1,0:T(8,128)}, f32[128,1536]{1,0:T(8,128)S(1)}, u32[]{:S(2)}) copy-start(f32[128,1536]{1,0:T(8,128)S(1)} %get-tuple-element.70.hidden_ref) | copy-start | bytes 2359300
  234.6 7.5 %copy-start.2 = (bf16[512,1536]{1,0:T(8,128)(2,1)}, bf16[512,1536]{1,0:T(8,128)(2,1)S(1)}, u32[]{:S(2)}) copy-start(bf16[512,1536]{1,0:T(8,128)(2,1)S(1)} %get-tuple-element.82.normed_hbm) | copy-start | bytes 4718596
  234.6 7.5 %copy-start.3 = (bf16[512,1024]{1,0:T(8,128)(2,1)}, bf16[512,1024]{1,0:T(8,128)(2,1)S(1)}, u32[]{:S(2)}) copy-start(bf16[512,1024]{1,0:T(8,128)(2,1)S(1)} %get-tuple-element.81.active_ref) | copy-start | bytes 3145732
  234.6 7.5 %copy-start.6 = (bf16[512,1536]{1,0:T(8,128)(2,1)S(1)}, bf16[512,1536]{1,0:T(8,128)(2,1)}, u32[]{:S(2)}) copy-start(bf16[512,1536]{1,0:T(8,128)(2,1)} %get-tuple-element.67.cotangent_hbm) | copy-start | bytes 4718596

commit v9 on v8

--- a/solution.py
+++ b/solution.py
@@ -805,12 +805,12 @@
     doc_key_ref,
     out_home_ref,
     feed_unit_ref,
-    rows_ref,
+    rows_out,
     query_ref,
     value_ref,
-    within_ref,
-    map_ref,
-    inverse_ref,
+    within_out,
+    map_out,
+    inverse_out,
     attended_ref,
     low_ref,
     stats_ref,
@@ -822,6 +822,10 @@
     first_ref,
     normed_ref,
     load_sem,
+    rows_ref,
+    within_ref,
+    map_ref,
+    inverse_ref,
     key_ref,
     leave_ref,
     top_ref,
@@ -862,6 +866,14 @@
     prepare_blocks(0, GROUP // 2, *prepared)
     pauses()
     prepare_blocks(GROUP // 2, GROUP, *prepared)
+    stores = [
+        pltpu.make_async_copy(source, target, load_sem.at[2 + index])
+        for index, (source, target) in enumerate(
+            ((rows_ref, rows_out), (within_ref, within_out), (map_ref, map_out), (inverse_ref, inverse_out))
+        )
+    ]
+    for copy in stores:
+        copy.start()
 
     def value_copy(source, slot):
         return remote(source, values_ref.at[slot], value_send.at[slot], value_recv.at[slot], following)
@@ -986,7 +998,7 @@
 
     lax.fori_loop(0, hops, settle, 0)
     pauses.rest()
-    for copy in out_copies:
+    for copy in out_copies + stores:
         copy.wait()
     feed_gather.finish()
 
@@ -1031,12 +1043,16 @@
             shape(BF16, *feed_full.shape),
         ],
         in_specs=anywhere(2) + in_vmem(3) + anywhere(2),
-        out_specs=in_vmem(11) + anywhere(2),
+        out_specs=anywhere(1) + in_vmem(2) + anywhere(3) + in_vmem(5) + anywhere(2),
         scratch_shapes=[
             pltpu.VMEM(tokens.shape, BF16),
             pltpu.VMEM(first.shape, BF16),
             pltpu.VMEM(tokens.shape, BF16),
-            dma((2,)),
+            dma((6,)),
+            pltpu.VMEM((length, first.shape[1]), F32),
+            pltpu.VMEM((length, WIDE), F32),
+            pltpu.VMEM((length, WIDE), F32),
+            pltpu.VMEM((length, WIDE), F32),
             pltpu.VMEM((length, WIDE), BF16),
             pltpu.VMEM((hops, length, WIDE), BF16),
             pltpu.VMEM((OWN, length, BLOCK), F32),

time: 483 us -> 481 us (level)
  no operation moved by 1% of the time
where the time goes in v9:
time: 481 us; the launch traced here: 474 us
  Pallas kernels  449 us (93%)
  matrix products  13.5 us (3%)
  local copies, waits for them, and re-layouts  5.43 us (1%)
  other arithmetic  5.17 us (1%)
    pallas_call x1, Pallas kernels, back(): pl.pallas_call(functools.partial(back_kernel, groups, hops), out_shape=[s...  144 us
    pallas_call x1, Pallas kernels, attend(): pl.pallas_call(functools.partial(attend_kernel, groups, hops), out_shape=...  88.5 us
    pallas_call x1, Pallas kernels, gather_first(): pl.pallas_call(functools.partial(gather_kernel, groups), out_shape=[shape...  81 us
    pallas_call x1, Pallas kernels, finish(): pl.pallas_call(functools.partial(finish_kernel, groups), out_shape=[shape...  80.2 us
    pallas_call x1, Pallas kernels, branch(): pl.pallas_call(functools.partial(branch_kernel, groups), out_shape=[shape...  50.7 us
    dot_general x3, matrix products, dot(): return lax.dot_general(left, right, dims, preferred_element_type=F32)  13.5 us

profile of v9, /device:TPU:0, one launch (start us, length us, event | category | flops | bytes accessed | tf_op | source)
XLA Modules:
  0.0 474.5 jit_solution(9246574840882206342)
XLA Ops:
  0.7 0.7 convert_bitcast_fusion
  1.3 0.7 convert_bitcast_fusion.1
  2.0 0.6 maximum_convert_fusion.gains_ref
  2.6 0.7 convert_element_type.62
  3.3 0.1 reshape.93
  3.4 0.1 copy.46
  3.5 0.1 copy.45
  3.7 0.1 pad_maximum_fusion
  3.8 0.1 copy.44
  3.9 0.7 fusion.2
  4.6 81.0 %gather_first.1 = (bf16[4,4,2,48,1664]{4,3,2,1,0:T(8,128)(2,1)}, bf16[4,4,2,48,2048]{4,3,2,1,0:T(8,128)(2,1)}, bf16[1,4,2,48,1536]{4,3,2,1,0:T(8,128)(2,1)}, bf1...) custom-call(f32[48,1536]{1,0:T(8,128)} %refs_0_.1, f32[48,1536]{1,0:T(8,128)} %refs_1_.1, ...), custom_call_target="tpu_custom_call" | custom-call | tf_op jit(solution)/shard_map/gather_first/pallas_call | solution.py:1540
  85.6 1.7 convert_reduce_fusion
  87.3 0.0 copy-start.5
  87.3 0.6 reshape.104.gain_ref
  87.9 1.2 slice.22
  89.1 0.3 reshape.95
  89.5 0.6 broadcast_in_dim.37.doc_key_ref
  90.1 0.9 copy.48.doc_query_ref
  91.0 88.5 %attend.1 = (f32[512,1664]{1,0:T(8,128)}, bf16[512,384]{1,0:T(8,128)(2,1)}, bf16[512,384]{1,0:T(8,128)(2,1)}, f32[512,384]{1,0:T(8,128)}, f32[512,384]{1,0:T(8,1...) custom-call(bf16[512,1536]{1,0:T(8,128)(2,1)} %get-tuple-element.60., ...), custom_call_target="tpu_custom_call", output_to_operand_aliasing={{11}: (5, {}), {12}: (6, {})} | custom-call | tf_op jit(solution)/shard_map/attend/pallas_call | solution.py:1028
  179.5 0.0 copy-start
  179.5 0.0 slice-start
  179.5 2.5 convolution_convert_fusion.2.partial_ref
  182.1 0.0 slice-start.1
  182.1 50.7 %branch.1 = (f32[128,1536]{1,0:T(8,128)S(1)}, bf16[512,1536]{1,0:T(8,128)(2,1)S(1)}, bf16[512,1024]{1,0:T(8,128)(2,1)S(1)}, bf16[512,2048]{1,0:T(8,128)(2,1)}, bf16[4,2,128,1536]{3,2,1,0:T(8,128)(2,1)}) custom-call(bf16[512,1536]{1,0:T(8,128)(2,1)S(1)} %convolution_convert_fusion.2.partial_ref, bf16[128,1536]{1,0:T(8,128)(2,1)S(1)} %bitcast.44, ...), custom_call_target="tpu_custom_call" | custom-call | tf_op jit(solution)/shard_map/branch/pallas_call | solution.py:1657
  232.8 0.0 copy-start.1
  232.8 0.0 copy-start.6
  232.8 7.5 %convolution_convert_fusion.1.partial_ref = bf16[512,1536]{1,0:T(8,128)(2,1)} fusion(bf16[512,2048]{1,0:T(8,128)(2,1)} %get-tuple-element.69.feed_grads_hbm, bf16[1536,2048]{1,0:T(8,128)(2,1)S(1)} %bitcast.48), kind=kOutput, calls=%fused_computation.1 | convolution fusion | flops 3222011904 | bytes 9961472 | tf_op jit(solution)/shard_map/dot_general | solution.py:30
  240.3 3.6 convolution_convert_fusion
  243.9 143.6 %back.1 = (f32[128,1536]{1,0:T(8,128)}, f32[1,128,1536]{2,1,0:T(8,128)}, bf16[512,1664]{1,0:T(8,128)(2,1)}, bf16[4,48,2048]{2,1,0:T(8,128)(2,1)}, bf16[1,4,48,1536]{3,2,1,0:T(8,128)(2,1)}) custom-call(bf16[512,1536]{1,0:T(8,128)(2,1)} %convolution_convert_fusion.1.partial_ref, f32[128,1536]{1,0:T(8,128)} %copy-done.1, bf16[128,1536]{1,0:T(8,128)(2,1)} %bitcast.58, ...), custom_call_target="tpu_custom_call" | custom-call | tf_op jit(solution)/shard_map/back/pallas_call | solution.py:1426
  387.5 80.2 %finish.1 = (bf16[4,48,1664]{2,1,0:T(8,128)(2,1)}, bf16[48,1536]{1,0:T(8,128)(2,1)}, bf16[128,1536]{1,0:T(8,128)(2,1)}, bf16[128,1536]{1,0:T(8,128)(2,1)}) custom-call(bf16[4,4,2,48,1664]{4,3,2,1,0:T(8,128)(2,1)} %get-tuple-element.59.first_partial_ref, bf16[512,1536]{1,0:T(8,128)(2,1)} %get-tuple-element.60.tokens_hbm.wide_hbm, ...), custom_call_target="tpu_custom_call" | custom-call | tf_op jit(solution)/shard_map/finish/pallas_call | solution.py:1763
  467.7 5.0 %layout.1 = (f32[48,1536]{1,0:T(8,128)}, f32[48,1536]{1,0:T(8,128)}, f32[48,1536]{1,0:T(8,128)}, f32[48,1536]{1,0:T(8,128)}, f32[48,1536]{1,0:T(8,128)}, /*index...) custom-call(bf16[4,48,1664]{2,1,0:T(8,128)(2,1)} %get-tuple-element., ...), custom_call_target="tpu_custom_call" | custom-call | tf_op jit(solution)/shard_map/layout/pallas_call | solution.py:1841
  472.7 1.3 reshape.103
  (22 shorter events, 0.1 us)
Async XLA Ops:
  87.3 94.7 %copy-start.5 = (f32[1,1536]{1,0:T(1,128)}, f32[1,1536]{1,0:T(1,128)S(1)}, u32[]{:S(2)}) copy-start(f32[1,1536]{1,0:T(1,128)S(1)} %reshape.107.gain_ref) | copy-start | bytes 18436
  179.5 2.6 copy-start
  179.5 2.6 copy-start.4
  179.5 53.3 %slice-start = ((s8[6291456]{0:T(1024)(128)(4,1)}), s8[4194304]{0:T(1024)(128)(4,1)S(1)}, s32[]{:S(2)}) async-start(s8[6291456]{0:T(1024)(128)(4,1)} %bitcast.46), calls=%async_computation | async-start | bytes 8388608
  182.1 50.7 %slice-start.1 = ((s8[6291456]{0:T(1024)(128)(4,1)}), s8[2097152]{0:T(1024)(128)(4,1)S(1)}, s32[]{:S(2)}) async-start(s8[6291456]{0:T(1024)(128)(4,1)} %bitcast.46), calls=%async_computation.1 | async-start | bytes 4194304
  232.8 7.5 %copy-start.1 = (f32[128,1536]{1,0:T(8,128)}, f32[128,1536]{1,0:T(8,128)S(1)}, u32[]{:S(2)}) copy-start(f32[128,1536]{1,0:T(8,128)S(1)} %get-tuple-element.70.hidden_ref) | copy-start | bytes 2359300
  232.8 7.5 %copy-start.2 = (bf16[512,1536]{1,0:T(8,128)(2,1)}, bf16[512,1536]{1,0:T(8,128)(2,1)S(1)}, u32[]{:S(2)}) copy-start(bf16[512,1536]{1,0:T(8,128)(2,1)S(1)} %get-tuple-element.82.normed_hbm) | copy-start | bytes 4718596
  232.8 7.5 %copy-start.3 = (bf16[512,1024]{1,0:T(8,128)(2,1)}, bf16[512,1024]{1,0:T(8,128)(2,1)S(1)}, u32[]{:S(2)}) copy-start(bf16[512,1024]{1,0:T(8,128)(2,1)S(1)} %get-tuple-element.81.active_ref) | copy-start | bytes 3145732
  232.8 7.5 %copy-start.6 = (bf16[512,1536]{1,0:T(8,128)(2,1)S(1)}, bf16[512,1536]{1,0:T(8,128)(2,1)}, u32[]{:S(2)}) copy-start(bf16[512,1536]{1,0:T(8,128)(2,1)} %get-tuple-element.67.cotangent_hbm) | copy-start | bytes 4718596
